TPU v7x, 32 devices: a whole 2x2x4 slice. The times are simulated.
32 devices in a mesh: section: 2 (over x), tensor: 4 (over z), replica: 4 (over y, core).
Axes of the slice: x: 2, y: 2, z: 4, core: 2. Of those that a mesh axis runs over, the one named last changes fastest.
Arguments:
- state: bfloat16 [2, 4, 8192], P('section', None, 'replica'), may hold values from -6 to 6
- next_embed: bfloat16 [2, 4, 8192], P(None, None, 'replica'), may hold values from -6 to 6
- tenant: int32 [2, 4], replicated, may hold values from 0 to 399
- lengths: int32 [2, 4], P(None, 'replica'), may hold values from 1 to 64, 160 in all within a row
- gain: bfloat16 [2, 400, 8192], P('section', 'tensor', 'replica'), may hold values from 0.099609375 to 1.8984375
- bias: bfloat16 [2, 400, 8192], P('section', 'tensor', 'replica'), may hold values from -3 to 3
- wq: bfloat16 [2, 8192, 8192], P('section', 'replica', 'tensor'), may hold values from -0.0625 to 0.0625
- wo: bfloat16 [2, 8192, 8192], P('section', 'tensor', 'replica'), may hold values from -0.0625 to 0.0625
- keys: bfloat16 [2, 2, 4, 8, 64, 128], P('section', None, 'replica', None, 'tensor'), may hold values from -300 to 300
- values: bfloat16 [2, 2, 4, 8, 64, 128], P('section', None, 'replica', None, 'tensor'), may hold values from -6 to 6
Outputs:
- state_out: bfloat16 [2, 4, 8192], P('section', None, 'replica')
- emitted: bfloat16 [2, 4, 8192], P('section', None, 'replica')
Inputs may be any that keep to these rules, and one draw needn't show every extreme that they name: Each entry lengths[m, r] is the length of one row's cache, between 1 and 64. The total is not per row: the 4 entries of one micro-batch m (the row lengths[m] of the array) add up to 160, and one row of every micro-batch has all 64 positions.
All inputs are finite; a program needn't handle non-finite values. No bound on the sum of `lengths` on one device may be relied on, other than what follows from the above.
Results may differ from a plain program's by a relative error of at most 0.02.
Values may be sent and summed in bfloat16 or wider, within the bound.
No kernel may reach another device: no remote copies, remote signals or barrier semaphores. Data moves between devices by JAX's collectives and lax.ppermute only.
A program may use at most 64 MiB of HBM per device.

v0:
```python
import jax
import jax.numpy as jnp
from jax import lax
from jax.sharding import PartitionSpec as P

HD = 128


def merged(value, axis, join):
    pieces = jax.tree.map(lambda part: lax.all_gather(part, axis), value)
    head = jax.tree.map(lambda part: part[0], pieces)
    tail = jax.tree.map(lambda part: part[1:], pieces)
    running, _ = lax.scan(lambda running, slab: (join(running, slab), None), head, tail)
    return running


def from_behind(block, axis, distance):
    devices = range(lax.axis_size(axis))
    route = [((i - distance) % len(devices), i) for i in devices]
    return lax.ppermute(block, axis, route)


def combine_parts(first, second):
    top = jnp.maximum(first[0], second[0])
    scale_a = jnp.exp(first[0] - top)
    scale_b = jnp.exp(second[0] - top)
    total = first[1] * scale_a + second[1] * scale_b
    acc = first[2] * scale_a[..., None] + second[2] * scale_b[..., None]
    return (top, total, acc)


def on_device(state, next_embed, tenant, lengths, gain, bias, wq, wo, keys, values):
    sections = lax.axis_size("section")
    section_at = lax.axis_index("section")
    tensor_at = lax.axis_index("tensor")
    rows_mb = state.shape[1]
    width_part = state.shape[2]
    width_all = width_part * lax.axis_size("replica")
    rows_dev = rows_mb // lax.axis_size("replica")
    query_part = wq.shape[2]
    pos_dev = keys.shape[4]
    head_count = query_part * lax.axis_size("tensor") // HD
    key_heads = keys.shape[3]
    batches = tenant.shape[0]
    flat_ids = tenant.reshape(-1)
    tables = (
        lax.all_gather(gain[0], "tensor", axis=0, tiled=True),
        lax.all_gather(bias[0], "tensor", axis=0, tiled=True),
    )
    onehot = (flat_ids[:, None] == jnp.arange(tables[0].shape[0])[None, :]).astype(jnp.bfloat16)
    gain_rows = jnp.dot(onehot, tables[0], preferred_element_type=jnp.float32)
    bias_rows = jnp.dot(onehot, tables[1], preferred_element_type=jnp.float32)
    gain_rows = gain_rows.reshape(batches, rows_mb, width_part)
    bias_rows = bias_rows.reshape(batches, rows_mb, width_part)
    wq_layer = wq[0]
    wo_layer = wo[0]
    positions = tensor_at * pos_dev + jnp.arange(pos_dev)
    h = state[0]
    emitted = jnp.zeros_like(h)
    at_first = section_at == 0
    for tick in range(sections):
        batch = (section_at - tick) % sections
        hf = h.astype(jnp.float32)
        sums, squares = lax.psum((jnp.sum(hf, axis=-1), jnp.sum(hf * hf, axis=-1)), "replica")
        mean = (sums / width_all)[:, None]
        var = (squares / width_all)[:, None] - mean * mean
        gain_now = lax.dynamic_index_in_dim(gain_rows, batch, 0, keepdims=False)
        bias_now = lax.dynamic_index_in_dim(bias_rows, batch, 0, keepdims=False)
        normed = ((hf - mean) * lax.rsqrt(var + 1e-05) * gain_now + bias_now).astype(jnp.bfloat16)
        query_mine = lax.psum_scatter(
            jnp.dot(normed, wq_layer, preferred_element_type=jnp.float32),
            "replica",
            scatter_dimension=0,
            tiled=True,
        )
        query = lax.all_gather(query_mine.astype(jnp.bfloat16), "tensor", axis=1, tiled=True)
        grouped = query.reshape(rows_dev, key_heads, head_count // key_heads, HD)
        keys_now = lax.dynamic_index_in_dim(keys[0], batch, 0, keepdims=False)
        values_now = lax.dynamic_index_in_dim(values[0], batch, 0, keepdims=False)
        lengths_now = lax.dynamic_index_in_dim(lengths, batch, 0, keepdims=False)
        scores = jnp.einsum(
            "rgjd,rgpd->rgjp", grouped, keys_now, preferred_element_type=jnp.float32
        ) / jnp.sqrt(jnp.float32(HD))
        valid = positions[None, None, None, :] < lengths_now[:, None, None, None]
        scores = jnp.where(valid, scores, -1e30)
        top = jnp.max(scores, axis=-1)
        probs = jnp.exp(scores - top[..., None]) * valid.astype(jnp.float32)
        total = jnp.sum(probs, axis=-1)
        acc = jnp.einsum("rgjp,rgpd->rgjd", probs, values_now.astype(jnp.float32))
        top, total, acc = merged((top, total, acc), "tensor", combine_parts)
        att = (acc / total[..., None]).reshape(rows_dev, head_count * HD).astype(jnp.bfloat16)
        att_mine = lax.dynamic_slice_in_dim(att, tensor_at * query_part, query_part, 1)
        out_part = jnp.dot(
            lax.all_gather(att_mine, "replica", axis=0, tiled=True),
            wo_layer,
            preferred_element_type=jnp.float32,
        )
        out = lax.psum(out_part, "tensor")
        h = (hf + out).astype(jnp.bfloat16)
        h, emitted = from_behind((h, emitted), "section", 1)
        arriving = -(tick + 1) % sections
        emitted = jnp.where(at_first, h, emitted)
        h = jnp.where(at_first, next_embed[arriving], h)
    return (h[None], emitted[None])


def solution(mesh):
    in_specs = (
        P("section", None, "replica"),
        P(None, None, "replica"),
        P(),
        P(None, "replica"),
        P("section", "tensor", "replica"),
        P("section", "tensor", "replica"),
        P("section", "replica", "tensor"),
        P("section", "tensor", "replica"),
        P("section", None, "replica", None, "tensor", None),
        P("section", None, "replica", None, "tensor", None),
    )
    out_specs = (P("section", None, "replica"), P("section", None, "replica"))
    return jax.shard_map(
        on_device, mesh=mesh, in_specs=in_specs, out_specs=out_specs, check_vma=False
    )
```

profile of v0, /device:TPU:0, one launch (start us, length us, event | category | flops | bytes accessed | tf_op | source)
XLA Modules:
  0.0 363.1 jit_solution(109691792063303435)
XLA Ops:
  7.2 2.5 copy.32
  9.8 2.6 copy.33
  12.4 0.8 convert_reduce_fusion.1
  13.3 0.8 fusion.28
  14.1 3.0 collective-permute-start.2
  17.1 6.3 %all-reduce.3 = (f32[4]{0:T(128)S(1)}, f32[4]{0:T(128)S(1)}) all-reduce(f32[4]{0:T(128)S(1)} %fusion.28, f32[4]{0:T(128)S(1)} %convert_reduce_fusion.1), channel_id=1, replica_groups=mesh['section'=2,'tensor'=4,'replica'=4] {'replica'}, use_global_device_ids=true, to_apply=%region_3.4 | all-reduce | flops 8 | bytes 64 | tf_op jit(solution)/shard_map/psum | solution.py:64
  23.4 0.8 eq.22
  24.2 1.2 dynamic-slice.4
  25.4 1.3 constant_dynamic-slice_fusion
  26.8 0.6 fusion.83
  27.4 51.0 %all-gather.13.cloned.1.call-done = bf16[1,400,2048]{2,0,1:T(2,128)(2,1)} async-done(((bf16[1,100,2048]{2,0,1:T(2,128)(2,1)}), bf16[1,400,2048]{2,0,1:T(2,128)(2,1)}) %all-gather.13.cloned.1.call-update) | async-done | bytes 1638416 | tf_op jit(solution)/shard_map/all_gather | solution.py:47
  78.3 2.9 fusion.21
  81.2 63.0 %all-gather.15.cloned.1.call-done = bf16[1,400,2048]{2,0,1:T(2,128)(2,1)} async-done(((bf16[1,100,2048]{2,0,1:T(2,128)(2,1)}), bf16[1,400,2048]{2,0,1:T(2,128)(2,1)}) %all-gather.15.cloned.1.call-update) | async-done | bytes 1638416 | tf_op jit(solution)/shard_map/all_gather | solution.py:48
  144.2 2.9 fusion.18
  147.2 4.6 %fusion.16 = f32[4,2048]{1,0:T(4,128)S(1)} fusion(bf16[1,2048,2048]{2,1,0:T(8,128)(2,1)} %param.20, bf16[1,4,2048]{2,1,0:T(4,128)(2,1)} %param.14, f32[2,4,2048]{2,1,0:T(4,128)S(1)} %reshape.210, s32[]{:T(128)S(6)} %select_n.63, f32[2,4,2048]{2,1,0:T(4,128)S(1)} %reshape.209, f32[4]{0:T(128)S(1)} %get-tuple-element.192, f32[4]{0:T(128)S(1)} %get-tuple-element.191), kind=kOutput, calls=%fused_computation.26 | convolution fusion | flops 33603584 | bytes 8504324 | tf_op jit(solution)/shard_map/dot_general | solution.py:71
  151.8 11.4 %all-reduce = bf16[4,2048]{1,0:T(4,128)(2,1)S(1)} all-reduce(f32[4,2048]{1,0:T(4,128)S(1)} %fusion.16), channel_id=10, replica_groups=mesh['section'=2,'tensor'=4,'replica'=4] {'replica'}, use_global_device_ids=true, to_apply=%region_4.5.clone | all-reduce | flops 8192 | bytes 49152
  163.2 0.6 dynamic-slice_convert_fusion.1
  163.8 13.1 %all_gather.56 = bf16[1,8192]{1,0:T(2,128)(2,1)S(1)} all-gather(bf16[1,2048]{1,0:T(2,128)(2,1)S(1)} %dynamic-slice_convert_fusion.1), channel_id=1, replica_groups=mesh['section'=2,'tensor'=4,'replica'=4] {'tensor'}, dimensions={1}, use_global_device_ids=true | all-gather | bytes 20480 | tf_op jit(solution)/shard_map/all_gather | solution.py:76
  177.1 0.2 fusion.85
  177.5 13.3 %all-gather.4 = f32[32,8,128]{2,1,0:T(8,128)S(1)} all-gather(f32[8,8,128]{2,1,0:T(8,128)S(1)} %fusion.43), channel_id=6, replica_groups=mesh['section'=2,'tensor'=4,'replica'=4] {'tensor'}, dimensions={0}, use_global_device_ids=true | all-gather | bytes 163840 | tf_op jit(solution)/shard_map/all_gather | solution.py:10
  191.0 13.1 %all-gather.3 = f32[32,8]{1,0:T(8,128)S(1)} all-gather(f32[8,8]{1,0:T(8,128)S(1)} %fusion.50), channel_id=5, replica_groups=mesh['section'=2,'tensor'=4,'replica'=4] {'tensor'}, dimensions={0}, use_global_device_ids=true | all-gather | bytes 1280 | tf_op jit(solution)/shard_map/all_gather | solution.py:10
  204.1 13.1 %all-gather.2 = f32[32,8]{1,0:T(8,128)S(1)} all-gather(f32[8,8]{1,0:T(8,128)S(1)} %get-tuple-element.193), channel_id=4, replica_groups=mesh['section'=2,'tensor'=4,'replica'=4] {'tensor'}, dimensions={0}, use_global_device_ids=true | all-gather | bytes 1280 | tf_op jit(solution)/shard_map/all_gather | solution.py:10
  217.3 0.5 while.28
  217.9 5.2 %all-gather.8 = bf16[4,1,2048]{2,1,0:T(2,128)(2,1)S(1)} all-gather(bf16[1,1,2048]{2,1,0:T(2,128)(2,1)S(1)} %dynamic-slice_bitcast_fusion.1), channel_id=1, replica_groups=mesh['section'=2,'tensor'=4,'replica'=4] {'replica'}, dimensions={0}, use_global_device_ids=true | all-gather | bytes 20480 | tf_op jit(solution)/shard_map/all_gather | solution.py:94
  223.1 4.6 %fusion.12 = f32[4,2048]{1,0:T(4,128)S(1)} fusion(bf16[1,2048,2048]{2,1,0:T(8,128)(2,1)} %param.21, bf16[4,1,2048]{2,1,0:T(2,128)(2,1)S(1)} %all-gather.8), kind=kOutput, calls=%fused_computation.22 | convolution fusion | flops 33554432 | bytes 8437760 | tf_op jit(solution)/shard_map/dot_general | solution.py:93
  227.7 16.7 %psum.44 = f32[4,2048]{1,0:T(4,128)S(1)} all-reduce(f32[4,2048]{1,0:T(4,128)S(1)} %fusion.12), channel_id=1, replica_groups=mesh['section'=2,'tensor'=4,'replica'=4] {'tensor'}, use_global_device_ids=true, to_apply=%region_9.10 | all-reduce | flops 8192 | bytes 65536 | tf_op jit(solution)/shard_map/psum | solution.py:98
  244.4 1.5 collective-permute-start
  245.9 0.6 fusion.81
  246.4 1.8 collective-permute-done
  248.4 5.7 %all-reduce.2 = (f32[4]{0:T(128)S(1)}, f32[4]{0:T(128)S(1)}) all-reduce(f32[4]{0:T(128)S(1)} %get-tuple-element.139, f32[4]{0:T(128)S(1)} %get-tuple-element.138), channel_id=1, replica_groups=mesh['section'=2,'tensor'=4,'replica'=4] {'replica'}, use_global_device_ids=true, to_apply=%region_13.14 | all-reduce | flops 8 | bytes 64 | tf_op jit(solution)/shard_map/psum | solution.py:64
  254.0 4.6 %fusion.14 = f32[4,2048]{1,0:T(4,128)S(1)} fusion(bf16[1,2048,2048]{2,1,0:T(8,128)(2,1)} %param.20, bf16[4,2048]{1,0:T(4,128)(2,1)S(1)} %get-tuple-element.178, f32[2,4,2048]{2,1,0:T(4,128)S(1)} %reshape.210, s32[]{:T(128)S(6)} %select_n.68, f32[2,4,2048]{2,1,0:T(4,128)S(1)} %reshape.209, f32[4]{0:T(128)S(1)} %get-tuple-element.190, ...), kind=kOutput, calls=%fused_computation.24 | convolution fusion | flops 33603584 | bytes 8504324 | tf_op jit(solution)/shard_map/dot_general | solution.py:71
  258.6 10.6 %all-reduce.1 = bf16[4,2048]{1,0:T(4,128)(2,1)S(1)} all-reduce(f32[4,2048]{1,0:T(4,128)S(1)} %fusion.14), channel_id=11, replica_groups=mesh['section'=2,'tensor'=4,'replica'=4] {'replica'}, use_global_device_ids=true, to_apply=%region_14.15.clone | all-reduce | flops 8192 | bytes 49152
  269.2 0.6 dynamic-slice_convert_fusion
  269.9 13.1 %all_gather.64 = bf16[1,8192]{1,0:T(2,128)(2,1)S(1)} all-gather(bf16[1,2048]{1,0:T(2,128)(2,1)S(1)} %dynamic-slice_convert_fusion), channel_id=1, replica_groups=mesh['section'=2,'tensor'=4,'replica'=4] {'tensor'}, dimensions={1}, use_global_device_ids=true | all-gather | bytes 20480 | tf_op jit(solution)/shard_map/all_gather | solution.py:76
  283.1 0.2 fusion.86
  283.3 0.2 fusion.40
  283.5 13.4 %all-gather.7 = f32[32,8,128]{2,1,0:T(8,128)S(1)} all-gather(f32[8,8,128]{2,1,0:T(8,128)S(1)} %fusion.40), channel_id=9, replica_groups=mesh['section'=2,'tensor'=4,'replica'=4] {'tensor'}, dimensions={0}, use_global_device_ids=true | all-gather | bytes 163840 | tf_op jit(solution)/shard_map/all_gather | solution.py:10
  297.0 13.1 %all-gather.6 = f32[32,8]{1,0:T(8,128)S(1)} all-gather(f32[8,8]{1,0:T(8,128)S(1)} %fusion.51), channel_id=8, replica_groups=mesh['section'=2,'tensor'=4,'replica'=4] {'tensor'}, dimensions={0}, use_global_device_ids=true | all-gather | bytes 1280 | tf_op jit(solution)/shard_map/all_gather | solution.py:10
  310.2 13.1 %all-gather.5 = f32[32,8]{1,0:T(8,128)S(1)} all-gather(f32[8,8]{1,0:T(8,128)S(1)} %get-tuple-element.195), channel_id=7, replica_groups=mesh['section'=2,'tensor'=4,'replica'=4] {'tensor'}, dimensions={0}, use_global_device_ids=true | all-gather | bytes 1280 | tf_op jit(solution)/shard_map/all_gather | solution.py:10
  323.3 0.5 while.29
  323.9 5.2 %all-gather.9 = bf16[4,1,2048]{2,1,0:T(2,128)(2,1)S(1)} all-gather(bf16[1,1,2048]{2,1,0:T(2,128)(2,1)S(1)} %dynamic-slice_bitcast_fusion), channel_id=1, replica_groups=mesh['section'=2,'tensor'=4,'replica'=4] {'replica'}, dimensions={0}, use_global_device_ids=true | all-gather | bytes 20480 | tf_op jit(solution)/shard_map/all_gather | solution.py:94
  329.1 4.6 %fusion.10 = f32[4,2048]{1,0:T(4,128)S(1)} fusion(bf16[1,2048,2048]{2,1,0:T(8,128)(2,1)} %param.21, bf16[4,1,2048]{2,1,0:T(2,128)(2,1)S(1)} %all-gather.9), kind=kOutput, calls=%fused_computation.20 | convolution fusion | flops 33554432 | bytes 8437760 | tf_op jit(solution)/shard_map/dot_general | solution.py:93
  333.7 16.8 %psum.47 = f32[4,2048]{1,0:T(4,128)S(1)} all-reduce(f32[4,2048]{1,0:T(4,128)S(1)} %fusion.10), channel_id=1, replica_groups=mesh['section'=2,'tensor'=4,'replica'=4] {'tensor'}, use_global_device_ids=true, to_apply=%region_19.20 | all-reduce | flops 8192 | bytes 65536 | tf_op jit(solution)/shard_map/psum | solution.py:98
  350.5 1.3 collective-permute-start.1
  351.8 0.8 collective-permute-start.3
  352.7 1.6 collective-permute-done.1
  354.3 1.3 collective-permute-done.3
  355.6 0.6 select_bitcast_fusion
  (69 shorter events, 2.1 us)
Async XLA Ops:
  7.2 170.1 %copy-start = (bf16[1,2,1,8,16,128]{5,4,3,2,1,0:T(8,128)(2,1)S(1)}, bf16[1,2,1,8,16,128]{5,4,3,2,1,0:T(8,128)(2,1)}, u32[]{:S(2)}) copy-start(bf16[1,2,1,8,16,128]{5,4,3,2,1,0:T(8,128)(2,1)} %param.23) | copy-start | bytes 196612
  7.2 71.1 %all-gather.13.cloned.1.call-start = ((), (), s32[]{:S(2)}) async-start(), calls=%async_computation | async-start | bytes 4096000 | tf_op jit(solution)/shard_map/all_gather | solution.py:47
  9.8 134.5 %all-gather.15.cloned.1.call-start = ((), (), s32[]{:S(2)}) async-start(), calls=%async_computation.1 | async-start | bytes 4096000 | tf_op jit(solution)/shard_map/all_gather | solution.py:48
  14.1 337.7 %collective-permute-start.2 = (bf16[4,2048]{1,0:T(4,128)(2,1)S(1)}, bf16[4,2048]{1,0:T(4,128)(2,1)S(1)}, u32[]{:S(2)}, u32[]{:S(2)}) collective-permute-start(bf16[4,2048]{1,0:T(4,128)(2,1)S(1)} %broadcast_in_dim.48), channel_id=1, source_target_pairs={{16,0},{0,16},{17,1},{1,17},{18,2},{2,18},{19,3},{3,19},{20,4},{4,... | collective-permute-start | bytes 49160 | tf_op jit(solution)/shard_map/ppermute | solution.py:20
  147.1 29.9 %copy-start.2 = (bf16[1,2,1,8,16,128]{5,4,3,2,1,0:T(8,128)(2,1)S(1)}, bf16[1,2,1,8,16,128]{5,4,3,2,1,0:T(8,128)(2,1)}, u32[]{:S(2)}) copy-start(bf16[1,2,1,8,16,128]{5,4,3,2,1,0:T(8,128)(2,1)} %param.22) | copy-start | bytes 196612
  217.2 27.1 %copy-start.1 = (bf16[1,4,2048]{2,1,0:T(4,128)(2,1)S(1)}, bf16[1,4,2048]{2,1,0:T(4,128)(2,1)}, u32[]{:S(2)}) copy-start(bf16[1,4,2048]{2,1,0:T(4,128)(2,1)} %param.14) | copy-start | bytes 49156
  217.3 30.9 %copy-start.3 = (bf16[2,4,2048]{2,1,0:T(4,128)(2,1)S(1)}, bf16[2,4,2048]{2,1,0:T(4,128)(2,1)}, u32[]{:S(2)}) copy-start(bf16[2,4,2048]{2,1,0:T(4,128)(2,1)} %param.15) | copy-start | bytes 98308
  244.4 3.8 %collective-permute-start = (bf16[4,2048]{1,0:T(4,128)(2,1)S(1)}, bf16[4,2048]{1,0:T(4,128)(2,1)S(1)}, u32[]{:S(2)}, u32[]{:S(2)}) collective-permute-start(bf16[4,2048]{1,0:T(4,128)(2,1)S(1)} %fusion.29), channel_id=1, source_target_pairs={{16,0},{0,16},{17,1},{1,17},{18,2},{2,18},{19,3},{3,19},{20,4},{4,... | collective-permute-start | bytes 49160 | tf_op jit(solution)/shard_map/ppermute | solution.py:20
  350.5 3.8 %collective-permute-start.1 = (bf16[4,2048]{1,0:T(4,128)(2,1)S(1)}, bf16[4,2048]{1,0:T(4,128)(2,1)S(1)}, u32[]{:S(2)}, u32[]{:S(2)}) collective-permute-start(bf16[4,2048]{1,0:T(4,128)(2,1)S(1)} %fusion.39), channel_id=1, source_target_pairs={{16,0},{0,16},{17,1},{1,17},{18,2},{2,18},{19,3},{3,19},{20,4},{4,... | collective-permute-start | bytes 49160 | tf_op jit(solution)/shard_map/ppermute | solution.py:20
  351.8 3.8 %collective-permute-start.3 = (bf16[4,2048]{1,0:T(4,128)(2,1)S(1)}, bf16[4,2048]{1,0:T(4,128)(2,1)S(1)}, u32[]{:S(2)}, u32[]{:S(2)}) collective-permute-start(bf16[4,2048]{1,0:T(4,128)(2,1)S(1)} %broadcast_select_fusion), channel_id=1, source_target_pairs={{16,0},{0,16},{17,1},{1,17},{18,2},{2,18},{19,3},{3,19},{20,4},{4,... | collective-permute-start | bytes 49160 | tf_op jit(solution)/shard_map/ppermute | solution.py:20
Sparse Core Ops, SparseCore 0:
  9.9 68.3 all-gather.12
  79.9 64.3 all-gather.14
where the time goes:
time: 364 us; the launch traced here: 363 us
  blocking collectives  183 us (50%)
  waiting for transfers between devices  119 us (33%)
  matrix products  25 us (7%)
  between operations  14.3 us (4%)
  local copies, waits for them, and re-layouts  9.92 us (3%)
  starting transfers between devices  6.73 us (2%)
  other arithmetic  5.04 us (1%)
    all_gather x6, blocking collectives, merged(): pieces = jax.tree.map(lambda part: lax.all_gather(part, axis), value)  79.2 us
    all_gather x1, waiting for transfers between devices, on_device(): lax.all_gather(bias[0], 'tensor', axis=0, tiled=True)  63 us
    all_gather x1, waiting for transfers between devices, on_device(): lax.all_gather(gain[0], 'tensor', axis=0, tiled=True)  51 us
    psum x2, blocking collectives, on_device(): out = lax.psum(out_part, 'tensor')  33.5 us
    all_gather x2, blocking collectives, on_device(): lax.all_gather(query_mine.astype(jnp.bfloat16), 'tensor', axis=1, tiled=T...  26.3 us
    unnamed x2, blocking collectives  22 us
    psum x2, blocking collectives, on_device(): lax.psum((jnp.sum(hf, axis=-1), jnp.sum(hf * hf, axis=-1)), 'replica')  12 us
    all_gather x2, blocking collectives, on_device(): lax.all_gather(att_mine, 'replica', axis=0, tiled=True)  10.4 us
  transfers between devices with their start and end apart: 6, of which 5 were waited for; matrix products, arithmetic and copies ran while one was open for 10% of the time, Pallas kernels for 0%

commit v1 on v0

v1 whole, which is shorter than its diff:
```python
import jax
import jax.numpy as jnp
from jax import lax
from jax.sharding import PartitionSpec as P

HD = 128
BF = jnp.bfloat16
F32 = jnp.float32


def swapped(block, axis, bits):
    route = [(i, i ^ bits) for i in range(lax.axis_size(axis))]
    return lax.ppermute(block, axis, route)


def peers(block, axis):
    return [block] + [swapped(block, axis, d) for d in range(1, lax.axis_size(axis))]


def tree_sum(pieces):
    pieces = [piece.astype(F32) for piece in pieces]
    while len(pieces) > 1:
        pieces = [pieces[i] + pieces[i + 1] for i in range(0, len(pieces), 2)]
    return pieces[0]


def unswap(rows, place):
    count = rows.shape[0]
    bit = 1
    while bit < count:
        flipped = rows.reshape((count // (2 * bit), 2, bit) + rows.shape[1:])[:, ::-1].reshape(rows.shape)
        rows = jnp.where((place & bit) > 0, flipped, rows)
        bit *= 2
    return rows


def on_device(state, next_embed, tenant, lengths, gain, bias, wq, wo, keys, values):
    sections = lax.axis_size("section")
    tensors = lax.axis_size("tensor")
    section_at = lax.axis_index("section")
    tensor_at = lax.axis_index("tensor")
    replica_at = lax.axis_index("replica")
    rows_mb = state.shape[1]
    width_part = state.shape[2]
    width_all = width_part * lax.axis_size("replica")
    query_part = wq.shape[2]
    heads_dev = query_part // HD
    key_heads = keys.shape[3]
    group = heads_dev * tensors // key_heads
    kv_dev = max(1, heads_dev // group)
    per_kv = heads_dev // kv_dev
    pos_dev = keys.shape[4]
    batches = tenant.shape[0]
    order = jnp.stack([(section_at - tick) % sections for tick in range(sections)])

    ids = tenant[order].reshape(-1)
    local = ids - tensor_at * gain.shape[1]
    onehot = (local[:, None] == jnp.arange(gain.shape[1])[None, :]).astype(BF)
    gain_mine = jnp.dot(onehot, gain[0], preferred_element_type=F32).astype(BF)
    bias_mine = jnp.dot(onehot, bias[0], preferred_element_type=F32).astype(BF)
    affine = jnp.stack([gain_mine, bias_mine], 0).reshape(2, sections, rows_mb, width_part)
    affine = tree_sum(peers(affine, "tensor"))

    kv = jnp.stack([keys[0, :, 0], values[0, :, 0]], 0)

    def heads_of(place):
        start = place * heads_dev // group
        return lax.dynamic_slice_in_dim(kv, start, kv_dev, 2)

    parts = [heads_of(tensor_at)]
    spots = [tensor_at * pos_dev + jnp.arange(pos_dev)]
    for d in range(1, tensors):
        parts.append(swapped(heads_of(tensor_at ^ d), "tensor", d))
        spots.append((tensor_at ^ d) * pos_dev + jnp.arange(pos_dev))
    kv = jnp.concatenate(parts, 3)
    spots = jnp.concatenate(spots)
    kv_rows = unswap(jnp.stack(peers(kv, "replica"), 0), replica_at)
    length_rows = unswap(jnp.stack(peers(lengths[:, 0].astype(F32), "replica"), 0), replica_at)

    h = state[0]
    emitted = jnp.zeros_like(h)
    at_first = section_at == 0
    for tick in range(sections):
        batch = order[tick]
        hf = h.astype(F32)
        stats = jnp.stack([jnp.sum(hf, axis=-1), jnp.sum(hf * hf, axis=-1)], 0)
        stats = tree_sum(peers(stats, "replica")) / width_all
        mean = stats[0][:, None]
        var = stats[1][:, None] - mean * mean
        normed = ((hf - mean) * lax.rsqrt(var + 1e-05) * affine[0, tick] + affine[1, tick]).astype(BF)
        query_part_sum = jnp.dot(normed, wq[0], preferred_element_type=F32).astype(BF)
        query = tree_sum(peers(query_part_sum, "replica")).astype(BF)
        grouped = query.reshape(rows_mb, kv_dev, per_kv, HD)
        kv_now = lax.dynamic_index_in_dim(kv_rows, batch, 2, keepdims=False)
        lengths_now = lax.dynamic_index_in_dim(length_rows, batch, 1, keepdims=False)
        scores = jnp.einsum("rgjd,rgpd->rgjp", grouped, kv_now[:, 0], preferred_element_type=F32)
        scores = scores / jnp.sqrt(F32(HD))
        valid = spots.astype(F32)[None, None, None, :] < lengths_now[:, None, None, None]
        scores = jnp.where(valid, scores, -1e30)
        top = jnp.max(scores, axis=-1, keepdims=True)
        probs = jnp.exp(scores - top) * valid.astype(F32)
        weight = probs / jnp.sum(probs, axis=-1, keepdims=True)
        att = jnp.einsum("rgjp,rgpd->rgjd", weight, kv_now[:, 1].astype(F32))
        att = att.reshape(rows_mb, query_part).astype(BF)
        out = jnp.dot(att, wo[0], preferred_element_type=F32).astype(BF)
        out = tree_sum(peers(out, "tensor"))
        h = (hf + out).astype(BF)
        ring = [(i, (i + 1) % sections) for i in range(sections)]
        h = lax.ppermute(h, "section", ring)
        if tick > 0:
            emitted = lax.ppermute(emitted, "section", ring)
        arriving = -(tick + 1) % sections
        emitted = jnp.where(at_first, h, emitted)
        h = jnp.where(at_first, next_embed[arriving], h)
    return (h[None], emitted[None])


def solution(mesh):
    in_specs = (
        P("section", None, "replica"),
        P(None, None, "replica"),
        P(),
        P(None, "replica"),
        P("section", "tensor", "replica"),
        P("section", "tensor", "replica"),
        P("section", "replica", "tensor"),
        P("section", "tensor", "replica"),
        P("section", None, "replica", None, "tensor", None),
        P("section", None, "replica", None, "tensor", None),
    )
    out_specs = (P("section", None, "replica"), P("section", None, "replica"))
    return jax.shard_map(
        on_device, mesh=mesh, in_specs=in_specs, out_specs=out_specs, check_vma=False
    )
```

time: 364 us -> 86 us (0.24)
  blocking collectives: 183 us -> 0 us
  waiting for transfers between devices: 119 us -> 21.3 us
  starting transfers between devices: 6.73 us -> 35.2 us
  between operations: 14.3 us -> 0.92 us
  local copies, waits for them, and re-layouts: 9.92 us -> 2.13 us
  matrix products: 25 us -> 21 us
    all_gather x10 -> x0, blocking collectives: 116 us -> none  [the longest x6 79.2 us: merged(): pieces = jax.tree.map(lambda part: lax.all_gather(part, axis), value)]
    all_gather x2 -> x0, waiting for transfers between devices: 114 us -> none  [the longest x1 63 us: on_device(): lax.all_gather(bias[0], 'tensor', axis=0, tiled=True)]
    psum x4 -> x0, blocking collectives: 45.4 us -> none  [the longest x2 33.5 us: on_device(): out = lax.psum(out_part, 'tensor')]
    ppermute x4 -> x33, starting transfers between devices: 6.65 us -> 35.2 us  [the longest x30 30.5 us: swapped(): return lax.ppermute(block, axis, route)]
    unnamed x2 -> x0, blocking collectives: 22 us -> none
    ppermute x4 -> x33, waiting for transfers between devices: 4.72 us -> 21.3 us  [the longest x30 16.8 us: swapped(): return lax.ppermute(block, axis, route)]
    unnamed x15 -> x7, local copies, waits for them, and re-layouts: 6.46 us -> 0.04 us
    dot_general x10 -> x8, matrix products: 25 us -> 20.3 us  [the longest x2 9.24 us: on_device(): jnp.dot(normed, wq[0], preferred_element_type=F32).astype(BF)]
  transfers between devices with their start and end apart: 6 -> 33, of which waited for: 5 -> 15; matrix products, arithmetic and copies ran while one was open for 10% -> 13% of each run, Pallas kernels for 0% -> 0%
where the time goes in v1:
time: 86 us; the launch traced here: 85.5 us
  starting transfers between devices  35.2 us (41%)
  waiting for transfers between devices  21.3 us (25%)
  matrix products  21 us (24%)
  other arithmetic  5.01 us (6%)
  local copies, waits for them, and re-layouts  2.13 us (2%)
  between operations  0.92 us (1%)
    ppermute x30, starting transfers between devices, swapped(): return lax.ppermute(block, axis, route)  30.5 us
    ppermute x30, waiting for transfers between devices, swapped(): return lax.ppermute(block, axis, route)  16.8 us
    dot_general x2, matrix products, on_device(): jnp.dot(normed, wq[0], preferred_element_type=F32).astype(BF)  9.24 us
    dot_general x2, matrix products, on_device(): out = jnp.dot(att, wo[0], preferred_element_type=F32).astype(BF)  9.16 us
    ppermute x2, waiting for transfers between devices, on_device(): h = lax.ppermute(h, 'section', ring)  4.06 us
    ppermute x2, starting transfers between devices, on_device(): h = lax.ppermute(h, 'section', ring)  3.11 us
    reduce_sum x3, other arithmetic, on_device(): stats = jnp.stack([jnp.sum(hf, axis=-1), jnp.sum(hf * hf, axis=-1)], 0)  1.86 us
  transfers between devices with their start and end apart: 33, of which 15 were waited for; matrix products, arithmetic and copies ran while one was open for 13% of the time, Pallas kernels for 0%

profile of v1, /device:TPU:0, one launch (start us, length us, event | category | flops | bytes accessed | tf_op | source)
XLA Modules:
  0.0 85.5 jit_solution(17102733451519491892)
XLA Ops:
  0.6 0.7 convert_bitcast_fusion.3
  1.4 2.4 %collective-permute-start.2 = (f32[2]{0:T(128)S(1)}, f32[2]{0:T(128)S(1)}, u32[]{:S(2)}, u32[]{:S(2)}) collective-permute-start(f32[2]{0:T(128)S(1)} %get-tuple-element.24), channel_id=1, source_target_pairs={{0,3},{1,2},{2,1},{3,0},{4,7},{5,6},{6,5},{7,4},{8,11},{9,10},{10,... | collective-permute-start | bytes 32 | tf_op jit(solution)/shard_map/ppermute | solution.py:13
  3.8 0.6 collective-permute-start.1
  4.5 1.2 %gather_fusion = s32[2,4]{1,0:T(2,128)S(1)} fusion(s32[2,4]{1,0:T(2,128)} %param.12, s32[1024]{0:T(1024)S(1)} %pad_clamp_fusion), kind=kCustom, calls=%fused_computation | custom fusion | bytes 72 | tf_op jit(solution)/shard_map/gather | solution.py:56
  6.1 1.2 %convolution_convert_fusion = bf16[8,2048]{1,0:T(8,128)(2,1)S(1)} fusion(bf16[1,100,2048]{2,1,0:T(8,128)(2,1)} %param.15, s32[8]{0:T(128)S(1)} %sub.92), kind=kOutput, calls=%fused_computation.11 | convolution fusion | flops 3293984 | bytes 442400 | tf_op jit(solution)/shard_map/dot_general | solution.py:60
  7.4 3.9 %collective-permute-start.8 = (bf16[2,2,4,2048]{3,2,1,0:T(4,128)(2,1)S(1)}, bf16[2,2,4,2048]{3,2,1,0:T(4,128)(2,1)S(1)}, u32[]{:S(2)}, u32[]{:S(2)}) collective-permute-start(bf16[2,2,4,2048]{3,2,1,0:T(4,128)(2,1)S(1)} %constant_dynamic-update-slice_fusion), channel_id=1, source_target_pairs={{0,12},{4,8},{8,4},{12,0},{1,13},{5,9},{9,5},{13,1},{2,14},{6,10},... | collective-permute-start | bytes 196616 | tf_op jit(solution)/shard_map/ppermute | solution.py:13
  11.3 0.8 fusion.37
  12.2 0.8 convert_reduce_fusion.1
  13.2 0.9 fusion.51
  14.0 0.7 collective-permute-start.6
  14.7 1.7 %collective-permute-start.4 = (f32[2,4]{1,0:T(2,128)S(1)}, f32[2,4]{1,0:T(2,128)S(1)}, u32[]{:S(2)}, u32[]{:S(2)}) collective-permute-start(f32[2,4]{1,0:T(2,128)S(1)} %pad_maximum_fusion.3), channel_id=1, source_target_pairs={{0,2},{1,3},{2,0},{3,1},{4,6},{5,7},{6,4},{7,5},{8,10},{9,11},{10,... | collective-permute-start | bytes 104 | tf_op jit(solution)/shard_map/ppermute | solution.py:13
  17.0 1.3 %collective-permute-done.4 = f32[2,4]{1,0:T(2,128)S(1)} collective-permute-done((f32[2,4]{1,0:T(2,128)S(1)}, f32[2,4]{1,0:T(2,128)S(1)}, u32[]{:S(2)}, u32[]{:S(2)}) %collective-permute-start.4) | collective-permute-done | bytes 64 | tf_op jit(solution)/shard_map/ppermute | solution.py:13
  18.3 1.1 %collective-permute-done.5 = f32[2,4]{1,0:T(2,128)S(1)} collective-permute-done((f32[2,4]{1,0:T(2,128)S(1)}, f32[2,4]{1,0:T(2,128)S(1)}, u32[]{:S(2)}, u32[]{:S(2)}) %collective-permute-start.5) | collective-permute-done | bytes 64 | tf_op jit(solution)/shard_map/ppermute | solution.py:13
  19.4 3.6 %collective-permute-start.14 = (bf16[2,2,2,16,128]{4,3,2,1,0:T(8,128)(2,1)S(1)}, bf16[2,2,2,16,128]{4,3,2,1,0:T(8,128)(2,1)S(1)}, u32[]{:S(2)}, u32[]{:S(2)}) collective-permute-start(bf16[2,2,2,16,128]{4,3,2,1,0:T(8,128)(2,1)S(1)} %get-tuple-element.18), channel_id=1, source_target_pairs={{0,12},{4,8},{8,4},{12,0},{1,13},{5,9},{9,5},{13,1},{2,14},{6,10},... | collective-permute-start | bytes 98312 | tf_op jit(solution)/shard_map/ppermute | solution.py:13
  23.1 0.8 collective-permute-start.12
  23.9 4.6 %fusion.10 = bf16[4,2048]{1,0:T(4,128)(2,1)S(1)} fusion(bf16[1,2048,2048]{2,1,0:T(8,128)(2,1)} %param.16, bf16[1,4,2048]{2,1,0:T(4,128)(2,1)} %param.10, f32[2,2,4,2048]{3,2,1,0:T(4,128)S(1)} %bitcast.195, f32[4]{0:T(128)S(1)} %fusion.83, f32[4]{0:T(128)S(1)} %slice_bitcast_fusion.11), kind=kOutput, calls=%fused_computation.13 | convolution fusion | flops 33611776 | bytes 8487936 | tf_op jit(solution)/shard_map/dot_general | solution.py:91
  28.6 0.7 collective-permute-start.11
  29.3 0.8 collective-permute-start.10
  30.5 1.2 %collective-permute-start.17 = (bf16[2,2,2,64,128]{4,3,2,1,0:T(8,128)(2,1)S(1)}, bf16[2,2,2,64,128]{4,3,2,1,0:T(8,128)(2,1)S(1)}, u32[]{:S(2)}, u32[]{:S(2)}) collective-permute-start(bf16[2,2,2,64,128]{4,3,2,1,0:T(8,128)(2,1)S(1)} %get-tuple-element.14), channel_id=1, source_target_pairs={{0,3},{1,2},{2,1},{3,0},{4,7},{5,6},{6,5},{7,4},{8,11},{9,10},{10,... | collective-permute-start | bytes 393224 | tf_op jit(solution)/shard_map/ppermute | solution.py:13
  31.7 0.7 collective-permute-start.16
  32.4 0.7 collective-permute-done.10
  33.2 2.9 %collective-permute-done.17 = bf16[2,2,2,64,128]{4,3,2,1,0:T(8,128)(2,1)S(1)} collective-permute-done((bf16[2,2,2,64,128]{4,3,2,1,0:T(8,128)(2,1)S(1)}, bf16[2,2,2,64,128]{4,3,2,1,0:T(8,128)(2,1)S(1)}, u32[]{:S(2)}, u32[]{:S(2)}) %collective-permute-start.17) | collective-permute-done | bytes 131104 | tf_op jit(solution)/shard_map/ppermute | solution.py:13
  36.1 3.1 %collective-permute-done.16 = bf16[2,2,2,64,128]{4,3,2,1,0:T(8,128)(2,1)S(1)} collective-permute-done((bf16[2,2,2,64,128]{4,3,2,1,0:T(8,128)(2,1)S(1)}, bf16[2,2,2,64,128]{4,3,2,1,0:T(8,128)(2,1)S(1)}, u32[]{:S(2)}, u32[]{:S(2)}) %collective-permute-start.16) | collective-permute-done | bytes 131104 | tf_op jit(solution)/shard_map/ppermute | solution.py:13
  39.8 0.3 fusion.87
  40.4 4.6 %fusion.16 = bf16[4,2048]{1,0:T(4,128)(2,1)S(1)} fusion(bf16[1,2048,2048]{2,1,0:T(8,128)(2,1)} %param.17, bf16[1,4,16,128]{3,2,1,0:T(8,128)(2,1)S(1)} %fusion.30), kind=kOutput, calls=%fused_computation.15 | convolution fusion | flops 33562624 | bytes 8421376 | tf_op jit(solution)/shard_map/dot_general | solution.py:105
  45.0 3.6 %collective-permute-start.20 = (bf16[4,2048]{1,0:T(4,128)(2,1)S(1)}, bf16[4,2048]{1,0:T(4,128)(2,1)S(1)}, u32[]{:S(2)}, u32[]{:S(2)}) collective-permute-start(bf16[4,2048]{1,0:T(4,128)(2,1)S(1)} %fusion.16), channel_id=1, source_target_pairs={{0,12},{4,8},{8,4},{12,0},{1,13},{5,9},{9,5},{13,1},{2,14},{6,10},... | collective-permute-start | bytes 49160 | tf_op jit(solution)/shard_map/ppermute | solution.py:13
  48.6 0.8 collective-permute-start.18
  49.4 1.3 %collective-permute-done.20 = bf16[4,2048]{1,0:T(4,128)(2,1)S(1)} collective-permute-done((bf16[4,2048]{1,0:T(4,128)(2,1)S(1)}, bf16[4,2048]{1,0:T(4,128)(2,1)S(1)}, u32[]{:S(2)}, u32[]{:S(2)}) %collective-permute-start.20) | collective-permute-done | bytes 16416 | tf_op jit(solution)/shard_map/ppermute | solution.py:13
  50.6 2.6 %collective-permute-done.19 = bf16[4,2048]{1,0:T(4,128)(2,1)S(1)} collective-permute-done((bf16[4,2048]{1,0:T(4,128)(2,1)S(1)}, bf16[4,2048]{1,0:T(4,128)(2,1)S(1)}, u32[]{:S(2)}, u32[]{:S(2)}) %collective-permute-start.19) | collective-permute-done | bytes 16416 | tf_op jit(solution)/shard_map/ppermute | solution.py:13
  53.3 1.6 %collective-permute-start.21 = (bf16[4,2048]{1,0:T(4,128)(2,1)S(1)}, bf16[4,2048]{1,0:T(4,128)(2,1)S(1)}, u32[]{:S(2)}, u32[]{:S(2)}) collective-permute-start(bf16[4,2048]{1,0:T(4,128)(2,1)S(1)} %fusion.38), channel_id=1, source_target_pairs={{0,16},{16,0},{1,17},{17,1},{2,18},{18,2},{3,19},{19,3},{4,20},{20... | collective-permute-start | bytes 49160 | tf_op jit(solution)/shard_map/ppermute | solution.py:109
  54.8 2.2 %collective-permute-done.21 = bf16[4,2048]{1,0:T(4,128)(2,1)S(1)} collective-permute-done((bf16[4,2048]{1,0:T(4,128)(2,1)S(1)}, bf16[4,2048]{1,0:T(4,128)(2,1)S(1)}, u32[]{:S(2)}, u32[]{:S(2)}) %collective-permute-start.21) | collective-permute-done | bytes 16416 | tf_op jit(solution)/shard_map/ppermute | solution.py:109
  57.3 0.6 collective-permute-start.23
  57.9 1.6 %collective-permute-start.22 = (f32[2,4]{1,0:T(2,128)S(1)}, f32[2,4]{1,0:T(2,128)S(1)}, u32[]{:S(2)}, u32[]{:S(2)}) collective-permute-start(f32[2,4]{1,0:T(2,128)S(1)} %pad_maximum_fusion.4), channel_id=1, source_target_pairs={{0,1},{1,0},{2,3},{3,2},{4,5},{5,4},{6,7},{7,6},{8,9},{9,8},{10,11... | collective-permute-start | bytes 104 | tf_op jit(solution)/shard_map/ppermute | solution.py:13
  59.5 1.4 %collective-permute-done.23 = f32[2,4]{1,0:T(2,128)S(1)} collective-permute-done((f32[2,4]{1,0:T(2,128)S(1)}, f32[2,4]{1,0:T(2,128)S(1)}, u32[]{:S(2)}, u32[]{:S(2)}) %collective-permute-start.23) | collective-permute-done | bytes 64 | tf_op jit(solution)/shard_map/ppermute | solution.py:13
  60.9 4.6 %fusion.13 = bf16[4,2048]{1,0:T(4,128)(2,1)S(1)} fusion(bf16[1,2048,2048]{2,1,0:T(8,128)(2,1)} %param.16, bf16[4,2048]{1,0:T(4,128)(2,1)S(1)} %get-tuple-element.8, f32[2,2,4,2048]{3,2,1,0:T(4,128)S(1)} %bitcast.196, f32[4]{0:T(128)S(1)} %fusion.81, f32[4]{0:T(128)S(1)} %slice_bitcast_fusion.10), kind=kOutput, calls=%fused_computation.14 | convolution fusion | flops 33611776 | bytes 8487936 | tf_op jit(solution)/shard_map/dot_general | solution.py:91
  65.8 1.5 %collective-permute-start.26 = (bf16[4,2048]{1,0:T(4,128)(2,1)S(1)}, bf16[4,2048]{1,0:T(4,128)(2,1)S(1)}, u32[]{:S(2)}, u32[]{:S(2)}) collective-permute-start(bf16[4,2048]{1,0:T(4,128)(2,1)S(1)} %fusion.13), channel_id=1, source_target_pairs={{0,2},{1,3},{2,0},{3,1},{4,6},{5,7},{6,4},{7,5},{8,10},{9,11},{10,... | collective-permute-start | bytes 49160 | tf_op jit(solution)/shard_map/ppermute | solution.py:13
  67.5 1.2 %collective-permute-done.27 = bf16[4,2048]{1,0:T(4,128)(2,1)S(1)} collective-permute-done((bf16[4,2048]{1,0:T(4,128)(2,1)S(1)}, bf16[4,2048]{1,0:T(4,128)(2,1)S(1)}, u32[]{:S(2)}, u32[]{:S(2)}) %collective-permute-start.27) | collective-permute-done | bytes 16416 | tf_op jit(solution)/shard_map/ppermute | solution.py:13
  68.7 0.9 %collective-permute-done.26 = bf16[4,2048]{1,0:T(4,128)(2,1)S(1)} collective-permute-done((bf16[4,2048]{1,0:T(4,128)(2,1)S(1)}, bf16[4,2048]{1,0:T(4,128)(2,1)S(1)}, u32[]{:S(2)}, u32[]{:S(2)}) %collective-permute-start.26) | collective-permute-done | bytes 16416 | tf_op jit(solution)/shard_map/ppermute | solution.py:13
  69.6 0.3 fusion.88
  70.2 4.6 %fusion.19 = bf16[4,2048]{1,0:T(4,128)(2,1)S(1)} fusion(bf16[1,2048,2048]{2,1,0:T(8,128)(2,1)} %param.17, bf16[1,4,16,128]{3,2,1,0:T(8,128)(2,1)S(1)} %fusion.31), kind=kOutput, calls=%fused_computation.16 | convolution fusion | flops 33562624 | bytes 8421376 | tf_op jit(solution)/shard_map/dot_general | solution.py:105
  74.8 1.5 %collective-permute-start.30 = (bf16[4,2048]{1,0:T(4,128)(2,1)S(1)}, bf16[4,2048]{1,0:T(4,128)(2,1)S(1)}, u32[]{:S(2)}, u32[]{:S(2)}) collective-permute-start(bf16[4,2048]{1,0:T(4,128)(2,1)S(1)} %fusion.19), channel_id=1, source_target_pairs={{0,12},{4,8},{8,4},{12,0},{1,13},{5,9},{9,5},{13,1},{2,14},{6,10},... | collective-permute-start | bytes 49160 | tf_op jit(solution)/shard_map/ppermute | solution.py:13
  76.2 0.8 collective-permute-start.29
  77.0 2.1 %collective-permute-start.28 = (bf16[4,2048]{1,0:T(4,128)(2,1)S(1)}, bf16[4,2048]{1,0:T(4,128)(2,1)S(1)}, u32[]{:S(2)}, u32[]{:S(2)}) collective-permute-start(bf16[4,2048]{1,0:T(4,128)(2,1)S(1)} %fusion.19), channel_id=1, source_target_pairs={{0,4},{4,0},{8,12},{12,8},{1,5},{5,1},{9,13},{13,9},{2,6},{6,2},{1... | collective-permute-start | bytes 49160 | tf_op jit(solution)/shard_map/ppermute | solution.py:13
  79.2 1.6 %collective-permute-start.32 = (bf16[4,2048]{1,0:T(4,128)(2,1)S(1)}, bf16[4,2048]{1,0:T(4,128)(2,1)S(1)}, u32[]{:S(2)}, u32[]{:S(2)}) collective-permute-start(bf16[4,2048]{1,0:T(4,128)(2,1)S(1)} %broadcast_select_fusion), channel_id=1, source_target_pairs={{0,16},{16,0},{1,17},{17,1},{2,18},{18,2},{3,19},{19,3},{4,20},{20... | collective-permute-start | bytes 49160 | tf_op jit(solution)/shard_map/ppermute | solution.py:111
  81.1 1.6 %collective-permute-start.31 = (bf16[4,2048]{1,0:T(4,128)(2,1)S(1)}, bf16[4,2048]{1,0:T(4,128)(2,1)S(1)}, u32[]{:S(2)}, u32[]{:S(2)}) collective-permute-start(bf16[4,2048]{1,0:T(4,128)(2,1)S(1)} %fusion.49), channel_id=1, source_target_pairs={{0,16},{16,0},{1,17},{17,1},{2,18},{18,2},{3,19},{19,3},{4,20},{20... | collective-permute-start | bytes 49160 | tf_op jit(solution)/shard_map/ppermute | solution.py:109
  82.6 0.4 collective-permute-done.32
  83.1 1.8 %collective-permute-done.31 = bf16[4,2048]{1,0:T(4,128)(2,1)S(1)} collective-permute-done((bf16[4,2048]{1,0:T(4,128)(2,1)S(1)}, bf16[4,2048]{1,0:T(4,128)(2,1)S(1)}, u32[]{:S(2)}, u32[]{:S(2)}) %collective-permute-start.31) | collective-permute-done | bytes 16416 | tf_op jit(solution)/shard_map/ppermute | solution.py:109
  84.9 0.6 select_bitcast_fusion
  (84 shorter events, 4.0 us)
Async XLA Ops:
  0.6 5.2 %copy-start = (bf16[1,100,2048]{2,1,0:T(8,128)(2,1)S(1)}, bf16[1,100,2048]{2,1,0:T(8,128)(2,1)}, u32[]{:S(2)}) copy-start(bf16[1,100,2048]{2,1,0:T(8,128)(2,1)} %param.14) | copy-start | bytes 1228804
  1.4 12.7 %collective-permute-start.2 = (f32[2]{0:T(128)S(1)}, f32[2]{0:T(128)S(1)}, u32[]{:S(2)}, u32[]{:S(2)}) collective-permute-start(f32[2]{0:T(128)S(1)} %get-tuple-element.24), channel_id=1, source_target_pairs={{0,3},{1,2},{2,1},{3,0},{4,7},{5,6},{6,5},{7,4},{8,11},{9,10},{10,... | collective-permute-start | bytes 32 | tf_op jit(solution)/shard_map/ppermute | solution.py:13
  3.8 11.0 %collective-permute-start.1 = (f32[2]{0:T(128)S(1)}, f32[2]{0:T(128)S(1)}, u32[]{:S(2)}, u32[]{:S(2)}) collective-permute-start(f32[2]{0:T(128)S(1)} %get-tuple-element.24), channel_id=1, source_target_pairs={{0,2},{1,3},{2,0},{3,1},{4,6},{5,7},{6,4},{7,5},{8,10},{9,11},{10,... | collective-permute-start | bytes 32 | tf_op jit(solution)/shard_map/ppermute | solution.py:13
  4.4 12.1 %collective-permute-start = (f32[2]{0:T(128)S(1)}, f32[2]{0:T(128)S(1)}, u32[]{:S(2)}, u32[]{:S(2)}) collective-permute-start(f32[2]{0:T(128)S(1)} %get-tuple-element.24), channel_id=1, source_target_pairs={{0,1},{1,0},{2,3},{3,2},{4,5},{5,4},{6,7},{7,6},{8,9},{9,8},{10,11... | collective-permute-start | bytes 32 | tf_op jit(solution)/shard_map/ppermute | solution.py:13
  7.4 15.6 %collective-permute-start.8 = (bf16[2,2,4,2048]{3,2,1,0:T(4,128)(2,1)S(1)}, bf16[2,2,4,2048]{3,2,1,0:T(4,128)(2,1)S(1)}, u32[]{:S(2)}, u32[]{:S(2)}) collective-permute-start(bf16[2,2,4,2048]{3,2,1,0:T(4,128)(2,1)S(1)} %constant_dynamic-update-slice_fusion), channel_id=1, source_target_pairs={{0,12},{4,8},{8,4},{12,0},{1,13},{5,9},{9,5},{13,1},{2,14},{6,10},... | collective-permute-start | bytes 196616 | tf_op jit(solution)/shard_map/ppermute | solution.py:13
  11.3 12.6 %collective-permute-start.7 = (bf16[2,2,4,2048]{3,2,1,0:T(4,128)(2,1)S(1)}, bf16[2,2,4,2048]{3,2,1,0:T(4,128)(2,1)S(1)}, u32[]{:S(2)}, u32[]{:S(2)}) collective-permute-start(bf16[2,2,4,2048]{3,2,1,0:T(4,128)(2,1)S(1)} %constant_dynamic-update-slice_fusion), channel_id=1, source_target_pairs={{0,8},{4,12},{8,0},{12,4},{1,9},{5,13},{9,1},{13,5},{2,10},{6,14},... | collective-permute-start | bytes 196616 | tf_op jit(solution)/shard_map/ppermute | solution.py:13
  14.0 9.9 %collective-permute-start.6 = (bf16[2,2,4,2048]{3,2,1,0:T(4,128)(2,1)S(1)}, bf16[2,2,4,2048]{3,2,1,0:T(4,128)(2,1)S(1)}, u32[]{:S(2)}, u32[]{:S(2)}) collective-permute-start(bf16[2,2,4,2048]{3,2,1,0:T(4,128)(2,1)S(1)} %constant_dynamic-update-slice_fusion), channel_id=1, source_target_pairs={{0,4},{4,0},{8,12},{12,8},{1,5},{5,1},{9,13},{13,9},{2,6},{6,2},{1... | collective-permute-start | bytes 196616 | tf_op jit(solution)/shard_map/ppermute | solution.py:13
  14.7 3.6 %collective-permute-start.4 = (f32[2,4]{1,0:T(2,128)S(1)}, f32[2,4]{1,0:T(2,128)S(1)}, u32[]{:S(2)}, u32[]{:S(2)}) collective-permute-start(f32[2,4]{1,0:T(2,128)S(1)} %pad_maximum_fusion.3), channel_id=1, source_target_pairs={{0,2},{1,3},{2,0},{3,1},{4,6},{5,7},{6,4},{7,5},{8,10},{9,11},{10,... | collective-permute-start | bytes 104 | tf_op jit(solution)/shard_map/ppermute | solution.py:13
  16.4 3.0 %collective-permute-start.5 = (f32[2,4]{1,0:T(2,128)S(1)}, f32[2,4]{1,0:T(2,128)S(1)}, u32[]{:S(2)}, u32[]{:S(2)}) collective-permute-start(f32[2,4]{1,0:T(2,128)S(1)} %pad_maximum_fusion.3), channel_id=1, source_target_pairs={{0,3},{1,2},{2,1},{3,0},{4,7},{5,6},{6,5},{7,4},{8,11},{9,10},{10,... | collective-permute-start | bytes 104 | tf_op jit(solution)/shard_map/ppermute | solution.py:13
  18.3 4.7 %collective-permute-start.3 = (f32[2,4]{1,0:T(2,128)S(1)}, f32[2,4]{1,0:T(2,128)S(1)}, u32[]{:S(2)}, u32[]{:S(2)}) collective-permute-start(f32[2,4]{1,0:T(2,128)S(1)} %pad_maximum_fusion.3), channel_id=1, source_target_pairs={{0,1},{1,0},{2,3},{3,2},{4,5},{5,4},{6,7},{7,6},{8,9},{9,8},{10,11... | collective-permute-start | bytes 104 | tf_op jit(solution)/shard_map/ppermute | solution.py:13
  19.4 10.7 %collective-permute-start.14 = (bf16[2,2,2,16,128]{4,3,2,1,0:T(8,128)(2,1)S(1)}, bf16[2,2,2,16,128]{4,3,2,1,0:T(8,128)(2,1)S(1)}, u32[]{:S(2)}, u32[]{:S(2)}) collective-permute-start(bf16[2,2,2,16,128]{4,3,2,1,0:T(8,128)(2,1)S(1)} %get-tuple-element.18), channel_id=1, source_target_pairs={{0,12},{4,8},{8,4},{12,0},{1,13},{5,9},{9,5},{13,1},{2,14},{6,10},... | collective-permute-start | bytes 98312 | tf_op jit(solution)/shard_map/ppermute | solution.py:13
  23.0 7.4 %collective-permute-start.13 = (bf16[2,2,2,16,128]{4,3,2,1,0:T(8,128)(2,1)S(1)}, bf16[2,2,2,16,128]{4,3,2,1,0:T(8,128)(2,1)S(1)}, u32[]{:S(2)}, u32[]{:S(2)}) collective-permute-start(bf16[2,2,2,16,128]{4,3,2,1,0:T(8,128)(2,1)S(1)} %get-tuple-element.17), channel_id=1, source_target_pairs={{0,8},{4,12},{8,0},{12,4},{1,9},{5,13},{9,1},{13,5},{2,10},{6,14},... | collective-permute-start | bytes 98312 | tf_op jit(solution)/shard_map/ppermute | solution.py:13
  23.1 7.4 %collective-permute-start.12 = (bf16[2,2,2,16,128]{4,3,2,1,0:T(8,128)(2,1)S(1)}, bf16[2,2,2,16,128]{4,3,2,1,0:T(8,128)(2,1)S(1)}, u32[]{:S(2)}, u32[]{:S(2)}) collective-permute-start(bf16[2,2,2,16,128]{4,3,2,1,0:T(8,128)(2,1)S(1)} %get-tuple-element.16), channel_id=1, source_target_pairs={{0,4},{4,0},{8,12},{12,8},{1,5},{5,1},{9,13},{13,9},{2,6},{6,2},{1... | collective-permute-start | bytes 98312 | tf_op jit(solution)/shard_map/ppermute | solution.py:13
  28.6 3.8 %collective-permute-start.11 = (bf16[4,2048]{1,0:T(4,128)(2,1)S(1)}, bf16[4,2048]{1,0:T(4,128)(2,1)S(1)}, u32[]{:S(2)}, u32[]{:S(2)}) collective-permute-start(bf16[4,2048]{1,0:T(4,128)(2,1)S(1)} %fusion.10), channel_id=1, source_target_pairs={{0,3},{1,2},{2,1},{3,0},{4,7},{5,6},{6,5},{7,4},{8,11},{9,10},{10,... | collective-permute-start | bytes 49160 | tf_op jit(solution)/shard_map/ppermute | solution.py:13
  29.3 3.8 %collective-permute-start.10 = (bf16[4,2048]{1,0:T(4,128)(2,1)S(1)}, bf16[4,2048]{1,0:T(4,128)(2,1)S(1)}, u32[]{:S(2)}, u32[]{:S(2)}) collective-permute-start(bf16[4,2048]{1,0:T(4,128)(2,1)S(1)} %fusion.10), channel_id=1, source_target_pairs={{0,2},{1,3},{2,0},{3,1},{4,6},{5,7},{6,4},{7,5},{8,10},{9,11},{10,... | collective-permute-start | bytes 49160 | tf_op jit(solution)/shard_map/ppermute | solution.py:13
  30.1 3.0 %collective-permute-start.9 = (bf16[4,2048]{1,0:T(4,128)(2,1)S(1)}, bf16[4,2048]{1,0:T(4,128)(2,1)S(1)}, u32[]{:S(2)}, u32[]{:S(2)}) collective-permute-start(bf16[4,2048]{1,0:T(4,128)(2,1)S(1)} %fusion.10), channel_id=1, source_target_pairs={{0,1},{1,0},{2,3},{3,2},{4,5},{5,4},{6,7},{7,6},{8,9},{9,8},{10,11... | collective-permute-start | bytes 49160 | tf_op jit(solution)/shard_map/ppermute | solution.py:13
  30.5 5.6 %collective-permute-start.17 = (bf16[2,2,2,64,128]{4,3,2,1,0:T(8,128)(2,1)S(1)}, bf16[2,2,2,64,128]{4,3,2,1,0:T(8,128)(2,1)S(1)}, u32[]{:S(2)}, u32[]{:S(2)}) collective-permute-start(bf16[2,2,2,64,128]{4,3,2,1,0:T(8,128)(2,1)S(1)} %get-tuple-element.14), channel_id=1, source_target_pairs={{0,3},{1,2},{2,1},{3,0},{4,7},{5,6},{6,5},{7,4},{8,11},{9,10},{10,... | collective-permute-start | bytes 393224 | tf_op jit(solution)/shard_map/ppermute | solution.py:13
  31.7 7.5 %collective-permute-start.16 = (bf16[2,2,2,64,128]{4,3,2,1,0:T(8,128)(2,1)S(1)}, bf16[2,2,2,64,128]{4,3,2,1,0:T(8,128)(2,1)S(1)}, u32[]{:S(2)}, u32[]{:S(2)}) collective-permute-start(bf16[2,2,2,64,128]{4,3,2,1,0:T(8,128)(2,1)S(1)} %get-tuple-element.14), channel_id=1, source_target_pairs={{0,2},{1,3},{2,0},{3,1},{4,6},{5,7},{6,4},{7,5},{8,10},{9,11},{10,... | collective-permute-start | bytes 393224 | tf_op jit(solution)/shard_map/ppermute | solution.py:13
  32.4 6.8 %collective-permute-start.15 = (bf16[2,2,2,64,128]{4,3,2,1,0:T(8,128)(2,1)S(1)}, bf16[2,2,2,64,128]{4,3,2,1,0:T(8,128)(2,1)S(1)}, u32[]{:S(2)}, u32[]{:S(2)}) collective-permute-start(bf16[2,2,2,64,128]{4,3,2,1,0:T(8,128)(2,1)S(1)} %get-tuple-element.14), channel_id=1, source_target_pairs={{0,1},{1,0},{2,3},{3,2},{4,5},{5,4},{6,7},{7,6},{8,9},{9,8},{10,11... | collective-permute-start | bytes 393224 | tf_op jit(solution)/shard_map/ppermute | solution.py:13
  39.8 13.4 %copy-start.1 = (bf16[1,4,2048]{2,1,0:T(4,128)(2,1)S(1)}, bf16[1,4,2048]{2,1,0:T(4,128)(2,1)}, u32[]{:S(2)}) copy-start(bf16[1,4,2048]{2,1,0:T(4,128)(2,1)} %param.10) | copy-start | bytes 49156
  39.8 17.3 %copy-start.2 = (bf16[2,4,2048]{2,1,0:T(4,128)(2,1)S(1)}, bf16[2,4,2048]{2,1,0:T(4,128)(2,1)}, u32[]{:S(2)}) copy-start(bf16[2,4,2048]{2,1,0:T(4,128)(2,1)} %param.11) | copy-start | bytes 98308
  45.0 5.7 %collective-permute-start.20 = (bf16[4,2048]{1,0:T(4,128)(2,1)S(1)}, bf16[4,2048]{1,0:T(4,128)(2,1)S(1)}, u32[]{:S(2)}, u32[]{:S(2)}) collective-permute-start(bf16[4,2048]{1,0:T(4,128)(2,1)S(1)} %fusion.16), channel_id=1, source_target_pairs={{0,12},{4,8},{8,4},{12,0},{1,13},{5,9},{9,5},{13,1},{2,14},{6,10},... | collective-permute-start | bytes 49160 | tf_op jit(solution)/shard_map/ppermute | solution.py:13
  48.6 4.6 %collective-permute-start.19 = (bf16[4,2048]{1,0:T(4,128)(2,1)S(1)}, bf16[4,2048]{1,0:T(4,128)(2,1)S(1)}, u32[]{:S(2)}, u32[]{:S(2)}) collective-permute-start(bf16[4,2048]{1,0:T(4,128)(2,1)S(1)} %fusion.16), channel_id=1, source_target_pairs={{0,8},{4,12},{8,0},{12,4},{1,9},{5,13},{9,1},{13,5},{2,10},{6,14},... | collective-permute-start | bytes 49160 | tf_op jit(solution)/shard_map/ppermute | solution.py:13
  48.6 4.6 %collective-permute-start.18 = (bf16[4,2048]{1,0:T(4,128)(2,1)S(1)}, bf16[4,2048]{1,0:T(4,128)(2,1)S(1)}, u32[]{:S(2)}, u32[]{:S(2)}) collective-permute-start(bf16[4,2048]{1,0:T(4,128)(2,1)S(1)} %fusion.16), channel_id=1, source_target_pairs={{0,4},{4,0},{8,12},{12,8},{1,5},{5,1},{9,13},{13,9},{2,6},{6,2},{1... | collective-permute-start | bytes 49160 | tf_op jit(solution)/shard_map/ppermute | solution.py:13
  53.3 3.8 %collective-permute-start.21 = (bf16[4,2048]{1,0:T(4,128)(2,1)S(1)}, bf16[4,2048]{1,0:T(4,128)(2,1)S(1)}, u32[]{:S(2)}, u32[]{:S(2)}) collective-permute-start(bf16[4,2048]{1,0:T(4,128)(2,1)S(1)} %fusion.38), channel_id=1, source_target_pairs={{0,16},{16,0},{1,17},{17,1},{2,18},{18,2},{3,19},{19,3},{4,20},{20... | collective-permute-start | bytes 49160 | tf_op jit(solution)/shard_map/ppermute | solution.py:109
  57.3 3.6 %collective-permute-start.23 = (f32[2,4]{1,0:T(2,128)S(1)}, f32[2,4]{1,0:T(2,128)S(1)}, u32[]{:S(2)}, u32[]{:S(2)}) collective-permute-start(f32[2,4]{1,0:T(2,128)S(1)} %pad_maximum_fusion.4), channel_id=1, source_target_pairs={{0,2},{1,3},{2,0},{3,1},{4,6},{5,7},{6,4},{7,5},{8,10},{9,11},{10,... | collective-permute-start | bytes 104 | tf_op jit(solution)/shard_map/ppermute | solution.py:13
  57.9 3.0 %collective-permute-start.24 = (f32[2,4]{1,0:T(2,128)S(1)}, f32[2,4]{1,0:T(2,128)S(1)}, u32[]{:S(2)}, u32[]{:S(2)}) collective-permute-start(f32[2,4]{1,0:T(2,128)S(1)} %pad_maximum_fusion.4), channel_id=1, source_target_pairs={{0,3},{1,2},{2,1},{3,0},{4,7},{5,6},{6,5},{7,4},{8,11},{9,10},{10,... | collective-permute-start | bytes 104 | tf_op jit(solution)/shard_map/ppermute | solution.py:13
  57.9 3.0 %collective-permute-start.22 = (f32[2,4]{1,0:T(2,128)S(1)}, f32[2,4]{1,0:T(2,128)S(1)}, u32[]{:S(2)}, u32[]{:S(2)}) collective-permute-start(f32[2,4]{1,0:T(2,128)S(1)} %pad_maximum_fusion.4), channel_id=1, source_target_pairs={{0,1},{1,0},{2,3},{3,2},{4,5},{5,4},{6,7},{7,6},{8,9},{9,8},{10,11... | collective-permute-start | bytes 104 | tf_op jit(solution)/shard_map/ppermute | solution.py:13
  65.6 3.2 %collective-permute-start.27 = (bf16[4,2048]{1,0:T(4,128)(2,1)S(1)}, bf16[4,2048]{1,0:T(4,128)(2,1)S(1)}, u32[]{:S(2)}, u32[]{:S(2)}) collective-permute-start(bf16[4,2048]{1,0:T(4,128)(2,1)S(1)} %fusion.13), channel_id=1, source_target_pairs={{0,3},{1,2},{2,1},{3,0},{4,7},{5,6},{6,5},{7,4},{8,11},{9,10},{10,... | collective-permute-start | bytes 49160 | tf_op jit(solution)/shard_map/ppermute | solution.py:13
  65.8 3.7 %collective-permute-start.26 = (bf16[4,2048]{1,0:T(4,128)(2,1)S(1)}, bf16[4,2048]{1,0:T(4,128)(2,1)S(1)}, u32[]{:S(2)}, u32[]{:S(2)}) collective-permute-start(bf16[4,2048]{1,0:T(4,128)(2,1)S(1)} %fusion.13), channel_id=1, source_target_pairs={{0,2},{1,3},{2,0},{3,1},{4,6},{5,7},{6,4},{7,5},{8,10},{9,11},{10,... | collective-permute-start | bytes 49160 | tf_op jit(solution)/shard_map/ppermute | solution.py:13
  67.3 2.3 %collective-permute-start.25 = (bf16[4,2048]{1,0:T(4,128)(2,1)S(1)}, bf16[4,2048]{1,0:T(4,128)(2,1)S(1)}, u32[]{:S(2)}, u32[]{:S(2)}) collective-permute-start(bf16[4,2048]{1,0:T(4,128)(2,1)S(1)} %fusion.13), channel_id=1, source_target_pairs={{0,1},{1,0},{2,3},{3,2},{4,5},{5,4},{6,7},{7,6},{8,9},{9,8},{10,11... | collective-permute-start | bytes 49160 | tf_op jit(solution)/shard_map/ppermute | solution.py:13
  74.8 6.0 %collective-permute-start.30 = (bf16[4,2048]{1,0:T(4,128)(2,1)S(1)}, bf16[4,2048]{1,0:T(4,128)(2,1)S(1)}, u32[]{:S(2)}, u32[]{:S(2)}) collective-permute-start(bf16[4,2048]{1,0:T(4,128)(2,1)S(1)} %fusion.19), channel_id=1, source_target_pairs={{0,12},{4,8},{8,4},{12,0},{1,13},{5,9},{9,5},{13,1},{2,14},{6,10},... | collective-permute-start | bytes 49160 | tf_op jit(solution)/shard_map/ppermute | solution.py:13
  76.2 4.7 %collective-permute-start.29 = (bf16[4,2048]{1,0:T(4,128)(2,1)S(1)}, bf16[4,2048]{1,0:T(4,128)(2,1)S(1)}, u32[]{:S(2)}, u32[]{:S(2)}) collective-permute-start(bf16[4,2048]{1,0:T(4,128)(2,1)S(1)} %fusion.19), channel_id=1, source_target_pairs={{0,8},{4,12},{8,0},{12,4},{1,9},{5,13},{9,1},{13,5},{2,10},{6,14},... | collective-permute-start | bytes 49160 | tf_op jit(solution)/shard_map/ppermute | solution.py:13
  77.0 4.0 %collective-permute-start.28 = (bf16[4,2048]{1,0:T(4,128)(2,1)S(1)}, bf16[4,2048]{1,0:T(4,128)(2,1)S(1)}, u32[]{:S(2)}, u32[]{:S(2)}) collective-permute-start(bf16[4,2048]{1,0:T(4,128)(2,1)S(1)} %fusion.19), channel_id=1, source_target_pairs={{0,4},{4,0},{8,12},{12,8},{1,5},{5,1},{9,13},{13,9},{2,6},{6,2},{1... | collective-permute-start | bytes 49160 | tf_op jit(solution)/shard_map/ppermute | solution.py:13
  79.2 3.9 %collective-permute-start.32 = (bf16[4,2048]{1,0:T(4,128)(2,1)S(1)}, bf16[4,2048]{1,0:T(4,128)(2,1)S(1)}, u32[]{:S(2)}, u32[]{:S(2)}) collective-permute-start(bf16[4,2048]{1,0:T(4,128)(2,1)S(1)} %broadcast_select_fusion), channel_id=1, source_target_pairs={{0,16},{16,0},{1,17},{17,1},{2,18},{18,2},{3,19},{19,3},{4,20},{20... | collective-permute-start | bytes 49160 | tf_op jit(solution)/shard_map/ppermute | solution.py:111
  81.1 3.8 %collective-permute-start.31 = (bf16[4,2048]{1,0:T(4,128)(2,1)S(1)}, bf16[4,2048]{1,0:T(4,128)(2,1)S(1)}, u32[]{:S(2)}, u32[]{:S(2)}) collective-permute-start(bf16[4,2048]{1,0:T(4,128)(2,1)S(1)} %fusion.49), channel_id=1, source_target_pairs={{0,16},{16,0},{1,17},{17,1},{2,18},{18,2},{3,19},{19,3},{4,20},{20... | collective-permute-start | bytes 49160 | tf_op jit(solution)/shard_map/ppermute | solution.py:109

commit v2 on v1

--- a/solution.py
+++ b/solution.py
@@ -14,7 +14,10 @@
 
 
 def peers(block, axis):
-    return [block] + [swapped(block, axis, d) for d in range(1, lax.axis_size(axis))]
+    count = lax.axis_size(axis)
+    sent = jnp.broadcast_to(block[None], (count,) + block.shape)
+    got = lax.all_to_all(sent, axis, 0, 0)
+    return [got[i] for i in range(count)]
 
 
 def tree_sum(pieces):
@@ -63,25 +66,28 @@
 
     kv = jnp.stack([keys[0, :, 0], values[0, :, 0]], 0)
 
-    def heads_of(place):
-        start = place * heads_dev // group
-        return lax.dynamic_slice_in_dim(kv, start, kv_dev, 2)
-
-    parts = [heads_of(tensor_at)]
-    spots = [tensor_at * pos_dev + jnp.arange(pos_dev)]
-    for d in range(1, tensors):
-        parts.append(swapped(heads_of(tensor_at ^ d), "tensor", d))
-        spots.append((tensor_at ^ d) * pos_dev + jnp.arange(pos_dev))
-    kv = jnp.concatenate(parts, 3)
-    spots = jnp.concatenate(spots)
-    kv_rows = unswap(jnp.stack(peers(kv, "replica"), 0), replica_at)
-    length_rows = unswap(jnp.stack(peers(lengths[:, 0].astype(F32), "replica"), 0), replica_at)
+    picks = jnp.stack(
+        [
+            lax.slice_in_dim(kv, i * heads_dev // group, i * heads_dev // group + kv_dev, axis=2)
+            for i in range(tensors)
+        ],
+        0,
+    )
+    got = lax.all_to_all(picks, "tensor", 0, 0)
+    kv = jnp.concatenate([got[i] for i in range(tensors)], 3)
+    spots = jnp.arange(tensors * pos_dev)
+    kv_rows = jnp.stack(peers(kv, "replica"), 0)
+    length_rows = jnp.stack(peers(lengths[:, 0].astype(F32), "replica"), 0)
 
     h = state[0]
     emitted = jnp.zeros_like(h)
     at_first = section_at == 0
     for tick in range(sections):
         batch = order[tick]
+        ring = [(i, (i + 1) % sections) for i in range(sections)]
+        h_behind = lax.ppermute(h, "section", ring)
+        if tick > 0:
+            emitted_behind = lax.ppermute(emitted, "section", ring)
         hf = h.astype(F32)
         stats = jnp.stack([jnp.sum(hf, axis=-1), jnp.sum(hf * hf, axis=-1)], 0)
         stats = tree_sum(peers(stats, "replica")) / width_all
@@ -103,12 +109,14 @@
         att = jnp.einsum("rgjp,rgpd->rgjd", weight, kv_now[:, 1].astype(F32))
         att = att.reshape(rows_mb, query_part).astype(BF)
         out = jnp.dot(att, wo[0], preferred_element_type=F32).astype(BF)
-        out = tree_sum(peers(out, "tensor"))
-        h = (hf + out).astype(BF)
-        ring = [(i, (i + 1) % sections) for i in range(sections)]
-        h = lax.ppermute(h, "section", ring)
+        sent = jnp.broadcast_to(out[None], (sections * tensors,) + out.shape)
+        got = lax.all_to_all(sent, ("section", "tensor"), 0, 0)
+        behind = (section_at + sections - 1) % sections
+        got = lax.dynamic_slice_in_dim(got, behind * tensors, tensors, 0)
+        out = tree_sum([got[i] for i in range(tensors)])
+        h = (h_behind.astype(F32) + out).astype(BF)
         if tick > 0:
-            emitted = lax.ppermute(emitted, "section", ring)
+            emitted = emitted_behind
         arriving = -(tick + 1) % sections
         emitted = jnp.where(at_first, h, emitted)
         h = jnp.where(at_first, next_embed[arriving], h)

time: 86 us -> 124 us (1.44)
  waiting for transfers between devices: 21.3 us -> 44.4 us
  blocking collectives: 0 us -> 6.13 us
  local copies, waits for them, and re-layouts: 2.13 us -> 7.24 us
  starting transfers between devices: 35.2 us -> 37.9 us
    all_to_all x0 -> x9, waiting for transfers between devices: none -> 38.8 us  [the longest x6 27.4 us: peers(): got = lax.all_to_all(sent, axis, 0, 0)]
    all_to_all x0 -> x9, starting transfers between devices: none -> 33.8 us  [the longest x6 21 us: peers(): got = lax.all_to_all(sent, axis, 0, 0)]
    ppermute x33 -> x3, starting transfers between devices: 35.2 us -> 4.11 us  [the longest x2 3.96 us: on_device(): h_behind = lax.ppermute(h, 'section', ring)]
    ppermute x33 -> x3, waiting for transfers between devices: 21.3 us -> 5.68 us  [the longest x2 4.15 us: on_device(): h_behind = lax.ppermute(h, 'section', ring)]
    all_to_all x0 -> x1, blocking collectives: none -> 6.13 us  [peers(): got = lax.all_to_all(sent, axis, 0, 0)]
    broadcast_in_dim x0 -> x9, local copies, waits for them, and re-layouts: none -> 5.55 us  [the longest x7 4.17 us: peers(): sent = jnp.broadcast_to(block[None], (count,) + block.shape)]
  transfers between devices with their start and end apart: 33 -> 12, of which waited for: 15 -> 11; matrix products, arithmetic and copies ran while one was open for 13% -> 5% of each run, Pallas kernels for 0% -> 0%
where the time goes in v2:
time: 124 us; the launch traced here: 122 us
  waiting for transfers between devices  44.4 us (36%)
  starting transfers between devices  37.9 us (31%)
  matrix products  21 us (17%)
  local copies, waits for them, and re-layouts  7.24 us (6%)
  blocking collectives  6.13 us (5%)
  other arithmetic  4.95 us (4%)
    all_to_all x6, waiting for transfers between devices, peers(): got = lax.all_to_all(sent, axis, 0, 0)  27.4 us
    all_to_all x6, starting transfers between devices, peers(): got = lax.all_to_all(sent, axis, 0, 0)  21 us
    dot_general x2, matrix products, on_device(): jnp.dot(normed, wq[0], preferred_element_type=F32).astype(BF)  9.24 us
    dot_general x2, matrix products, on_device(): out = jnp.dot(att, wo[0], preferred_element_type=F32).astype(BF)  9.16 us
    all_to_all x2, starting transfers between devices, on_device(): got = lax.all_to_all(sent, ('section', 'tensor'), 0, 0)  7.53 us
    all_to_all x1, blocking collectives, peers(): got = lax.all_to_all(sent, axis, 0, 0)  6.13 us
    all_to_all x1, waiting for transfers between devices, on_device(): got = lax.all_to_all(picks, 'tensor', 0, 0)  6.06 us
    all_to_all x1, starting transfers between devices, on_device(): got = lax.all_to_all(picks, 'tensor', 0, 0)  5.28 us
  transfers between devices with their start and end apart: 12, of which 11 were waited for; matrix products, arithmetic and copies ran while one was open for 5% of the time, Pallas kernels for 0%

profile of v2, /device:TPU:0, one launch (start us, length us, event | category | flops | bytes accessed | tf_op | source)
XLA Modules:
  0.0 122.5 jit_solution(7609061451491007639)
XLA Ops:
  0.6 0.7 convert_bitcast_fusion
  1.4 0.6 broadcast_in_dim.44
  1.9 4.2 %all-to-all-start = ((f32[4,1,2]{2,1,0:T(1,128)}), f32[4,1,2]{2,1,0:T(1,128)S(1)}, u32[]{:S(2)}, u32[]{:S(2)}) async-start(f32[4,1,2]{2,1,0:T(1,128)} %broadcast_in_dim.44), calls=%async_computation | async-start | bytes 4096 | tf_op jit(solution)/shard_map/all_to_all | solution.py:19
  6.3 1.2 %gather_fusion = s32[2,4]{1,0:T(2,128)S(1)} fusion(s32[2,4]{1,0:T(2,128)} %param.12, s32[1024]{0:T(1024)S(1)} %pad_clamp_fusion), kind=kCustom, calls=%fused_computation | custom fusion | bytes 72 | tf_op jit(solution)/shard_map/gather | solution.py:59
  7.6 0.2 convolution_convert_fusion.1
  7.9 1.2 %convolution_convert_fusion = bf16[8,2048]{1,0:T(8,128)(2,1)S(1)} fusion(bf16[1,100,2048]{2,1,0:T(8,128)(2,1)} %param.15, s32[8]{0:T(128)S(1)} %sub.83), kind=kOutput, calls=%fused_computation.11 | convolution fusion | flops 3293984 | bytes 442400 | tf_op jit(solution)/shard_map/dot_general | solution.py:63
  9.1 0.9 convert_reduce_fusion.1
  10.0 0.9 fusion.43
  10.9 0.7 pad_maximum_fusion
  11.6 0.6 broadcast_in_dim.46
  12.2 3.3 %all-to-all-start.1 = ((f32[4,2,4]{2,1,0:T(2,128)}), f32[4,2,4]{2,1,0:T(2,128)S(1)}, u32[]{:S(2)}, u32[]{:S(2)}) async-start(f32[4,2,4]{2,1,0:T(2,128)} %broadcast_in_dim.46), calls=%async_computation.1 | async-start | bytes 8192 | tf_op jit(solution)/shard_map/all_to_all | solution.py:19
  15.7 3.6 %all-to-all-done.1 = f32[4,2,4]{2,1,0:T(2,128)S(1)} async-done(((f32[4,2,4]{2,1,0:T(2,128)}), f32[4,2,4]{2,1,0:T(2,128)S(1)}, u32[]{:S(2)}, u32[]{:S(2)}) %all-to-all-start.1) | async-done | bytes 160 | tf_op jit(solution)/shard_map/all_to_all | solution.py:19
  19.3 5.3 %all-to-all-start.4 = ((bf16[4,2,2,2,16,128]{5,4,3,2,1,0:T(8,128)(2,1)}), bf16[4,2,2,2,16,128]{5,4,3,2,1,0:T(8,128)(2,1)S(1)}, u32[]{:S(2)}, u32[]{:S(2)}) async-start(bf16[4,2,2,2,16,128]{5,4,3,2,1,0:T(8,128)(2,1)} %pad_maximum_fusion), calls=%async_computation.4 | async-start | bytes 262144 | tf_op jit(solution)/shard_map/all_to_all | solution.py:76
  24.6 6.1 %all-to-all-done.4 = bf16[4,2,2,2,16,128]{5,4,3,2,1,0:T(8,128)(2,1)S(1)} async-done(((bf16[4,2,2,2,16,128]{5,4,3,2,1,0:T(8,128)(2,1)}), bf16[4,2,2,2,16,128]{5,4,3,2,1,0:T(8,128)(2,1)S(1)}, u32[]{:S(2)}, u32[]{:S(2)}) %all-to-all-start.4) | async-done | bytes 131104 | tf_op jit(solution)/shard_map/all_to_all | solution.py:76
  30.6 0.8 broadcast_in_dim.48
  31.4 3.4 %all-to-all-start.2 = ((bf16[4,2,2,4,2048]{4,3,2,1,0:T(4,128)(2,1)}), bf16[4,2,2,4,2048]{4,3,2,1,0:T(4,128)(2,1)S(1)}, u32[]{:S(2)}, u32[]{:S(2)}) async-start(bf16[4,2,2,4,2048]{4,3,2,1,0:T(4,128)(2,1)} %broadcast_in_dim.48), calls=%async_computation.2 | async-start | bytes 524288 | tf_op jit(solution)/shard_map/all_to_all | solution.py:19
  34.9 7.0 %all-to-all-done.2 = bf16[4,2,2,4,2048]{4,3,2,1,0:T(4,128)(2,1)S(1)} async-done(((bf16[4,2,2,4,2048]{4,3,2,1,0:T(4,128)(2,1)}), bf16[4,2,2,4,2048]{4,3,2,1,0:T(4,128)(2,1)S(1)}, u32[]{:S(2)}, u32[]{:S(2)}) %all-to-all-start.2) | async-done | bytes 262176 | tf_op jit(solution)/shard_map/all_to_all | solution.py:19
  42.0 4.6 %fusion.10 = bf16[4,2048]{1,0:T(4,128)(2,1)S(1)} fusion(bf16[1,2048,2048]{2,1,0:T(8,128)(2,1)} %param.16, f32[2,2,4,2048]{3,2,1,0:T(4,128)S(1)} %add_bitcast_fusion, bf16[1,4,2048]{2,1,0:T(4,128)(2,1)} %param.10, f32[4]{0:T(128)S(1)} %fusion.84, f32[4]{0:T(128)S(1)} %slice_bitcast_fusion.15), kind=kOutput, calls=%fused_computation.13 | convolution fusion | flops 33611776 | bytes 8487936 | tf_op jit(solution)/shard_map/dot_general | solution.py:97
  46.6 0.6 broadcast_in_dim.49
  47.3 3.3 %all-to-all-start.3 = ((bf16[4,4,2048]{2,1,0:T(4,128)(2,1)}), bf16[4,4,2048]{2,1,0:T(4,128)(2,1)S(1)}, u32[]{:S(2)}, u32[]{:S(2)}) async-start(bf16[4,4,2048]{2,1,0:T(4,128)(2,1)} %broadcast_in_dim.49), calls=%async_computation.3 | async-start | bytes 131072 | tf_op jit(solution)/shard_map/all_to_all | solution.py:19
  50.6 4.0 %all-to-all-done.3 = bf16[4,4,2048]{2,1,0:T(4,128)(2,1)S(1)} async-done(((bf16[4,4,2048]{2,1,0:T(4,128)(2,1)}), bf16[4,4,2048]{2,1,0:T(4,128)(2,1)S(1)}, u32[]{:S(2)}, u32[]{:S(2)}) %all-to-all-start.3) | async-done | bytes 65568 | tf_op jit(solution)/shard_map/all_to_all | solution.py:19
  54.6 0.9 broadcast_in_dim.50
  55.5 3.5 %all-to-all-start.5 = ((bf16[4,2,2,2,64,128]{5,4,3,1,2,0:T(8,128)(2,1)}), bf16[4,2,2,2,64,128]{5,4,3,1,2,0:T(8,128)(2,1)S(1)}, u32[]{:S(2)}, u32[]{:S(2)}) async-start(bf16[4,2,2,2,64,128]{5,4,3,1,2,0:T(8,128)(2,1)} %broadcast_in_dim.50), calls=%async_computation.5 | async-start | bytes 1048576 | tf_op jit(solution)/shard_map/all_to_all | solution.py:19
  59.1 8.7 %all-to-all-done.5 = bf16[4,2,2,2,64,128]{5,4,3,1,2,0:T(8,128)(2,1)S(1)} async-done(((bf16[4,2,2,2,64,128]{5,4,3,1,2,0:T(8,128)(2,1)}), bf16[4,2,2,2,64,128]{5,4,3,1,2,0:T(8,128)(2,1)S(1)}, u32[]{:S(2)}, u32[]{:S(2)}) %all-to-all-start.5) | async-done | bytes 524320 | tf_op jit(solution)/shard_map/all_to_all | solution.py:19
  67.9 0.3 fusion.89
  68.3 0.2 fusion.30
  68.5 4.6 %fusion.16 = bf16[4,2048]{1,0:T(4,128)(2,1)S(1)} fusion(bf16[1,2048,2048]{2,1,0:T(8,128)(2,1)} %param.17, bf16[1,4,16,128]{3,2,1,0:T(8,128)(2,1)S(1)} %fusion.30), kind=kOutput, calls=%fused_computation.15 | convolution fusion | flops 33562624 | bytes 8421376 | tf_op jit(solution)/shard_map/dot_general | solution.py:111
  73.1 0.7 broadcast_in_dim.52
  73.8 4.2 %all-to-all-start.6 = ((bf16[8,4,2048]{2,1,0:T(4,128)(2,1)}), bf16[8,4,2048]{2,1,0:T(4,128)(2,1)S(1)}, u32[]{:S(2)}, u32[]{:S(2)}) async-start(bf16[8,4,2048]{2,1,0:T(4,128)(2,1)} %broadcast_in_dim.52), calls=%async_computation.6 | async-start | bytes 262144 | tf_op jit(solution)/shard_map/all_to_all | solution.py:113
  77.9 2.0 %collective-permute-start = (bf16[4,2048]{1,0:T(4,128)(2,1)S(1)}, bf16[4,2048]{1,0:T(4,128)(2,1)S(1)}, u32[]{:S(2)}, u32[]{:S(2)}) collective-permute-start(bf16[4,2048]{1,0:T(4,128)(2,1)S(1)} %bitcast.175), channel_id=1, source_target_pairs={{0,16},{16,0},{1,17},{17,1},{2,18},{18,2},{3,19},{19,3},{4,20},{20... | collective-permute-start | bytes 49160 | tf_op jit(solution)/shard_map/ppermute | solution.py:88
  79.9 2.1 %collective-permute-done = bf16[4,2048]{1,0:T(4,128)(2,1)S(1)} collective-permute-done((bf16[4,2048]{1,0:T(4,128)(2,1)S(1)}, bf16[4,2048]{1,0:T(4,128)(2,1)S(1)}, u32[]{:S(2)}, u32[]{:S(2)}) %collective-permute-start) | collective-permute-done | bytes 16416 | tf_op jit(solution)/shard_map/ppermute | solution.py:88
  82.0 3.4 %all-to-all-done.6 = bf16[8,4,2048]{2,1,0:T(4,128)(2,1)S(1)} async-done(((bf16[8,4,2048]{2,1,0:T(4,128)(2,1)}), bf16[8,4,2048]{2,1,0:T(4,128)(2,1)S(1)}, u32[]{:S(2)}, u32[]{:S(2)}) %all-to-all-start.6) | async-done | bytes 131104 | tf_op jit(solution)/shard_map/all_to_all | solution.py:113
  85.7 6.1 %all_to_all.51 = f32[4,2,4]{2,1,0:T(2,128)S(1)} all-to-all(f32[4,2,4]{2,1,0:T(2,128)S(1)} %broadcast_in_dim.54), channel_id=1, replica_groups=mesh['section'=2,'tensor'=4,'replica'=4] {'replica'}, dimensions={0} | all-to-all | bytes 256 | tf_op jit(solution)/shard_map/all_to_all | solution.py:19
  91.8 4.6 %fusion.13 = bf16[4,2048]{1,0:T(4,128)(2,1)S(1)} fusion(bf16[1,2048,2048]{2,1,0:T(8,128)(2,1)} %param.16, bf16[4,2048]{1,0:T(4,128)(2,1)S(1)} %get-tuple-element.14, f32[2,2,4,2048]{3,2,1,0:T(4,128)S(1)} %add_bitcast_fusion, f32[4]{0:T(128)S(1)} %fusion.82, f32[4]{0:T(128)S(1)} %slice_bitcast_fusion.14), kind=kOutput, calls=%fused_computation.14 | convolution fusion | flops 33611776 | bytes 8487936 | tf_op jit(solution)/shard_map/dot_general | solution.py:97
  96.4 0.6 broadcast_in_dim.55
  97.1 3.3 %all-to-all-start.8 = ((bf16[4,4,2048]{2,1,0:T(4,128)(2,1)}), bf16[4,4,2048]{2,1,0:T(4,128)(2,1)S(1)}, u32[]{:S(2)}, u32[]{:S(2)}) async-start(bf16[4,4,2048]{2,1,0:T(4,128)(2,1)} %broadcast_in_dim.55), calls=%async_computation.8 | async-start | bytes 131072 | tf_op jit(solution)/shard_map/all_to_all | solution.py:19
  100.4 4.1 %all-to-all-done.8 = bf16[4,4,2048]{2,1,0:T(4,128)(2,1)S(1)} async-done(((bf16[4,4,2048]{2,1,0:T(4,128)(2,1)}), bf16[4,4,2048]{2,1,0:T(4,128)(2,1)S(1)}, u32[]{:S(2)}, u32[]{:S(2)}) %all-to-all-start.8) | async-done | bytes 65568 | tf_op jit(solution)/shard_map/all_to_all | solution.py:19
  104.5 0.3 fusion.90
  104.8 0.2 fusion.31
  105.0 4.6 %fusion.19 = bf16[4,2048]{1,0:T(4,128)(2,1)S(1)} fusion(bf16[1,2048,2048]{2,1,0:T(8,128)(2,1)} %param.17, bf16[1,4,16,128]{3,2,1,0:T(8,128)(2,1)S(1)} %fusion.31), kind=kOutput, calls=%fused_computation.16 | convolution fusion | flops 33562624 | bytes 8421376 | tf_op jit(solution)/shard_map/dot_general | solution.py:111
  109.6 0.7 broadcast_in_dim.56
  110.3 3.4 %all-to-all-start.9 = ((bf16[8,4,2048]{2,1,0:T(4,128)(2,1)}), bf16[8,4,2048]{2,1,0:T(4,128)(2,1)S(1)}, u32[]{:S(2)}, u32[]{:S(2)}) async-start(bf16[8,4,2048]{2,1,0:T(4,128)(2,1)} %broadcast_in_dim.56), calls=%async_computation.9 | async-start | bytes 262144 | tf_op jit(solution)/shard_map/all_to_all | solution.py:113
  113.7 1.9 %collective-permute-start.1 = (bf16[4,2048]{1,0:T(4,128)(2,1)S(1)}, bf16[4,2048]{1,0:T(4,128)(2,1)S(1)}, u32[]{:S(2)}, u32[]{:S(2)}) collective-permute-start(bf16[4,2048]{1,0:T(4,128)(2,1)S(1)} %get-tuple-element.14), channel_id=1, source_target_pairs={{0,16},{16,0},{1,17},{17,1},{2,18},{18,2},{3,19},{19,3},{4,20},{20... | collective-permute-start | bytes 49160 | tf_op jit(solution)/shard_map/ppermute | solution.py:88
  115.8 2.1 %collective-permute-done.1 = bf16[4,2048]{1,0:T(4,128)(2,1)S(1)} collective-permute-done((bf16[4,2048]{1,0:T(4,128)(2,1)S(1)}, bf16[4,2048]{1,0:T(4,128)(2,1)S(1)}, u32[]{:S(2)}, u32[]{:S(2)}) %collective-permute-start.1) | collective-permute-done | bytes 16416 | tf_op jit(solution)/shard_map/ppermute | solution.py:88
  117.8 1.5 %collective-permute-done.2 = bf16[4,2048]{1,0:T(4,128)(2,1)S(1)} collective-permute-done((bf16[4,2048]{1,0:T(4,128)(2,1)S(1)}, bf16[4,2048]{1,0:T(4,128)(2,1)S(1)}, u32[]{:S(2)}, u32[]{:S(2)}) %collective-permute-start.2) | collective-permute-done | bytes 16416 | tf_op jit(solution)/shard_map/ppermute | solution.py:90
  119.4 1.9 %all-to-all-done.9 = bf16[8,4,2048]{2,1,0:T(4,128)(2,1)S(1)} async-done(((bf16[8,4,2048]{2,1,0:T(4,128)(2,1)}), bf16[8,4,2048]{2,1,0:T(4,128)(2,1)S(1)}, u32[]{:S(2)}, u32[]{:S(2)}) %all-to-all-start.9) | async-done | bytes 131104 | tf_op jit(solution)/shard_map/all_to_all | solution.py:113
  121.2 0.6 select_bitcast_fusion
  121.9 0.6 fusion.65
  (38 shorter events, 1.2 us)
Async XLA Ops:
  0.6 7.0 %copy-start = (bf16[1,100,2048]{2,1,0:T(8,128)(2,1)S(1)}, bf16[1,100,2048]{2,1,0:T(8,128)(2,1)}, u32[]{:S(2)}) copy-start(bf16[1,100,2048]{2,1,0:T(8,128)(2,1)} %param.14) | copy-start | bytes 1228804
  1.9 9.7 %all-to-all-start = ((f32[4,1,2]{2,1,0:T(1,128)}), f32[4,1,2]{2,1,0:T(1,128)S(1)}, u32[]{:S(2)}, u32[]{:S(2)}) async-start(f32[4,1,2]{2,1,0:T(1,128)} %broadcast_in_dim.44), calls=%async_computation | async-start | bytes 4096 | tf_op jit(solution)/shard_map/all_to_all | solution.py:19
  12.2 7.1 %all-to-all-start.1 = ((f32[4,2,4]{2,1,0:T(2,128)}), f32[4,2,4]{2,1,0:T(2,128)S(1)}, u32[]{:S(2)}, u32[]{:S(2)}) async-start(f32[4,2,4]{2,1,0:T(2,128)} %broadcast_in_dim.46), calls=%async_computation.1 | async-start | bytes 8192 | tf_op jit(solution)/shard_map/all_to_all | solution.py:19
  19.3 11.4 %all-to-all-start.4 = ((bf16[4,2,2,2,16,128]{5,4,3,2,1,0:T(8,128)(2,1)}), bf16[4,2,2,2,16,128]{5,4,3,2,1,0:T(8,128)(2,1)S(1)}, u32[]{:S(2)}, u32[]{:S(2)}) async-start(bf16[4,2,2,2,16,128]{5,4,3,2,1,0:T(8,128)(2,1)} %pad_maximum_fusion), calls=%async_computation.4 | async-start | bytes 262144 | tf_op jit(solution)/shard_map/all_to_all | solution.py:76
  31.4 10.5 %all-to-all-start.2 = ((bf16[4,2,2,4,2048]{4,3,2,1,0:T(4,128)(2,1)}), bf16[4,2,2,4,2048]{4,3,2,1,0:T(4,128)(2,1)S(1)}, u32[]{:S(2)}, u32[]{:S(2)}) async-start(bf16[4,2,2,4,2048]{4,3,2,1,0:T(4,128)(2,1)} %broadcast_in_dim.48), calls=%async_computation.2 | async-start | bytes 524288 | tf_op jit(solution)/shard_map/all_to_all | solution.py:19
  47.3 7.4 %all-to-all-start.3 = ((bf16[4,4,2048]{2,1,0:T(4,128)(2,1)}), bf16[4,4,2048]{2,1,0:T(4,128)(2,1)S(1)}, u32[]{:S(2)}, u32[]{:S(2)}) async-start(bf16[4,4,2048]{2,1,0:T(4,128)(2,1)} %broadcast_in_dim.49), calls=%async_computation.3 | async-start | bytes 131072 | tf_op jit(solution)/shard_map/all_to_all | solution.py:19
  55.5 12.3 %all-to-all-start.5 = ((bf16[4,2,2,2,64,128]{5,4,3,1,2,0:T(8,128)(2,1)}), bf16[4,2,2,2,64,128]{5,4,3,1,2,0:T(8,128)(2,1)S(1)}, u32[]{:S(2)}, u32[]{:S(2)}) async-start(bf16[4,2,2,2,64,128]{5,4,3,1,2,0:T(8,128)(2,1)} %broadcast_in_dim.50), calls=%async_computation.5 | async-start | bytes 1048576 | tf_op jit(solution)/shard_map/all_to_all | solution.py:19
  67.9 10.0 %copy-start.1 = (bf16[1,4,2048]{2,1,0:T(4,128)(2,1)S(1)}, bf16[1,4,2048]{2,1,0:T(4,128)(2,1)}, u32[]{:S(2)}) copy-start(bf16[1,4,2048]{2,1,0:T(4,128)(2,1)} %param.10) | copy-start | bytes 49156
  67.9 17.6 %copy-start.2 = (bf16[2,4,2048]{2,1,0:T(4,128)(2,1)S(1)}, bf16[2,4,2048]{2,1,0:T(4,128)(2,1)}, u32[]{:S(2)}) copy-start(bf16[2,4,2048]{2,1,0:T(4,128)(2,1)} %param.11) | copy-start | bytes 98308
  73.8 11.7 %all-to-all-start.6 = ((bf16[8,4,2048]{2,1,0:T(4,128)(2,1)}), bf16[8,4,2048]{2,1,0:T(4,128)(2,1)S(1)}, u32[]{:S(2)}, u32[]{:S(2)}) async-start(bf16[8,4,2048]{2,1,0:T(4,128)(2,1)} %broadcast_in_dim.52), calls=%async_computation.6 | async-start | bytes 262144 | tf_op jit(solution)/shard_map/all_to_all | solution.py:113
  77.9 4.1 %collective-permute-start = (bf16[4,2048]{1,0:T(4,128)(2,1)S(1)}, bf16[4,2048]{1,0:T(4,128)(2,1)S(1)}, u32[]{:S(2)}, u32[]{:S(2)}) collective-permute-start(bf16[4,2048]{1,0:T(4,128)(2,1)S(1)} %bitcast.175), channel_id=1, source_target_pairs={{0,16},{16,0},{1,17},{17,1},{2,18},{18,2},{3,19},{19,3},{4,20},{20... | collective-permute-start | bytes 49160 | tf_op jit(solution)/shard_map/ppermute | solution.py:88
  97.1 7.4 %all-to-all-start.8 = ((bf16[4,4,2048]{2,1,0:T(4,128)(2,1)}), bf16[4,4,2048]{2,1,0:T(4,128)(2,1)S(1)}, u32[]{:S(2)}, u32[]{:S(2)}) async-start(bf16[4,4,2048]{2,1,0:T(4,128)(2,1)} %broadcast_in_dim.55), calls=%async_computation.8 | async-start | bytes 131072 | tf_op jit(solution)/shard_map/all_to_all | solution.py:19
  110.3 10.9 %all-to-all-start.9 = ((bf16[8,4,2048]{2,1,0:T(4,128)(2,1)}), bf16[8,4,2048]{2,1,0:T(4,128)(2,1)S(1)}, u32[]{:S(2)}, u32[]{:S(2)}) async-start(bf16[8,4,2048]{2,1,0:T(4,128)(2,1)} %broadcast_in_dim.56), calls=%async_computation.9 | async-start | bytes 262144 | tf_op jit(solution)/shard_map/all_to_all | solution.py:113
  113.7 4.1 %collective-permute-start.1 = (bf16[4,2048]{1,0:T(4,128)(2,1)S(1)}, bf16[4,2048]{1,0:T(4,128)(2,1)S(1)}, u32[]{:S(2)}, u32[]{:S(2)}) collective-permute-start(bf16[4,2048]{1,0:T(4,128)(2,1)S(1)} %get-tuple-element.14), channel_id=1, source_target_pairs={{0,16},{16,0},{1,17},{17,1},{2,18},{18,2},{3,19},{19,3},{4,20},{20... | collective-permute-start | bytes 49160 | tf_op jit(solution)/shard_map/ppermute | solution.py:88
  115.6 3.7 %collective-permute-start.2 = (bf16[4,2048]{1,0:T(4,128)(2,1)S(1)}, bf16[4,2048]{1,0:T(4,128)(2,1)S(1)}, u32[]{:S(2)}, u32[]{:S(2)}) collective-permute-start(bf16[4,2048]{1,0:T(4,128)(2,1)S(1)} %get-tuple-element.10), channel_id=1, source_target_pairs={{0,16},{16,0},{1,17},{17,1},{2,18},{18,2},{3,19},{19,3},{4,20},{20... | collective-permute-start | bytes 49160 | tf_op jit(solution)/shard_map/ppermute | solution.py:90

commit v3 on v1

v3 whole, which is shorter than its diff:
```python
import jax
import jax.numpy as jnp
from jax import lax
from jax.experimental import pallas as pl
from jax.experimental.pallas import tpu as pltpu
from jax.sharding import PartitionSpec as P

HD = 128
BF = jnp.bfloat16
F32 = jnp.float32
VMEM = pl.BlockSpec(memory_space=pltpu.VMEM)
LIMIT = 12 * 1024 * 1024


def swapped(block, axis, bits):
    route = [(i, i ^ bits) for i in range(lax.axis_size(axis))]
    return lax.ppermute(block, axis, route)


def peers(block, axis):
    return [block] + [swapped(block, axis, d) for d in range(1, lax.axis_size(axis))]


def from_behind(block, bits):
    sections, tensors = lax.axis_size("section"), lax.axis_size("tensor")
    route = [
        (s * tensors + (t ^ bits), (s + 1) % sections * tensors + t)
        for s in range(sections)
        for t in range(tensors)
    ]
    return lax.ppermute(block, ("section", "tensor"), route)


def tree_sum(pieces):
    pieces = [piece.astype(F32) for piece in pieces]
    while len(pieces) > 1:
        pieces = [pieces[i] + pieces[i + 1] for i in range(0, len(pieces), 2)]
    return pieces[0]


def hold_kernel(parts, after_ref, w_ref, out_ref, sems):
    rows = w_ref.shape[0] // parts
    copies = [
        pltpu.make_async_copy(
            w_ref.at[pl.ds(i * rows, rows)], out_ref.at[pl.ds(i * rows, rows)], sems.at[i]
        )
        for i in range(parts)
    ]
    for copy in copies:
        copy.start()
    for copy in copies:
        copy.wait()


def hold(weights, after):
    weights = pltpu.with_memory_space_constraint(weights, pltpu.HBM)
    parts = 8
    return pl.pallas_call(
        lambda *refs: hold_kernel(parts, *refs),
        out_shape=pltpu.VMEM(weights.shape, weights.dtype),
        in_specs=[VMEM, pl.BlockSpec(memory_space=pltpu.HBM)],
        out_specs=VMEM,
        scratch_shapes=[pltpu.SemaphoreType.DMA((parts,))],
        compiler_params=pltpu.CompilerParams(vmem_limit_bytes=LIMIT),
        cost_estimate=pl.CostEstimate(
            flops=0, bytes_accessed=2 * weights.size, transcendentals=0
        ),
    )(after, weights)


def tiled_dot(x, w_ref, out_ref):
    width = min(512, w_ref.shape[1])
    for i in range(w_ref.shape[1] // width):
        at = slice(i * width, (i + 1) * width)
        out_ref[:, at] = jnp.dot(x, w_ref[:, at], preferred_element_type=F32).astype(out_ref.dtype)


def times_kernel(x_ref, w_ref, out_ref):
    tiled_dot(x_ref[...], w_ref, out_ref)


def times(x, w, dtype):
    return pl.pallas_call(
        times_kernel,
        out_shape=jax.ShapeDtypeStruct((x.shape[0], w.shape[1]), dtype),
        in_specs=[VMEM, VMEM],
        out_specs=VMEM,
        compiler_params=pltpu.CompilerParams(vmem_limit_bytes=LIMIT),
        cost_estimate=pl.CostEstimate(
            flops=2 * x.shape[0] * w.size, bytes_accessed=2 * w.size, transcendentals=0
        ),
    )(x, w)


def attend_kernel(count, batch_ref, *refs):
    pieces, (keep_ref, kv_ref, w_ref, out_ref) = refs[:count], refs[count:]
    batch = batch_ref[0]
    query = tree_sum([piece[...] for piece in pieces]).astype(BF).astype(F32)
    slots, kv_dev = kv_ref.shape[0], kv_ref.shape[3]
    heads = query.shape[1] // HD
    per_kv = heads // kv_dev
    rows = query.shape[0]
    keep = jnp.concatenate([keep_ref[...]] * per_kv, 0)
    att = []
    for g in range(kv_dev):
        mine = jnp.concatenate(
            [query[:, h * HD : (h + 1) * HD] for h in range(g * per_kv, (g + 1) * per_kv)], 0
        ).astype(BF)
        keys = jnp.concatenate([kv_ref[i, 0, batch, g] for i in range(slots)], 0)
        values = jnp.concatenate([kv_ref[i, 1, batch, g] for i in range(slots)], 0)
        scores = lax.dot_general(
            mine, keys, (((1,), (1,)), ((), ())), preferred_element_type=F32
        )
        scores = scores * (HD**-0.5) + keep
        probs = jnp.exp(scores - jnp.max(scores, axis=-1, keepdims=True))
        total = jnp.sum(probs, axis=-1, keepdims=True)
        got = jnp.dot(probs.astype(BF), values, preferred_element_type=F32) / total
        att += [got[h * rows : (h + 1) * rows] for h in range(per_kv)]
    tiled_dot(jnp.concatenate(att, 1).astype(BF), w_ref, out_ref)


def attend(batch, pieces, keep, kv, w):
    count = len(pieces)
    return pl.pallas_call(
        lambda *refs: attend_kernel(count, *refs),
        out_shape=jax.ShapeDtypeStruct((pieces[0].shape[0], w.shape[1]), BF),
        in_specs=[pl.BlockSpec(memory_space=pltpu.SMEM)] + [VMEM] * (count + 3),
        out_specs=VMEM,
        compiler_params=pltpu.CompilerParams(vmem_limit_bytes=LIMIT),
        cost_estimate=pl.CostEstimate(
            flops=8 * w.size, bytes_accessed=2 * w.size, transcendentals=0
        ),
    )(batch.reshape(1).astype(jnp.int32), *pieces, keep, kv, w)


def on_device(state, next_embed, tenant, lengths, gain, bias, wq, wo, keys, values):
    sections = lax.axis_size("section")
    tensors = lax.axis_size("tensor")
    replicas = lax.axis_size("replica")
    section_at = lax.axis_index("section")
    tensor_at = lax.axis_index("tensor")
    replica_at = lax.axis_index("replica")
    rows_mb = state.shape[1]
    width_part = state.shape[2]
    width_all = width_part * replicas
    query_part = wq.shape[2]
    heads_dev = query_part // HD
    key_heads = keys.shape[3]
    group = heads_dev * tensors // key_heads
    kv_dev = max(1, heads_dev // group)
    pos_dev = keys.shape[4]
    batches = [(section_at - tick) % sections for tick in range(sections)]

    local = tenant.reshape(-1) - tensor_at * gain.shape[1]
    onehot = (local[:, None] == jnp.arange(gain.shape[1])[None, :]).astype(BF)
    shape = (sections, rows_mb, width_part)
    gain_mine = jnp.dot(onehot, gain[0], preferred_element_type=F32).astype(BF).reshape(shape)
    bias_mine = jnp.dot(onehot, bias[0], preferred_element_type=F32).astype(BF).reshape(shape)

    def affine_mine(tick):
        pick = lambda rows: lax.dynamic_index_in_dim(rows, batches[tick], 0, keepdims=False)
        return jnp.concatenate([pick(gain_mine), pick(bias_mine)], 0)

    affine = [tree_sum(peers(affine_mine(0), "tensor"))]

    def local_stats(hf):
        return jnp.concatenate([jnp.sum(hf, axis=-1), jnp.sum(hf * hf, axis=-1)])

    h = state[0]
    hf = h.astype(F32)
    first = peers(jnp.concatenate([local_stats(hf), lengths[:, 0].astype(F32)]), "replica")
    stats = tree_sum([piece[: 2 * rows_mb] for piece in first])

    kv = jnp.stack([keys[0, :, 0], values[0, :, 0]], 0)
    later = [affine_mine(tick) for tick in range(1, sections)]
    later = [] if sections == 1 else [jnp.concatenate(later, 0)]

    def heads_of(place):
        start = place * heads_dev // group
        return lax.dynamic_slice_in_dim(kv, start, kv_dev, 2)

    sent = [
        jnp.concatenate(later + [heads_of(tensor_at ^ d).reshape(-1, width_part)], 0)
        for d in range(tensors)
    ]
    got = [sent[0]] + [swapped(sent[d], "tensor", d) for d in range(1, tensors)]
    split = sum(rows.shape[0] for rows in later)
    if split:
        rest = tree_sum([piece[:split] for piece in got])
        affine += [rest[i : i + 2 * rows_mb] for i in range(0, split, 2 * rows_mb)]
    kv_shape = (2, sections, kv_dev, pos_dev, HD)
    kv = jnp.concatenate([piece[split:].reshape(kv_shape) for piece in got], 3)[None]
    turns = [0]
    bit = replicas // 2
    while bit:
        kv = jnp.concatenate([kv, swapped(kv, "replica", bit)], 0)
        turns = turns + [turn ^ bit for turn in turns]
        bit //= 2

    spots = jnp.concatenate([(tensor_at ^ d) * pos_dev + jnp.arange(pos_dev) for d in range(tensors)])
    spots = spots.astype(F32)

    def keep_of(tick):
        cols = []
        for turn in turns:
            length = lax.dynamic_index_in_dim(first[turn][2 * rows_mb :], batches[tick], 0)
            own = jnp.arange(rows_mb)[:, None] == (replica_at ^ turn)
            cols.append(jnp.where(own & (spots < length)[None, :], 0.0, -1e30))
        return jnp.concatenate(cols, 1)

    def scale_of(stats):
        mean = (stats[:rows_mb] / width_all)[:, None]
        var = (stats[rows_mb:] / width_all)[:, None] - mean * mean
        return mean, lax.rsqrt(var + 1e-05)

    wq_held = hold(wq[0], h)
    wo_held = None
    emitted = jnp.zeros_like(h)
    at_first = section_at == 0
    for tick in range(sections):
        gain_now, bias_now = affine[tick][:rows_mb], affine[tick][rows_mb:]
        if tick == 0:
            mean, rstd = scale_of(stats)
            normed = ((hf - mean) * rstd * gain_now + bias_now).astype(BF)
            query = times(normed, wq_held, BF)
            wo_held = hold(wo[0], query)
        else:
            mine = jnp.mean(hf, axis=-1, keepdims=True)
            centred = ((hf - mine) * gain_now).astype(BF)
            rows = jnp.concatenate([centred, affine[tick].astype(BF)], 0)
            stats = tree_sum(peers(local_stats(hf), "replica"))
            three = times(rows, wq_held, F32)
            mean, rstd = scale_of(stats)
            query = rstd * (three[:rows_mb] + (mine - mean) * three[rows_mb : 2 * rows_mb])
            query = (query + three[2 * rows_mb :]).astype(BF)
        if tick == 0:
            behind = from_behind(h, 0)
        else:
            both = from_behind(jnp.concatenate([h, emitted], 0), 0)
            behind, emitted = both[:rows_mb], both[rows_mb:]
        out = attend(batches[tick], peers(query, "replica"), keep_of(tick), kv, wo_held)
        out = tree_sum([from_behind(out, d) for d in range(tensors)])
        h = (behind.astype(F32) + out).astype(BF)
        arriving = -(tick + 1) % sections
        emitted = jnp.where(at_first, h, emitted)
        h = jnp.where(at_first, next_embed[arriving], h)
        hf = h.astype(F32)
    return (h[None], emitted[None])


def solution(mesh):
    in_specs = (
        P("section", None, "replica"),
        P(None, None, "replica"),
        P(),
        P(None, "replica"),
        P("section", "tensor", "replica"),
        P("section", "tensor", "replica"),
        P("section", "replica", "tensor"),
        P("section", "tensor", "replica"),
        P("section", None, "replica", None, "tensor", None),
        P("section", None, "replica", None, "tensor", None),
    )
    out_specs = (P("section", None, "replica"), P("section", None, "replica"))
    return jax.shard_map(
        on_device, mesh=mesh, in_specs=in_specs, out_specs=out_specs, check_vma=False
    )
```

time: 86 us -> 86.1 us (level)
  matrix products: 21 us -> 1.45 us
  Pallas kernels: 0 us -> 12.7 us
  other arithmetic: 5.01 us -> 11 us
  waiting for transfers between devices: 21.3 us -> 18.4 us
  starting transfers between devices: 35.2 us -> 38.1 us
  local copies, waits for them, and re-layouts: 2.13 us -> 3.15 us
    dot_general x8 -> x2, matrix products: 20.3 us -> 1.45 us  [the longest x1 1.23 us: on_device(): jnp.dot(onehot, gain[0], preferred_element_type=F32).astype(BF)]
    pallas_call x0 -> x6, Pallas kernels: none -> 12.7 us  [the longest x2 6.94 us: hold(): pl.pallas_call(lambda *refs: hold_kernel(parts, *refs), out_shape=pltpu.V...]
    ppermute x3 -> x10, starting transfers between devices: 4.67 us -> 16.8 us  [from_behind(): return lax.ppermute(block, ('section', 'tensor'), route)]
    ppermute x30 -> x20, starting transfers between devices: 30.5 us -> 21.3 us  [swapped(): return lax.ppermute(block, axis, route)]
    lt x0 -> x2, other arithmetic: none -> 5.03 us  [keep_of(): cols.append(jnp.where(own & (spots < length)[None, :], 0.0, -1e+30))]
    ppermute x30 -> x20, waiting for transfers between devices: 16.8 us -> 13.3 us  [swapped(): return lax.ppermute(block, axis, route)]
    dynamic_slice x4 -> x3, local copies, waits for them, and re-layouts: 0.3 us -> 1.98 us  [keep_of(): lax.dynamic_index_in_dim(first[turn][2 * rows_mb:], batches[tick], 0)]
    gather x1 -> x0, local copies, waits for them, and re-layouts: 1.24 us -> none  [on_device(): ids = tenant[order].reshape(-1)]
  transfers between devices with their start and end apart: 33 -> 30, of which waited for: 15 -> 10; matrix products, arithmetic and copies ran while one was open for 13% -> 14% of each run, Pallas kernels for 0% -> 15%
where the time goes in v3:
time: 86.1 us; the launch traced here: 85.7 us
  starting transfers between devices  38.1 us (44%)
  waiting for transfers between devices  18.4 us (21%)
  Pallas kernels  12.7 us (15%)
  other arithmetic  11 us (13%)
  local copies, waits for them, and re-layouts  3.15 us (4%)
  matrix products  1.45 us (2%)
  between operations  0.96 us (1%)
    ppermute x20, starting transfers between devices, swapped(): return lax.ppermute(block, axis, route)  21.3 us
    ppermute x10, starting transfers between devices, from_behind(): return lax.ppermute(block, ('section', 'tensor'), route)  16.8 us
    ppermute x20, waiting for transfers between devices, swapped(): return lax.ppermute(block, axis, route)  13.3 us
    pallas_call x2, Pallas kernels, hold(): pl.pallas_call(lambda *refs: hold_kernel(parts, *refs), out_shape=pltpu.V...  6.94 us
    ppermute x10, waiting for transfers between devices, from_behind(): return lax.ppermute(block, ('section', 'tensor'), route)  5.11 us
    lt x2, other arithmetic, keep_of(): cols.append(jnp.where(own & (spots < length)[None, :], 0.0, -1e+30))  5.03 us
    pallas_call x2, Pallas kernels, attend(): pl.pallas_call(lambda *refs: attend_kernel(count, *refs), out_shape=jax.S...  3.33 us
    pallas_call x2, Pallas kernels, times(): pl.pallas_call(times_kernel, out_shape=jax.ShapeDtypeStruct((x.shape[0],...  2.38 us
  transfers between devices with their start and end apart: 30, of which 10 were waited for; matrix products, arithmetic and copies ran while one was open for 14% of the time, Pallas kernels for 15%

profile of v3, /device:TPU:0, one launch (start us, length us, event | category | flops | bytes accessed | tf_op | source)
XLA Modules:
  0.0 85.7 jit_solution(471018408723379601)
XLA Ops:
  0.6 0.7 fusion.27
  1.4 0.9 %convert_reduce_fusion.1 = (f32[4]{0:T(128)S(1)}, f32[4]{0:T(128)S(1)}) fusion(bf16[1,4,2048]{2,1,0:T(4,128)(2,1)} %param.10), kind=kLoop, calls=%fused_computation.27 | loop fusion | flops 32760 | bytes 16416 | tf_op jit(solution)/shard_map/reduce_sum | solution.py:167
  2.3 2.4 %collective-permute-start.3 = (f32[10]{0:T(128)S(1)}, f32[10]{0:T(128)S(1)}, u32[]{:S(2)}, u32[]{:S(2)}) collective-permute-start(f32[10]{0:T(128)S(1)} %pad_maximum_fusion.11), channel_id=1, source_target_pairs={{0,3},{1,2},{2,1},{3,0},{4,7},{5,6},{6,5},{7,4},{8,11},{9,10},{10,... | collective-permute-start | bytes 128 | tf_op jit(solution)/shard_map/ppermute | solution.py:17
  4.7 0.6 collective-permute-start.2
  5.4 1.7 %collective-permute-start = (bf16[4,2048]{1,0:T(4,128)(2,1)}, bf16[4,2048]{1,0:T(4,128)(2,1)S(1)}, u32[]{:S(2)}, u32[]{:S(2)}) collective-permute-start(bf16[4,2048]{1,0:T(4,128)(2,1)} %bitcast.72), channel_id=1, source_target_pairs={{0,16},{4,20},{8,24},{12,28},{16,0},{20,4},{24,8},{28,12},{1,17},{... | collective-permute-start | bytes 49160 | tf_op jit(solution)/shard_map/ppermute | solution.py:31
  7.1 0.7 broadcast_subtract_fusion
  8.1 1.2 %convolution_convert_fusion.1 = bf16[8,2048]{1,0:T(8,128)(2,1)S(1)} fusion(bf16[1,100,2048]{2,1,0:T(8,128)(2,1)} %param.14, s32[8]{0:T(128)S(1)} %sub.62), kind=kOutput, calls=%fused_computation.1 | convolution fusion | flops 3293984 | bytes 442400 | tf_op jit(solution)/shard_map/dot_general | solution.py:157
  9.5 2.7 %collective-permute-start.5 = (bf16[8,2048]{1,0:T(8,128)(2,1)S(1)}, bf16[8,2048]{1,0:T(8,128)(2,1)S(1)}, u32[]{:S(2)}, u32[]{:S(2)}) collective-permute-start(bf16[8,2048]{1,0:T(8,128)(2,1)S(1)} %pad_maximum_fusion.7), channel_id=1, source_target_pairs={{0,8},{4,12},{8,0},{12,4},{1,9},{5,13},{9,1},{13,5},{2,10},{6,14},... | collective-permute-start | bytes 98312 | tf_op jit(solution)/shard_map/ppermute | solution.py:17
  12.2 0.7 constant_dynamic-slice_fusion.1
  12.9 0.9 fusion.11
  13.7 0.7 copy-done.1
  14.5 3.5 %shard_map.113.w_ref = bf16[2048,2048]{1,0:T(8,128)(2,1)S(1)} custom-call(bf16[4,2048]{1,0:T(4,128)(2,1)S(1)} %bitcast.73, bf16[2048,2048]{1,0:T(8,128)(2,1)} %bitcast.74), custom_call_target="tpu_custom_call" | custom-call | bytes 8388608 | tf_op jit(solution)/shard_map/pallas_call | solution.py:58
  18.0 0.8 broadcast_compare_fusion.3
  18.8 1.6 %collective-permute-start.4 = (bf16[8,2048]{1,0:T(8,128)(2,1)S(1)}, bf16[8,2048]{1,0:T(8,128)(2,1)S(1)}, u32[]{:S(2)}, u32[]{:S(2)}) collective-permute-start(bf16[8,2048]{1,0:T(8,128)(2,1)S(1)} %pad_maximum_fusion.7), channel_id=1, source_target_pairs={{0,4},{4,0},{8,12},{12,8},{1,5},{5,1},{9,13},{13,9},{2,6},{6,2},{1... | collective-permute-start | bytes 98312 | tf_op jit(solution)/shard_map/ppermute | solution.py:17
  20.5 0.7 fusion.26
  21.4 0.7 collective-permute-start.10
  22.3 0.7 fusion.24
  23.0 4.3 %broadcast_compare_fusion.2 = (pred[64]{0:T(512)(128)(4,1)S(1)}, pred[64]{0:T(512)(128)(4,1)S(1)}, pred[64]{0:T(512)(128)(4,1)S(1)}, pred[64]{0:T(512)(128)(4,1)...) fusion(f32[64]{0:T(128)S(1)} %get-tuple-element.11, f32[]{:T(128)} %bitcast.22, ...), kind=kLoop, calls=%fused_computation.101 | loop fusion | flops 448 | bytes 732 | tf_op jit(solution)/shard_map/lt | solution.py:208
  27.7 3.5 %collective-permute-start.11 = (bf16[16,2048]{1,0:T(8,128)(2,1)S(1)}, bf16[16,2048]{1,0:T(8,128)(2,1)S(1)}, u32[]{:S(2)}, u32[]{:S(2)}) collective-permute-start(bf16[16,2048]{1,0:T(8,128)(2,1)S(1)} %get-tuple-element.20), channel_id=1, source_target_pairs={{0,8},{4,12},{8,0},{12,4},{1,9},{5,13},{9,1},{13,5},{2,10},{6,14},... | collective-permute-start | bytes 196616 | tf_op jit(solution)/shard_map/ppermute | solution.py:17
  31.2 2.9 %collective-permute-done.11 = bf16[16,2048]{1,0:T(8,128)(2,1)S(1)} collective-permute-done((bf16[16,2048]{1,0:T(8,128)(2,1)S(1)}, bf16[16,2048]{1,0:T(8,128)(2,1)S(1)}, u32[]{:S(2)}, u32[]{:S(2)}) %collective-permute-start.11) | collective-permute-done | bytes 65568 | tf_op jit(solution)/shard_map/ppermute | solution.py:17
  34.1 1.7 %collective-permute-start.12 = (bf16[16,2048]{1,0:T(8,128)(2,1)S(1)}, bf16[16,2048]{1,0:T(8,128)(2,1)S(1)}, u32[]{:S(2)}, u32[]{:S(2)}) collective-permute-start(bf16[16,2048]{1,0:T(8,128)(2,1)S(1)} %get-tuple-element.21), channel_id=1, source_target_pairs={{0,12},{4,8},{8,4},{12,0},{1,13},{5,9},{9,5},{13,1},{2,14},{6,10},... | collective-permute-start | bytes 196616 | tf_op jit(solution)/shard_map/ppermute | solution.py:17
  35.8 4.3 %collective-permute-done.12 = bf16[16,2048]{1,0:T(8,128)(2,1)S(1)} collective-permute-done((bf16[16,2048]{1,0:T(8,128)(2,1)S(1)}, bf16[16,2048]{1,0:T(8,128)(2,1)S(1)}, u32[]{:S(2)}, u32[]{:S(2)}) %collective-permute-start.12) | collective-permute-done | bytes 65568 | tf_op jit(solution)/shard_map/ppermute | solution.py:17
  40.2 1.6 %collective-permute-start.13 = (bf16[1,2,2,2,64,128]{5,4,3,2,1,0:T(8,128)(2,1)S(1)}, bf16[1,2,2,2,64,128]{5,4,3,2,1,0:T(8,128)(2,1)S(1)}, u32[]{:S(2)}, u32[]{:S(2)}) collective-permute-start(bf16[1,2,2,2,64,128]{5,4,3,2,1,0:T(8,128)(2,1)S(1)} %maximum_bitcast_fusion), channel_id=1, source_target_pairs={{0,2},{1,3},{2,0},{3,1},{4,6},{5,7},{6,4},{7,5},{8,10},{9,11},{10,... | collective-permute-start | bytes 393224 | tf_op jit(solution)/shard_map/ppermute | solution.py:17
  41.9 3.4 %collective-permute-done.13 = bf16[1,2,2,2,64,128]{5,4,3,2,1,0:T(8,128)(2,1)S(1)} collective-permute-done((bf16[1,2,2,2,64,128]{5,4,3,2,1,0:T(8,128)(2,1)S(1)}, bf16[1,2,2,2,64,128]{5,4,3,2,1,0:T(8,128)(2,1)S(1)}, u32[]{:S(2)}, u32[]{:S(2)}) %collective-permute-start.13) | collective-permute-done | bytes 131104 | tf_op jit(solution)/shard_map/ppermute | solution.py:17
  45.4 1.2 %shard_map.114.refs_0_.refs_1_ = bf16[4,2048]{1,0:T(4,128)(2,1)S(1)} custom-call(bf16[4,2048]{1,0:T(4,128)(2,1)S(1)} %fusion.6.x_ref, bf16[2048,2048]{1,0:T(8,128)(2,1)S(1)} %shard_map.113.w_ref), custom_call_target="tpu_custom_call" | custom-call | flops 33554432 | bytes 8388608 | tf_op jit(solution)/shard_map/pallas_call | solution.py:83
  46.6 1.6 %collective-permute-start.9 = (bf16[4,2048]{1,0:T(4,128)(2,1)S(1)}, bf16[4,2048]{1,0:T(4,128)(2,1)S(1)}, u32[]{:S(2)}, u32[]{:S(2)}) collective-permute-start(bf16[4,2048]{1,0:T(4,128)(2,1)S(1)} %shard_map.114.refs_0_.refs_1_), channel_id=1, source_target_pairs={{0,3},{1,2},{2,1},{3,0},{4,7},{5,6},{6,5},{7,4},{8,11},{9,10},{10,... | collective-permute-start | bytes 49160 | tf_op jit(solution)/shard_map/ppermute | solution.py:17
  48.8 3.5 %shard_map.115.refs_7_ = bf16[2048,2048]{1,0:T(8,128)(2,1)S(1)} custom-call(bf16[4,2048]{1,0:T(4,128)(2,1)S(1)} %shard_map.114.refs_0_.refs_1_, bf16[2048,2048]{1,0:T(8,128)(2,1)} %bitcast.75), custom_call_target="tpu_custom_call" | custom-call | bytes 8388608 | tf_op jit(solution)/shard_map/pallas_call | solution.py:58
  52.4 1.7 %shard_map.116 = bf16[4,2048]{1,0:T(4,128)(2,1)S(1)} custom-call(s32[1]{0:T(128)} %bitcast.3.refs_0_, bf16[4,2048]{1,0:T(4,128)(2,1)S(1)} %shard_map.114.refs_0_.refs_1_, bf16[4,2048]{1,0:T(4,128)(2,1)S(1)} %collective-permute-done.7.refs_2_, bf16[4,2048]{1,0:T(4,128)(2,1)S(1)} %collective-permute-done.8.refs_3_, ...), custom_call_target="tpu_custom_call" | custom-call | flops 33554432 | bytes 8388608 | tf_op jit(solution)/shard_map/pallas_call | solution.py:124
  54.0 1.8 %collective-permute-start.18 = (bf16[4,2048]{1,0:T(4,128)(2,1)S(1)}, bf16[4,2048]{1,0:T(4,128)(2,1)S(1)}, u32[]{:S(2)}, u32[]{:S(2)}) collective-permute-start(bf16[4,2048]{1,0:T(4,128)(2,1)S(1)} %shard_map.116), channel_id=1, source_target_pairs={{12,16},{8,20},{4,24},{0,28},{28,0},{24,4},{20,8},{16,12},{13,17},... | collective-permute-start | bytes 49160 | tf_op jit(solution)/shard_map/ppermute | solution.py:31
  55.8 3.5 %collective-permute-start.16 = (bf16[4,2048]{1,0:T(4,128)(2,1)S(1)}, bf16[4,2048]{1,0:T(4,128)(2,1)S(1)}, u32[]{:S(2)}, u32[]{:S(2)}) collective-permute-start(bf16[4,2048]{1,0:T(4,128)(2,1)S(1)} %shard_map.116), channel_id=1, source_target_pairs={{4,16},{0,20},{12,24},{8,28},{20,0},{16,4},{28,8},{24,12},{5,17},{... | collective-permute-start | bytes 49160 | tf_op jit(solution)/shard_map/ppermute | solution.py:31
  59.3 1.5 %collective-permute-start.15 = (bf16[4,2048]{1,0:T(4,128)(2,1)S(1)}, bf16[4,2048]{1,0:T(4,128)(2,1)S(1)}, u32[]{:S(2)}, u32[]{:S(2)}) collective-permute-start(bf16[4,2048]{1,0:T(4,128)(2,1)S(1)} %shard_map.116), channel_id=1, source_target_pairs={{0,16},{4,20},{8,24},{12,28},{16,0},{20,4},{24,8},{28,12},{1,17},{... | collective-permute-start | bytes 49160 | tf_op jit(solution)/shard_map/ppermute | solution.py:31
  61.4 1.7 %collective-permute-done.15 = bf16[4,2048]{1,0:T(4,128)(2,1)S(1)} collective-permute-done((bf16[4,2048]{1,0:T(4,128)(2,1)S(1)}, bf16[4,2048]{1,0:T(4,128)(2,1)S(1)}, u32[]{:S(2)}, u32[]{:S(2)}) %collective-permute-start.15) | collective-permute-done | bytes 16416 | tf_op jit(solution)/shard_map/ppermute | solution.py:31
  63.4 1.6 %collective-permute-start.21 = (f32[8]{0:T(128)S(1)}, f32[8]{0:T(128)S(1)}, u32[]{:S(2)}, u32[]{:S(2)}) collective-permute-start(f32[8]{0:T(128)S(1)} %pad_maximum_fusion.12), channel_id=1, source_target_pairs={{0,2},{1,3},{2,0},{3,1},{4,6},{5,7},{6,4},{7,5},{8,10},{9,11},{10,... | collective-permute-start | bytes 104 | tf_op jit(solution)/shard_map/ppermute | solution.py:17
  65.2 1.6 %collective-permute-start.19 = (bf16[8,2048]{1,0:T(8,128)(2,1)S(1)}, bf16[8,2048]{1,0:T(8,128)(2,1)S(1)}, u32[]{:S(2)}, u32[]{:S(2)}) collective-permute-start(bf16[8,2048]{1,0:T(8,128)(2,1)S(1)} %pad_maximum_fusion.8), channel_id=1, source_target_pairs={{0,16},{4,20},{8,24},{12,28},{16,0},{20,4},{24,8},{28,12},{1,17},{... | collective-permute-start | bytes 98312 | tf_op jit(solution)/shard_map/ppermute | solution.py:31
  67.2 1.2 %shard_map.117 = f32[12,2048]{1,0:T(8,128)S(1)} custom-call(bf16[12,2048]{1,0:T(8,128)(2,1)S(1)} %pad_maximum_fusion.6.x_ref, bf16[2048,2048]{1,0:T(8,128)(2,1)S(1)} %shard_map.113.w_ref), custom_call_target="tpu_custom_call" | custom-call | flops 100663296 | bytes 8388608 | tf_op jit(solution)/shard_map/pallas_call | solution.py:83
  68.5 0.8 collective-permute-start.25
  69.2 1.4 %collective-permute-start.24 = (bf16[4,2048]{1,0:T(4,128)(2,1)S(1)}, bf16[4,2048]{1,0:T(4,128)(2,1)S(1)}, u32[]{:S(2)}, u32[]{:S(2)}) collective-permute-start(bf16[4,2048]{1,0:T(4,128)(2,1)S(1)} %fusion.14.refs_1_), channel_id=1, source_target_pairs={{0,2},{1,3},{2,0},{3,1},{4,6},{5,7},{6,4},{7,5},{8,10},{9,11},{10,... | collective-permute-start | bytes 49160 | tf_op jit(solution)/shard_map/ppermute | solution.py:17
  70.7 1.0 %collective-permute-done.25.refs_4_ = bf16[4,2048]{1,0:T(4,128)(2,1)S(1)} collective-permute-done((bf16[4,2048]{1,0:T(4,128)(2,1)S(1)}, bf16[4,2048]{1,0:T(4,128)(2,1)S(1)}, u32[]{:S(2)}, u32[]{:S(2)}) %collective-permute-start.25) | collective-permute-done | bytes 16416 | tf_op jit(solution)/shard_map/ppermute | solution.py:17
  71.7 1.4 %collective-permute-done.24.refs_3_ = bf16[4,2048]{1,0:T(4,128)(2,1)S(1)} collective-permute-done((bf16[4,2048]{1,0:T(4,128)(2,1)S(1)}, bf16[4,2048]{1,0:T(4,128)(2,1)S(1)}, u32[]{:S(2)}, u32[]{:S(2)}) %collective-permute-start.24) | collective-permute-done | bytes 16416 | tf_op jit(solution)/shard_map/ppermute | solution.py:17
  73.1 1.7 %shard_map.118 = bf16[4,2048]{1,0:T(4,128)(2,1)S(1)} custom-call(s32[1]{0:T(128)} %bitcast.20.refs_0_, bf16[4,2048]{1,0:T(4,128)(2,1)S(1)} %fusion.14.refs_1_, bf16[4,2048]{1,0:T(4,128)(2,1)S(1)} %collective-permute-done.23.refs_2_, bf16[4,2048]{1,0:T(4,128)(2,1)S(1)} %collective-permute-done.24.refs_3_, ...), custom_call_target="tpu_custom_call" | custom-call | flops 33554432 | bytes 8388608 | tf_op jit(solution)/shard_map/pallas_call | solution.py:124
  74.8 2.5 %collective-permute-start.29 = (bf16[4,2048]{1,0:T(4,128)(2,1)S(1)}, bf16[4,2048]{1,0:T(4,128)(2,1)S(1)}, u32[]{:S(2)}, u32[]{:S(2)}) collective-permute-start(bf16[4,2048]{1,0:T(4,128)(2,1)S(1)} %shard_map.118), channel_id=1, source_target_pairs={{12,16},{8,20},{4,24},{0,28},{28,0},{24,4},{20,8},{16,12},{13,17},... | collective-permute-start | bytes 49160 | tf_op jit(solution)/shard_map/ppermute | solution.py:31
  77.3 0.5 collective-permute-start.28
  77.8 2.9 %collective-permute-start.27 = (bf16[4,2048]{1,0:T(4,128)(2,1)S(1)}, bf16[4,2048]{1,0:T(4,128)(2,1)S(1)}, u32[]{:S(2)}, u32[]{:S(2)}) collective-permute-start(bf16[4,2048]{1,0:T(4,128)(2,1)S(1)} %shard_map.118), channel_id=1, source_target_pairs={{4,16},{0,20},{12,24},{8,28},{20,0},{16,4},{28,8},{24,12},{5,17},{... | collective-permute-start | bytes 49160 | tf_op jit(solution)/shard_map/ppermute | solution.py:31
  80.7 0.8 collective-permute-start.26
  81.5 1.4 %collective-permute-done.28 = bf16[4,2048]{1,0:T(4,128)(2,1)S(1)} collective-permute-done((bf16[4,2048]{1,0:T(4,128)(2,1)S(1)}, bf16[4,2048]{1,0:T(4,128)(2,1)S(1)}, u32[]{:S(2)}, u32[]{:S(2)}) %collective-permute-start.28) | collective-permute-done | bytes 16416 | tf_op jit(solution)/shard_map/ppermute | solution.py:31
  82.9 1.5 %collective-permute-done.26 = bf16[4,2048]{1,0:T(4,128)(2,1)S(1)} collective-permute-done((bf16[4,2048]{1,0:T(4,128)(2,1)S(1)}, bf16[4,2048]{1,0:T(4,128)(2,1)S(1)}, u32[]{:S(2)}, u32[]{:S(2)}) %collective-permute-start.26) | collective-permute-done | bytes 16416 | tf_op jit(solution)/shard_map/ppermute | solution.py:31
  84.5 0.6 fusion.17
  85.1 0.6 fusion.18
  (84 shorter events, 4.1 us)
Async XLA Ops:
  0.6 7.3 %copy-start = (bf16[1,100,2048]{2,1,0:T(8,128)(2,1)S(1)}, bf16[1,100,2048]{2,1,0:T(8,128)(2,1)}, u32[]{:S(2)}) copy-start(bf16[1,100,2048]{2,1,0:T(8,128)(2,1)} %param.15) | copy-start | bytes 1228804
  2.3 16.5 %collective-permute-start.3 = (f32[10]{0:T(128)S(1)}, f32[10]{0:T(128)S(1)}, u32[]{:S(2)}, u32[]{:S(2)}) collective-permute-start(f32[10]{0:T(128)S(1)} %pad_maximum_fusion.11), channel_id=1, source_target_pairs={{0,3},{1,2},{2,1},{3,0},{4,7},{5,6},{6,5},{7,4},{8,11},{9,10},{10,... | collective-permute-start | bytes 128 | tf_op jit(solution)/shard_map/ppermute | solution.py:17
  4.7 16.4 %collective-permute-start.2 = (f32[10]{0:T(128)S(1)}, f32[10]{0:T(128)S(1)}, u32[]{:S(2)}, u32[]{:S(2)}) collective-permute-start(f32[10]{0:T(128)S(1)} %pad_maximum_fusion.11), channel_id=1, source_target_pairs={{0,2},{1,3},{2,0},{3,1},{4,6},{5,7},{6,4},{7,5},{8,10},{9,11},{10,... | collective-permute-start | bytes 128 | tf_op jit(solution)/shard_map/ppermute | solution.py:17
  5.4 16.0 %collective-permute-start.1 = (f32[10]{0:T(128)S(1)}, f32[10]{0:T(128)S(1)}, u32[]{:S(2)}, u32[]{:S(2)}) collective-permute-start(f32[10]{0:T(128)S(1)} %pad_maximum_fusion.11), channel_id=1, source_target_pairs={{0,1},{1,0},{2,3},{3,2},{4,5},{5,4},{6,7},{7,6},{8,9},{9,8},{10,11... | collective-permute-start | bytes 128 | tf_op jit(solution)/shard_map/ppermute | solution.py:17
  5.4 55.5 %collective-permute-start = (bf16[4,2048]{1,0:T(4,128)(2,1)}, bf16[4,2048]{1,0:T(4,128)(2,1)S(1)}, u32[]{:S(2)}, u32[]{:S(2)}) collective-permute-start(bf16[4,2048]{1,0:T(4,128)(2,1)} %bitcast.72), channel_id=1, source_target_pairs={{0,16},{4,20},{8,24},{12,28},{16,0},{20,4},{24,8},{28,12},{1,17},{... | collective-permute-start | bytes 49160 | tf_op jit(solution)/shard_map/ppermute | solution.py:31
  9.5 32.3 %collective-permute-start.5 = (bf16[8,2048]{1,0:T(8,128)(2,1)S(1)}, bf16[8,2048]{1,0:T(8,128)(2,1)S(1)}, u32[]{:S(2)}, u32[]{:S(2)}) collective-permute-start(bf16[8,2048]{1,0:T(8,128)(2,1)S(1)} %pad_maximum_fusion.7), channel_id=1, source_target_pairs={{0,8},{4,12},{8,0},{12,4},{1,9},{5,13},{9,1},{13,5},{2,10},{6,14},... | collective-permute-start | bytes 98312 | tf_op jit(solution)/shard_map/ppermute | solution.py:17
  13.7 0.7 copy-start.1
  18.8 23.0 %collective-permute-start.4 = (bf16[8,2048]{1,0:T(8,128)(2,1)S(1)}, bf16[8,2048]{1,0:T(8,128)(2,1)S(1)}, u32[]{:S(2)}, u32[]{:S(2)}) collective-permute-start(bf16[8,2048]{1,0:T(8,128)(2,1)S(1)} %pad_maximum_fusion.7), channel_id=1, source_target_pairs={{0,4},{4,0},{8,12},{12,8},{1,5},{5,1},{9,13},{13,9},{2,6},{6,2},{1... | collective-permute-start | bytes 98312 | tf_op jit(solution)/shard_map/ppermute | solution.py:17
  21.1 20.7 %collective-permute-start.6 = (bf16[8,2048]{1,0:T(8,128)(2,1)S(1)}, bf16[8,2048]{1,0:T(8,128)(2,1)S(1)}, u32[]{:S(2)}, u32[]{:S(2)}) collective-permute-start(bf16[8,2048]{1,0:T(8,128)(2,1)S(1)} %pad_maximum_fusion.7), channel_id=1, source_target_pairs={{0,12},{4,8},{8,4},{12,0},{1,13},{5,9},{9,5},{13,1},{2,14},{6,10},... | collective-permute-start | bytes 98312 | tf_op jit(solution)/shard_map/ppermute | solution.py:17
  21.4 6.3 %collective-permute-start.10 = (bf16[16,2048]{1,0:T(8,128)(2,1)S(1)}, bf16[16,2048]{1,0:T(8,128)(2,1)S(1)}, u32[]{:S(2)}, u32[]{:S(2)}) collective-permute-start(bf16[16,2048]{1,0:T(8,128)(2,1)S(1)} %get-tuple-element.19), channel_id=1, source_target_pairs={{0,4},{4,0},{8,12},{12,8},{1,5},{5,1},{9,13},{13,9},{2,6},{6,2},{1... | collective-permute-start | bytes 196616 | tf_op jit(solution)/shard_map/ppermute | solution.py:17
  27.7 6.4 %collective-permute-start.11 = (bf16[16,2048]{1,0:T(8,128)(2,1)S(1)}, bf16[16,2048]{1,0:T(8,128)(2,1)S(1)}, u32[]{:S(2)}, u32[]{:S(2)}) collective-permute-start(bf16[16,2048]{1,0:T(8,128)(2,1)S(1)} %get-tuple-element.20), channel_id=1, source_target_pairs={{0,8},{4,12},{8,0},{12,4},{1,9},{5,13},{9,1},{13,5},{2,10},{6,14},... | collective-permute-start | bytes 196616 | tf_op jit(solution)/shard_map/ppermute | solution.py:17
  34.1 6.1 %collective-permute-start.12 = (bf16[16,2048]{1,0:T(8,128)(2,1)S(1)}, bf16[16,2048]{1,0:T(8,128)(2,1)S(1)}, u32[]{:S(2)}, u32[]{:S(2)}) collective-permute-start(bf16[16,2048]{1,0:T(8,128)(2,1)S(1)} %get-tuple-element.21), channel_id=1, source_target_pairs={{0,12},{4,8},{8,4},{12,0},{1,13},{5,9},{9,5},{13,1},{2,14},{6,10},... | collective-permute-start | bytes 196616 | tf_op jit(solution)/shard_map/ppermute | solution.py:17
  40.2 5.0 %collective-permute-start.13 = (bf16[1,2,2,2,64,128]{5,4,3,2,1,0:T(8,128)(2,1)S(1)}, bf16[1,2,2,2,64,128]{5,4,3,2,1,0:T(8,128)(2,1)S(1)}, u32[]{:S(2)}, u32[]{:S(2)}) collective-permute-start(bf16[1,2,2,2,64,128]{5,4,3,2,1,0:T(8,128)(2,1)S(1)} %maximum_bitcast_fusion), channel_id=1, source_target_pairs={{0,2},{1,3},{2,0},{3,1},{4,6},{5,7},{6,4},{7,5},{8,10},{9,11},{10,... | collective-permute-start | bytes 393224 | tf_op jit(solution)/shard_map/ppermute | solution.py:17
  45.3 7.0 %collective-permute-start.14 = (bf16[2,2,2,2,64,128]{5,4,3,2,1,0:T(8,128)(2,1)S(1)}, bf16[2,2,2,2,64,128]{5,4,3,2,1,0:T(8,128)(2,1)S(1)}, u32[]{:S(2)}, u32[]{:S(2)}) collective-permute-start(bf16[2,2,2,2,64,128]{5,4,3,2,1,0:T(8,128)(2,1)S(1)} %pad_maximum_fusion.1), channel_id=1, source_target_pairs={{0,1},{1,0},{2,3},{3,2},{4,5},{5,4},{6,7},{7,6},{8,9},{9,8},{10,11... | collective-permute-start | bytes 786440 | tf_op jit(solution)/shard_map/ppermute | solution.py:17
  46.6 5.7 %collective-permute-start.9 = (bf16[4,2048]{1,0:T(4,128)(2,1)S(1)}, bf16[4,2048]{1,0:T(4,128)(2,1)S(1)}, u32[]{:S(2)}, u32[]{:S(2)}) collective-permute-start(bf16[4,2048]{1,0:T(4,128)(2,1)S(1)} %shard_map.114.refs_0_.refs_1_), channel_id=1, source_target_pairs={{0,3},{1,2},{2,1},{3,0},{4,7},{5,6},{6,5},{7,4},{8,11},{9,10},{10,... | collective-permute-start | bytes 49160 | tf_op jit(solution)/shard_map/ppermute | solution.py:17
  48.3 4.1 %collective-permute-start.8 = (bf16[4,2048]{1,0:T(4,128)(2,1)S(1)}, bf16[4,2048]{1,0:T(4,128)(2,1)S(1)}, u32[]{:S(2)}, u32[]{:S(2)}) collective-permute-start(bf16[4,2048]{1,0:T(4,128)(2,1)S(1)} %shard_map.114.refs_0_.refs_1_), channel_id=1, source_target_pairs={{0,2},{1,3},{2,0},{3,1},{4,6},{5,7},{6,4},{7,5},{8,10},{9,11},{10,... | collective-permute-start | bytes 49160 | tf_op jit(solution)/shard_map/ppermute | solution.py:17
  48.8 3.6 %collective-permute-start.7 = (bf16[4,2048]{1,0:T(4,128)(2,1)S(1)}, bf16[4,2048]{1,0:T(4,128)(2,1)S(1)}, u32[]{:S(2)}, u32[]{:S(2)}) collective-permute-start(bf16[4,2048]{1,0:T(4,128)(2,1)S(1)} %shard_map.114.refs_0_.refs_1_), channel_id=1, source_target_pairs={{0,1},{1,0},{2,3},{3,2},{4,5},{5,4},{6,7},{7,6},{8,9},{9,8},{10,11... | collective-permute-start | bytes 49160 | tf_op jit(solution)/shard_map/ppermute | solution.py:17
  52.3 10.8 %copy-start.2 = (bf16[2,4,2048]{2,1,0:T(4,128)(2,1)S(1)}, bf16[2,4,2048]{2,1,0:T(4,128)(2,1)}, u32[]{:S(2)}) copy-start(bf16[2,4,2048]{2,1,0:T(4,128)(2,1)} %param.11) | copy-start | bytes 98308
  54.0 6.8 %collective-permute-start.18 = (bf16[4,2048]{1,0:T(4,128)(2,1)S(1)}, bf16[4,2048]{1,0:T(4,128)(2,1)S(1)}, u32[]{:S(2)}, u32[]{:S(2)}) collective-permute-start(bf16[4,2048]{1,0:T(4,128)(2,1)S(1)} %shard_map.116), channel_id=1, source_target_pairs={{12,16},{8,20},{4,24},{0,28},{28,0},{24,4},{20,8},{16,12},{13,17},... | collective-permute-start | bytes 49160 | tf_op jit(solution)/shard_map/ppermute | solution.py:31
  55.8 5.5 %collective-permute-start.17 = (bf16[4,2048]{1,0:T(4,128)(2,1)S(1)}, bf16[4,2048]{1,0:T(4,128)(2,1)S(1)}, u32[]{:S(2)}, u32[]{:S(2)}) collective-permute-start(bf16[4,2048]{1,0:T(4,128)(2,1)S(1)} %shard_map.116), channel_id=1, source_target_pairs={{8,16},{12,20},{0,24},{4,28},{24,0},{28,4},{16,8},{20,12},{9,17},{... | collective-permute-start | bytes 49160 | tf_op jit(solution)/shard_map/ppermute | solution.py:31
  55.8 5.5 %collective-permute-start.16 = (bf16[4,2048]{1,0:T(4,128)(2,1)S(1)}, bf16[4,2048]{1,0:T(4,128)(2,1)S(1)}, u32[]{:S(2)}, u32[]{:S(2)}) collective-permute-start(bf16[4,2048]{1,0:T(4,128)(2,1)S(1)} %shard_map.116), channel_id=1, source_target_pairs={{4,16},{0,20},{12,24},{8,28},{20,0},{16,4},{28,8},{24,12},{5,17},{... | collective-permute-start | bytes 49160 | tf_op jit(solution)/shard_map/ppermute | solution.py:31
  59.3 3.7 %collective-permute-start.15 = (bf16[4,2048]{1,0:T(4,128)(2,1)S(1)}, bf16[4,2048]{1,0:T(4,128)(2,1)S(1)}, u32[]{:S(2)}, u32[]{:S(2)}) collective-permute-start(bf16[4,2048]{1,0:T(4,128)(2,1)S(1)} %shard_map.116), channel_id=1, source_target_pairs={{0,16},{4,20},{8,24},{12,28},{16,0},{20,4},{24,8},{28,12},{1,17},{... | collective-permute-start | bytes 49160 | tf_op jit(solution)/shard_map/ppermute | solution.py:31
  63.3 3.5 %collective-permute-start.22 = (f32[8]{0:T(128)S(1)}, f32[8]{0:T(128)S(1)}, u32[]{:S(2)}, u32[]{:S(2)}) collective-permute-start(f32[8]{0:T(128)S(1)} %pad_maximum_fusion.12), channel_id=1, source_target_pairs={{0,3},{1,2},{2,1},{3,0},{4,7},{5,6},{6,5},{7,4},{8,11},{9,10},{10,... | collective-permute-start | bytes 104 | tf_op jit(solution)/shard_map/ppermute | solution.py:17
  63.4 3.6 %collective-permute-start.21 = (f32[8]{0:T(128)S(1)}, f32[8]{0:T(128)S(1)}, u32[]{:S(2)}, u32[]{:S(2)}) collective-permute-start(f32[8]{0:T(128)S(1)} %pad_maximum_fusion.12), channel_id=1, source_target_pairs={{0,2},{1,3},{2,0},{3,1},{4,6},{5,7},{6,4},{7,5},{8,10},{9,11},{10,... | collective-permute-start | bytes 104 | tf_op jit(solution)/shard_map/ppermute | solution.py:17
  64.9 2.0 %collective-permute-start.20 = (f32[8]{0:T(128)S(1)}, f32[8]{0:T(128)S(1)}, u32[]{:S(2)}, u32[]{:S(2)}) collective-permute-start(f32[8]{0:T(128)S(1)} %pad_maximum_fusion.12), channel_id=1, source_target_pairs={{0,1},{1,0},{2,3},{3,2},{4,5},{5,4},{6,7},{7,6},{8,9},{9,8},{10,11... | collective-permute-start | bytes 104 | tf_op jit(solution)/shard_map/ppermute | solution.py:17
  65.2 16.3 %collective-permute-start.19 = (bf16[8,2048]{1,0:T(8,128)(2,1)S(1)}, bf16[8,2048]{1,0:T(8,128)(2,1)S(1)}, u32[]{:S(2)}, u32[]{:S(2)}) collective-permute-start(bf16[8,2048]{1,0:T(8,128)(2,1)S(1)} %pad_maximum_fusion.8), channel_id=1, source_target_pairs={{0,16},{4,20},{8,24},{12,28},{16,0},{20,4},{24,8},{28,12},{1,17},{... | collective-permute-start | bytes 98312 | tf_op jit(solution)/shard_map/ppermute | solution.py:31
  68.5 3.2 %collective-permute-start.25 = (bf16[4,2048]{1,0:T(4,128)(2,1)S(1)}, bf16[4,2048]{1,0:T(4,128)(2,1)S(1)}, u32[]{:S(2)}, u32[]{:S(2)}) collective-permute-start(bf16[4,2048]{1,0:T(4,128)(2,1)S(1)} %fusion.14.refs_1_), channel_id=1, source_target_pairs={{0,3},{1,2},{2,1},{3,0},{4,7},{5,6},{6,5},{7,4},{8,11},{9,10},{10,... | collective-permute-start | bytes 49160 | tf_op jit(solution)/shard_map/ppermute | solution.py:17
  69.2 3.9 %collective-permute-start.24 = (bf16[4,2048]{1,0:T(4,128)(2,1)S(1)}, bf16[4,2048]{1,0:T(4,128)(2,1)S(1)}, u32[]{:S(2)}, u32[]{:S(2)}) collective-permute-start(bf16[4,2048]{1,0:T(4,128)(2,1)S(1)} %fusion.14.refs_1_), channel_id=1, source_target_pairs={{0,2},{1,3},{2,0},{3,1},{4,6},{5,7},{6,4},{7,5},{8,10},{9,11},{10,... | collective-permute-start | bytes 49160 | tf_op jit(solution)/shard_map/ppermute | solution.py:17
  70.6 2.5 %collective-permute-start.23 = (bf16[4,2048]{1,0:T(4,128)(2,1)S(1)}, bf16[4,2048]{1,0:T(4,128)(2,1)S(1)}, u32[]{:S(2)}, u32[]{:S(2)}) collective-permute-start(bf16[4,2048]{1,0:T(4,128)(2,1)S(1)} %fusion.14.refs_1_), channel_id=1, source_target_pairs={{0,1},{1,0},{2,3},{3,2},{4,5},{5,4},{6,7},{7,6},{8,9},{9,8},{10,11... | collective-permute-start | bytes 49160 | tf_op jit(solution)/shard_map/ppermute | solution.py:17
  74.8 6.8 %collective-permute-start.29 = (bf16[4,2048]{1,0:T(4,128)(2,1)S(1)}, bf16[4,2048]{1,0:T(4,128)(2,1)S(1)}, u32[]{:S(2)}, u32[]{:S(2)}) collective-permute-start(bf16[4,2048]{1,0:T(4,128)(2,1)S(1)} %shard_map.118), channel_id=1, source_target_pairs={{12,16},{8,20},{4,24},{0,28},{28,0},{24,4},{20,8},{16,12},{13,17},... | collective-permute-start | bytes 49160 | tf_op jit(solution)/shard_map/ppermute | solution.py:31
  77.3 5.6 %collective-permute-start.28 = (bf16[4,2048]{1,0:T(4,128)(2,1)S(1)}, bf16[4,2048]{1,0:T(4,128)(2,1)S(1)}, u32[]{:S(2)}, u32[]{:S(2)}) collective-permute-start(bf16[4,2048]{1,0:T(4,128)(2,1)S(1)} %shard_map.118), channel_id=1, source_target_pairs={{8,16},{12,20},{0,24},{4,28},{24,0},{28,4},{16,8},{20,12},{9,17},{... | collective-permute-start | bytes 49160 | tf_op jit(solution)/shard_map/ppermute | solution.py:31
  77.8 5.1 %collective-permute-start.27 = (bf16[4,2048]{1,0:T(4,128)(2,1)S(1)}, bf16[4,2048]{1,0:T(4,128)(2,1)S(1)}, u32[]{:S(2)}, u32[]{:S(2)}) collective-permute-start(bf16[4,2048]{1,0:T(4,128)(2,1)S(1)} %shard_map.118), channel_id=1, source_target_pairs={{4,16},{0,20},{12,24},{8,28},{20,0},{16,4},{28,8},{24,12},{5,17},{... | collective-permute-start | bytes 49160 | tf_op jit(solution)/shard_map/ppermute | solution.py:31
  80.7 3.7 %collective-permute-start.26 = (bf16[4,2048]{1,0:T(4,128)(2,1)S(1)}, bf16[4,2048]{1,0:T(4,128)(2,1)S(1)}, u32[]{:S(2)}, u32[]{:S(2)}) collective-permute-start(bf16[4,2048]{1,0:T(4,128)(2,1)S(1)} %shard_map.118), channel_id=1, source_target_pairs={{0,16},{4,20},{8,24},{12,28},{16,0},{20,4},{24,8},{28,12},{1,17},{... | collective-permute-start | bytes 49160 | tf_op jit(solution)/shard_map/ppermute | solution.py:31

commit v4 on v1

v4 whole, which is shorter than its diff:
```python
import jax
import jax.numpy as jnp
from jax import lax
from jax.experimental import pallas as pl
from jax.experimental.pallas import tpu as pltpu
from jax.sharding import PartitionSpec as P

HD = 128
BF = jnp.bfloat16
F32 = jnp.float32
VMEM = pl.BlockSpec(memory_space=pltpu.VMEM)
SMEM = pl.BlockSpec(memory_space=pltpu.SMEM)
HBM = pl.BlockSpec(memory_space=pltpu.HBM)
PARAMS = pltpu.CompilerParams(vmem_limit_bytes=12 * 1024 * 1024)


def in_hbm(x):
    return pltpu.with_memory_space_constraint(x, pltpu.HBM)


def shape(dims, dtype=BF):
    return jax.ShapeDtypeStruct(tuple(dims), dtype)


def cost(flops, size):
    return pl.CostEstimate(flops=flops, bytes_accessed=size, transcendentals=0)


def swapped(block, axis, bits):
    route = [(i, i ^ bits) for i in range(lax.axis_size(axis))]
    return lax.ppermute(block, axis, route)


def from_behind(block, bits):
    sections, tensors = lax.axis_size("section"), lax.axis_size("tensor")
    route = [
        (s * tensors + (t ^ bits), (s + 1) % sections * tensors + t)
        for s in range(sections)
        for t in range(tensors)
    ]
    return lax.ppermute(block, ("section", "tensor"), route)


def tree_sum(pieces):
    pieces = [piece.astype(F32) for piece in pieces]
    while len(pieces) > 1:
        pieces = [pieces[i] + pieces[i + 1] for i in range(0, len(pieces), 2)]
    return pieces[0]


def batch_at(tick, sections):
    return lax.rem(lax.axis_index("section") + (sections - tick), sections)


def pack_kernel(dims, ids_ref, gain_ref, bias_ref, keys_ref, values_ref, *refs):
    sections, tensors, rows, heads_dev, group, kv_dev = dims
    packs, later_ref = refs[:tensors], refs[tensors] if sections > 1 else None
    gains, biases, keys, values, sems = refs[-5:]
    copies = [
        pltpu.make_async_copy(source, target, sems.at[i])
        for i, (source, target) in enumerate(
            [(gain_ref, gains), (bias_ref, biases), (keys_ref, keys), (values_ref, values)]
        )
    ]
    for copy in copies:
        copy.start()
    at = lax.axis_index("tensor")
    tenants = gains.shape[0]
    count = sections * rows
    spot = lax.broadcasted_iota(jnp.int32, (count, tenants), 0)
    wanted = jnp.zeros((count, tenants), jnp.int32)
    for tick in range(sections):
        batch = batch_at(tick, sections)
        for i in range(rows):
            wanted = jnp.where(spot == tick * rows + i, ids_ref[batch, i], wanted)
    wanted = wanted - at * tenants
    onehot = jnp.where(wanted == lax.broadcasted_iota(jnp.int32, (count, tenants), 1), 1.0, 0.0)
    onehot = onehot.astype(BF)
    copies[2].wait()
    copies[3].wait()
    pos, lanes = keys.shape[2:]
    width = gains.shape[1]
    per = pos // (2 * rows)
    blocks = width // lanes // per
    for d in range(tensors):
        start = lax.bitwise_xor(at, d) * heads_dev // group
        for which, cache in enumerate((keys, values)):
            for b in range(sections):
                for g in range(kv_dev):
                    to = blocks + (which * sections + b) * kv_dev + g
                    packs[d][to] = cache[b, start + g]
    copies[0].wait()
    gain_rows = jnp.dot(onehot, gains[...], preferred_element_type=F32)
    copies[1].wait()
    bias_rows = jnp.dot(onehot, biases[...], preferred_element_type=F32)
    for tick in range(sections):
        mine = slice(tick * rows, (tick + 1) * rows)
        both = jnp.concatenate([gain_rows[mine], bias_rows[mine]], 0)
        for j in range(blocks):
            block = jnp.concatenate(
                [both[:, (j * per + k) * lanes : (j * per + k + 1) * lanes] for k in range(per)], 0
            ).astype(BF)
            if tick == 0:
                for d in range(tensors):
                    packs[d][j] = block
            else:
                later_ref[(tick - 1) * blocks + j] = block


def pack(dims, tenant, gain, bias, keys, values):
    sections, tensors, rows, heads_dev, group, kv_dev = dims
    pos = keys.shape[2]
    blocks = 2 * rows * gain.shape[1] // (pos * HD)
    out_shape = [shape((blocks + 2 * sections * kv_dev, pos, HD))] * tensors
    if sections > 1:
        out_shape += [shape(((sections - 1) * blocks, pos, HD))]
    return pl.pallas_call(
        lambda *refs: pack_kernel(dims, *refs),
        out_shape=out_shape,
        in_specs=[SMEM] + [HBM] * 4,
        out_specs=[VMEM] * len(out_shape),
        scratch_shapes=[pltpu.VMEM(x.shape, BF) for x in (gain, bias, keys, values)]
        + [pltpu.SemaphoreType.DMA((4,))],
        compiler_params=PARAMS,
        cost_estimate=cost(0, 4 * gain.size),
    )(tenant, in_hbm(gain), in_hbm(bias), in_hbm(keys), in_hbm(values))


def hold_kernel(parts, after_ref, w_ref, out_ref, sems):
    rows = w_ref.shape[0] // parts
    copies = [
        pltpu.make_async_copy(
            w_ref.at[pl.ds(i * rows, rows)], out_ref.at[pl.ds(i * rows, rows)], sems.at[i]
        )
        for i in range(parts)
    ]
    for copy in copies:
        copy.start()
    for copy in copies:
        copy.wait()


def hold(weights, after):
    parts = 8
    return pl.pallas_call(
        lambda *refs: hold_kernel(parts, *refs),
        out_shape=pltpu.VMEM(weights.shape, weights.dtype),
        in_specs=[VMEM, HBM],
        out_specs=VMEM,
        scratch_shapes=[pltpu.SemaphoreType.DMA((parts,))],
        compiler_params=PARAMS,
        cost_estimate=cost(0, 2 * weights.size),
    )(after, in_hbm(weights))


def tiles(w_ref):
    width = min(512, w_ref.shape[1])
    return [slice(i, i + width) for i in range(0, w_ref.shape[1], width)]


def thirds(x):
    high = x.astype(BF).astype(F32)
    middle = (x - high).astype(BF).astype(F32)
    return [high, middle, x - high - middle]


def query_sums(first_block, length, h, pieces, w_ref, out_ref):
    rows, width = h.shape
    pos, lanes = pieces[0].shape[1:]
    per = pos // (2 * rows)
    cols = []
    for j in range(width // lanes // per):
        block = tree_sum([piece[first_block + j] for piece in pieces])
        cols += [block[k * 2 * rows : (k + 1) * 2 * rows] for k in range(per)]
    affine = jnp.concatenate(cols, 1)
    total = jnp.sum(h, axis=-1, keepdims=True)
    squares = jnp.sum(h * h, axis=-1, keepdims=True)
    centred = (h - total * (1.0 / width)) * affine[:rows]
    x = jnp.concatenate([centred, affine], 0).astype(BF)
    count = w_ref.shape[1]
    for at in tiles(w_ref):
        got = jnp.dot(x, w_ref[:, at], preferred_element_type=F32)
        for k in range(3):
            to = slice(k * count + at.start, k * count + at.stop)
            out_ref[:, to] = got[k * rows : (k + 1) * rows].astype(BF)
    lane = lax.broadcasted_iota(jnp.int32, (rows, HD), 1)
    tail = jnp.full((rows, HD), length.astype(F32))
    for i, term in enumerate(thirds(total) + thirds(squares)):
        tail = jnp.where(lane == i, term, tail)
    out_ref[:, 3 * count :] = tail.astype(BF)


def first_kernel(tensors, sections, lengths_ref, h_ref, *refs):
    pieces, (w_ref, out_ref) = refs[:tensors], refs[tensors:]
    length = lengths_ref[batch_at(0, sections), 0]
    query_sums(0, length, h_ref[...].astype(F32), pieces, w_ref, out_ref)


def first_sums(sections, lengths, h, pieces, w):
    tensors = len(pieces)
    return pl.pallas_call(
        lambda *refs: first_kernel(tensors, sections, *refs),
        out_shape=shape((h.shape[0], 3 * w.shape[1] + HD)),
        in_specs=[SMEM] + [VMEM] * (tensors + 2),
        out_specs=VMEM,
        compiler_params=PARAMS,
        cost_estimate=cost(24 * w.size, 2 * w.size),
    )(lengths, h, *pieces, w)


def arrive(arrivals, next_ref):
    width = next_ref.shape[1]
    rest = arrivals[0][:, width:]
    came = tree_sum([arrival[:, :width] for arrival in arrivals]) + rest[:, :width].astype(F32)
    came = came.astype(BF).astype(F32)
    at_first = jnp.full(came.shape, lax.axis_index("section")) == 0
    carried = rest[:, width:].astype(F32) if rest.shape[1] > width else jnp.zeros_like(came)
    h = jnp.where(at_first, next_ref[...].astype(F32), came)
    return h, jnp.where(at_first, came, carried)


def later_kernel(tensors, sections, tick, lengths_ref, *refs):
    arrivals, next_ref = refs[:tensors], refs[tensors]
    pieces, (w_ref, out_ref, carry_ref) = refs[tensors + 1 : 2 * tensors + 1], refs[2 * tensors + 1 :]
    h, emitted = arrive(arrivals, next_ref)
    width = h.shape[1]
    carry_ref[:, :width] = h.astype(BF)
    carry_ref[:, width:] = emitted.astype(BF)
    length = lengths_ref[batch_at(tick, sections), 0]
    blocks = 2 * h.shape[0] * width // (pieces[0].shape[1] * HD)
    query_sums((tick - 1) * blocks, length, h, pieces, w_ref, out_ref)


def later_sums(sections, tick, lengths, arrivals, following, pieces, w):
    tensors = len(pieces)
    rows, width = following.shape
    return pl.pallas_call(
        lambda *refs: later_kernel(tensors, sections, tick, *refs),
        out_shape=[shape((rows, 3 * w.shape[1] + HD)), shape((rows, 2 * width))],
        in_specs=[SMEM] + [VMEM] * (2 * tensors + 2),
        out_specs=[VMEM] * 2,
        compiler_params=PARAMS,
        cost_estimate=cost(24 * w.size, 2 * w.size),
    )(lengths, *arrivals, following, *pieces, w)


def last_kernel(tensors, *refs):
    state_ref, emitted_ref = refs[-2:]
    h, emitted = arrive(refs[:tensors], refs[tensors])
    state_ref[0] = h.astype(BF)
    emitted_ref[0] = emitted.astype(BF)


def last(arrivals, following):
    return pl.pallas_call(
        lambda *refs: last_kernel(len(arrivals), *refs),
        out_shape=[shape((1,) + following.shape)] * 2,
        in_specs=[VMEM] * (len(arrivals) + 1),
        out_specs=[VMEM] * 2,
        compiler_params=PARAMS,
    )(*arrivals, following)


def attend_kernel(dims, turns, tick, *refs):
    sections, tensors, rows, kv_dev = dims
    count = len(turns)
    pieces, (kv_ref, carry_ref, w_ref, out_ref, full_ref) = refs[:count], refs[count:]
    span = w_ref.shape[0]
    width = w_ref.shape[1]
    batch = batch_at(tick, sections)

    tails = [piece[:, 3 * span :].astype(F32) for piece in pieces]
    totals = [tail[:, 0:1] + tail[:, 1:2] + tail[:, 2:3] for tail in tails]
    squares = [tail[:, 3:4] + tail[:, 4:5] + tail[:, 5:6] for tail in tails]
    scale = 1.0 / (width * count)
    mean = tree_sum(totals) * scale
    rstd = lax.rsqrt(tree_sum(squares) * scale - mean * mean + 1e-05)
    query = tree_sum(
        [
            piece[:, :span].astype(F32)
            + (total * (1.0 / width) - mean) * piece[:, span : 2 * span].astype(F32)
            for piece, total in zip(pieces, totals)
        ]
    )
    query = rstd * query + tree_sum([piece[:, 2 * span : 3 * span] for piece in pieces])
    query = query.astype(BF).astype(F32)

    pos = kv_ref.shape[3]
    tensor_at, replica_at = lax.axis_index("tensor"), lax.axis_index("replica")
    cols = lax.broadcasted_iota(jnp.int32, (rows, tensors * pos), 1)
    row = lax.broadcasted_iota(jnp.int32, (rows, tensors * pos), 0)
    spots = jnp.bitwise_xor(cols // pos, tensor_at) * pos + cols % pos
    spots = spots.astype(F32)
    keep = []
    for turn in turns:
        valid = jnp.logical_and(row == jnp.bitwise_xor(replica_at, turn), spots < tails[turn][:, 6:7])
        keep.append(jnp.where(valid, 0.0, -1e30))
    per_kv = span // HD // kv_dev
    keep = jnp.concatenate([jnp.concatenate(keep, 1)] * per_kv, 0)

    att = []
    for g in range(kv_dev):
        mine = jnp.concatenate(
            [query[:, h * HD : (h + 1) * HD] for h in range(g * per_kv, (g + 1) * per_kv)], 0
        ).astype(BF)
        keys, values = (
            jnp.concatenate(
                [
                    kv_ref[i, d, (which * sections + batch) * kv_dev + g]
                    for i in range(count)
                    for d in range(tensors)
                ],
                0,
            )
            for which in range(2)
        )
        scores = lax.dot_general(mine, keys, (((1,), (1,)), ((), ())), preferred_element_type=F32)
        scores = scores * (HD**-0.5) + keep
        probs = jnp.exp(scores - jnp.max(scores, axis=-1, keepdims=True))
        total = jnp.sum(probs, axis=-1, keepdims=True)
        got = jnp.dot(probs.astype(BF), values, preferred_element_type=F32) / total
        att += [got[h * rows : (h + 1) * rows] for h in range(per_kv)]
    att = jnp.concatenate(att, 1).astype(BF)
    for at in tiles(w_ref):
        got = jnp.dot(att, w_ref[:, at], preferred_element_type=F32).astype(BF)
        out_ref[:, at] = got
        full_ref[:, at] = got
    full_ref[:, width:] = carry_ref[...]


def attend(dims, turns, tick, pieces, kv, carry, w):
    rows, width = carry.shape[0], w.shape[1]
    return pl.pallas_call(
        lambda *refs: attend_kernel(dims, turns, tick, *refs),
        out_shape=[shape((rows, width)), shape((rows, width + carry.shape[1]))],
        in_specs=[VMEM] * (len(pieces) + 3),
        out_specs=[VMEM] * 2,
        compiler_params=PARAMS,
        cost_estimate=cost(8 * w.size, 2 * w.size),
    )(*pieces, kv, carry, w)


def on_device(state, next_embed, tenant, lengths, gain, bias, wq, wo, keys, values):
    sections = lax.axis_size("section")
    tensors = lax.axis_size("tensor")
    replicas = lax.axis_size("replica")
    rows, width = state.shape[1:]
    heads_dev = wq.shape[2] // HD
    group = heads_dev * tensors // keys.shape[3]
    kv_dev = max(1, heads_dev // group)
    pos = keys.shape[4]
    dims = (sections, tensors, rows, heads_dev, group, kv_dev)

    packs = pack(dims, tenant, gain[0], bias[0], keys[0, :, 0], values[0, :, 0])
    packs, later = packs[:tensors], packs[tensors:]
    got = [packs[0]] + [swapped(packs[d], "tensor", d) for d in range(1, tensors)]
    wq_held = hold(wq[0], packs[0])

    blocks = 2 * rows * width // (pos * HD)
    kv = jnp.stack([piece[blocks:] for piece in got], 0)[None]
    turns = [0]
    bit = replicas // 2
    while bit:
        kv = jnp.concatenate([kv, swapped(kv, "replica", bit)], 0)
        turns = turns + [turn ^ bit for turn in turns]
        if bit == replicas // 2 and later:
            later = list(lax.optimization_barrier((later[0], kv))[:1])
            later = later + [swapped(later[0], "tensor", d) for d in range(1, tensors)]
        bit //= 2

    carry = state[0]
    wo_held = None
    arrivals = None
    for tick in range(sections):
        following = next_embed[-tick % sections]
        if tick == 0:
            sums = first_sums(sections, lengths, carry, got, wq_held)
            wo_held = hold(wo[0], sums)
        else:
            sums, carry = later_sums(sections, tick, lengths, arrivals, following, later, wq_held)
        pieces = [sums] + [swapped(sums, "replica", d) for d in range(1, replicas)]
        out, full = attend(
            (sections, tensors, rows, kv_dev), turns, tick, pieces, kv, carry, wo_held
        )
        arrivals = [from_behind(full, 0)] + [from_behind(out, d) for d in range(1, tensors)]
    return tuple(last(arrivals, next_embed[0]))


def solution(mesh):
    in_specs = (
        P("section", None, "replica"),
        P(None, None, "replica"),
        P(),
        P(None, "replica"),
        P("section", "tensor", "replica"),
        P("section", "tensor", "replica"),
        P("section", "replica", "tensor"),
        P("section", "tensor", "replica"),
        P("section", None, "replica", None, "tensor", None),
        P("section", None, "replica", None, "tensor", None),
    )
    out_specs = (P("section", None, "replica"), P("section", None, "replica"))
    return jax.shard_map(
        on_device, mesh=mesh, in_specs=in_specs, out_specs=out_specs, check_vma=False
    )
```

time: 86 us -> 66.9 us (0.78)
  matrix products: 21 us -> 0 us
  Pallas kernels: 0 us -> 17 us
  starting transfers between devices: 35.2 us -> 29.4 us
  other arithmetic: 5.01 us -> 0.1 us
  waiting for transfers between devices: 21.3 us -> 18 us
    dot_general x8 -> x0, matrix products: 20.3 us -> none  [the longest x2 9.24 us: on_device(): jnp.dot(normed, wq[0], preferred_element_type=F32).astype(BF)]
    pallas_call x0 -> x8, Pallas kernels: none -> 17 us  [the longest x2 6.95 us: hold(): pl.pallas_call(lambda *refs: hold_kernel(parts, *refs), out_shape=pltpu.V...]
    ppermute x30 -> x14, starting transfers between devices: 30.5 us -> 15.9 us  [swapped(): return lax.ppermute(block, axis, route)]
    ppermute x3 -> x8, starting transfers between devices: 4.67 us -> 13.5 us  [from_behind(): return lax.ppermute(block, ('section', 'tensor'), route)]
    ppermute x30 -> x14, waiting for transfers between devices: 16.8 us -> 12.6 us  [swapped(): return lax.ppermute(block, axis, route)]
    reduce_sum x3 -> x0, other arithmetic: 1.86 us -> none  [on_device(): stats = jnp.stack([jnp.sum(hf, axis=-1), jnp.sum(hf * hf, axis=-1)], 0)]
    unnamed x7, local copies, waits for them, and re-layouts: 0.04 us -> 1.43 us
    gather x1 -> x0, local copies, waits for them, and re-layouts: 1.24 us -> none  [on_device(): ids = tenant[order].reshape(-1)]
  transfers between devices with their start and end apart: 33 -> 22, of which waited for: 15 -> 9; matrix products, arithmetic and copies ran while one was open for 13% -> 1% of each run, Pallas kernels for 0% -> 16%
where the time goes in v4:
time: 66.9 us; the launch traced here: 66.7 us
  starting transfers between devices  29.4 us (44%)
  waiting for transfers between devices  18 us (27%)
  Pallas kernels  17 us (25%)
  local copies, waits for them, and re-layouts  1.45 us (2%)
  between operations  0.76 us (1%)
    ppermute x14, starting transfers between devices, swapped(): return lax.ppermute(block, axis, route)  15.9 us
    ppermute x8, starting transfers between devices, from_behind(): return lax.ppermute(block, ('section', 'tensor'), route)  13.5 us
    ppermute x14, waiting for transfers between devices, swapped(): return lax.ppermute(block, axis, route)  12.6 us
    pallas_call x2, Pallas kernels, hold(): pl.pallas_call(lambda *refs: hold_kernel(parts, *refs), out_shape=pltpu.V...  6.95 us
    ppermute x8, waiting for transfers between devices, from_behind(): return lax.ppermute(block, ('section', 'tensor'), route)  5.38 us
    pallas_call x2, Pallas kernels, attend(): pl.pallas_call(lambda *refs: attend_kernel(dims, turns, tick, *refs), out...  3.71 us
    pallas_call x1, Pallas kernels, pack(): pl.pallas_call(lambda *refs: pack_kernel(dims, *refs), out_shape=out_shap...  2.07 us
    pallas_call x1, Pallas kernels, later_sums(): pl.pallas_call(lambda *refs: later_kernel(tensors, sections, tick, *refs)...  1.83 us
  transfers between devices with their start and end apart: 22, of which 9 were waited for; matrix products, arithmetic and copies ran while one was open for 1% of the time, Pallas kernels for 16%

profile of v4, /device:TPU:0, one launch (start us, length us, event | category | flops | bytes accessed | tf_op | source)
XLA Modules:
  0.0 66.7 jit_solution(4821066648467831742)
XLA Ops:
  0.6 0.7 %copy-done.1 = s32[2,4]{1,0:T(2,128)S(1)} copy-done((s32[2,4]{1,0:T(2,128)S(1)}, s32[2,4]{1,0:T(2,128)}, u32[]{:S(2)}) %copy-start.1) | copy-done | bytes 56
  1.3 2.1 %shard_map.113 = (bf16[16,16,128]{2,1,0:T(8,128)(2,1)S(1)}, bf16[16,16,128]{2,1,0:T(8,128)(2,1)S(1)}, bf16[16,16,128]{2,1,0:T(8,128)(2,1)S(1)}, bf16[16,16,128]{2,1,0:T(8,128)(2,1)S(1)}, bf16[8,16,128]{2,1,0:T(8,128)(2,1)S(1)}) custom-call(s32[2,4]{1,0:T(2,128)S(1)} %copy-done.1, bf16[100,2048]{1,0:T(8,128)(2,1)} %bitcast.25, bf16[100,2048]{1,0:T(8,128)(2,1)} %bitcast.26, ...), custom_call_target="tpu_custom_call" | custom-call | bytes 819200 | tf_op jit(solution)/shard_map/pallas_call | solution.py:117
  3.4 3.1 %collective-permute-start = (bf16[16,16,128]{2,1,0:T(8,128)(2,1)S(1)}, bf16[16,16,128]{2,1,0:T(8,128)(2,1)S(1)}, u32[]{:S(2)}, u32[]{:S(2)}) collective-permute-start(bf16[16,16,128]{2,1,0:T(8,128)(2,1)S(1)} %get-tuple-element.15), channel_id=1, source_target_pairs={{0,4},{4,0},{8,12},{12,8},{1,5},{5,1},{9,13},{13,9},{2,6},{6,2},{1... | collective-permute-start | bytes 196616 | tf_op jit(solution)/shard_map/ppermute | solution.py:31
  6.5 2.6 %collective-permute-start.1 = (bf16[16,16,128]{2,1,0:T(8,128)(2,1)S(1)}, bf16[16,16,128]{2,1,0:T(8,128)(2,1)S(1)}, u32[]{:S(2)}, u32[]{:S(2)}) collective-permute-start(bf16[16,16,128]{2,1,0:T(8,128)(2,1)S(1)} %get-tuple-element.16), channel_id=1, source_target_pairs={{0,8},{4,12},{8,0},{12,4},{1,9},{5,13},{9,1},{13,5},{2,10},{6,14},... | collective-permute-start | bytes 196616 | tf_op jit(solution)/shard_map/ppermute | solution.py:31
  9.1 0.0 collective-permute-start.2
  9.1 0.0 collective-permute-done.refs_3_
  9.1 4.6 %collective-permute-done.1.refs_4_ = bf16[16,16,128]{2,1,0:T(8,128)(2,1)S(1)} collective-permute-done((bf16[16,16,128]{2,1,0:T(8,128)(2,1)S(1)}, bf16[16,16,128]{2,1,0:T(8,128)(2,1)S(1)}, u32[]{:S(2)}, u32[]{:S(2)}) %collective-permute-start.1) | collective-permute-done | bytes 65568 | tf_op jit(solution)/shard_map/ppermute | solution.py:31
  13.7 1.4 %collective-permute-done.2.refs_5_ = bf16[16,16,128]{2,1,0:T(8,128)(2,1)S(1)} collective-permute-done((bf16[16,16,128]{2,1,0:T(8,128)(2,1)S(1)}, bf16[16,16,128]{2,1,0:T(8,128)(2,1)S(1)}, u32[]{:S(2)}, u32[]{:S(2)}) %collective-permute-start.2) | collective-permute-done | bytes 65568 | tf_op jit(solution)/shard_map/ppermute | solution.py:31
  15.2 1.6 %collective-permute-start.6 = (bf16[1,4,8,16,128]{4,3,2,1,0:T(8,128)(2,1)S(1)}, bf16[1,4,8,16,128]{4,3,2,1,0:T(8,128)(2,1)S(1)}, u32[]{:S(2)}, u32[]{:S(2)}) collective-permute-start(bf16[1,4,8,16,128]{4,3,2,1,0:T(8,128)(2,1)S(1)} %maximum_bitcast_fusion), channel_id=1, source_target_pairs={{0,2},{1,3},{2,0},{3,1},{4,6},{5,7},{6,4},{7,5},{8,10},{9,11},{10,... | collective-permute-start | bytes 393224 | tf_op jit(solution)/shard_map/ppermute | solution.py:31
  16.8 3.4 %collective-permute-done.6 = bf16[1,4,8,16,128]{4,3,2,1,0:T(8,128)(2,1)S(1)} collective-permute-done((bf16[1,4,8,16,128]{4,3,2,1,0:T(8,128)(2,1)S(1)}, bf16[1,4,8,16,128]{4,3,2,1,0:T(8,128)(2,1)S(1)}, u32[]{:S(2)}, u32[]{:S(2)}) %collective-permute-start.6) | collective-permute-done | bytes 131104 | tf_op jit(solution)/shard_map/ppermute | solution.py:31
  20.2 0.1 collective-permute-start.7
  20.3 0.7 %copy.13.refs_0_ = s32[2,1]{1,0:T(2,128)S(1)} copy(s32[2,1]{0,1:T(1,128)} %param.13) | data formatting | bytes 16 | tf_op args[3]
  21.1 3.5 %shard_map.114.refs_6_.refs_10_ = bf16[2048,2048]{1,0:T(8,128)(2,1)S(1)} custom-call(bf16[16,16,128]{2,1,0:T(8,128)(2,1)S(1)} %get-tuple-element.14.refs_0_.refs_2_, bf16[2048,2048]{1,0:T(8,128)(2,1)} %bitcast.24), custom_call_target="tpu_custom_call" | custom-call | bytes 8388608 | tf_op jit(solution)/shard_map/pallas_call | solution.py:145
  24.6 1.8 %shard_map.115.refs_0_ = bf16[4,6272]{1,0:T(4,128)(2,1)S(1)} custom-call(s32[2,1]{1,0:T(2,128)S(1)} %copy.13.refs_0_, bf16[4,2048]{1,0:T(4,128)(2,1)S(1)} %bitcast.21, bf16[16,16,128]{2,1,0:T(8,128)(2,1)S(1)} %get-tuple-element.14.refs_0_.refs_2_, bf16[16,16,128]{2,1,0:T(8,128)(2,1)S(1)} %collective-permute-done.refs_3_, ...), custom_call_target="tpu_custom_call" | custom-call | flops 100663296 | bytes 8388608 | tf_op jit(solution)/shard_map/pallas_call | solution.py:201
  26.4 1.6 %collective-permute-start.5 = (bf16[4,6272]{1,0:T(4,128)(2,1)S(1)}, bf16[4,6272]{1,0:T(4,128)(2,1)S(1)}, u32[]{:S(2)}, u32[]{:S(2)}) collective-permute-start(bf16[4,6272]{1,0:T(4,128)(2,1)S(1)} %shard_map.115.refs_0_), channel_id=1, source_target_pairs={{0,3},{1,2},{2,1},{3,0},{4,7},{5,6},{6,5},{7,4},{8,11},{9,10},{10,... | collective-permute-start | bytes 150536 | tf_op jit(solution)/shard_map/ppermute | solution.py:31
  28.0 0.5 collective-permute-start.4
  28.5 0.0 collective-permute-start.3
  28.5 3.5 %shard_map.116.refs_6_ = bf16[2048,2048]{1,0:T(8,128)(2,1)S(1)} custom-call(bf16[4,6272]{1,0:T(4,128)(2,1)S(1)} %shard_map.115.refs_0_, bf16[2048,2048]{1,0:T(8,128)(2,1)} %bitcast.23), custom_call_target="tpu_custom_call" | custom-call | bytes 8388608 | tf_op jit(solution)/shard_map/pallas_call | solution.py:145
  32.0 0.0 copy-start.2
  32.0 1.9 %collective-permute-start.14 = (bf16[8,16,128]{2,1,0:T(8,128)(2,1)S(1)}, bf16[8,16,128]{2,1,0:T(8,128)(2,1)S(1)}, u32[]{:S(2)}, u32[]{:S(2)}) collective-permute-start(bf16[8,16,128]{2,1,0:T(8,128)(2,1)S(1)} %get-tuple-element.21.refs_6_), channel_id=1, source_target_pairs={{0,12},{4,8},{8,4},{12,0},{1,13},{5,9},{9,5},{13,1},{2,14},{6,10},... | collective-permute-start | bytes 98312 | tf_op jit(solution)/shard_map/ppermute | solution.py:31
  33.9 0.0 collective-permute-done.7
  33.9 0.0 collective-permute-start.13
  33.9 0.1 pad_maximum_fusion.refs_4_
  33.9 2.7 %collective-permute-start.12 = (bf16[8,16,128]{2,1,0:T(8,128)(2,1)S(1)}, bf16[8,16,128]{2,1,0:T(8,128)(2,1)S(1)}, u32[]{:S(2)}, u32[]{:S(2)}) collective-permute-start(bf16[8,16,128]{2,1,0:T(8,128)(2,1)S(1)} %get-tuple-element.21.refs_6_), channel_id=1, source_target_pairs={{0,4},{4,0},{8,12},{12,8},{1,5},{5,1},{9,13},{13,9},{2,6},{6,2},{1... | collective-permute-start | bytes 98312 | tf_op jit(solution)/shard_map/ppermute | solution.py:31
  36.6 1.9 %shard_map.117 = (bf16[4,2048]{1,0:T(4,128)(2,1)S(1)}, bf16[4,4096]{1,0:T(4,128)(2,1)S(1)}) custom-call(bf16[4,6272]{1,0:T(4,128)(2,1)S(1)} %shard_map.115.refs_0_, bf16[4,6272]{1,0:T(4,128)(2,1)S(1)} %collective-permute-done.3.refs_1_, bf16[4,6272]{1,0:T(4,128)(2,1)S(1)} %collective-permute-done.4.refs_2_, ...), custom_call_target="tpu_custom_call" | custom-call | flops 33554432 | bytes 8388608 | tf_op jit(solution)/shard_map/pallas_call | solution.py:333
  38.4 2.7 %collective-permute-start.11 = (bf16[4,2048]{1,0:T(4,128)(2,1)S(1)}, bf16[4,2048]{1,0:T(4,128)(2,1)S(1)}, u32[]{:S(2)}, u32[]{:S(2)}) collective-permute-start(bf16[4,2048]{1,0:T(4,128)(2,1)S(1)} %get-tuple-element.19), channel_id=1, source_target_pairs={{12,16},{8,20},{4,24},{0,28},{28,0},{24,4},{20,8},{16,12},{13,17},... | collective-permute-start | bytes 49160 | tf_op jit(solution)/shard_map/ppermute | solution.py:41
  41.2 0.0 collective-permute-done.14.refs_9_
  41.2 3.5 %collective-permute-start.9 = (bf16[4,2048]{1,0:T(4,128)(2,1)S(1)}, bf16[4,2048]{1,0:T(4,128)(2,1)S(1)}, u32[]{:S(2)}, u32[]{:S(2)}) collective-permute-start(bf16[4,2048]{1,0:T(4,128)(2,1)S(1)} %get-tuple-element.19), channel_id=1, source_target_pairs={{4,16},{0,20},{12,24},{8,28},{20,0},{16,4},{28,8},{24,12},{5,17},{... | collective-permute-start | bytes 49160 | tf_op jit(solution)/shard_map/ppermute | solution.py:41
  44.7 0.0 collective-permute-done.13.refs_8_
  44.7 0.5 collective-permute-start.8
  45.2 0.0 collective-permute-done.12.refs_7_
  45.3 0.0 collective-permute-done.11.refs_4_
  45.3 1.5 %collective-permute-done.10.refs_3_ = bf16[4,2048]{1,0:T(4,128)(2,1)S(1)} collective-permute-done((bf16[4,2048]{1,0:T(4,128)(2,1)S(1)}, bf16[4,2048]{1,0:T(4,128)(2,1)S(1)}, u32[]{:S(2)}, u32[]{:S(2)}) %collective-permute-start.10) | collective-permute-done | bytes 16416 | tf_op jit(solution)/shard_map/ppermute | solution.py:41
  46.7 0.0 collective-permute-done.9.refs_2_
  46.7 1.9 %collective-permute-done.8.refs_1_ = bf16[4,4096]{1,0:T(4,128)(2,1)S(1)} collective-permute-done((bf16[4,4096]{1,0:T(4,128)(2,1)S(1)}, bf16[4,4096]{1,0:T(4,128)(2,1)S(1)}, u32[]{:S(2)}, u32[]{:S(2)}) %collective-permute-start.8) | collective-permute-done | bytes 32800 | tf_op jit(solution)/shard_map/ppermute | solution.py:41
  48.6 1.8 %shard_map.118 = (bf16[4,6272]{1,0:T(4,128)(2,1)S(1)}, bf16[4,4096]{1,0:T(4,128)(2,1)S(1)}) custom-call(s32[2,1]{1,0:T(2,128)S(1)} %copy.13.refs_0_, bf16[4,4096]{1,0:T(4,128)(2,1)S(1)} %collective-permute-done.8.refs_1_, bf16[4,2048]{1,0:T(4,128)(2,1)S(1)} %collective-permute-done.9.refs_2_, bf16[4,2048]{1,0:T(4,128)(2,1)S(1)} %collective-permute-done.10.refs_3_, ...), custom_call_target="tpu_custom_call" | custom-call | flops 100663296 | bytes 8388608 | tf_op jit(solution)/shard_map/pallas_call | solution.py:237
  50.4 1.6 %collective-permute-start.16 = (bf16[4,6272]{1,0:T(4,128)(2,1)S(1)}, bf16[4,6272]{1,0:T(4,128)(2,1)S(1)}, u32[]{:S(2)}, u32[]{:S(2)}) collective-permute-start(bf16[4,6272]{1,0:T(4,128)(2,1)S(1)} %get-tuple-element.22.refs_0_), channel_id=1, source_target_pairs={{0,2},{1,3},{2,0},{3,1},{4,6},{5,7},{6,4},{7,5},{8,10},{9,11},{10,... | collective-permute-start | bytes 150536 | tf_op jit(solution)/shard_map/ppermute | solution.py:31
  52.0 0.3 collective-permute-start.15
  52.3 2.1 %collective-permute-done.17.refs_3_ = bf16[4,6272]{1,0:T(4,128)(2,1)S(1)} collective-permute-done((bf16[4,6272]{1,0:T(4,128)(2,1)S(1)}, bf16[4,6272]{1,0:T(4,128)(2,1)S(1)}, u32[]{:S(2)}, u32[]{:S(2)}) %collective-permute-start.17) | collective-permute-done | bytes 50208 | tf_op jit(solution)/shard_map/ppermute | solution.py:31
  54.4 1.0 %collective-permute-done.16.refs_2_ = bf16[4,6272]{1,0:T(4,128)(2,1)S(1)} collective-permute-done((bf16[4,6272]{1,0:T(4,128)(2,1)S(1)}, bf16[4,6272]{1,0:T(4,128)(2,1)S(1)}, u32[]{:S(2)}, u32[]{:S(2)}) %collective-permute-start.16) | collective-permute-done | bytes 50208 | tf_op jit(solution)/shard_map/ppermute | solution.py:31
  55.4 1.9 %shard_map.119 = (bf16[4,2048]{1,0:T(4,128)(2,1)S(1)}, bf16[4,6144]{1,0:T(4,128)(2,1)S(1)}) custom-call(bf16[4,6272]{1,0:T(4,128)(2,1)S(1)} %get-tuple-element.22.refs_0_, bf16[4,6272]{1,0:T(4,128)(2,1)S(1)} %collective-permute-done.15.refs_1_, bf16[4,6272]{1,0:T(4,128)(2,1)S(1)} %collective-permute-done.16.refs_2_, ...), custom_call_target="tpu_custom_call" | custom-call | flops 33554432 | bytes 8388608 | tf_op jit(solution)/shard_map/pallas_call | solution.py:333
  57.3 0.5 collective-permute-start.18
  57.8 2.7 %collective-permute-start.21 = (bf16[4,2048]{1,0:T(4,128)(2,1)S(1)}, bf16[4,2048]{1,0:T(4,128)(2,1)S(1)}, u32[]{:S(2)}, u32[]{:S(2)}) collective-permute-start(bf16[4,2048]{1,0:T(4,128)(2,1)S(1)} %get-tuple-element.25), channel_id=1, source_target_pairs={{12,16},{8,20},{4,24},{0,28},{28,0},{24,4},{20,8},{16,12},{13,17},... | collective-permute-start | bytes 49160 | tf_op jit(solution)/shard_map/ppermute | solution.py:41
  60.5 0.4 collective-permute-start.20
  60.9 3.1 %collective-permute-start.19 = (bf16[4,2048]{1,0:T(4,128)(2,1)S(1)}, bf16[4,2048]{1,0:T(4,128)(2,1)S(1)}, u32[]{:S(2)}, u32[]{:S(2)}) collective-permute-start(bf16[4,2048]{1,0:T(4,128)(2,1)S(1)} %get-tuple-element.25), channel_id=1, source_target_pairs={{4,16},{0,20},{12,24},{8,28},{20,0},{16,4},{28,8},{24,12},{5,17},{... | collective-permute-start | bytes 49160 | tf_op jit(solution)/shard_map/ppermute | solution.py:41
  64.0 0.2 collective-permute-done.21.refs_3_
  64.2 1.8 %collective-permute-done.20.refs_2_ = bf16[4,2048]{1,0:T(4,128)(2,1)S(1)} collective-permute-done((bf16[4,2048]{1,0:T(4,128)(2,1)S(1)}, bf16[4,2048]{1,0:T(4,128)(2,1)S(1)}, u32[]{:S(2)}, u32[]{:S(2)}) %collective-permute-start.20) | collective-permute-done | bytes 16416 | tf_op jit(solution)/shard_map/ppermute | solution.py:41
  66.1 0.6 shard_map.120
  (19 shorter events, 0.1 us)
Async XLA Ops:
  0.6 0.7 %copy-start.1 = (s32[2,4]{1,0:T(2,128)S(1)}, s32[2,4]{1,0:T(2,128)}, u32[]{:S(2)}) copy-start(s32[2,4]{1,0:T(2,128)} %refs_0_.3) | copy-start | bytes 100
  3.4 5.7 %collective-permute-start = (bf16[16,16,128]{2,1,0:T(8,128)(2,1)S(1)}, bf16[16,16,128]{2,1,0:T(8,128)(2,1)S(1)}, u32[]{:S(2)}, u32[]{:S(2)}) collective-permute-start(bf16[16,16,128]{2,1,0:T(8,128)(2,1)S(1)} %get-tuple-element.15), channel_id=1, source_target_pairs={{0,4},{4,0},{8,12},{12,8},{1,5},{5,1},{9,13},{13,9},{2,6},{6,2},{1... | collective-permute-start | bytes 196616 | tf_op jit(solution)/shard_map/ppermute | solution.py:31
  6.5 7.3 %collective-permute-start.1 = (bf16[16,16,128]{2,1,0:T(8,128)(2,1)S(1)}, bf16[16,16,128]{2,1,0:T(8,128)(2,1)S(1)}, u32[]{:S(2)}, u32[]{:S(2)}) collective-permute-start(bf16[16,16,128]{2,1,0:T(8,128)(2,1)S(1)} %get-tuple-element.16), channel_id=1, source_target_pairs={{0,8},{4,12},{8,0},{12,4},{1,9},{5,13},{9,1},{13,5},{2,10},{6,14},... | collective-permute-start | bytes 196616 | tf_op jit(solution)/shard_map/ppermute | solution.py:31
  9.1 6.1 %collective-permute-start.2 = (bf16[16,16,128]{2,1,0:T(8,128)(2,1)S(1)}, bf16[16,16,128]{2,1,0:T(8,128)(2,1)S(1)}, u32[]{:S(2)}, u32[]{:S(2)}) collective-permute-start(bf16[16,16,128]{2,1,0:T(8,128)(2,1)S(1)} %get-tuple-element.17), channel_id=1, source_target_pairs={{0,12},{4,8},{8,4},{12,0},{1,13},{5,9},{9,5},{13,1},{2,14},{6,10},... | collective-permute-start | bytes 196616 | tf_op jit(solution)/shard_map/ppermute | solution.py:31
  15.2 5.0 %collective-permute-start.6 = (bf16[1,4,8,16,128]{4,3,2,1,0:T(8,128)(2,1)S(1)}, bf16[1,4,8,16,128]{4,3,2,1,0:T(8,128)(2,1)S(1)}, u32[]{:S(2)}, u32[]{:S(2)}) collective-permute-start(bf16[1,4,8,16,128]{4,3,2,1,0:T(8,128)(2,1)S(1)} %maximum_bitcast_fusion), channel_id=1, source_target_pairs={{0,2},{1,3},{2,0},{3,1},{4,6},{5,7},{6,4},{7,5},{8,10},{9,11},{10,... | collective-permute-start | bytes 393224 | tf_op jit(solution)/shard_map/ppermute | solution.py:31
  20.2 13.6 %collective-permute-start.7 = (bf16[2,4,8,16,128]{4,3,2,1,0:T(8,128)(2,1)S(1)}, bf16[2,4,8,16,128]{4,3,2,1,0:T(8,128)(2,1)S(1)}, u32[]{:S(2)}, u32[]{:S(2)}) collective-permute-start(bf16[2,4,8,16,128]{4,3,2,1,0:T(8,128)(2,1)S(1)} %pad_maximum_fusion.1), channel_id=1, source_target_pairs={{0,1},{1,0},{2,3},{3,2},{4,5},{5,4},{6,7},{7,6},{8,9},{9,8},{10,11... | collective-permute-start | bytes 786440 | tf_op jit(solution)/shard_map/ppermute | solution.py:31
  21.1 3.5 %copy-start = (bf16[1,4,2048]{2,1,0:T(4,128)(2,1)S(1)}, bf16[1,4,2048]{2,1,0:T(4,128)(2,1)}, u32[]{:S(2)}) copy-start(bf16[1,4,2048]{2,1,0:T(4,128)(2,1)} %param.10) | copy-start | bytes 49156
  26.4 7.5 %collective-permute-start.5 = (bf16[4,6272]{1,0:T(4,128)(2,1)S(1)}, bf16[4,6272]{1,0:T(4,128)(2,1)S(1)}, u32[]{:S(2)}, u32[]{:S(2)}) collective-permute-start(bf16[4,6272]{1,0:T(4,128)(2,1)S(1)} %shard_map.115.refs_0_), channel_id=1, source_target_pairs={{0,3},{1,2},{2,1},{3,0},{4,7},{5,6},{6,5},{7,4},{8,11},{9,10},{10,... | collective-permute-start | bytes 150536 | tf_op jit(solution)/shard_map/ppermute | solution.py:31
  28.0 8.6 %collective-permute-start.4 = (bf16[4,6272]{1,0:T(4,128)(2,1)S(1)}, bf16[4,6272]{1,0:T(4,128)(2,1)S(1)}, u32[]{:S(2)}, u32[]{:S(2)}) collective-permute-start(bf16[4,6272]{1,0:T(4,128)(2,1)S(1)} %shard_map.115.refs_0_), channel_id=1, source_target_pairs={{0,2},{1,3},{2,0},{3,1},{4,6},{5,7},{6,4},{7,5},{8,10},{9,11},{10,... | collective-permute-start | bytes 150536 | tf_op jit(solution)/shard_map/ppermute | solution.py:31
  28.5 8.1 %collective-permute-start.3 = (bf16[4,6272]{1,0:T(4,128)(2,1)S(1)}, bf16[4,6272]{1,0:T(4,128)(2,1)S(1)}, u32[]{:S(2)}, u32[]{:S(2)}) collective-permute-start(bf16[4,6272]{1,0:T(4,128)(2,1)S(1)} %shard_map.115.refs_0_), channel_id=1, source_target_pairs={{0,1},{1,0},{2,3},{3,2},{4,5},{5,4},{6,7},{7,6},{8,9},{9,8},{10,11... | collective-permute-start | bytes 150536 | tf_op jit(solution)/shard_map/ppermute | solution.py:31
  32.0 13.2 %copy-start.2 = (bf16[2,4,2048]{2,1,0:T(4,128)(2,1)S(1)}, bf16[2,4,2048]{2,1,0:T(4,128)(2,1)}, u32[]{:S(2)}) copy-start(bf16[2,4,2048]{2,1,0:T(4,128)(2,1)} %param.11) | copy-start | bytes 98308
  32.0 9.2 %collective-permute-start.14 = (bf16[8,16,128]{2,1,0:T(8,128)(2,1)S(1)}, bf16[8,16,128]{2,1,0:T(8,128)(2,1)S(1)}, u32[]{:S(2)}, u32[]{:S(2)}) collective-permute-start(bf16[8,16,128]{2,1,0:T(8,128)(2,1)S(1)} %get-tuple-element.21.refs_6_), channel_id=1, source_target_pairs={{0,12},{4,8},{8,4},{12,0},{1,13},{5,9},{9,5},{13,1},{2,14},{6,10},... | collective-permute-start | bytes 98312 | tf_op jit(solution)/shard_map/ppermute | solution.py:31
  33.9 10.8 %collective-permute-start.13 = (bf16[8,16,128]{2,1,0:T(8,128)(2,1)S(1)}, bf16[8,16,128]{2,1,0:T(8,128)(2,1)S(1)}, u32[]{:S(2)}, u32[]{:S(2)}) collective-permute-start(bf16[8,16,128]{2,1,0:T(8,128)(2,1)S(1)} %get-tuple-element.21.refs_6_), channel_id=1, source_target_pairs={{0,8},{4,12},{8,0},{12,4},{1,9},{5,13},{9,1},{13,5},{2,10},{6,14},... | collective-permute-start | bytes 98312 | tf_op jit(solution)/shard_map/ppermute | solution.py:31
  33.9 11.3 %collective-permute-start.12 = (bf16[8,16,128]{2,1,0:T(8,128)(2,1)S(1)}, bf16[8,16,128]{2,1,0:T(8,128)(2,1)S(1)}, u32[]{:S(2)}, u32[]{:S(2)}) collective-permute-start(bf16[8,16,128]{2,1,0:T(8,128)(2,1)S(1)} %get-tuple-element.21.refs_6_), channel_id=1, source_target_pairs={{0,4},{4,0},{8,12},{12,8},{1,5},{5,1},{9,13},{13,9},{2,6},{6,2},{1... | collective-permute-start | bytes 98312 | tf_op jit(solution)/shard_map/ppermute | solution.py:31
  38.4 6.8 %collective-permute-start.11 = (bf16[4,2048]{1,0:T(4,128)(2,1)S(1)}, bf16[4,2048]{1,0:T(4,128)(2,1)S(1)}, u32[]{:S(2)}, u32[]{:S(2)}) collective-permute-start(bf16[4,2048]{1,0:T(4,128)(2,1)S(1)} %get-tuple-element.19), channel_id=1, source_target_pairs={{12,16},{8,20},{4,24},{0,28},{28,0},{24,4},{20,8},{16,12},{13,17},... | collective-permute-start | bytes 49160 | tf_op jit(solution)/shard_map/ppermute | solution.py:41
  41.2 5.6 %collective-permute-start.10 = (bf16[4,2048]{1,0:T(4,128)(2,1)S(1)}, bf16[4,2048]{1,0:T(4,128)(2,1)S(1)}, u32[]{:S(2)}, u32[]{:S(2)}) collective-permute-start(bf16[4,2048]{1,0:T(4,128)(2,1)S(1)} %get-tuple-element.19), channel_id=1, source_target_pairs={{8,16},{12,20},{0,24},{4,28},{24,0},{28,4},{16,8},{20,12},{9,17},{... | collective-permute-start | bytes 49160 | tf_op jit(solution)/shard_map/ppermute | solution.py:41
  41.2 5.6 %collective-permute-start.9 = (bf16[4,2048]{1,0:T(4,128)(2,1)S(1)}, bf16[4,2048]{1,0:T(4,128)(2,1)S(1)}, u32[]{:S(2)}, u32[]{:S(2)}) collective-permute-start(bf16[4,2048]{1,0:T(4,128)(2,1)S(1)} %get-tuple-element.19), channel_id=1, source_target_pairs={{4,16},{0,20},{12,24},{8,28},{20,0},{16,4},{28,8},{24,12},{5,17},{... | collective-permute-start | bytes 49160 | tf_op jit(solution)/shard_map/ppermute | solution.py:41
  44.7 3.9 %collective-permute-start.8 = (bf16[4,4096]{1,0:T(4,128)(2,1)S(1)}, bf16[4,4096]{1,0:T(4,128)(2,1)S(1)}, u32[]{:S(2)}, u32[]{:S(2)}) collective-permute-start(bf16[4,4096]{1,0:T(4,128)(2,1)S(1)} %get-tuple-element.18), channel_id=1, source_target_pairs={{0,16},{4,20},{8,24},{12,28},{16,0},{20,4},{24,8},{28,12},{1,17},{... | collective-permute-start | bytes 98312 | tf_op jit(solution)/shard_map/ppermute | solution.py:41
  50.4 4.0 %collective-permute-start.17 = (bf16[4,6272]{1,0:T(4,128)(2,1)S(1)}, bf16[4,6272]{1,0:T(4,128)(2,1)S(1)}, u32[]{:S(2)}, u32[]{:S(2)}) collective-permute-start(bf16[4,6272]{1,0:T(4,128)(2,1)S(1)} %get-tuple-element.22.refs_0_), channel_id=1, source_target_pairs={{0,3},{1,2},{2,1},{3,0},{4,7},{5,6},{6,5},{7,4},{8,11},{9,10},{10,... | collective-permute-start | bytes 150536 | tf_op jit(solution)/shard_map/ppermute | solution.py:31
  50.4 5.0 %collective-permute-start.16 = (bf16[4,6272]{1,0:T(4,128)(2,1)S(1)}, bf16[4,6272]{1,0:T(4,128)(2,1)S(1)}, u32[]{:S(2)}, u32[]{:S(2)}) collective-permute-start(bf16[4,6272]{1,0:T(4,128)(2,1)S(1)} %get-tuple-element.22.refs_0_), channel_id=1, source_target_pairs={{0,2},{1,3},{2,0},{3,1},{4,6},{5,7},{6,4},{7,5},{8,10},{9,11},{10,... | collective-permute-start | bytes 150536 | tf_op jit(solution)/shard_map/ppermute | solution.py:31
  52.0 3.4 %collective-permute-start.15 = (bf16[4,6272]{1,0:T(4,128)(2,1)S(1)}, bf16[4,6272]{1,0:T(4,128)(2,1)S(1)}, u32[]{:S(2)}, u32[]{:S(2)}) collective-permute-start(bf16[4,6272]{1,0:T(4,128)(2,1)S(1)} %get-tuple-element.22.refs_0_), channel_id=1, source_target_pairs={{0,1},{1,0},{2,3},{3,2},{4,5},{5,4},{6,7},{7,6},{8,9},{9,8},{10,11... | collective-permute-start | bytes 150536 | tf_op jit(solution)/shard_map/ppermute | solution.py:31
  57.3 8.8 %collective-permute-start.18 = (bf16[4,6144]{1,0:T(4,128)(2,1)S(1)}, bf16[4,6144]{1,0:T(4,128)(2,1)S(1)}, u32[]{:S(2)}, u32[]{:S(2)}) collective-permute-start(bf16[4,6144]{1,0:T(4,128)(2,1)S(1)} %get-tuple-element.24), channel_id=1, source_target_pairs={{0,16},{4,20},{8,24},{12,28},{16,0},{20,4},{24,8},{28,12},{1,17},{... | collective-permute-start | bytes 147464 | tf_op jit(solution)/shard_map/ppermute | solution.py:41
  57.8 6.4 %collective-permute-start.21 = (bf16[4,2048]{1,0:T(4,128)(2,1)S(1)}, bf16[4,2048]{1,0:T(4,128)(2,1)S(1)}, u32[]{:S(2)}, u32[]{:S(2)}) collective-permute-start(bf16[4,2048]{1,0:T(4,128)(2,1)S(1)} %get-tuple-element.25), channel_id=1, source_target_pairs={{12,16},{8,20},{4,24},{0,28},{28,0},{24,4},{20,8},{16,12},{13,17},... | collective-permute-start | bytes 49160 | tf_op jit(solution)/shard_map/ppermute | solution.py:41
  60.5 5.5 %collective-permute-start.20 = (bf16[4,2048]{1,0:T(4,128)(2,1)S(1)}, bf16[4,2048]{1,0:T(4,128)(2,1)S(1)}, u32[]{:S(2)}, u32[]{:S(2)}) collective-permute-start(bf16[4,2048]{1,0:T(4,128)(2,1)S(1)} %get-tuple-element.25), channel_id=1, source_target_pairs={{8,16},{12,20},{0,24},{4,28},{24,0},{28,4},{16,8},{20,12},{9,17},{... | collective-permute-start | bytes 49160 | tf_op jit(solution)/shard_map/ppermute | solution.py:41
  60.9 5.1 %collective-permute-start.19 = (bf16[4,2048]{1,0:T(4,128)(2,1)S(1)}, bf16[4,2048]{1,0:T(4,128)(2,1)S(1)}, u32[]{:S(2)}, u32[]{:S(2)}) collective-permute-start(bf16[4,2048]{1,0:T(4,128)(2,1)S(1)} %get-tuple-element.25), channel_id=1, source_target_pairs={{4,16},{0,20},{12,24},{8,28},{20,0},{16,4},{28,8},{24,12},{5,17},{... | collective-permute-start | bytes 49160 | tf_op jit(solution)/shard_map/ppermute | solution.py:41

commit v5 on v4

--- a/solution.py
+++ b/solution.py
@@ -52,15 +52,15 @@
     return lax.rem(lax.axis_index("section") + (sections - tick), sections)
 
 
-def pack_kernel(dims, ids_ref, gain_ref, bias_ref, keys_ref, values_ref, *refs):
+def pack_kernel(dims, *refs):
     sections, tensors, rows, heads_dev, group, kv_dev = dims
-    packs, later_ref = refs[:tensors], refs[tensors] if sections > 1 else None
-    gains, biases, keys, values, sems = refs[-5:]
+    sources, refs = refs[:8], refs[8:]
+    packs, (h_ref, next_ref, lengths_ref) = refs[:tensors], refs[tensors : tensors + 3]
+    ids, lengths, gains, biases, keys, values, sems = refs[tensors + 3 :]
+    targets = (ids, lengths, keys, values, gains, biases, h_ref, next_ref)
     copies = [
         pltpu.make_async_copy(source, target, sems.at[i])
-        for i, (source, target) in enumerate(
-            [(gain_ref, gains), (bias_ref, biases), (keys_ref, keys), (values_ref, values)]
-        )
+        for i, (source, target) in enumerate(zip(sources, targets))
     ]
     for copy in copies:
         copy.start()
@@ -68,11 +68,17 @@
     tenants = gains.shape[0]
     count = sections * rows
     spot = lax.broadcasted_iota(jnp.int32, (count, tenants), 0)
+    line = lax.broadcasted_iota(jnp.int32, lengths_ref.shape, 0)
     wanted = jnp.zeros((count, tenants), jnp.int32)
+    kept = jnp.zeros(lengths_ref.shape, jnp.int32)
+    copies[0].wait()
+    copies[1].wait()
     for tick in range(sections):
         batch = batch_at(tick, sections)
+        kept = jnp.where(line == tick, lengths[batch], kept)
         for i in range(rows):
-            wanted = jnp.where(spot == tick * rows + i, ids_ref[batch, i], wanted)
+            wanted = jnp.where(spot == tick * rows + i, ids[batch, i], wanted)
+    lengths_ref[...] = kept.astype(F32)
     wanted = wanted - at * tenants
     onehot = jnp.where(wanted == lax.broadcasted_iota(jnp.int32, (count, tenants), 1), 1.0, 0.0)
     onehot = onehot.astype(BF)
@@ -87,11 +93,11 @@
         for which, cache in enumerate((keys, values)):
             for b in range(sections):
                 for g in range(kv_dev):
-                    to = blocks + (which * sections + b) * kv_dev + g
+                    to = sections * blocks + (which * sections + b) * kv_dev + g
                     packs[d][to] = cache[b, start + g]
-    copies[0].wait()
+    copies[4].wait()
     gain_rows = jnp.dot(onehot, gains[...], preferred_element_type=F32)
-    copies[1].wait()
+    copies[5].wait()
     bias_rows = jnp.dot(onehot, biases[...], preferred_element_type=F32)
     for tick in range(sections):
         mine = slice(tick * rows, (tick + 1) * rows)
@@ -100,57 +106,76 @@
             block = jnp.concatenate(
                 [both[:, (j * per + k) * lanes : (j * per + k + 1) * lanes] for k in range(per)], 0
             ).astype(BF)
-            if tick == 0:
-                for d in range(tensors):
-                    packs[d][j] = block
-            else:
-                later_ref[(tick - 1) * blocks + j] = block
-
-
-def pack(dims, tenant, gain, bias, keys, values):
+            for d in range(tensors):
+                packs[d][tick * blocks + j] = block
+    copies[6].wait()
+    copies[7].wait()
+
+
+def pack(dims, tenant, lengths, gain, bias, keys, values, h, following):
     sections, tensors, rows, heads_dev, group, kv_dev = dims
     pos = keys.shape[2]
     blocks = 2 * rows * gain.shape[1] // (pos * HD)
-    out_shape = [shape((blocks + 2 * sections * kv_dev, pos, HD))] * tensors
-    if sections > 1:
-        out_shape += [shape(((sections - 1) * blocks, pos, HD))]
+    out_shape = [shape((sections * (blocks + 2 * kv_dev), pos, HD))] * tensors
+    out_shape += [shape(h.shape), shape(following.shape), shape((sections, HD), F32)]
+    operands = (tenant, lengths, keys, values, gain, bias, h, following)
     return pl.pallas_call(
         lambda *refs: pack_kernel(dims, *refs),
         out_shape=out_shape,
-        in_specs=[SMEM] + [HBM] * 4,
+        in_specs=[HBM] * len(operands),
         out_specs=[VMEM] * len(out_shape),
-        scratch_shapes=[pltpu.VMEM(x.shape, BF) for x in (gain, bias, keys, values)]
-        + [pltpu.SemaphoreType.DMA((4,))],
+        scratch_shapes=[pltpu.SMEM(x.shape, jnp.int32) for x in (tenant, lengths)]
+        + [pltpu.VMEM(x.shape, BF) for x in (gain, bias, keys, values)]
+        + [pltpu.SemaphoreType.DMA((len(operands),))],
         compiler_params=PARAMS,
         cost_estimate=cost(0, 4 * gain.size),
-    )(tenant, in_hbm(gain), in_hbm(bias), in_hbm(keys), in_hbm(values))
-
-
-def hold_kernel(parts, after_ref, w_ref, out_ref, sems):
-    rows = w_ref.shape[0] // parts
-    copies = [
-        pltpu.make_async_copy(
-            w_ref.at[pl.ds(i * rows, rows)], out_ref.at[pl.ds(i * rows, rows)], sems.at[i]
-        )
-        for i in range(parts)
-    ]
+    )(*[in_hbm(x) for x in operands])
+
+
+def join_kernel(count, first, refs):
+    out_ref = refs[-1]
+    for i in range(count):
+        out_ref[i] = refs[i][first:]
+
+
+def join(pieces, first, after):
+    count = len(pieces)
+    dims = pieces[0].shape
+    return pl.pallas_call(
+        lambda *refs: join_kernel(count, first, refs),
+        out_shape=shape((count, dims[0] - first) + dims[1:]),
+        in_specs=[VMEM] * count + [pl.BlockSpec(memory_space=pl.ANY)] * len(after),
+        out_specs=VMEM,
+        compiler_params=PARAMS,
+    )(*pieces, *after)
+
+
+def hold_kernel(parts, after_ref, wq_ref, wo_ref, wq_out, wo_out, sems):
+    copies = []
+    for source, target in ((wq_ref, wq_out), (wo_ref, wo_out)):
+        rows = source.shape[0] // parts
+        for i in range(parts):
+            at = pl.ds(i * rows, rows)
+            copies.append(
+                pltpu.make_async_copy(source.at[at], target.at[at], sems.at[len(copies)])
+            )
     for copy in copies:
         copy.start()
     for copy in copies:
         copy.wait()
 
 
-def hold(weights, after):
+def hold(wq, wo, after):
     parts = 8
     return pl.pallas_call(
         lambda *refs: hold_kernel(parts, *refs),
-        out_shape=pltpu.VMEM(weights.shape, weights.dtype),
-        in_specs=[VMEM, HBM],
-        out_specs=VMEM,
-        scratch_shapes=[pltpu.SemaphoreType.DMA((parts,))],
-        compiler_params=PARAMS,
-        cost_estimate=cost(0, 2 * weights.size),
-    )(after, in_hbm(weights))
+        out_shape=[pltpu.VMEM(wq.shape, BF), pltpu.VMEM(wo.shape, BF)],
+        in_specs=[pl.BlockSpec(memory_space=pl.ANY), HBM, HBM],
+        out_specs=[VMEM] * 2,
+        scratch_shapes=[pltpu.SemaphoreType.DMA((2 * parts,))],
+        compiler_params=PARAMS,
+        cost_estimate=cost(0, 4 * wq.size),
+    )(after, in_hbm(wq), in_hbm(wo))
 
 
 def tiles(w_ref):
@@ -184,60 +209,58 @@
             to = slice(k * count + at.start, k * count + at.stop)
             out_ref[:, to] = got[k * rows : (k + 1) * rows].astype(BF)
     lane = lax.broadcasted_iota(jnp.int32, (rows, HD), 1)
-    tail = jnp.full((rows, HD), length.astype(F32))
+    tail = jnp.broadcast_to(length, (rows, HD))
     for i, term in enumerate(thirds(total) + thirds(squares)):
         tail = jnp.where(lane == i, term, tail)
     out_ref[:, 3 * count :] = tail.astype(BF)
 
 
-def first_kernel(tensors, sections, lengths_ref, h_ref, *refs):
+def first_kernel(tensors, lengths_ref, h_ref, *refs):
     pieces, (w_ref, out_ref) = refs[:tensors], refs[tensors:]
-    length = lengths_ref[batch_at(0, sections), 0]
-    query_sums(0, length, h_ref[...].astype(F32), pieces, w_ref, out_ref)
-
-
-def first_sums(sections, lengths, h, pieces, w):
+    query_sums(0, lengths_ref[0:1], h_ref[...].astype(F32), pieces, w_ref, out_ref)
+
+
+def first_sums(lengths, h, pieces, w):
     tensors = len(pieces)
     return pl.pallas_call(
-        lambda *refs: first_kernel(tensors, sections, *refs),
+        lambda *refs: first_kernel(tensors, *refs),
         out_shape=shape((h.shape[0], 3 * w.shape[1] + HD)),
-        in_specs=[SMEM] + [VMEM] * (tensors + 2),
+        in_specs=[VMEM] * (tensors + 3),
         out_specs=VMEM,
         compiler_params=PARAMS,
         cost_estimate=cost(24 * w.size, 2 * w.size),
     )(lengths, h, *pieces, w)
 
 
-def arrive(arrivals, next_ref):
-    width = next_ref.shape[1]
+def arrive(arrivals, following):
+    width = following.shape[1]
     rest = arrivals[0][:, width:]
     came = tree_sum([arrival[:, :width] for arrival in arrivals]) + rest[:, :width].astype(F32)
     came = came.astype(BF).astype(F32)
     at_first = jnp.full(came.shape, lax.axis_index("section")) == 0
     carried = rest[:, width:].astype(F32) if rest.shape[1] > width else jnp.zeros_like(came)
-    h = jnp.where(at_first, next_ref[...].astype(F32), came)
+    h = jnp.where(at_first, following.astype(F32), came)
     return h, jnp.where(at_first, came, carried)
 
 
-def later_kernel(tensors, sections, tick, lengths_ref, *refs):
+def later_kernel(tensors, tick, lengths_ref, *refs):
     arrivals, next_ref = refs[:tensors], refs[tensors]
     pieces, (w_ref, out_ref, carry_ref) = refs[tensors + 1 : 2 * tensors + 1], refs[2 * tensors + 1 :]
-    h, emitted = arrive(arrivals, next_ref)
+    h, emitted = arrive(arrivals, next_ref[-tick % next_ref.shape[0]])
     width = h.shape[1]
     carry_ref[:, :width] = h.astype(BF)
     carry_ref[:, width:] = emitted.astype(BF)
-    length = lengths_ref[batch_at(tick, sections), 0]
     blocks = 2 * h.shape[0] * width // (pieces[0].shape[1] * HD)
-    query_sums((tick - 1) * blocks, length, h, pieces, w_ref, out_ref)
-
-
-def later_sums(sections, tick, lengths, arrivals, following, pieces, w):
+    query_sums(tick * blocks, lengths_ref[tick : tick + 1], h, pieces, w_ref, out_ref)
+
+
+def later_sums(tick, lengths, arrivals, following, pieces, w):
     tensors = len(pieces)
-    rows, width = following.shape
-    return pl.pallas_call(
-        lambda *refs: later_kernel(tensors, sections, tick, *refs),
+    rows, width = following.shape[1:]
+    return pl.pallas_call(
+        lambda *refs: later_kernel(tensors, tick, *refs),
         out_shape=[shape((rows, 3 * w.shape[1] + HD)), shape((rows, 2 * width))],
-        in_specs=[SMEM] + [VMEM] * (2 * tensors + 2),
+        in_specs=[VMEM] * (2 * tensors + 3),
         out_specs=[VMEM] * 2,
         compiler_params=PARAMS,
         cost_estimate=cost(24 * w.size, 2 * w.size),
@@ -246,7 +269,7 @@
 
 def last_kernel(tensors, *refs):
     state_ref, emitted_ref = refs[-2:]
-    h, emitted = arrive(refs[:tensors], refs[tensors])
+    h, emitted = arrive(refs[:tensors], refs[tensors][0])
     state_ref[0] = h.astype(BF)
     emitted_ref[0] = emitted.astype(BF)
 
@@ -254,7 +277,7 @@
 def last(arrivals, following):
     return pl.pallas_call(
         lambda *refs: last_kernel(len(arrivals), *refs),
-        out_shape=[shape((1,) + following.shape)] * 2,
+        out_shape=[shape((1,) + following.shape[1:])] * 2,
         in_specs=[VMEM] * (len(arrivals) + 1),
         out_specs=[VMEM] * 2,
         compiler_params=PARAMS,
@@ -264,7 +287,9 @@
 def attend_kernel(dims, turns, tick, *refs):
     sections, tensors, rows, kv_dev = dims
     count = len(turns)
-    pieces, (kv_ref, carry_ref, w_ref, out_ref, full_ref) = refs[:count], refs[count:]
+    pieces, (carry_ref, w_ref), refs = refs[:count], refs[count : count + 2], refs[count + 2 :]
+    caches, (out_ref, full_ref) = refs[:-2], refs[-2:]
+    each = caches[0].shape[0] // tensors
     span = w_ref.shape[0]
     width = w_ref.shape[1]
     batch = batch_at(tick, sections)
@@ -285,7 +310,7 @@
     query = rstd * query + tree_sum([piece[:, 2 * span : 3 * span] for piece in pieces])
     query = query.astype(BF).astype(F32)
 
-    pos = kv_ref.shape[3]
+    pos = caches[0].shape[2]
     tensor_at, replica_at = lax.axis_index("tensor"), lax.axis_index("replica")
     cols = lax.broadcasted_iota(jnp.int32, (rows, tensors * pos), 1)
     row = lax.broadcasted_iota(jnp.int32, (rows, tensors * pos), 0)
@@ -306,9 +331,9 @@
         keys, values = (
             jnp.concatenate(
                 [
-                    kv_ref[i, d, (which * sections + batch) * kv_dev + g]
-                    for i in range(count)
-                    for d in range(tensors)
+                    cache[i, (which * sections + batch) * kv_dev + g]
+                    for cache in caches
+                    for i in range(each * tensors)
                 ],
                 0,
             )
@@ -328,16 +353,16 @@
     full_ref[:, width:] = carry_ref[...]
 
 
-def attend(dims, turns, tick, pieces, kv, carry, w):
+def attend(dims, turns, tick, pieces, caches, carry, w):
     rows, width = carry.shape[0], w.shape[1]
     return pl.pallas_call(
         lambda *refs: attend_kernel(dims, turns, tick, *refs),
         out_shape=[shape((rows, width)), shape((rows, width + carry.shape[1]))],
-        in_specs=[VMEM] * (len(pieces) + 3),
+        in_specs=[VMEM] * (len(pieces) + len(caches) + 2),
         out_specs=[VMEM] * 2,
         compiler_params=PARAMS,
         cost_estimate=cost(8 * w.size, 2 * w.size),
-    )(*pieces, kv, carry, w)
+    )(*pieces, carry, w, *caches)
 
 
 def on_device(state, next_embed, tenant, lengths, gain, bias, wq, wo, keys, values):
@@ -351,39 +376,45 @@
     pos = keys.shape[4]
     dims = (sections, tensors, rows, heads_dev, group, kv_dev)
 
-    packs = pack(dims, tenant, gain[0], bias[0], keys[0, :, 0], values[0, :, 0])
-    packs, later = packs[:tensors], packs[tensors:]
+    *packs, carry, following, lengths = pack(
+        dims,
+        tenant,
+        lengths.reshape(-1),
+        gain[0],
+        bias[0],
+        keys[0, :, 0],
+        values[0, :, 0],
+        state[0],
+        next_embed,
+    )
     got = [packs[0]] + [swapped(packs[d], "tensor", d) for d in range(1, tensors)]
-    wq_held = hold(wq[0], packs[0])
+    wq_held, wo_held = hold(wq[0], wo[0], packs[0])
 
     blocks = 2 * rows * width // (pos * HD)
-    kv = jnp.stack([piece[blocks:] for piece in got], 0)[None]
-    turns = [0]
-    bit = replicas // 2
-    while bit:
-        kv = jnp.concatenate([kv, swapped(kv, "replica", bit)], 0)
-        turns = turns + [turn ^ bit for turn in turns]
-        if bit == replicas // 2 and later:
-            later = list(lax.optimization_barrier((later[0], kv))[:1])
-            later = later + [swapped(later[0], "tensor", d) for d in range(1, tensors)]
-        bit //= 2
-
-    carry = state[0]
-    wo_held = None
+    kv = join(got, sections * blocks, [wq_held, wo_held])
+    turns, bit = [0], replicas // 2
+    caches, waiting = [kv], None
+    if bit:
+        waiting = swapped(kv, "replica", bit)
     arrivals = None
     for tick in range(sections):
-        following = next_embed[-tick % sections]
         if tick == 0:
-            sums = first_sums(sections, lengths, carry, got, wq_held)
-            wo_held = hold(wo[0], sums)
+            sums = first_sums(lengths, carry, got, wq_held)
+            while bit:
+                turns = turns + [turn ^ bit for turn in turns]
+                caches, bit = [kv, waiting], bit // 2
+                if bit:
+                    both = join(caches, 0, [sums])
+                    kv = both.reshape((-1,) + both.shape[2:])
+                    waiting = swapped(kv, "replica", bit)
         else:
-            sums, carry = later_sums(sections, tick, lengths, arrivals, following, later, wq_held)
+            sums, carry = later_sums(tick, lengths, arrivals, following, got, wq_held)
         pieces = [sums] + [swapped(sums, "replica", d) for d in range(1, replicas)]
         out, full = attend(
-            (sections, tensors, rows, kv_dev), turns, tick, pieces, kv, carry, wo_held
+            (sections, tensors, rows, kv_dev), turns, tick, pieces, caches, carry, wo_held
         )
         arrivals = [from_behind(full, 0)] + [from_behind(out, d) for d in range(1, tensors)]
-    return tuple(last(arrivals, next_embed[0]))
+    return tuple(last(arrivals, following))
 
 
 def solution(mesh):

time: 66.9 us -> 56.7 us (0.85)
  starting transfers between devices: 29.4 us -> 24.9 us
  Pallas kernels: 17 us -> 14.4 us
  local copies, waits for them, and re-layouts: 1.45 us -> 0 us
  waiting for transfers between devices: 18 us -> 16.6 us
    ppermute x14 -> x11, starting transfers between devices: 15.9 us -> 11.4 us  [swapped(): return lax.ppermute(block, axis, route)]
    ppermute x14 -> x11, waiting for transfers between devices: 12.6 us -> 10.4 us  [swapped(): return lax.ppermute(block, axis, route)]
    pallas_call x4 -> x5, Pallas kernels: 10.6 us -> 8.51 us  [the longest x1 5.93 us: hold(): pl.pallas_call(lambda *refs: hold_kernel(parts, *refs), out_shape=[pltpu....]
    unnamed x7 -> x0, local copies, waits for them, and re-layouts: 1.43 us -> none
    ppermute x8, waiting for transfers between devices: 5.38 us -> 6.18 us  [from_behind(): return lax.ppermute(block, ('section', 'tensor'), route)]
  transfers between devices with their start and end apart: 22 -> 19, of which waited for: 9 -> 11; matrix products, arithmetic and copies ran while one was open for 1% -> 0% of each run, Pallas kernels for 16% -> 13%
where the time goes in v5:
time: 56.7 us; the launch traced here: 56.5 us
  starting transfers between devices  24.9 us (44%)
  waiting for transfers between devices  16.6 us (29%)
  Pallas kernels  14.4 us (25%)
  between operations  0.69 us (1%)
    ppermute x8, starting transfers between devices, from_behind(): return lax.ppermute(block, ('section', 'tensor'), route)  13.5 us
    ppermute x11, starting transfers between devices, swapped(): return lax.ppermute(block, axis, route)  11.4 us
    ppermute x11, waiting for transfers between devices, swapped(): return lax.ppermute(block, axis, route)  10.4 us
    ppermute x8, waiting for transfers between devices, from_behind(): return lax.ppermute(block, ('section', 'tensor'), route)  6.18 us
    pallas_call x1, Pallas kernels, hold(): pl.pallas_call(lambda *refs: hold_kernel(parts, *refs), out_shape=[pltpu....  5.93 us
    pallas_call x2, Pallas kernels, attend(): pl.pallas_call(lambda *refs: attend_kernel(dims, turns, tick, *refs), out...  3.71 us
    pallas_call x1, Pallas kernels, pack(): pl.pallas_call(lambda *refs: pack_kernel(dims, *refs), out_shape=out_shap...  1.52 us
    pallas_call x1, Pallas kernels, later_sums(): pl.pallas_call(lambda *refs: later_kernel(tensors, tick, *refs), out_shap...  1.29 us
  transfers between devices with their start and end apart: 19, of which 11 were waited for; matrix products, arithmetic and copies ran while one was open for 0% of the time, Pallas kernels for 13%

profile of v5, /device:TPU:0, one launch (start us, length us, event | category | flops | bytes accessed | tf_op | source)
XLA Modules:
  0.0 56.5 jit_solution(7115342445663340208)
XLA Ops:
  0.6 1.5 %shard_map.113 = (bf16[24,16,128]{2,1,0:T(8,128)(2,1)S(1)}, bf16[24,16,128]{2,1,0:T(8,128)(2,1)S(1)}, bf16[24,16,128]{2,1,0:T(8,128)(2,1)S(1)}, bf16[24,16,128]{...) custom-call(s32[2,4]{1,0:T(2,128)} %refs_0_.1, ...), custom_call_target="tpu_custom_call" | custom-call | bytes 819200 | tf_op jit(solution)/shard_map/pallas_call | solution.py:122
  2.2 3.1 %collective-permute-start = (bf16[24,16,128]{2,1,0:T(8,128)(2,1)S(1)}, bf16[24,16,128]{2,1,0:T(8,128)(2,1)S(1)}, u32[]{:S(2)}, u32[]{:S(2)}) collective-permute-start(bf16[24,16,128]{2,1,0:T(8,128)(2,1)S(1)} %get-tuple-element.20), channel_id=1, source_target_pairs={{0,4},{4,0},{8,12},{12,8},{1,5},{5,1},{9,13},{13,9},{2,6},{6,2},{1... | collective-permute-start | bytes 294920 | tf_op jit(solution)/shard_map/ppermute | solution.py:31
  5.3 2.6 %collective-permute-start.1 = (bf16[24,16,128]{2,1,0:T(8,128)(2,1)S(1)}, bf16[24,16,128]{2,1,0:T(8,128)(2,1)S(1)}, u32[]{:S(2)}, u32[]{:S(2)}) collective-permute-start(bf16[24,16,128]{2,1,0:T(8,128)(2,1)S(1)} %get-tuple-element.21), channel_id=1, source_target_pairs={{0,8},{4,12},{8,0},{12,4},{1,9},{5,13},{9,1},{13,5},{2,10},{6,14},... | collective-permute-start | bytes 294920 | tf_op jit(solution)/shard_map/ppermute | solution.py:31
  7.8 0.0 collective-permute-start.2
  7.8 5.9 %shard_map.114 = (bf16[2048,2048]{1,0:T(8,128)(2,1)S(1)}, bf16[2048,2048]{1,0:T(8,128)(2,1)S(1)}) custom-call(bf16[24,16,128]{2,1,0:T(8,128)(2,1)S(1)} %get-tuple-element.19.refs_0_.refs_2_.refs_6_, bf16[2048,2048]{1,0:T(8,128)(2,1)} %bitcast.12, bf16[2048,2048]{1,0:T(8,128)(2,1)} %bitcast.13), custom_call_target="tpu_custom_call" | custom-call | bytes 16777216 | tf_op jit(solution)/shard_map/pallas_call | solution.py:170
  13.8 0.0 collective-permute-done.refs_3_.refs_1_.refs_7_
  13.8 1.9 %collective-permute-done.1.refs_4_.refs_2_.refs_8_ = bf16[24,16,128]{2,1,0:T(8,128)(2,1)S(1)} collective-permute-done((bf16[24,16,128]{2,1,0:T(8,128)(2,1)S(1)}, bf16[24,16,128]{2,1,0:T(8,128)(2,1)S(1)}, u32[]{:S(2)}, u32[]{:S(2)}) %collective-permute-start.1) | collective-permute-done | bytes 98336 | tf_op jit(solution)/shard_map/ppermute | solution.py:31
  15.7 0.0 collective-permute-done.2.refs_5_.refs_3_.refs_9_
  15.7 1.6 %collective-permute-start.6 = (bf16[4,8,16,128]{3,2,1,0:T(8,128)(2,1)S(1)}, bf16[4,8,16,128]{3,2,1,0:T(8,128)(2,1)S(1)}, u32[]{:S(2)}, u32[]{:S(2)}) collective-permute-start(bf16[4,8,16,128]{3,2,1,0:T(8,128)(2,1)S(1)} %shard_map.116.refs_0_), channel_id=1, source_target_pairs={{0,2},{1,3},{2,0},{3,1},{4,6},{5,7},{6,4},{7,5},{8,10},{9,11},{10,... | collective-permute-start | bytes 393224 | tf_op jit(solution)/shard_map/ppermute | solution.py:31
  17.3 1.3 %shard_map.115.refs_2_.refs_0_ = bf16[4,6272]{1,0:T(4,128)(2,1)S(1)} custom-call(f32[2,128]{1,0:T(2,128)S(1)} %get-tuple-element.17.refs_0_, bf16[4,2048]{1,0:T(4,128)(2,1)S(1)} %get-tuple-element.18.refs_1_.refs_4_, bf16[24,16,128]{2,1,0:T(8,128)(2,1)S(1)} %get-tuple-element.19.refs_0_.refs_2_.refs_6_, ...), custom_call_target="tpu_custom_call" | custom-call | flops 100663296 | bytes 8388608 | tf_op jit(solution)/shard_map/pallas_call | solution.py:225
  18.5 2.2 %collective-permute-done.6.refs_1_ = bf16[4,8,16,128]{3,2,1,0:T(8,128)(2,1)S(1)} collective-permute-done((bf16[4,8,16,128]{3,2,1,0:T(8,128)(2,1)S(1)}, bf16[4,8,16,128]{3,2,1,0:T(8,128)(2,1)S(1)}, u32[]{:S(2)}, u32[]{:S(2)}) %collective-permute-start.6) | collective-permute-done | bytes 131104 | tf_op jit(solution)/shard_map/ppermute | solution.py:31
  20.7 0.1 collective-permute-start.7
  20.8 1.6 %collective-permute-start.5 = (bf16[4,6272]{1,0:T(4,128)(2,1)S(1)}, bf16[4,6272]{1,0:T(4,128)(2,1)S(1)}, u32[]{:S(2)}, u32[]{:S(2)}) collective-permute-start(bf16[4,6272]{1,0:T(4,128)(2,1)S(1)} %shard_map.115.refs_2_.refs_0_), channel_id=1, source_target_pairs={{0,3},{1,2},{2,1},{3,0},{4,7},{5,6},{6,5},{7,4},{8,11},{9,10},{10,... | collective-permute-start | bytes 150536 | tf_op jit(solution)/shard_map/ppermute | solution.py:31
  22.5 0.5 collective-permute-start.4
  23.0 0.0 collective-permute-start.3
  23.0 1.6 %collective-permute-done.5.refs_3_ = bf16[4,6272]{1,0:T(4,128)(2,1)S(1)} collective-permute-done((bf16[4,6272]{1,0:T(4,128)(2,1)S(1)}, bf16[4,6272]{1,0:T(4,128)(2,1)S(1)}, u32[]{:S(2)}, u32[]{:S(2)}) %collective-permute-start.5) | collective-permute-done | bytes 50208 | tf_op jit(solution)/shard_map/ppermute | solution.py:31
  24.6 2.0 %collective-permute-done.4.refs_2_ = bf16[4,6272]{1,0:T(4,128)(2,1)S(1)} collective-permute-done((bf16[4,6272]{1,0:T(4,128)(2,1)S(1)}, bf16[4,6272]{1,0:T(4,128)(2,1)S(1)}, u32[]{:S(2)}, u32[]{:S(2)}) %collective-permute-start.4) | collective-permute-done | bytes 50208 | tf_op jit(solution)/shard_map/ppermute | solution.py:31
  26.6 0.0 collective-permute-done.3.refs_1_
  26.6 0.0 collective-permute-done.7.refs_7_
  26.6 1.9 %shard_map.118 = (bf16[4,2048]{1,0:T(4,128)(2,1)S(1)}, bf16[4,4096]{1,0:T(4,128)(2,1)S(1)}) custom-call(bf16[4,6272]{1,0:T(4,128)(2,1)S(1)} %shard_map.115.refs_2_.refs_0_, bf16[4,6272]{1,0:T(4,128)(2,1)S(1)} %collective-permute-done.3.refs_1_, bf16[4,6272]{1,0:T(4,128)(2,1)S(1)} %collective-permute-done.4.refs_2_, ...), custom_call_target="tpu_custom_call" | custom-call | flops 33554432 | bytes 8388608 | tf_op jit(solution)/shard_map/pallas_call | solution.py:358
  28.4 1.5 %collective-permute-start.8 = (bf16[4,4096]{1,0:T(4,128)(2,1)S(1)}, bf16[4,4096]{1,0:T(4,128)(2,1)S(1)}, u32[]{:S(2)}, u32[]{:S(2)}) collective-permute-start(bf16[4,4096]{1,0:T(4,128)(2,1)S(1)} %get-tuple-element.25), channel_id=1, source_target_pairs={{0,16},{4,20},{8,24},{12,28},{16,0},{20,4},{24,8},{28,12},{1,17},{... | collective-permute-start | bytes 98312 | tf_op jit(solution)/shard_map/ppermute | solution.py:41
  29.9 2.4 %collective-permute-start.11 = (bf16[4,2048]{1,0:T(4,128)(2,1)S(1)}, bf16[4,2048]{1,0:T(4,128)(2,1)S(1)}, u32[]{:S(2)}, u32[]{:S(2)}) collective-permute-start(bf16[4,2048]{1,0:T(4,128)(2,1)S(1)} %get-tuple-element.26), channel_id=1, source_target_pairs={{12,16},{8,20},{4,24},{0,28},{28,0},{24,4},{20,8},{16,12},{13,17},... | collective-permute-start | bytes 49160 | tf_op jit(solution)/shard_map/ppermute | solution.py:41
  32.4 1.5 %collective-permute-start.10 = (bf16[4,2048]{1,0:T(4,128)(2,1)S(1)}, bf16[4,2048]{1,0:T(4,128)(2,1)S(1)}, u32[]{:S(2)}, u32[]{:S(2)}) collective-permute-start(bf16[4,2048]{1,0:T(4,128)(2,1)S(1)} %get-tuple-element.26), channel_id=1, source_target_pairs={{8,16},{12,20},{0,24},{4,28},{24,0},{28,4},{16,8},{20,12},{9,17},{... | collective-permute-start | bytes 49160 | tf_op jit(solution)/shard_map/ppermute | solution.py:41
  33.9 1.3 %collective-permute-start.9 = (bf16[4,2048]{1,0:T(4,128)(2,1)S(1)}, bf16[4,2048]{1,0:T(4,128)(2,1)S(1)}, u32[]{:S(2)}, u32[]{:S(2)}) collective-permute-start(bf16[4,2048]{1,0:T(4,128)(2,1)S(1)} %get-tuple-element.26), channel_id=1, source_target_pairs={{4,16},{0,20},{12,24},{8,28},{20,0},{16,4},{28,8},{24,12},{5,17},{... | collective-permute-start | bytes 49160 | tf_op jit(solution)/shard_map/ppermute | solution.py:41
  35.2 1.2 %collective-permute-done.11.refs_4_ = bf16[4,2048]{1,0:T(4,128)(2,1)S(1)} collective-permute-done((bf16[4,2048]{1,0:T(4,128)(2,1)S(1)}, bf16[4,2048]{1,0:T(4,128)(2,1)S(1)}, u32[]{:S(2)}, u32[]{:S(2)}) %collective-permute-start.11) | collective-permute-done | bytes 16416 | tf_op jit(solution)/shard_map/ppermute | solution.py:41
  36.4 1.6 %collective-permute-done.10.refs_3_ = bf16[4,2048]{1,0:T(4,128)(2,1)S(1)} collective-permute-done((bf16[4,2048]{1,0:T(4,128)(2,1)S(1)}, bf16[4,2048]{1,0:T(4,128)(2,1)S(1)}, u32[]{:S(2)}, u32[]{:S(2)}) %collective-permute-start.10) | collective-permute-done | bytes 16416 | tf_op jit(solution)/shard_map/ppermute | solution.py:41
  37.9 0.6 %collective-permute-done.9.refs_2_ = bf16[4,2048]{1,0:T(4,128)(2,1)S(1)} collective-permute-done((bf16[4,2048]{1,0:T(4,128)(2,1)S(1)}, bf16[4,2048]{1,0:T(4,128)(2,1)S(1)}, u32[]{:S(2)}, u32[]{:S(2)}) %collective-permute-start.9) | collective-permute-done | bytes 16416 | tf_op jit(solution)/shard_map/ppermute | solution.py:41
  38.5 0.0 collective-permute-done.8.refs_1_
  38.6 1.3 %shard_map.119 = (bf16[4,6272]{1,0:T(4,128)(2,1)S(1)}, bf16[4,4096]{1,0:T(4,128)(2,1)S(1)}) custom-call(f32[2,128]{1,0:T(2,128)S(1)} %get-tuple-element.17.refs_0_, bf16[4,4096]{1,0:T(4,128)(2,1)S(1)} %collective-permute-done.8.refs_1_, bf16[4,2048]{1,0:T(4,128)(2,1)S(1)} %collective-permute-done.9.refs_2_, ...), custom_call_target="tpu_custom_call" | custom-call | flops 100663296 | bytes 8388608 | tf_op jit(solution)/shard_map/pallas_call | solution.py:260
  39.8 0.0 collective-permute-start.14
  39.8 1.0 %collective-permute-start.13 = (bf16[4,6272]{1,0:T(4,128)(2,1)S(1)}, bf16[4,6272]{1,0:T(4,128)(2,1)S(1)}, u32[]{:S(2)}, u32[]{:S(2)}) collective-permute-start(bf16[4,6272]{1,0:T(4,128)(2,1)S(1)} %get-tuple-element.28.refs_0_), channel_id=1, source_target_pairs={{0,2},{1,3},{2,0},{3,1},{4,6},{5,7},{6,4},{7,5},{8,10},{9,11},{10,... | collective-permute-start | bytes 150536 | tf_op jit(solution)/shard_map/ppermute | solution.py:31
  40.9 0.8 %collective-permute-start.12 = (bf16[4,6272]{1,0:T(4,128)(2,1)S(1)}, bf16[4,6272]{1,0:T(4,128)(2,1)S(1)}, u32[]{:S(2)}, u32[]{:S(2)}) collective-permute-start(bf16[4,6272]{1,0:T(4,128)(2,1)S(1)} %get-tuple-element.28.refs_0_), channel_id=1, source_target_pairs={{0,1},{1,0},{2,3},{3,2},{4,5},{5,4},{6,7},{7,6},{8,9},{9,8},{10,11... | collective-permute-start | bytes 150536 | tf_op jit(solution)/shard_map/ppermute | solution.py:31
  41.7 1.7 %collective-permute-done.14.refs_3_ = bf16[4,6272]{1,0:T(4,128)(2,1)S(1)} collective-permute-done((bf16[4,6272]{1,0:T(4,128)(2,1)S(1)}, bf16[4,6272]{1,0:T(4,128)(2,1)S(1)}, u32[]{:S(2)}, u32[]{:S(2)}) %collective-permute-start.14) | collective-permute-done | bytes 50208 | tf_op jit(solution)/shard_map/ppermute | solution.py:31
  43.5 1.0 %collective-permute-done.13.refs_2_ = bf16[4,6272]{1,0:T(4,128)(2,1)S(1)} collective-permute-done((bf16[4,6272]{1,0:T(4,128)(2,1)S(1)}, bf16[4,6272]{1,0:T(4,128)(2,1)S(1)}, u32[]{:S(2)}, u32[]{:S(2)}) %collective-permute-start.13) | collective-permute-done | bytes 50208 | tf_op jit(solution)/shard_map/ppermute | solution.py:31
  44.4 0.0 collective-permute-done.12.refs_1_
  44.5 1.9 %shard_map.120 = (bf16[4,2048]{1,0:T(4,128)(2,1)S(1)}, bf16[4,6144]{1,0:T(4,128)(2,1)S(1)}) custom-call(bf16[4,6272]{1,0:T(4,128)(2,1)S(1)} %get-tuple-element.28.refs_0_, bf16[4,6272]{1,0:T(4,128)(2,1)S(1)} %collective-permute-done.12.refs_1_, bf16[4,6272]{1,0:T(4,128)(2,1)S(1)} %collective-permute-done.13.refs_2_, ...), custom_call_target="tpu_custom_call" | custom-call | flops 33554432 | bytes 8388608 | tf_op jit(solution)/shard_map/pallas_call | solution.py:358
  46.3 0.9 %collective-permute-start.15 = (bf16[4,6144]{1,0:T(4,128)(2,1)S(1)}, bf16[4,6144]{1,0:T(4,128)(2,1)S(1)}, u32[]{:S(2)}, u32[]{:S(2)}) collective-permute-start(bf16[4,6144]{1,0:T(4,128)(2,1)S(1)} %get-tuple-element.30), channel_id=1, source_target_pairs={{0,16},{4,20},{8,24},{12,28},{16,0},{20,4},{24,8},{28,12},{1,17},{... | collective-permute-start | bytes 147464 | tf_op jit(solution)/shard_map/ppermute | solution.py:41
  47.2 3.1 %collective-permute-start.18 = (bf16[4,2048]{1,0:T(4,128)(2,1)S(1)}, bf16[4,2048]{1,0:T(4,128)(2,1)S(1)}, u32[]{:S(2)}, u32[]{:S(2)}) collective-permute-start(bf16[4,2048]{1,0:T(4,128)(2,1)S(1)} %get-tuple-element.31), channel_id=1, source_target_pairs={{12,16},{8,20},{4,24},{0,28},{28,0},{24,4},{20,8},{16,12},{13,17},... | collective-permute-start | bytes 49160 | tf_op jit(solution)/shard_map/ppermute | solution.py:41
  50.3 0.3 collective-permute-start.17
  50.5 2.5 %collective-permute-start.16 = (bf16[4,2048]{1,0:T(4,128)(2,1)S(1)}, bf16[4,2048]{1,0:T(4,128)(2,1)S(1)}, u32[]{:S(2)}, u32[]{:S(2)}) collective-permute-start(bf16[4,2048]{1,0:T(4,128)(2,1)S(1)} %get-tuple-element.31), channel_id=1, source_target_pairs={{4,16},{0,20},{12,24},{8,28},{20,0},{16,4},{28,8},{24,12},{5,17},{... | collective-permute-start | bytes 49160 | tf_op jit(solution)/shard_map/ppermute | solution.py:41
  53.1 0.6 %collective-permute-done.18.refs_3_ = bf16[4,2048]{1,0:T(4,128)(2,1)S(1)} collective-permute-done((bf16[4,2048]{1,0:T(4,128)(2,1)S(1)}, bf16[4,2048]{1,0:T(4,128)(2,1)S(1)}, u32[]{:S(2)}, u32[]{:S(2)}) %collective-permute-start.18) | collective-permute-done | bytes 16416 | tf_op jit(solution)/shard_map/ppermute | solution.py:41
  53.7 2.2 %collective-permute-done.17.refs_2_ = bf16[4,2048]{1,0:T(4,128)(2,1)S(1)} collective-permute-done((bf16[4,2048]{1,0:T(4,128)(2,1)S(1)}, bf16[4,2048]{1,0:T(4,128)(2,1)S(1)}, u32[]{:S(2)}, u32[]{:S(2)}) %collective-permute-start.17) | collective-permute-done | bytes 16416 | tf_op jit(solution)/shard_map/ppermute | solution.py:41
  55.9 0.0 collective-permute-done.16.refs_1_
  55.9 0.0 collective-permute-done.15.refs_0_
  55.9 0.6 %shard_map.121 = (bf16[1,4,2048]{2,1,0:T(4,128)(2,1)}, bf16[1,4,2048]{2,1,0:T(4,128)(2,1)}) custom-call(bf16[4,6144]{1,0:T(4,128)(2,1)S(1)} %collective-permute-done.15.refs_0_, bf16[4,2048]{1,0:T(4,128)(2,1)S(1)} %collective-permute-done.16.refs_1_, bf16[4,2048]{1,0:T(4,128)(2,1)S(1)} %collective-permute-done.17.refs_2_, ...), custom_call_target="tpu_custom_call" | custom-call | tf_op jit(solution)/shard_map/pallas_call | solution.py:278
  (2 shorter events, 0.0 us)
Async XLA Ops:
  2.2 11.6 %collective-permute-start = (bf16[24,16,128]{2,1,0:T(8,128)(2,1)S(1)}, bf16[24,16,128]{2,1,0:T(8,128)(2,1)S(1)}, u32[]{:S(2)}, u32[]{:S(2)}) collective-permute-start(bf16[24,16,128]{2,1,0:T(8,128)(2,1)S(1)} %get-tuple-element.20), channel_id=1, source_target_pairs={{0,4},{4,0},{8,12},{12,8},{1,5},{5,1},{9,13},{13,9},{2,6},{6,2},{1... | collective-permute-start | bytes 294920 | tf_op jit(solution)/shard_map/ppermute | solution.py:31
  5.3 10.4 %collective-permute-start.1 = (bf16[24,16,128]{2,1,0:T(8,128)(2,1)S(1)}, bf16[24,16,128]{2,1,0:T(8,128)(2,1)S(1)}, u32[]{:S(2)}, u32[]{:S(2)}) collective-permute-start(bf16[24,16,128]{2,1,0:T(8,128)(2,1)S(1)} %get-tuple-element.21), channel_id=1, source_target_pairs={{0,8},{4,12},{8,0},{12,4},{1,9},{5,13},{9,1},{13,5},{2,10},{6,14},... | collective-permute-start | bytes 294920 | tf_op jit(solution)/shard_map/ppermute | solution.py:31
  7.8 7.8 %collective-permute-start.2 = (bf16[24,16,128]{2,1,0:T(8,128)(2,1)S(1)}, bf16[24,16,128]{2,1,0:T(8,128)(2,1)S(1)}, u32[]{:S(2)}, u32[]{:S(2)}) collective-permute-start(bf16[24,16,128]{2,1,0:T(8,128)(2,1)S(1)} %get-tuple-element.22), channel_id=1, source_target_pairs={{0,12},{4,8},{8,4},{12,0},{1,13},{5,9},{9,5},{13,1},{2,14},{6,10},... | collective-permute-start | bytes 294920 | tf_op jit(solution)/shard_map/ppermute | solution.py:31
  15.7 5.0 %collective-permute-start.6 = (bf16[4,8,16,128]{3,2,1,0:T(8,128)(2,1)S(1)}, bf16[4,8,16,128]{3,2,1,0:T(8,128)(2,1)S(1)}, u32[]{:S(2)}, u32[]{:S(2)}) collective-permute-start(bf16[4,8,16,128]{3,2,1,0:T(8,128)(2,1)S(1)} %shard_map.116.refs_0_), channel_id=1, source_target_pairs={{0,2},{1,3},{2,0},{3,1},{4,6},{5,7},{6,4},{7,5},{8,10},{9,11},{10,... | collective-permute-start | bytes 393224 | tf_op jit(solution)/shard_map/ppermute | solution.py:31
  20.7 5.8 %collective-permute-start.7 = (bf16[8,8,16,128]{3,2,1,0:T(8,128)(2,1)S(1)}, bf16[8,8,16,128]{3,2,1,0:T(8,128)(2,1)S(1)}, u32[]{:S(2)}, u32[]{:S(2)}) collective-permute-start(bf16[8,8,16,128]{3,2,1,0:T(8,128)(2,1)S(1)} %bitcast.9), channel_id=1, source_target_pairs={{0,1},{1,0},{2,3},{3,2},{4,5},{5,4},{6,7},{7,6},{8,9},{9,8},{10,11... | collective-permute-start | bytes 786440 | tf_op jit(solution)/shard_map/ppermute | solution.py:31
  20.8 3.7 %collective-permute-start.5 = (bf16[4,6272]{1,0:T(4,128)(2,1)S(1)}, bf16[4,6272]{1,0:T(4,128)(2,1)S(1)}, u32[]{:S(2)}, u32[]{:S(2)}) collective-permute-start(bf16[4,6272]{1,0:T(4,128)(2,1)S(1)} %shard_map.115.refs_2_.refs_0_), channel_id=1, source_target_pairs={{0,3},{1,2},{2,1},{3,0},{4,7},{5,6},{6,5},{7,4},{8,11},{9,10},{10,... | collective-permute-start | bytes 150536 | tf_op jit(solution)/shard_map/ppermute | solution.py:31
  22.5 4.1 %collective-permute-start.4 = (bf16[4,6272]{1,0:T(4,128)(2,1)S(1)}, bf16[4,6272]{1,0:T(4,128)(2,1)S(1)}, u32[]{:S(2)}, u32[]{:S(2)}) collective-permute-start(bf16[4,6272]{1,0:T(4,128)(2,1)S(1)} %shard_map.115.refs_2_.refs_0_), channel_id=1, source_target_pairs={{0,2},{1,3},{2,0},{3,1},{4,6},{5,7},{6,4},{7,5},{8,10},{9,11},{10,... | collective-permute-start | bytes 150536 | tf_op jit(solution)/shard_map/ppermute | solution.py:31
  23.0 3.6 %collective-permute-start.3 = (bf16[4,6272]{1,0:T(4,128)(2,1)S(1)}, bf16[4,6272]{1,0:T(4,128)(2,1)S(1)}, u32[]{:S(2)}, u32[]{:S(2)}) collective-permute-start(bf16[4,6272]{1,0:T(4,128)(2,1)S(1)} %shard_map.115.refs_2_.refs_0_), channel_id=1, source_target_pairs={{0,1},{1,0},{2,3},{3,2},{4,5},{5,4},{6,7},{7,6},{8,9},{9,8},{10,11... | collective-permute-start | bytes 150536 | tf_op jit(solution)/shard_map/ppermute | solution.py:31
  28.4 10.1 %collective-permute-start.8 = (bf16[4,4096]{1,0:T(4,128)(2,1)S(1)}, bf16[4,4096]{1,0:T(4,128)(2,1)S(1)}, u32[]{:S(2)}, u32[]{:S(2)}) collective-permute-start(bf16[4,4096]{1,0:T(4,128)(2,1)S(1)} %get-tuple-element.25), channel_id=1, source_target_pairs={{0,16},{4,20},{8,24},{12,28},{16,0},{20,4},{24,8},{28,12},{1,17},{... | collective-permute-start | bytes 98312 | tf_op jit(solution)/shard_map/ppermute | solution.py:41
  29.9 6.4 %collective-permute-start.11 = (bf16[4,2048]{1,0:T(4,128)(2,1)S(1)}, bf16[4,2048]{1,0:T(4,128)(2,1)S(1)}, u32[]{:S(2)}, u32[]{:S(2)}) collective-permute-start(bf16[4,2048]{1,0:T(4,128)(2,1)S(1)} %get-tuple-element.26), channel_id=1, source_target_pairs={{12,16},{8,20},{4,24},{0,28},{28,0},{24,4},{20,8},{16,12},{13,17},... | collective-permute-start | bytes 49160 | tf_op jit(solution)/shard_map/ppermute | solution.py:41
  32.4 5.5 %collective-permute-start.10 = (bf16[4,2048]{1,0:T(4,128)(2,1)S(1)}, bf16[4,2048]{1,0:T(4,128)(2,1)S(1)}, u32[]{:S(2)}, u32[]{:S(2)}) collective-permute-start(bf16[4,2048]{1,0:T(4,128)(2,1)S(1)} %get-tuple-element.26), channel_id=1, source_target_pairs={{8,16},{12,20},{0,24},{4,28},{24,0},{28,4},{16,8},{20,12},{9,17},{... | collective-permute-start | bytes 49160 | tf_op jit(solution)/shard_map/ppermute | solution.py:41
  33.9 4.6 %collective-permute-start.9 = (bf16[4,2048]{1,0:T(4,128)(2,1)S(1)}, bf16[4,2048]{1,0:T(4,128)(2,1)S(1)}, u32[]{:S(2)}, u32[]{:S(2)}) collective-permute-start(bf16[4,2048]{1,0:T(4,128)(2,1)S(1)} %get-tuple-element.26), channel_id=1, source_target_pairs={{4,16},{0,20},{12,24},{8,28},{20,0},{16,4},{28,8},{24,12},{5,17},{... | collective-permute-start | bytes 49160 | tf_op jit(solution)/shard_map/ppermute | solution.py:41
  39.8 3.6 %collective-permute-start.14 = (bf16[4,6272]{1,0:T(4,128)(2,1)S(1)}, bf16[4,6272]{1,0:T(4,128)(2,1)S(1)}, u32[]{:S(2)}, u32[]{:S(2)}) collective-permute-start(bf16[4,6272]{1,0:T(4,128)(2,1)S(1)} %get-tuple-element.28.refs_0_), channel_id=1, source_target_pairs={{0,3},{1,2},{2,1},{3,0},{4,7},{5,6},{6,5},{7,4},{8,11},{9,10},{10,... | collective-permute-start | bytes 150536 | tf_op jit(solution)/shard_map/ppermute | solution.py:31
  39.8 4.6 %collective-permute-start.13 = (bf16[4,6272]{1,0:T(4,128)(2,1)S(1)}, bf16[4,6272]{1,0:T(4,128)(2,1)S(1)}, u32[]{:S(2)}, u32[]{:S(2)}) collective-permute-start(bf16[4,6272]{1,0:T(4,128)(2,1)S(1)} %get-tuple-element.28.refs_0_), channel_id=1, source_target_pairs={{0,2},{1,3},{2,0},{3,1},{4,6},{5,7},{6,4},{7,5},{8,10},{9,11},{10,... | collective-permute-start | bytes 150536 | tf_op jit(solution)/shard_map/ppermute | solution.py:31
  40.9 3.6 %collective-permute-start.12 = (bf16[4,6272]{1,0:T(4,128)(2,1)S(1)}, bf16[4,6272]{1,0:T(4,128)(2,1)S(1)}, u32[]{:S(2)}, u32[]{:S(2)}) collective-permute-start(bf16[4,6272]{1,0:T(4,128)(2,1)S(1)} %get-tuple-element.28.refs_0_), channel_id=1, source_target_pairs={{0,1},{1,0},{2,3},{3,2},{4,5},{5,4},{6,7},{7,6},{8,9},{9,8},{10,11... | collective-permute-start | bytes 150536 | tf_op jit(solution)/shard_map/ppermute | solution.py:31
  46.3 9.6 %collective-permute-start.15 = (bf16[4,6144]{1,0:T(4,128)(2,1)S(1)}, bf16[4,6144]{1,0:T(4,128)(2,1)S(1)}, u32[]{:S(2)}, u32[]{:S(2)}) collective-permute-start(bf16[4,6144]{1,0:T(4,128)(2,1)S(1)} %get-tuple-element.30), channel_id=1, source_target_pairs={{0,16},{4,20},{8,24},{12,28},{16,0},{20,4},{24,8},{28,12},{1,17},{... | collective-permute-start | bytes 147464 | tf_op jit(solution)/shard_map/ppermute | solution.py:41
  47.2 6.5 %collective-permute-start.18 = (bf16[4,2048]{1,0:T(4,128)(2,1)S(1)}, bf16[4,2048]{1,0:T(4,128)(2,1)S(1)}, u32[]{:S(2)}, u32[]{:S(2)}) collective-permute-start(bf16[4,2048]{1,0:T(4,128)(2,1)S(1)} %get-tuple-element.31), channel_id=1, source_target_pairs={{12,16},{8,20},{4,24},{0,28},{28,0},{24,4},{20,8},{16,12},{13,17},... | collective-permute-start | bytes 49160 | tf_op jit(solution)/shard_map/ppermute | solution.py:41
  50.3 5.6 %collective-permute-start.17 = (bf16[4,2048]{1,0:T(4,128)(2,1)S(1)}, bf16[4,2048]{1,0:T(4,128)(2,1)S(1)}, u32[]{:S(2)}, u32[]{:S(2)}) collective-permute-start(bf16[4,2048]{1,0:T(4,128)(2,1)S(1)} %get-tuple-element.31), channel_id=1, source_target_pairs={{8,16},{12,20},{0,24},{4,28},{24,0},{28,4},{16,8},{20,12},{9,17},{... | collective-permute-start | bytes 49160 | tf_op jit(solution)/shard_map/ppermute | solution.py:41
  50.5 5.4 %collective-permute-start.16 = (bf16[4,2048]{1,0:T(4,128)(2,1)S(1)}, bf16[4,2048]{1,0:T(4,128)(2,1)S(1)}, u32[]{:S(2)}, u32[]{:S(2)}) collective-permute-start(bf16[4,2048]{1,0:T(4,128)(2,1)S(1)} %get-tuple-element.31), channel_id=1, source_target_pairs={{4,16},{0,20},{12,24},{8,28},{20,0},{16,4},{28,8},{24,12},{5,17},{... | collective-permute-start | bytes 49160 | tf_op jit(solution)/shard_map/ppermute | solution.py:41

commit v6 on v5

--- a/solution.py
+++ b/solution.py
@@ -243,9 +243,9 @@
     return h, jnp.where(at_first, came, carried)
 
 
-def later_kernel(tensors, tick, lengths_ref, *refs):
-    arrivals, next_ref = refs[:tensors], refs[tensors]
-    pieces, (w_ref, out_ref, carry_ref) = refs[tensors + 1 : 2 * tensors + 1], refs[2 * tensors + 1 :]
+def later_kernel(count, tick, lengths_ref, *refs):
+    arrivals, next_ref = refs[:count], refs[count]
+    pieces, (w_ref, out_ref, carry_ref) = refs[count + 1 : -3], refs[-3:]
     h, emitted = arrive(arrivals, next_ref[-tick % next_ref.shape[0]])
     width = h.shape[1]
     carry_ref[:, :width] = h.astype(BF)
@@ -255,21 +255,20 @@
 
 
 def later_sums(tick, lengths, arrivals, following, pieces, w):
-    tensors = len(pieces)
     rows, width = following.shape[1:]
     return pl.pallas_call(
-        lambda *refs: later_kernel(tensors, tick, *refs),
+        lambda *refs: later_kernel(len(arrivals), tick, *refs),
         out_shape=[shape((rows, 3 * w.shape[1] + HD)), shape((rows, 2 * width))],
-        in_specs=[VMEM] * (2 * tensors + 3),
+        in_specs=[VMEM] * (len(arrivals) + len(pieces) + 3),
         out_specs=[VMEM] * 2,
         compiler_params=PARAMS,
         cost_estimate=cost(24 * w.size, 2 * w.size),
     )(lengths, *arrivals, following, *pieces, w)
 
 
-def last_kernel(tensors, *refs):
+def last_kernel(count, *refs):
     state_ref, emitted_ref = refs[-2:]
-    h, emitted = arrive(refs[:tensors], refs[tensors][0])
+    h, emitted = arrive(refs[:count], refs[count][0])
     state_ref[0] = h.astype(BF)
     emitted_ref[0] = emitted.astype(BF)
 
@@ -287,8 +286,7 @@
 def attend_kernel(dims, turns, tick, *refs):
     sections, tensors, rows, kv_dev = dims
     count = len(turns)
-    pieces, (carry_ref, w_ref), refs = refs[:count], refs[count : count + 2], refs[count + 2 :]
-    caches, (out_ref, full_ref) = refs[:-2], refs[-2:]
+    pieces, w_ref, caches, out_ref = refs[:count], refs[count], refs[count + 1 : -1], refs[-1]
     each = caches[0].shape[0] // tensors
     span = w_ref.shape[0]
     width = w_ref.shape[1]
@@ -347,22 +345,36 @@
         att += [got[h * rows : (h + 1) * rows] for h in range(per_kv)]
     att = jnp.concatenate(att, 1).astype(BF)
     for at in tiles(w_ref):
-        got = jnp.dot(att, w_ref[:, at], preferred_element_type=F32).astype(BF)
-        out_ref[:, at] = got
-        full_ref[:, at] = got
+        out_ref[:, at] = jnp.dot(att, w_ref[:, at], preferred_element_type=F32).astype(BF)
+
+
+def attend(dims, turns, tick, pieces, caches, w):
+    return pl.pallas_call(
+        lambda *refs: attend_kernel(dims, turns, tick, *refs),
+        out_shape=shape((dims[2], w.shape[1])),
+        in_specs=[VMEM] * (len(pieces) + len(caches) + 1),
+        out_specs=VMEM,
+        compiler_params=PARAMS,
+        cost_estimate=cost(8 * w.size, 2 * w.size),
+    )(*pieces, w, *caches)
+
+
+def pair_kernel(mine_ref, other_ref, carry_ref, out_ref, full_ref):
+    width = mine_ref.shape[1]
+    both = (mine_ref[...].astype(F32) + other_ref[...].astype(F32)).astype(BF)
+    out_ref[...] = both
+    full_ref[:, :width] = both
     full_ref[:, width:] = carry_ref[...]
 
 
-def attend(dims, turns, tick, pieces, caches, carry, w):
-    rows, width = carry.shape[0], w.shape[1]
-    return pl.pallas_call(
-        lambda *refs: attend_kernel(dims, turns, tick, *refs),
-        out_shape=[shape((rows, width)), shape((rows, width + carry.shape[1]))],
-        in_specs=[VMEM] * (len(pieces) + len(caches) + 2),
+def pair(mine, other, carry):
+    return pl.pallas_call(
+        pair_kernel,
+        out_shape=[shape(mine.shape), shape((mine.shape[0], mine.shape[1] + carry.shape[1]))],
+        in_specs=[VMEM] * 3,
         out_specs=[VMEM] * 2,
         compiler_params=PARAMS,
-        cost_estimate=cost(8 * w.size, 2 * w.size),
-    )(*pieces, carry, w, *caches)
+    )(mine, other, carry)
 
 
 def on_device(state, next_embed, tenant, lengths, gain, bias, wq, wo, keys, values):
@@ -400,20 +412,20 @@
     for tick in range(sections):
         if tick == 0:
             sums = first_sums(lengths, carry, got, wq_held)
+        else:
+            sums, carry = later_sums(tick, lengths, arrivals, following, got, wq_held)
+        pieces = [sums] + [swapped(sums, "replica", d) for d in range(1, replicas)]
+        if tick == 0:
             while bit:
                 turns = turns + [turn ^ bit for turn in turns]
                 caches, bit = [kv, waiting], bit // 2
                 if bit:
-                    both = join(caches, 0, [sums])
+                    both = join(caches, 0, pieces[2:])
                     kv = both.reshape((-1,) + both.shape[2:])
                     waiting = swapped(kv, "replica", bit)
-        else:
-            sums, carry = later_sums(tick, lengths, arrivals, following, got, wq_held)
-        pieces = [sums] + [swapped(sums, "replica", d) for d in range(1, replicas)]
-        out, full = attend(
-            (sections, tensors, rows, kv_dev), turns, tick, pieces, caches, carry, wo_held
-        )
-        arrivals = [from_behind(full, 0)] + [from_behind(out, d) for d in range(1, tensors)]
+        out = attend((sections, tensors, rows, kv_dev), turns, tick, pieces, caches, wo_held)
+        out, full = pair(out, swapped(out, "tensor", 1), carry)
+        arrivals = [from_behind(full, 0)] + [from_behind(out, d) for d in range(2, tensors, 2)]
     return tuple(last(arrivals, following))
 
 

time: 56.7 us -> 56.1 us (0.989)
  starting transfers between devices: 24.9 us -> 21.8 us
  waiting for transfers between devices: 16.6 us -> 19 us
    ppermute x8 -> x4, starting transfers between devices: 13.5 us -> 8.3 us  [from_behind(): return lax.ppermute(block, ('section', 'tensor'), route)]
    ppermute x11 -> x13, waiting for transfers between devices: 10.4 us -> 14.1 us  [swapped(): return lax.ppermute(block, axis, route)]
    ppermute x11 -> x13, starting transfers between devices: 11.4 us -> 13.5 us  [swapped(): return lax.ppermute(block, axis, route)]
    ppermute x8 -> x4, waiting for transfers between devices: 6.18 us -> 4.93 us  [from_behind(): return lax.ppermute(block, ('section', 'tensor'), route)]
    pallas_call x1 -> x3, Pallas kernels: 1.29 us -> 1.31 us  [the longest x1 1.29 us: later_sums(): pl.pallas_call(lambda *refs: later_kernel(len(arrivals), tick, *refs), ou...]
  transfers between devices with their start and end apart: 19 -> 17, of which waited for: 11 -> 10; matrix products, arithmetic and copies ran while one was open for 0% -> 0% of each run, Pallas kernels for 13% -> 13%
where the time goes in v6:
time: 56.1 us; the launch traced here: 56 us
  starting transfers between devices  21.8 us (39%)
  waiting for transfers between devices  19 us (34%)
  Pallas kernels  14.4 us (26%)
  between operations  0.69 us (1%)
    ppermute x13, waiting for transfers between devices, swapped(): return lax.ppermute(block, axis, route)  14.1 us
    ppermute x13, starting transfers between devices, swapped(): return lax.ppermute(block, axis, route)  13.5 us
    ppermute x4, starting transfers between devices, from_behind(): return lax.ppermute(block, ('section', 'tensor'), route)  8.3 us
    pallas_call x1, Pallas kernels, hold(): pl.pallas_call(lambda *refs: hold_kernel(parts, *refs), out_shape=[pltpu....  5.93 us
    ppermute x4, waiting for transfers between devices, from_behind(): return lax.ppermute(block, ('section', 'tensor'), route)  4.93 us
    pallas_call x2, Pallas kernels, attend(): pl.pallas_call(lambda *refs: attend_kernel(dims, turns, tick, *refs), out...  3.71 us
    pallas_call x1, Pallas kernels, pack(): pl.pallas_call(lambda *refs: pack_kernel(dims, *refs), out_shape=out_shap...  1.52 us
    pallas_call x1, Pallas kernels, later_sums(): pl.pallas_call(lambda *refs: later_kernel(len(arrivals), tick, *refs), ou...  1.29 us
  transfers between devices with their start and end apart: 17, of which 10 were waited for; matrix products, arithmetic and copies ran while one was open for 0% of the time, Pallas kernels for 13%

profile of v6, /device:TPU:0, one launch (start us, length us, event | category | flops | bytes accessed | tf_op | source)
XLA Modules:
  0.0 56.0 jit_solution(16071884156430820692)
XLA Ops:
  0.6 1.5 %shard_map.113 = (bf16[24,16,128]{2,1,0:T(8,128)(2,1)S(1)}, bf16[24,16,128]{2,1,0:T(8,128)(2,1)S(1)}, bf16[24,16,128]{2,1,0:T(8,128)(2,1)S(1)}, bf16[24,16,128]{...) custom-call(s32[2,4]{1,0:T(2,128)} %refs_0_.1, ...), custom_call_target="tpu_custom_call" | custom-call | bytes 819200 | tf_op jit(solution)/shard_map/pallas_call | solution.py:122
  2.2 3.1 %collective-permute-start = (bf16[24,16,128]{2,1,0:T(8,128)(2,1)S(1)}, bf16[24,16,128]{2,1,0:T(8,128)(2,1)S(1)}, u32[]{:S(2)}, u32[]{:S(2)}) collective-permute-start(bf16[24,16,128]{2,1,0:T(8,128)(2,1)S(1)} %get-tuple-element.20), channel_id=1, source_target_pairs={{0,4},{4,0},{8,12},{12,8},{1,5},{5,1},{9,13},{13,9},{2,6},{6,2},{1... | collective-permute-start | bytes 294920 | tf_op jit(solution)/shard_map/ppermute | solution.py:31
  5.3 2.6 %collective-permute-start.1 = (bf16[24,16,128]{2,1,0:T(8,128)(2,1)S(1)}, bf16[24,16,128]{2,1,0:T(8,128)(2,1)S(1)}, u32[]{:S(2)}, u32[]{:S(2)}) collective-permute-start(bf16[24,16,128]{2,1,0:T(8,128)(2,1)S(1)} %get-tuple-element.21), channel_id=1, source_target_pairs={{0,8},{4,12},{8,0},{12,4},{1,9},{5,13},{9,1},{13,5},{2,10},{6,14},... | collective-permute-start | bytes 294920 | tf_op jit(solution)/shard_map/ppermute | solution.py:31
  7.8 0.0 collective-permute-start.2
  7.8 5.9 %shard_map.114 = (bf16[2048,2048]{1,0:T(8,128)(2,1)S(1)}, bf16[2048,2048]{1,0:T(8,128)(2,1)S(1)}) custom-call(bf16[24,16,128]{2,1,0:T(8,128)(2,1)S(1)} %get-tuple-element.19.refs_0_.refs_2_.refs_4_, bf16[2048,2048]{1,0:T(8,128)(2,1)} %bitcast.12, bf16[2048,2048]{1,0:T(8,128)(2,1)} %bitcast.13), custom_call_target="tpu_custom_call" | custom-call | bytes 16777216 | tf_op jit(solution)/shard_map/pallas_call | solution.py:170
  13.8 0.0 collective-permute-done.refs_3_.refs_1_.refs_5_
  13.8 1.9 %collective-permute-done.1.refs_4_.refs_2_.refs_6_ = bf16[24,16,128]{2,1,0:T(8,128)(2,1)S(1)} collective-permute-done((bf16[24,16,128]{2,1,0:T(8,128)(2,1)S(1)}, bf16[24,16,128]{2,1,0:T(8,128)(2,1)S(1)}, u32[]{:S(2)}, u32[]{:S(2)}) %collective-permute-start.1) | collective-permute-done | bytes 98336 | tf_op jit(solution)/shard_map/ppermute | solution.py:31
  15.7 0.0 collective-permute-done.2.refs_5_.refs_3_.refs_7_
  15.7 1.6 %collective-permute-start.6 = (bf16[4,8,16,128]{3,2,1,0:T(8,128)(2,1)S(1)}, bf16[4,8,16,128]{3,2,1,0:T(8,128)(2,1)S(1)}, u32[]{:S(2)}, u32[]{:S(2)}) collective-permute-start(bf16[4,8,16,128]{3,2,1,0:T(8,128)(2,1)S(1)} %shard_map.116.refs_0_), channel_id=1, source_target_pairs={{0,2},{1,3},{2,0},{3,1},{4,6},{5,7},{6,4},{7,5},{8,10},{9,11},{10,... | collective-permute-start | bytes 393224 | tf_op jit(solution)/shard_map/ppermute | solution.py:31
  17.3 1.3 %shard_map.115.refs_0_ = bf16[4,6272]{1,0:T(4,128)(2,1)S(1)} custom-call(f32[2,128]{1,0:T(2,128)S(1)} %get-tuple-element.17.refs_0_, bf16[4,2048]{1,0:T(4,128)(2,1)S(1)} %get-tuple-element.18.refs_1_.carry_ref, bf16[24,16,128]{2,1,0:T(8,128)(2,1)S(1)} %get-tuple-element.19.refs_0_.refs_2_.refs_4_, ...), custom_call_target="tpu_custom_call" | custom-call | flops 100663296 | bytes 8388608 | tf_op jit(solution)/shard_map/pallas_call | solution.py:225
  18.5 0.0 collective-permute-start.5
  18.5 0.6 collective-permute-start.4
  19.1 3.0 %collective-permute-done.5.refs_3_ = bf16[4,6272]{1,0:T(4,128)(2,1)S(1)} collective-permute-done((bf16[4,6272]{1,0:T(4,128)(2,1)S(1)}, bf16[4,6272]{1,0:T(4,128)(2,1)S(1)}, u32[]{:S(2)}, u32[]{:S(2)}) %collective-permute-start.5) | collective-permute-done | bytes 50208 | tf_op jit(solution)/shard_map/ppermute | solution.py:31
  22.1 1.1 %collective-permute-done.4.refs_2_ = bf16[4,6272]{1,0:T(4,128)(2,1)S(1)} collective-permute-done((bf16[4,6272]{1,0:T(4,128)(2,1)S(1)}, bf16[4,6272]{1,0:T(4,128)(2,1)S(1)}, u32[]{:S(2)}, u32[]{:S(2)}) %collective-permute-start.4) | collective-permute-done | bytes 50208 | tf_op jit(solution)/shard_map/ppermute | solution.py:31
  23.2 0.0 collective-permute-done.6.refs_1_
  23.2 0.1 collective-permute-start.7
  23.3 0.4 collective-permute-start.3
  23.8 1.1 %collective-permute-done.3.refs_1_ = bf16[4,6272]{1,0:T(4,128)(2,1)S(1)} collective-permute-done((bf16[4,6272]{1,0:T(4,128)(2,1)S(1)}, bf16[4,6272]{1,0:T(4,128)(2,1)S(1)}, u32[]{:S(2)}, u32[]{:S(2)}) %collective-permute-start.3) | collective-permute-done | bytes 50208 | tf_op jit(solution)/shard_map/ppermute | solution.py:31
  24.9 0.0 collective-permute-done.7.refs_6_
  24.9 1.9 %shard_map.118.mine_ref = bf16[4,2048]{1,0:T(4,128)(2,1)S(1)} custom-call(bf16[4,6272]{1,0:T(4,128)(2,1)S(1)} %shard_map.115.refs_0_, bf16[4,6272]{1,0:T(4,128)(2,1)S(1)} %collective-permute-done.3.refs_1_, bf16[4,6272]{1,0:T(4,128)(2,1)S(1)} %collective-permute-done.4.refs_2_, bf16[4,6272]{1,0:T(4,128)(2,1)S(1)} %collective-permute-done.5.refs_3_, ...), custom_call_target="tpu_custom_call" | custom-call | flops 33554432 | bytes 8388608 | tf_op jit(solution)/shard_map/pallas_call | solution.py:352
  26.7 1.6 %collective-permute-start.8 = (bf16[4,2048]{1,0:T(4,128)(2,1)S(1)}, bf16[4,2048]{1,0:T(4,128)(2,1)S(1)}, u32[]{:S(2)}, u32[]{:S(2)}) collective-permute-start(bf16[4,2048]{1,0:T(4,128)(2,1)S(1)} %shard_map.118.mine_ref), channel_id=1, source_target_pairs={{0,4},{4,0},{8,12},{12,8},{1,5},{5,1},{9,13},{13,9},{2,6},{6,2},{1... | collective-permute-start | bytes 49160 | tf_op jit(solution)/shard_map/ppermute | solution.py:31
  28.3 2.1 %collective-permute-done.8.other_ref = bf16[4,2048]{1,0:T(4,128)(2,1)S(1)} collective-permute-done((bf16[4,2048]{1,0:T(4,128)(2,1)S(1)}, bf16[4,2048]{1,0:T(4,128)(2,1)S(1)}, u32[]{:S(2)}, u32[]{:S(2)}) %collective-permute-start.8) | collective-permute-done | bytes 16416 | tf_op jit(solution)/shard_map/ppermute | solution.py:31
  30.5 1.6 %collective-permute-start.9 = (bf16[4,4096]{1,0:T(4,128)(2,1)S(1)}, bf16[4,4096]{1,0:T(4,128)(2,1)S(1)}, u32[]{:S(2)}, u32[]{:S(2)}) collective-permute-start(bf16[4,4096]{1,0:T(4,128)(2,1)S(1)} %get-tuple-element.25), channel_id=1, source_target_pairs={{0,16},{4,20},{8,24},{12,28},{16,0},{20,4},{24,8},{28,12},{1,17},{... | collective-permute-start | bytes 98312 | tf_op jit(solution)/shard_map/ppermute | solution.py:41
  32.0 2.6 %collective-permute-start.10 = (bf16[4,2048]{1,0:T(4,128)(2,1)S(1)}, bf16[4,2048]{1,0:T(4,128)(2,1)S(1)}, u32[]{:S(2)}, u32[]{:S(2)}) collective-permute-start(bf16[4,2048]{1,0:T(4,128)(2,1)S(1)} %get-tuple-element.26), channel_id=1, source_target_pairs={{8,16},{12,20},{0,24},{4,28},{24,0},{28,4},{16,8},{20,12},{9,17},{... | collective-permute-start | bytes 49160 | tf_op jit(solution)/shard_map/ppermute | solution.py:41
  34.6 2.9 %collective-permute-done.10.refs_2_ = bf16[4,2048]{1,0:T(4,128)(2,1)S(1)} collective-permute-done((bf16[4,2048]{1,0:T(4,128)(2,1)S(1)}, bf16[4,2048]{1,0:T(4,128)(2,1)S(1)}, u32[]{:S(2)}, u32[]{:S(2)}) %collective-permute-start.10) | collective-permute-done | bytes 16416 | tf_op jit(solution)/shard_map/ppermute | solution.py:41
  37.6 0.0 collective-permute-done.9.refs_1_
  37.6 1.3 %shard_map.120 = (bf16[4,6272]{1,0:T(4,128)(2,1)S(1)}, bf16[4,4096]{1,0:T(4,128)(2,1)S(1)}) custom-call(f32[2,128]{1,0:T(2,128)S(1)} %get-tuple-element.17.refs_0_, bf16[4,4096]{1,0:T(4,128)(2,1)S(1)} %collective-permute-done.9.refs_1_, bf16[4,2048]{1,0:T(4,128)(2,1)S(1)} %collective-permute-done.10.refs_2_, ...), custom_call_target="tpu_custom_call" | custom-call | flops 100663296 | bytes 8388608 | tf_op jit(solution)/shard_map/pallas_call | solution.py:259
  38.9 0.0 collective-permute-start.13
  38.9 1.3 %collective-permute-start.12 = (bf16[4,6272]{1,0:T(4,128)(2,1)S(1)}, bf16[4,6272]{1,0:T(4,128)(2,1)S(1)}, u32[]{:S(2)}, u32[]{:S(2)}) collective-permute-start(bf16[4,6272]{1,0:T(4,128)(2,1)S(1)} %get-tuple-element.28.refs_0_), channel_id=1, source_target_pairs={{0,2},{1,3},{2,0},{3,1},{4,6},{5,7},{6,4},{7,5},{8,10},{9,11},{10,... | collective-permute-start | bytes 150536 | tf_op jit(solution)/shard_map/ppermute | solution.py:31
  40.1 0.6 %collective-permute-start.11 = (bf16[4,6272]{1,0:T(4,128)(2,1)S(1)}, bf16[4,6272]{1,0:T(4,128)(2,1)S(1)}, u32[]{:S(2)}, u32[]{:S(2)}) collective-permute-start(bf16[4,6272]{1,0:T(4,128)(2,1)S(1)} %get-tuple-element.28.refs_0_), channel_id=1, source_target_pairs={{0,1},{1,0},{2,3},{3,2},{4,5},{5,4},{6,7},{7,6},{8,9},{9,8},{10,11... | collective-permute-start | bytes 150536 | tf_op jit(solution)/shard_map/ppermute | solution.py:31
  40.7 2.2 %collective-permute-done.13.refs_3_ = bf16[4,6272]{1,0:T(4,128)(2,1)S(1)} collective-permute-done((bf16[4,6272]{1,0:T(4,128)(2,1)S(1)}, bf16[4,6272]{1,0:T(4,128)(2,1)S(1)}, u32[]{:S(2)}, u32[]{:S(2)}) %collective-permute-start.13) | collective-permute-done | bytes 50208 | tf_op jit(solution)/shard_map/ppermute | solution.py:31
  42.9 0.6 %collective-permute-done.12.refs_2_ = bf16[4,6272]{1,0:T(4,128)(2,1)S(1)} collective-permute-done((bf16[4,6272]{1,0:T(4,128)(2,1)S(1)}, bf16[4,6272]{1,0:T(4,128)(2,1)S(1)}, u32[]{:S(2)}, u32[]{:S(2)}) %collective-permute-start.12) | collective-permute-done | bytes 50208 | tf_op jit(solution)/shard_map/ppermute | solution.py:31
  43.6 0.0 collective-permute-done.11.refs_1_
  43.6 1.9 %shard_map.121.mine_ref = bf16[4,2048]{1,0:T(4,128)(2,1)S(1)} custom-call(bf16[4,6272]{1,0:T(4,128)(2,1)S(1)} %get-tuple-element.28.refs_0_, bf16[4,6272]{1,0:T(4,128)(2,1)S(1)} %collective-permute-done.11.refs_1_, bf16[4,6272]{1,0:T(4,128)(2,1)S(1)} %collective-permute-done.12.refs_2_, bf16[4,6272]{1,0:T(4,128)(2,1)S(1)} %collective-permute-done.13.refs_3_, ...), custom_call_target="tpu_custom_call" | custom-call | flops 33554432 | bytes 8388608 | tf_op jit(solution)/shard_map/pallas_call | solution.py:352
  45.4 1.6 %collective-permute-start.14 = (bf16[4,2048]{1,0:T(4,128)(2,1)S(1)}, bf16[4,2048]{1,0:T(4,128)(2,1)S(1)}, u32[]{:S(2)}, u32[]{:S(2)}) collective-permute-start(bf16[4,2048]{1,0:T(4,128)(2,1)S(1)} %shard_map.121.mine_ref), channel_id=1, source_target_pairs={{0,4},{4,0},{8,12},{12,8},{1,5},{5,1},{9,13},{13,9},{2,6},{6,2},{1... | collective-permute-start | bytes 49160 | tf_op jit(solution)/shard_map/ppermute | solution.py:31
  47.0 2.1 %collective-permute-done.14.other_ref = bf16[4,2048]{1,0:T(4,128)(2,1)S(1)} collective-permute-done((bf16[4,2048]{1,0:T(4,128)(2,1)S(1)}, bf16[4,2048]{1,0:T(4,128)(2,1)S(1)}, u32[]{:S(2)}, u32[]{:S(2)}) %collective-permute-start.14) | collective-permute-done | bytes 16416 | tf_op jit(solution)/shard_map/ppermute | solution.py:31
  49.2 0.6 %collective-permute-start.15 = (bf16[4,6144]{1,0:T(4,128)(2,1)S(1)}, bf16[4,6144]{1,0:T(4,128)(2,1)S(1)}, u32[]{:S(2)}, u32[]{:S(2)}) collective-permute-start(bf16[4,6144]{1,0:T(4,128)(2,1)S(1)} %get-tuple-element.30), channel_id=1, source_target_pairs={{0,16},{4,20},{8,24},{12,28},{16,0},{20,4},{24,8},{28,12},{1,17},{... | collective-permute-start | bytes 147464 | tf_op jit(solution)/shard_map/ppermute | solution.py:41
  49.8 3.6 %collective-permute-start.16 = (bf16[4,2048]{1,0:T(4,128)(2,1)S(1)}, bf16[4,2048]{1,0:T(4,128)(2,1)S(1)}, u32[]{:S(2)}, u32[]{:S(2)}) collective-permute-start(bf16[4,2048]{1,0:T(4,128)(2,1)S(1)} %get-tuple-element.31), channel_id=1, source_target_pairs={{8,16},{12,20},{0,24},{4,28},{24,0},{28,4},{16,8},{20,12},{9,17},{... | collective-permute-start | bytes 49160 | tf_op jit(solution)/shard_map/ppermute | solution.py:41
  53.3 2.0 %collective-permute-done.16.refs_1_ = bf16[4,2048]{1,0:T(4,128)(2,1)S(1)} collective-permute-done((bf16[4,2048]{1,0:T(4,128)(2,1)S(1)}, bf16[4,2048]{1,0:T(4,128)(2,1)S(1)}, u32[]{:S(2)}, u32[]{:S(2)}) %collective-permute-start.16) | collective-permute-done | bytes 16416 | tf_op jit(solution)/shard_map/ppermute | solution.py:41
  55.3 0.0 collective-permute-done.15.refs_0_
  55.3 0.6 %shard_map.123 = (bf16[1,4,2048]{2,1,0:T(4,128)(2,1)}, bf16[1,4,2048]{2,1,0:T(4,128)(2,1)}) custom-call(bf16[4,6144]{1,0:T(4,128)(2,1)S(1)} %collective-permute-done.15.refs_0_, bf16[4,2048]{1,0:T(4,128)(2,1)S(1)} %collective-permute-done.16.refs_1_, bf16[2,4,2048]{2,1,0:T(4,128)(2,1)S(1)} %get-tuple-element.27.refs_3_.refs_2_), custom_call_target="tpu_custom_call" | custom-call | tf_op jit(solution)/shard_map/pallas_call | solution.py:277
  (4 shorter events, 0.1 us)
Async XLA Ops:
  2.2 11.6 %collective-permute-start = (bf16[24,16,128]{2,1,0:T(8,128)(2,1)S(1)}, bf16[24,16,128]{2,1,0:T(8,128)(2,1)S(1)}, u32[]{:S(2)}, u32[]{:S(2)}) collective-permute-start(bf16[24,16,128]{2,1,0:T(8,128)(2,1)S(1)} %get-tuple-element.20), channel_id=1, source_target_pairs={{0,4},{4,0},{8,12},{12,8},{1,5},{5,1},{9,13},{13,9},{2,6},{6,2},{1... | collective-permute-start | bytes 294920 | tf_op jit(solution)/shard_map/ppermute | solution.py:31
  5.3 10.4 %collective-permute-start.1 = (bf16[24,16,128]{2,1,0:T(8,128)(2,1)S(1)}, bf16[24,16,128]{2,1,0:T(8,128)(2,1)S(1)}, u32[]{:S(2)}, u32[]{:S(2)}) collective-permute-start(bf16[24,16,128]{2,1,0:T(8,128)(2,1)S(1)} %get-tuple-element.21), channel_id=1, source_target_pairs={{0,8},{4,12},{8,0},{12,4},{1,9},{5,13},{9,1},{13,5},{2,10},{6,14},... | collective-permute-start | bytes 294920 | tf_op jit(solution)/shard_map/ppermute | solution.py:31
  7.8 7.8 %collective-permute-start.2 = (bf16[24,16,128]{2,1,0:T(8,128)(2,1)S(1)}, bf16[24,16,128]{2,1,0:T(8,128)(2,1)S(1)}, u32[]{:S(2)}, u32[]{:S(2)}) collective-permute-start(bf16[24,16,128]{2,1,0:T(8,128)(2,1)S(1)} %get-tuple-element.22), channel_id=1, source_target_pairs={{0,12},{4,8},{8,4},{12,0},{1,13},{5,9},{9,5},{13,1},{2,14},{6,10},... | collective-permute-start | bytes 294920 | tf_op jit(solution)/shard_map/ppermute | solution.py:31
  15.7 7.5 %collective-permute-start.6 = (bf16[4,8,16,128]{3,2,1,0:T(8,128)(2,1)S(1)}, bf16[4,8,16,128]{3,2,1,0:T(8,128)(2,1)S(1)}, u32[]{:S(2)}, u32[]{:S(2)}) collective-permute-start(bf16[4,8,16,128]{3,2,1,0:T(8,128)(2,1)S(1)} %shard_map.116.refs_0_), channel_id=1, source_target_pairs={{0,2},{1,3},{2,0},{3,1},{4,6},{5,7},{6,4},{7,5},{8,10},{9,11},{10,... | collective-permute-start | bytes 393224 | tf_op jit(solution)/shard_map/ppermute | solution.py:31
  18.5 3.5 %collective-permute-start.5 = (bf16[4,6272]{1,0:T(4,128)(2,1)S(1)}, bf16[4,6272]{1,0:T(4,128)(2,1)S(1)}, u32[]{:S(2)}, u32[]{:S(2)}) collective-permute-start(bf16[4,6272]{1,0:T(4,128)(2,1)S(1)} %shard_map.115.refs_0_), channel_id=1, source_target_pairs={{0,3},{1,2},{2,1},{3,0},{4,7},{5,6},{6,5},{7,4},{8,11},{9,10},{10,... | collective-permute-start | bytes 150536 | tf_op jit(solution)/shard_map/ppermute | solution.py:31
  18.5 4.6 %collective-permute-start.4 = (bf16[4,6272]{1,0:T(4,128)(2,1)S(1)}, bf16[4,6272]{1,0:T(4,128)(2,1)S(1)}, u32[]{:S(2)}, u32[]{:S(2)}) collective-permute-start(bf16[4,6272]{1,0:T(4,128)(2,1)S(1)} %shard_map.115.refs_0_), channel_id=1, source_target_pairs={{0,2},{1,3},{2,0},{3,1},{4,6},{5,7},{6,4},{7,5},{8,10},{9,11},{10,... | collective-permute-start | bytes 150536 | tf_op jit(solution)/shard_map/ppermute | solution.py:31
  23.2 1.7 %collective-permute-start.7 = (bf16[8,8,16,128]{3,2,1,0:T(8,128)(2,1)S(1)}, bf16[8,8,16,128]{3,2,1,0:T(8,128)(2,1)S(1)}, u32[]{:S(2)}, u32[]{:S(2)}) collective-permute-start(bf16[8,8,16,128]{3,2,1,0:T(8,128)(2,1)S(1)} %bitcast.9), channel_id=1, source_target_pairs={{0,1},{1,0},{2,3},{3,2},{4,5},{5,4},{6,7},{7,6},{8,9},{9,8},{10,11... | collective-permute-start | bytes 786440 | tf_op jit(solution)/shard_map/ppermute | solution.py:31
  23.3 1.5 %collective-permute-start.3 = (bf16[4,6272]{1,0:T(4,128)(2,1)S(1)}, bf16[4,6272]{1,0:T(4,128)(2,1)S(1)}, u32[]{:S(2)}, u32[]{:S(2)}) collective-permute-start(bf16[4,6272]{1,0:T(4,128)(2,1)S(1)} %shard_map.115.refs_0_), channel_id=1, source_target_pairs={{0,1},{1,0},{2,3},{3,2},{4,5},{5,4},{6,7},{7,6},{8,9},{9,8},{10,11... | collective-permute-start | bytes 150536 | tf_op jit(solution)/shard_map/ppermute | solution.py:31
  26.7 3.8 %collective-permute-start.8 = (bf16[4,2048]{1,0:T(4,128)(2,1)S(1)}, bf16[4,2048]{1,0:T(4,128)(2,1)S(1)}, u32[]{:S(2)}, u32[]{:S(2)}) collective-permute-start(bf16[4,2048]{1,0:T(4,128)(2,1)S(1)} %shard_map.118.mine_ref), channel_id=1, source_target_pairs={{0,4},{4,0},{8,12},{12,8},{1,5},{5,1},{9,13},{13,9},{2,6},{6,2},{1... | collective-permute-start | bytes 49160 | tf_op jit(solution)/shard_map/ppermute | solution.py:31
  30.5 7.1 %collective-permute-start.9 = (bf16[4,4096]{1,0:T(4,128)(2,1)S(1)}, bf16[4,4096]{1,0:T(4,128)(2,1)S(1)}, u32[]{:S(2)}, u32[]{:S(2)}) collective-permute-start(bf16[4,4096]{1,0:T(4,128)(2,1)S(1)} %get-tuple-element.25), channel_id=1, source_target_pairs={{0,16},{4,20},{8,24},{12,28},{16,0},{20,4},{24,8},{28,12},{1,17},{... | collective-permute-start | bytes 98312 | tf_op jit(solution)/shard_map/ppermute | solution.py:41
  32.0 5.5 %collective-permute-start.10 = (bf16[4,2048]{1,0:T(4,128)(2,1)S(1)}, bf16[4,2048]{1,0:T(4,128)(2,1)S(1)}, u32[]{:S(2)}, u32[]{:S(2)}) collective-permute-start(bf16[4,2048]{1,0:T(4,128)(2,1)S(1)} %get-tuple-element.26), channel_id=1, source_target_pairs={{8,16},{12,20},{0,24},{4,28},{24,0},{28,4},{16,8},{20,12},{9,17},{... | collective-permute-start | bytes 49160 | tf_op jit(solution)/shard_map/ppermute | solution.py:41
  38.9 4.0 %collective-permute-start.13 = (bf16[4,6272]{1,0:T(4,128)(2,1)S(1)}, bf16[4,6272]{1,0:T(4,128)(2,1)S(1)}, u32[]{:S(2)}, u32[]{:S(2)}) collective-permute-start(bf16[4,6272]{1,0:T(4,128)(2,1)S(1)} %get-tuple-element.28.refs_0_), channel_id=1, source_target_pairs={{0,3},{1,2},{2,1},{3,0},{4,7},{5,6},{6,5},{7,4},{8,11},{9,10},{10,... | collective-permute-start | bytes 150536 | tf_op jit(solution)/shard_map/ppermute | solution.py:31
  38.9 4.7 %collective-permute-start.12 = (bf16[4,6272]{1,0:T(4,128)(2,1)S(1)}, bf16[4,6272]{1,0:T(4,128)(2,1)S(1)}, u32[]{:S(2)}, u32[]{:S(2)}) collective-permute-start(bf16[4,6272]{1,0:T(4,128)(2,1)S(1)} %get-tuple-element.28.refs_0_), channel_id=1, source_target_pairs={{0,2},{1,3},{2,0},{3,1},{4,6},{5,7},{6,4},{7,5},{8,10},{9,11},{10,... | collective-permute-start | bytes 150536 | tf_op jit(solution)/shard_map/ppermute | solution.py:31
  40.1 3.4 %collective-permute-start.11 = (bf16[4,6272]{1,0:T(4,128)(2,1)S(1)}, bf16[4,6272]{1,0:T(4,128)(2,1)S(1)}, u32[]{:S(2)}, u32[]{:S(2)}) collective-permute-start(bf16[4,6272]{1,0:T(4,128)(2,1)S(1)} %get-tuple-element.28.refs_0_), channel_id=1, source_target_pairs={{0,1},{1,0},{2,3},{3,2},{4,5},{5,4},{6,7},{7,6},{8,9},{9,8},{10,11... | collective-permute-start | bytes 150536 | tf_op jit(solution)/shard_map/ppermute | solution.py:31
  45.4 3.8 %collective-permute-start.14 = (bf16[4,2048]{1,0:T(4,128)(2,1)S(1)}, bf16[4,2048]{1,0:T(4,128)(2,1)S(1)}, u32[]{:S(2)}, u32[]{:S(2)}) collective-permute-start(bf16[4,2048]{1,0:T(4,128)(2,1)S(1)} %shard_map.121.mine_ref), channel_id=1, source_target_pairs={{0,4},{4,0},{8,12},{12,8},{1,5},{5,1},{9,13},{13,9},{2,6},{6,2},{1... | collective-permute-start | bytes 49160 | tf_op jit(solution)/shard_map/ppermute | solution.py:31
  49.2 6.1 %collective-permute-start.15 = (bf16[4,6144]{1,0:T(4,128)(2,1)S(1)}, bf16[4,6144]{1,0:T(4,128)(2,1)S(1)}, u32[]{:S(2)}, u32[]{:S(2)}) collective-permute-start(bf16[4,6144]{1,0:T(4,128)(2,1)S(1)} %get-tuple-element.30), channel_id=1, source_target_pairs={{0,16},{4,20},{8,24},{12,28},{16,0},{20,4},{24,8},{28,12},{1,17},{... | collective-permute-start | bytes 147464 | tf_op jit(solution)/shard_map/ppermute | solution.py:41
  49.8 5.5 %collective-permute-start.16 = (bf16[4,2048]{1,0:T(4,128)(2,1)S(1)}, bf16[4,2048]{1,0:T(4,128)(2,1)S(1)}, u32[]{:S(2)}, u32[]{:S(2)}) collective-permute-start(bf16[4,2048]{1,0:T(4,128)(2,1)S(1)} %get-tuple-element.31), channel_id=1, source_target_pairs={{8,16},{12,20},{0,24},{4,28},{24,0},{28,4},{16,8},{20,12},{9,17},{... | collective-permute-start | bytes 49160 | tf_op jit(solution)/shard_map/ppermute | solution.py:41

commit v7 on v5

--- a/solution.py
+++ b/solution.py
@@ -232,44 +232,53 @@
     )(lengths, h, *pieces, w)
 
 
-def arrive(arrivals, following):
-    width = following.shape[1]
-    rest = arrivals[0][:, width:]
-    came = tree_sum([arrival[:, :width] for arrival in arrivals]) + rest[:, :width].astype(F32)
+def arrive(arrivals, following, tick):
+    sections, rows, width = following.shape
+    rest = arrivals[0][:, width:].astype(F32)
+    section = jnp.full((rows, width), lax.axis_index("section"))
+    left, carried = rest[:, :width], jnp.zeros((rows, width), F32)
+    if sections == 2 and tick > 0:
+        left = jnp.where(section == 1, following[-tick % sections].astype(F32), rest)
+        carried = rest
+    elif tick > 0:
+        carried = rest[:, width:]
+    came = tree_sum([arrival[:, :width] for arrival in arrivals]) + left
     came = came.astype(BF).astype(F32)
-    at_first = jnp.full(came.shape, lax.axis_index("section")) == 0
-    carried = rest[:, width:].astype(F32) if rest.shape[1] > width else jnp.zeros_like(came)
-    h = jnp.where(at_first, following.astype(F32), came)
-    return h, jnp.where(at_first, came, carried)
-
-
-def later_kernel(tensors, tick, lengths_ref, *refs):
-    arrivals, next_ref = refs[:tensors], refs[tensors]
-    pieces, (w_ref, out_ref, carry_ref) = refs[tensors + 1 : 2 * tensors + 1], refs[2 * tensors + 1 :]
-    h, emitted = arrive(arrivals, next_ref[-tick % next_ref.shape[0]])
+    h = jnp.where(section == 0, following[-(tick + 1) % sections].astype(F32), came)
+    return h, jnp.where(section == 0, came, carried)
+
+
+def later_kernel(count, tick, lengths_ref, *refs):
+    arrivals, next_ref = refs[:count], refs[count]
+    pieces, (w_ref, out_ref, carry_ref) = refs[count + 1 : -3], refs[-3:]
+    h, emitted = arrive(arrivals, next_ref, tick - 1)
     width = h.shape[1]
-    carry_ref[:, :width] = h.astype(BF)
-    carry_ref[:, width:] = emitted.astype(BF)
+    if carry_ref.shape[1] == width:
+        first = jnp.full(h.shape, lax.axis_index("section")) == 0
+        carry_ref[...] = jnp.where(first, emitted, h).astype(BF)
+    else:
+        carry_ref[:, :width] = h.astype(BF)
+        carry_ref[:, width:] = emitted.astype(BF)
     blocks = 2 * h.shape[0] * width // (pieces[0].shape[1] * HD)
     query_sums(tick * blocks, lengths_ref[tick : tick + 1], h, pieces, w_ref, out_ref)
 
 
 def later_sums(tick, lengths, arrivals, following, pieces, w):
-    tensors = len(pieces)
     rows, width = following.shape[1:]
-    return pl.pallas_call(
-        lambda *refs: later_kernel(tensors, tick, *refs),
-        out_shape=[shape((rows, 3 * w.shape[1] + HD)), shape((rows, 2 * width))],
-        in_specs=[VMEM] * (2 * tensors + 3),
+    parts = 1 if following.shape[0] == 2 else 2
+    return pl.pallas_call(
+        lambda *refs: later_kernel(len(arrivals), tick, *refs),
+        out_shape=[shape((rows, 3 * w.shape[1] + HD)), shape((rows, width * parts))],
+        in_specs=[VMEM] * (len(arrivals) + len(pieces) + 3),
         out_specs=[VMEM] * 2,
         compiler_params=PARAMS,
         cost_estimate=cost(24 * w.size, 2 * w.size),
     )(lengths, *arrivals, following, *pieces, w)
 
 
-def last_kernel(tensors, *refs):
+def last_kernel(count, *refs):
     state_ref, emitted_ref = refs[-2:]
-    h, emitted = arrive(refs[:tensors], refs[tensors][0])
+    h, emitted = arrive(refs[:count], refs[count], refs[count].shape[0] - 1)
     state_ref[0] = h.astype(BF)
     emitted_ref[0] = emitted.astype(BF)
 
@@ -323,7 +332,7 @@
     per_kv = span // HD // kv_dev
     keep = jnp.concatenate([jnp.concatenate(keep, 1)] * per_kv, 0)
 
-    att = []
+    sums = [0.0] * len(tiles(w_ref))
     for g in range(kv_dev):
         mine = jnp.concatenate(
             [query[:, h * HD : (h + 1) * HD] for h in range(g * per_kv, (g + 1) * per_kv)], 0
@@ -344,12 +353,14 @@
         probs = jnp.exp(scores - jnp.max(scores, axis=-1, keepdims=True))
         total = jnp.sum(probs, axis=-1, keepdims=True)
         got = jnp.dot(probs.astype(BF), values, preferred_element_type=F32) / total
-        att += [got[h * rows : (h + 1) * rows] for h in range(per_kv)]
-    att = jnp.concatenate(att, 1).astype(BF)
-    for at in tiles(w_ref):
-        got = jnp.dot(att, w_ref[:, at], preferred_element_type=F32).astype(BF)
-        out_ref[:, at] = got
-        full_ref[:, at] = got
+        att = jnp.concatenate([got[h * rows : (h + 1) * rows] for h in range(per_kv)], 1)
+        att = att.astype(BF)
+        depth = slice(g * per_kv * HD, (g + 1) * per_kv * HD)
+        for i, at in enumerate(tiles(w_ref)):
+            sums[i] += jnp.dot(att, w_ref[depth, at], preferred_element_type=F32)
+    for got, at in zip(sums, tiles(w_ref)):
+        out_ref[:, at] = got.astype(BF)
+        full_ref[:, at] = got.astype(BF)
     full_ref[:, width:] = carry_ref[...]
 
 
@@ -400,16 +411,17 @@
     for tick in range(sections):
         if tick == 0:
             sums = first_sums(lengths, carry, got, wq_held)
+        else:
+            sums, carry = later_sums(tick, lengths, arrivals, following, got, wq_held)
+        pieces = [sums] + [swapped(sums, "replica", d) for d in range(1, replicas)]
+        if tick == 0:
             while bit:
                 turns = turns + [turn ^ bit for turn in turns]
                 caches, bit = [kv, waiting], bit // 2
                 if bit:
-                    both = join(caches, 0, [sums])
+                    both = join(caches, 0, pieces[2:])
                     kv = both.reshape((-1,) + both.shape[2:])
                     waiting = swapped(kv, "replica", bit)
-        else:
-            sums, carry = later_sums(tick, lengths, arrivals, following, got, wq_held)
-        pieces = [sums] + [swapped(sums, "replica", d) for d in range(1, replicas)]
         out, full = attend(
             (sections, tensors, rows, kv_dev), turns, tick, pieces, caches, carry, wo_held
         )

time: 56.7 us -> 55.2 us (0.974)
  starting transfers between devices: 24.9 us -> 23.8 us
  waiting for transfers between devices: 16.6 us -> 16 us
    ppermute x11, starting transfers between devices: 11.4 us -> 10.3 us  [swapped(): return lax.ppermute(block, axis, route)]
where the time goes in v7:
time: 55.2 us; the launch traced here: 55.1 us
  starting transfers between devices  23.8 us (43%)
  waiting for transfers between devices  16 us (29%)
  Pallas kernels  14.6 us (26%)
  between operations  0.69 us (1%)
    ppermute x8, starting transfers between devices, from_behind(): return lax.ppermute(block, ('section', 'tensor'), route)  13.5 us
    ppermute x11, starting transfers between devices, swapped(): return lax.ppermute(block, axis, route)  10.3 us
    ppermute x11, waiting for transfers between devices, swapped(): return lax.ppermute(block, axis, route)  9.86 us
    ppermute x8, waiting for transfers between devices, from_behind(): return lax.ppermute(block, ('section', 'tensor'), route)  6.18 us
    pallas_call x1, Pallas kernels, hold(): pl.pallas_call(lambda *refs: hold_kernel(parts, *refs), out_shape=[pltpu....  5.93 us
    pallas_call x2, Pallas kernels, attend(): pl.pallas_call(lambda *refs: attend_kernel(dims, turns, tick, *refs), out...  3.89 us
    pallas_call x1, Pallas kernels, pack(): pl.pallas_call(lambda *refs: pack_kernel(dims, *refs), out_shape=out_shap...  1.52 us
    pallas_call x1, Pallas kernels, later_sums(): pl.pallas_call(lambda *refs: later_kernel(len(arrivals), tick, *refs), ou...  1.28 us
  transfers between devices with their start and end apart: 19, of which 11 were waited for; matrix products, arithmetic and copies ran while one was open for 0% of the time, Pallas kernels for 13%

profile of v7, /device:TPU:0, one launch (start us, length us, event | category | flops | bytes accessed | tf_op | source)
XLA Modules:
  0.0 55.1 jit_solution(3037948105202307663)
XLA Ops:
  0.6 1.5 %shard_map.113 = (bf16[24,16,128]{2,1,0:T(8,128)(2,1)S(1)}, bf16[24,16,128]{2,1,0:T(8,128)(2,1)S(1)}, bf16[24,16,128]{2,1,0:T(8,128)(2,1)S(1)}, bf16[24,16,128]{...) custom-call(s32[2,4]{1,0:T(2,128)} %refs_0_.1, ...), custom_call_target="tpu_custom_call" | custom-call | bytes 819200 | tf_op jit(solution)/shard_map/pallas_call | solution.py:122
  2.2 3.1 %collective-permute-start = (bf16[24,16,128]{2,1,0:T(8,128)(2,1)S(1)}, bf16[24,16,128]{2,1,0:T(8,128)(2,1)S(1)}, u32[]{:S(2)}, u32[]{:S(2)}) collective-permute-start(bf16[24,16,128]{2,1,0:T(8,128)(2,1)S(1)} %get-tuple-element.20), channel_id=1, source_target_pairs={{0,4},{4,0},{8,12},{12,8},{1,5},{5,1},{9,13},{13,9},{2,6},{6,2},{1... | collective-permute-start | bytes 294920 | tf_op jit(solution)/shard_map/ppermute | solution.py:31
  5.3 2.6 %collective-permute-start.1 = (bf16[24,16,128]{2,1,0:T(8,128)(2,1)S(1)}, bf16[24,16,128]{2,1,0:T(8,128)(2,1)S(1)}, u32[]{:S(2)}, u32[]{:S(2)}) collective-permute-start(bf16[24,16,128]{2,1,0:T(8,128)(2,1)S(1)} %get-tuple-element.21), channel_id=1, source_target_pairs={{0,8},{4,12},{8,0},{12,4},{1,9},{5,13},{9,1},{13,5},{2,10},{6,14},... | collective-permute-start | bytes 294920 | tf_op jit(solution)/shard_map/ppermute | solution.py:31
  7.8 0.0 collective-permute-start.2
  7.8 5.9 %shard_map.114 = (bf16[2048,2048]{1,0:T(8,128)(2,1)S(1)}, bf16[2048,2048]{1,0:T(8,128)(2,1)S(1)}) custom-call(bf16[24,16,128]{2,1,0:T(8,128)(2,1)S(1)} %get-tuple-element.19.refs_0_.refs_2_.refs_6_, bf16[2048,2048]{1,0:T(8,128)(2,1)} %bitcast.12, bf16[2048,2048]{1,0:T(8,128)(2,1)} %bitcast.13), custom_call_target="tpu_custom_call" | custom-call | bytes 16777216 | tf_op jit(solution)/shard_map/pallas_call | solution.py:170
  13.8 0.0 collective-permute-done.refs_3_.refs_1_.refs_7_
  13.8 1.9 %collective-permute-done.1.refs_4_.refs_2_.refs_8_ = bf16[24,16,128]{2,1,0:T(8,128)(2,1)S(1)} collective-permute-done((bf16[24,16,128]{2,1,0:T(8,128)(2,1)S(1)}, bf16[24,16,128]{2,1,0:T(8,128)(2,1)S(1)}, u32[]{:S(2)}, u32[]{:S(2)}) %collective-permute-start.1) | collective-permute-done | bytes 98336 | tf_op jit(solution)/shard_map/ppermute | solution.py:31
  15.7 0.0 collective-permute-done.2.refs_5_.refs_3_.refs_9_
  15.7 1.6 %collective-permute-start.6 = (bf16[4,8,16,128]{3,2,1,0:T(8,128)(2,1)S(1)}, bf16[4,8,16,128]{3,2,1,0:T(8,128)(2,1)S(1)}, u32[]{:S(2)}, u32[]{:S(2)}) collective-permute-start(bf16[4,8,16,128]{3,2,1,0:T(8,128)(2,1)S(1)} %shard_map.116.refs_0_), channel_id=1, source_target_pairs={{0,2},{1,3},{2,0},{3,1},{4,6},{5,7},{6,4},{7,5},{8,10},{9,11},{10,... | collective-permute-start | bytes 393224 | tf_op jit(solution)/shard_map/ppermute | solution.py:31
  17.3 1.3 %shard_map.115.refs_0_ = bf16[4,6272]{1,0:T(4,128)(2,1)S(1)} custom-call(f32[2,128]{1,0:T(2,128)S(1)} %get-tuple-element.17.refs_0_, bf16[4,2048]{1,0:T(4,128)(2,1)S(1)} %get-tuple-element.18.refs_1_.refs_4_, bf16[24,16,128]{2,1,0:T(8,128)(2,1)S(1)} %get-tuple-element.19.refs_0_.refs_2_.refs_6_, ...), custom_call_target="tpu_custom_call" | custom-call | flops 100663296 | bytes 8388608 | tf_op jit(solution)/shard_map/pallas_call | solution.py:225
  18.5 0.0 collective-permute-start.5
  18.5 0.6 %collective-permute-start.4 = (bf16[4,6272]{1,0:T(4,128)(2,1)S(1)}, bf16[4,6272]{1,0:T(4,128)(2,1)S(1)}, u32[]{:S(2)}, u32[]{:S(2)}) collective-permute-start(bf16[4,6272]{1,0:T(4,128)(2,1)S(1)} %shard_map.115.refs_0_), channel_id=1, source_target_pairs={{0,2},{1,3},{2,0},{3,1},{4,6},{5,7},{6,4},{7,5},{8,10},{9,11},{10,... | collective-permute-start | bytes 150536 | tf_op jit(solution)/shard_map/ppermute | solution.py:31
  19.1 3.0 %collective-permute-done.5.refs_3_ = bf16[4,6272]{1,0:T(4,128)(2,1)S(1)} collective-permute-done((bf16[4,6272]{1,0:T(4,128)(2,1)S(1)}, bf16[4,6272]{1,0:T(4,128)(2,1)S(1)}, u32[]{:S(2)}, u32[]{:S(2)}) %collective-permute-start.5) | collective-permute-done | bytes 50208 | tf_op jit(solution)/shard_map/ppermute | solution.py:31
  22.1 1.1 %collective-permute-done.4.refs_2_ = bf16[4,6272]{1,0:T(4,128)(2,1)S(1)} collective-permute-done((bf16[4,6272]{1,0:T(4,128)(2,1)S(1)}, bf16[4,6272]{1,0:T(4,128)(2,1)S(1)}, u32[]{:S(2)}, u32[]{:S(2)}) %collective-permute-start.4) | collective-permute-done | bytes 50208 | tf_op jit(solution)/shard_map/ppermute | solution.py:31
  23.2 0.0 collective-permute-done.6.refs_1_
  23.2 0.1 collective-permute-start.7
  23.3 0.4 collective-permute-start.3
  23.8 1.1 %collective-permute-done.3.refs_1_ = bf16[4,6272]{1,0:T(4,128)(2,1)S(1)} collective-permute-done((bf16[4,6272]{1,0:T(4,128)(2,1)S(1)}, bf16[4,6272]{1,0:T(4,128)(2,1)S(1)}, u32[]{:S(2)}, u32[]{:S(2)}) %collective-permute-start.3) | collective-permute-done | bytes 50208 | tf_op jit(solution)/shard_map/ppermute | solution.py:31
  24.9 0.0 collective-permute-done.7.refs_7_
  24.9 1.9 %shard_map.118 = (bf16[4,2048]{1,0:T(4,128)(2,1)S(1)}, bf16[4,4096]{1,0:T(4,128)(2,1)S(1)}) custom-call(bf16[4,6272]{1,0:T(4,128)(2,1)S(1)} %shard_map.115.refs_0_, bf16[4,6272]{1,0:T(4,128)(2,1)S(1)} %collective-permute-done.3.refs_1_, bf16[4,6272]{1,0:T(4,128)(2,1)S(1)} %collective-permute-done.4.refs_2_, ...), custom_call_target="tpu_custom_call" | custom-call | flops 33554432 | bytes 8388608 | tf_op jit(solution)/shard_map/pallas_call | solution.py:369
  26.8 1.5 %collective-permute-start.8 = (bf16[4,4096]{1,0:T(4,128)(2,1)S(1)}, bf16[4,4096]{1,0:T(4,128)(2,1)S(1)}, u32[]{:S(2)}, u32[]{:S(2)}) collective-permute-start(bf16[4,4096]{1,0:T(4,128)(2,1)S(1)} %get-tuple-element.25), channel_id=1, source_target_pairs={{0,16},{4,20},{8,24},{12,28},{16,0},{20,4},{24,8},{28,12},{1,17},{... | collective-permute-start | bytes 98312 | tf_op jit(solution)/shard_map/ppermute | solution.py:41
  28.3 2.4 %collective-permute-start.11 = (bf16[4,2048]{1,0:T(4,128)(2,1)S(1)}, bf16[4,2048]{1,0:T(4,128)(2,1)S(1)}, u32[]{:S(2)}, u32[]{:S(2)}) collective-permute-start(bf16[4,2048]{1,0:T(4,128)(2,1)S(1)} %get-tuple-element.26), channel_id=1, source_target_pairs={{12,16},{8,20},{4,24},{0,28},{28,0},{24,4},{20,8},{16,12},{13,17},... | collective-permute-start | bytes 49160 | tf_op jit(solution)/shard_map/ppermute | solution.py:41
  30.7 1.5 %collective-permute-start.10 = (bf16[4,2048]{1,0:T(4,128)(2,1)S(1)}, bf16[4,2048]{1,0:T(4,128)(2,1)S(1)}, u32[]{:S(2)}, u32[]{:S(2)}) collective-permute-start(bf16[4,2048]{1,0:T(4,128)(2,1)S(1)} %get-tuple-element.26), channel_id=1, source_target_pairs={{8,16},{12,20},{0,24},{4,28},{24,0},{28,4},{16,8},{20,12},{9,17},{... | collective-permute-start | bytes 49160 | tf_op jit(solution)/shard_map/ppermute | solution.py:41
  32.3 1.3 %collective-permute-start.9 = (bf16[4,2048]{1,0:T(4,128)(2,1)S(1)}, bf16[4,2048]{1,0:T(4,128)(2,1)S(1)}, u32[]{:S(2)}, u32[]{:S(2)}) collective-permute-start(bf16[4,2048]{1,0:T(4,128)(2,1)S(1)} %get-tuple-element.26), channel_id=1, source_target_pairs={{4,16},{0,20},{12,24},{8,28},{20,0},{16,4},{28,8},{24,12},{5,17},{... | collective-permute-start | bytes 49160 | tf_op jit(solution)/shard_map/ppermute | solution.py:41
  33.6 1.2 %collective-permute-done.11.refs_4_ = bf16[4,2048]{1,0:T(4,128)(2,1)S(1)} collective-permute-done((bf16[4,2048]{1,0:T(4,128)(2,1)S(1)}, bf16[4,2048]{1,0:T(4,128)(2,1)S(1)}, u32[]{:S(2)}, u32[]{:S(2)}) %collective-permute-start.11) | collective-permute-done | bytes 16416 | tf_op jit(solution)/shard_map/ppermute | solution.py:41
  34.7 1.6 %collective-permute-done.10.refs_3_ = bf16[4,2048]{1,0:T(4,128)(2,1)S(1)} collective-permute-done((bf16[4,2048]{1,0:T(4,128)(2,1)S(1)}, bf16[4,2048]{1,0:T(4,128)(2,1)S(1)}, u32[]{:S(2)}, u32[]{:S(2)}) %collective-permute-start.10) | collective-permute-done | bytes 16416 | tf_op jit(solution)/shard_map/ppermute | solution.py:41
  36.3 0.6 %collective-permute-done.9.refs_2_ = bf16[4,2048]{1,0:T(4,128)(2,1)S(1)} collective-permute-done((bf16[4,2048]{1,0:T(4,128)(2,1)S(1)}, bf16[4,2048]{1,0:T(4,128)(2,1)S(1)}, u32[]{:S(2)}, u32[]{:S(2)}) %collective-permute-start.9) | collective-permute-done | bytes 16416 | tf_op jit(solution)/shard_map/ppermute | solution.py:41
  36.9 0.0 collective-permute-done.8.refs_1_
  36.9 1.3 %shard_map.119 = (bf16[4,6272]{1,0:T(4,128)(2,1)S(1)}, bf16[4,2048]{1,0:T(4,128)(2,1)S(1)}) custom-call(f32[2,128]{1,0:T(2,128)S(1)} %get-tuple-element.17.refs_0_, bf16[4,4096]{1,0:T(4,128)(2,1)S(1)} %collective-permute-done.8.refs_1_, bf16[4,2048]{1,0:T(4,128)(2,1)S(1)} %collective-permute-done.9.refs_2_, ...), custom_call_target="tpu_custom_call" | custom-call | flops 100663296 | bytes 8388608 | tf_op jit(solution)/shard_map/pallas_call | solution.py:269
  38.2 0.0 collective-permute-start.14
  38.2 1.3 %collective-permute-start.13 = (bf16[4,6272]{1,0:T(4,128)(2,1)S(1)}, bf16[4,6272]{1,0:T(4,128)(2,1)S(1)}, u32[]{:S(2)}, u32[]{:S(2)}) collective-permute-start(bf16[4,6272]{1,0:T(4,128)(2,1)S(1)} %get-tuple-element.28.refs_0_), channel_id=1, source_target_pairs={{0,2},{1,3},{2,0},{3,1},{4,6},{5,7},{6,4},{7,5},{8,10},{9,11},{10,... | collective-permute-start | bytes 150536 | tf_op jit(solution)/shard_map/ppermute | solution.py:31
  39.5 0.6 %collective-permute-start.12 = (bf16[4,6272]{1,0:T(4,128)(2,1)S(1)}, bf16[4,6272]{1,0:T(4,128)(2,1)S(1)}, u32[]{:S(2)}, u32[]{:S(2)}) collective-permute-start(bf16[4,6272]{1,0:T(4,128)(2,1)S(1)} %get-tuple-element.28.refs_0_), channel_id=1, source_target_pairs={{0,1},{1,0},{2,3},{3,2},{4,5},{5,4},{6,7},{7,6},{8,9},{9,8},{10,11... | collective-permute-start | bytes 150536 | tf_op jit(solution)/shard_map/ppermute | solution.py:31
  40.1 2.2 %collective-permute-done.14.refs_3_ = bf16[4,6272]{1,0:T(4,128)(2,1)S(1)} collective-permute-done((bf16[4,6272]{1,0:T(4,128)(2,1)S(1)}, bf16[4,6272]{1,0:T(4,128)(2,1)S(1)}, u32[]{:S(2)}, u32[]{:S(2)}) %collective-permute-start.14) | collective-permute-done | bytes 50208 | tf_op jit(solution)/shard_map/ppermute | solution.py:31
  42.2 0.6 %collective-permute-done.13.refs_2_ = bf16[4,6272]{1,0:T(4,128)(2,1)S(1)} collective-permute-done((bf16[4,6272]{1,0:T(4,128)(2,1)S(1)}, bf16[4,6272]{1,0:T(4,128)(2,1)S(1)}, u32[]{:S(2)}, u32[]{:S(2)}) %collective-permute-start.13) | collective-permute-done | bytes 50208 | tf_op jit(solution)/shard_map/ppermute | solution.py:31
  42.9 0.0 collective-permute-done.12.refs_1_
  42.9 1.9 %shard_map.120 = (bf16[4,2048]{1,0:T(4,128)(2,1)S(1)}, bf16[4,4096]{1,0:T(4,128)(2,1)S(1)}) custom-call(bf16[4,6272]{1,0:T(4,128)(2,1)S(1)} %get-tuple-element.28.refs_0_, bf16[4,6272]{1,0:T(4,128)(2,1)S(1)} %collective-permute-done.12.refs_1_, bf16[4,6272]{1,0:T(4,128)(2,1)S(1)} %collective-permute-done.13.refs_2_, ...), custom_call_target="tpu_custom_call" | custom-call | flops 33554432 | bytes 8388608 | tf_op jit(solution)/shard_map/pallas_call | solution.py:369
  44.8 0.9 %collective-permute-start.15 = (bf16[4,4096]{1,0:T(4,128)(2,1)S(1)}, bf16[4,4096]{1,0:T(4,128)(2,1)S(1)}, u32[]{:S(2)}, u32[]{:S(2)}) collective-permute-start(bf16[4,4096]{1,0:T(4,128)(2,1)S(1)} %get-tuple-element.30), channel_id=1, source_target_pairs={{0,16},{4,20},{8,24},{12,28},{16,0},{20,4},{24,8},{28,12},{1,17},{... | collective-permute-start | bytes 98312 | tf_op jit(solution)/shard_map/ppermute | solution.py:41
  45.7 3.1 %collective-permute-start.18 = (bf16[4,2048]{1,0:T(4,128)(2,1)S(1)}, bf16[4,2048]{1,0:T(4,128)(2,1)S(1)}, u32[]{:S(2)}, u32[]{:S(2)}) collective-permute-start(bf16[4,2048]{1,0:T(4,128)(2,1)S(1)} %get-tuple-element.31), channel_id=1, source_target_pairs={{12,16},{8,20},{4,24},{0,28},{28,0},{24,4},{20,8},{16,12},{13,17},... | collective-permute-start | bytes 49160 | tf_op jit(solution)/shard_map/ppermute | solution.py:41
  48.8 0.3 collective-permute-start.17
  49.1 2.5 %collective-permute-start.16 = (bf16[4,2048]{1,0:T(4,128)(2,1)S(1)}, bf16[4,2048]{1,0:T(4,128)(2,1)S(1)}, u32[]{:S(2)}, u32[]{:S(2)}) collective-permute-start(bf16[4,2048]{1,0:T(4,128)(2,1)S(1)} %get-tuple-element.31), channel_id=1, source_target_pairs={{4,16},{0,20},{12,24},{8,28},{20,0},{16,4},{28,8},{24,12},{5,17},{... | collective-permute-start | bytes 49160 | tf_op jit(solution)/shard_map/ppermute | solution.py:41
  51.6 0.6 %collective-permute-done.18.refs_3_ = bf16[4,2048]{1,0:T(4,128)(2,1)S(1)} collective-permute-done((bf16[4,2048]{1,0:T(4,128)(2,1)S(1)}, bf16[4,2048]{1,0:T(4,128)(2,1)S(1)}, u32[]{:S(2)}, u32[]{:S(2)}) %collective-permute-start.18) | collective-permute-done | bytes 16416 | tf_op jit(solution)/shard_map/ppermute | solution.py:41
  52.2 2.2 %collective-permute-done.17.refs_2_ = bf16[4,2048]{1,0:T(4,128)(2,1)S(1)} collective-permute-done((bf16[4,2048]{1,0:T(4,128)(2,1)S(1)}, bf16[4,2048]{1,0:T(4,128)(2,1)S(1)}, u32[]{:S(2)}, u32[]{:S(2)}) %collective-permute-start.17) | collective-permute-done | bytes 16416 | tf_op jit(solution)/shard_map/ppermute | solution.py:41
  54.4 0.0 collective-permute-done.16.refs_1_
  54.4 0.0 collective-permute-done.15.refs_0_
  54.4 0.6 %shard_map.121 = (bf16[1,4,2048]{2,1,0:T(4,128)(2,1)}, bf16[1,4,2048]{2,1,0:T(4,128)(2,1)}) custom-call(bf16[4,4096]{1,0:T(4,128)(2,1)S(1)} %collective-permute-done.15.refs_0_, bf16[4,2048]{1,0:T(4,128)(2,1)S(1)} %collective-permute-done.16.refs_1_, bf16[4,2048]{1,0:T(4,128)(2,1)S(1)} %collective-permute-done.17.refs_2_, ...), custom_call_target="tpu_custom_call" | custom-call | tf_op jit(solution)/shard_map/pallas_call | solution.py:287
  (2 shorter events, 0.0 us)
Async XLA Ops:
  2.2 11.6 %collective-permute-start = (bf16[24,16,128]{2,1,0:T(8,128)(2,1)S(1)}, bf16[24,16,128]{2,1,0:T(8,128)(2,1)S(1)}, u32[]{:S(2)}, u32[]{:S(2)}) collective-permute-start(bf16[24,16,128]{2,1,0:T(8,128)(2,1)S(1)} %get-tuple-element.20), channel_id=1, source_target_pairs={{0,4},{4,0},{8,12},{12,8},{1,5},{5,1},{9,13},{13,9},{2,6},{6,2},{1... | collective-permute-start | bytes 294920 | tf_op jit(solution)/shard_map/ppermute | solution.py:31
  5.3 10.4 %collective-permute-start.1 = (bf16[24,16,128]{2,1,0:T(8,128)(2,1)S(1)}, bf16[24,16,128]{2,1,0:T(8,128)(2,1)S(1)}, u32[]{:S(2)}, u32[]{:S(2)}) collective-permute-start(bf16[24,16,128]{2,1,0:T(8,128)(2,1)S(1)} %get-tuple-element.21), channel_id=1, source_target_pairs={{0,8},{4,12},{8,0},{12,4},{1,9},{5,13},{9,1},{13,5},{2,10},{6,14},... | collective-permute-start | bytes 294920 | tf_op jit(solution)/shard_map/ppermute | solution.py:31
  7.8 7.8 %collective-permute-start.2 = (bf16[24,16,128]{2,1,0:T(8,128)(2,1)S(1)}, bf16[24,16,128]{2,1,0:T(8,128)(2,1)S(1)}, u32[]{:S(2)}, u32[]{:S(2)}) collective-permute-start(bf16[24,16,128]{2,1,0:T(8,128)(2,1)S(1)} %get-tuple-element.22), channel_id=1, source_target_pairs={{0,12},{4,8},{8,4},{12,0},{1,13},{5,9},{9,5},{13,1},{2,14},{6,10},... | collective-permute-start | bytes 294920 | tf_op jit(solution)/shard_map/ppermute | solution.py:31
  15.7 7.5 %collective-permute-start.6 = (bf16[4,8,16,128]{3,2,1,0:T(8,128)(2,1)S(1)}, bf16[4,8,16,128]{3,2,1,0:T(8,128)(2,1)S(1)}, u32[]{:S(2)}, u32[]{:S(2)}) collective-permute-start(bf16[4,8,16,128]{3,2,1,0:T(8,128)(2,1)S(1)} %shard_map.116.refs_0_), channel_id=1, source_target_pairs={{0,2},{1,3},{2,0},{3,1},{4,6},{5,7},{6,4},{7,5},{8,10},{9,11},{10,... | collective-permute-start | bytes 393224 | tf_op jit(solution)/shard_map/ppermute | solution.py:31
  18.5 3.5 %collective-permute-start.5 = (bf16[4,6272]{1,0:T(4,128)(2,1)S(1)}, bf16[4,6272]{1,0:T(4,128)(2,1)S(1)}, u32[]{:S(2)}, u32[]{:S(2)}) collective-permute-start(bf16[4,6272]{1,0:T(4,128)(2,1)S(1)} %shard_map.115.refs_0_), channel_id=1, source_target_pairs={{0,3},{1,2},{2,1},{3,0},{4,7},{5,6},{6,5},{7,4},{8,11},{9,10},{10,... | collective-permute-start | bytes 150536 | tf_op jit(solution)/shard_map/ppermute | solution.py:31
  18.5 4.6 %collective-permute-start.4 = (bf16[4,6272]{1,0:T(4,128)(2,1)S(1)}, bf16[4,6272]{1,0:T(4,128)(2,1)S(1)}, u32[]{:S(2)}, u32[]{:S(2)}) collective-permute-start(bf16[4,6272]{1,0:T(4,128)(2,1)S(1)} %shard_map.115.refs_0_), channel_id=1, source_target_pairs={{0,2},{1,3},{2,0},{3,1},{4,6},{5,7},{6,4},{7,5},{8,10},{9,11},{10,... | collective-permute-start | bytes 150536 | tf_op jit(solution)/shard_map/ppermute | solution.py:31
  23.2 1.7 %collective-permute-start.7 = (bf16[8,8,16,128]{3,2,1,0:T(8,128)(2,1)S(1)}, bf16[8,8,16,128]{3,2,1,0:T(8,128)(2,1)S(1)}, u32[]{:S(2)}, u32[]{:S(2)}) collective-permute-start(bf16[8,8,16,128]{3,2,1,0:T(8,128)(2,1)S(1)} %bitcast.9), channel_id=1, source_target_pairs={{0,1},{1,0},{2,3},{3,2},{4,5},{5,4},{6,7},{7,6},{8,9},{9,8},{10,11... | collective-permute-start | bytes 786440 | tf_op jit(solution)/shard_map/ppermute | solution.py:31
  23.3 1.5 %collective-permute-start.3 = (bf16[4,6272]{1,0:T(4,128)(2,1)S(1)}, bf16[4,6272]{1,0:T(4,128)(2,1)S(1)}, u32[]{:S(2)}, u32[]{:S(2)}) collective-permute-start(bf16[4,6272]{1,0:T(4,128)(2,1)S(1)} %shard_map.115.refs_0_), channel_id=1, source_target_pairs={{0,1},{1,0},{2,3},{3,2},{4,5},{5,4},{6,7},{7,6},{8,9},{9,8},{10,11... | collective-permute-start | bytes 150536 | tf_op jit(solution)/shard_map/ppermute | solution.py:31
  26.8 10.1 %collective-permute-start.8 = (bf16[4,4096]{1,0:T(4,128)(2,1)S(1)}, bf16[4,4096]{1,0:T(4,128)(2,1)S(1)}, u32[]{:S(2)}, u32[]{:S(2)}) collective-permute-start(bf16[4,4096]{1,0:T(4,128)(2,1)S(1)} %get-tuple-element.25), channel_id=1, source_target_pairs={{0,16},{4,20},{8,24},{12,28},{16,0},{20,4},{24,8},{28,12},{1,17},{... | collective-permute-start | bytes 98312 | tf_op jit(solution)/shard_map/ppermute | solution.py:41
  28.3 6.4 %collective-permute-start.11 = (bf16[4,2048]{1,0:T(4,128)(2,1)S(1)}, bf16[4,2048]{1,0:T(4,128)(2,1)S(1)}, u32[]{:S(2)}, u32[]{:S(2)}) collective-permute-start(bf16[4,2048]{1,0:T(4,128)(2,1)S(1)} %get-tuple-element.26), channel_id=1, source_target_pairs={{12,16},{8,20},{4,24},{0,28},{28,0},{24,4},{20,8},{16,12},{13,17},... | collective-permute-start | bytes 49160 | tf_op jit(solution)/shard_map/ppermute | solution.py:41
  30.7 5.5 %collective-permute-start.10 = (bf16[4,2048]{1,0:T(4,128)(2,1)S(1)}, bf16[4,2048]{1,0:T(4,128)(2,1)S(1)}, u32[]{:S(2)}, u32[]{:S(2)}) collective-permute-start(bf16[4,2048]{1,0:T(4,128)(2,1)S(1)} %get-tuple-element.26), channel_id=1, source_target_pairs={{8,16},{12,20},{0,24},{4,28},{24,0},{28,4},{16,8},{20,12},{9,17},{... | collective-permute-start | bytes 49160 | tf_op jit(solution)/shard_map/ppermute | solution.py:41
  32.3 4.6 %collective-permute-start.9 = (bf16[4,2048]{1,0:T(4,128)(2,1)S(1)}, bf16[4,2048]{1,0:T(4,128)(2,1)S(1)}, u32[]{:S(2)}, u32[]{:S(2)}) collective-permute-start(bf16[4,2048]{1,0:T(4,128)(2,1)S(1)} %get-tuple-element.26), channel_id=1, source_target_pairs={{4,16},{0,20},{12,24},{8,28},{20,0},{16,4},{28,8},{24,12},{5,17},{... | collective-permute-start | bytes 49160 | tf_op jit(solution)/shard_map/ppermute | solution.py:41
  38.2 4.0 %collective-permute-start.14 = (bf16[4,6272]{1,0:T(4,128)(2,1)S(1)}, bf16[4,6272]{1,0:T(4,128)(2,1)S(1)}, u32[]{:S(2)}, u32[]{:S(2)}) collective-permute-start(bf16[4,6272]{1,0:T(4,128)(2,1)S(1)} %get-tuple-element.28.refs_0_), channel_id=1, source_target_pairs={{0,3},{1,2},{2,1},{3,0},{4,7},{5,6},{6,5},{7,4},{8,11},{9,10},{10,... | collective-permute-start | bytes 150536 | tf_op jit(solution)/shard_map/ppermute | solution.py:31
  38.2 4.7 %collective-permute-start.13 = (bf16[4,6272]{1,0:T(4,128)(2,1)S(1)}, bf16[4,6272]{1,0:T(4,128)(2,1)S(1)}, u32[]{:S(2)}, u32[]{:S(2)}) collective-permute-start(bf16[4,6272]{1,0:T(4,128)(2,1)S(1)} %get-tuple-element.28.refs_0_), channel_id=1, source_target_pairs={{0,2},{1,3},{2,0},{3,1},{4,6},{5,7},{6,4},{7,5},{8,10},{9,11},{10,... | collective-permute-start | bytes 150536 | tf_op jit(solution)/shard_map/ppermute | solution.py:31
  39.5 3.4 %collective-permute-start.12 = (bf16[4,6272]{1,0:T(4,128)(2,1)S(1)}, bf16[4,6272]{1,0:T(4,128)(2,1)S(1)}, u32[]{:S(2)}, u32[]{:S(2)}) collective-permute-start(bf16[4,6272]{1,0:T(4,128)(2,1)S(1)} %get-tuple-element.28.refs_0_), channel_id=1, source_target_pairs={{0,1},{1,0},{2,3},{3,2},{4,5},{5,4},{6,7},{7,6},{8,9},{9,8},{10,11... | collective-permute-start | bytes 150536 | tf_op jit(solution)/shard_map/ppermute | solution.py:31
  44.8 9.6 %collective-permute-start.15 = (bf16[4,4096]{1,0:T(4,128)(2,1)S(1)}, bf16[4,4096]{1,0:T(4,128)(2,1)S(1)}, u32[]{:S(2)}, u32[]{:S(2)}) collective-permute-start(bf16[4,4096]{1,0:T(4,128)(2,1)S(1)} %get-tuple-element.30), channel_id=1, source_target_pairs={{0,16},{4,20},{8,24},{12,28},{16,0},{20,4},{24,8},{28,12},{1,17},{... | collective-permute-start | bytes 98312 | tf_op jit(solution)/shard_map/ppermute | solution.py:41
  45.7 6.5 %collective-permute-start.18 = (bf16[4,2048]{1,0:T(4,128)(2,1)S(1)}, bf16[4,2048]{1,0:T(4,128)(2,1)S(1)}, u32[]{:S(2)}, u32[]{:S(2)}) collective-permute-start(bf16[4,2048]{1,0:T(4,128)(2,1)S(1)} %get-tuple-element.31), channel_id=1, source_target_pairs={{12,16},{8,20},{4,24},{0,28},{28,0},{24,4},{20,8},{16,12},{13,17},... | collective-permute-start | bytes 49160 | tf_op jit(solution)/shard_map/ppermute | solution.py:41
  48.8 5.6 %collective-permute-start.17 = (bf16[4,2048]{1,0:T(4,128)(2,1)S(1)}, bf16[4,2048]{1,0:T(4,128)(2,1)S(1)}, u32[]{:S(2)}, u32[]{:S(2)}) collective-permute-start(bf16[4,2048]{1,0:T(4,128)(2,1)S(1)} %get-tuple-element.31), channel_id=1, source_target_pairs={{8,16},{12,20},{0,24},{4,28},{24,0},{28,4},{16,8},{20,12},{9,17},{... | collective-permute-start | bytes 49160 | tf_op jit(solution)/shard_map/ppermute | solution.py:41
  49.1 5.4 %collective-permute-start.16 = (bf16[4,2048]{1,0:T(4,128)(2,1)S(1)}, bf16[4,2048]{1,0:T(4,128)(2,1)S(1)}, u32[]{:S(2)}, u32[]{:S(2)}) collective-permute-start(bf16[4,2048]{1,0:T(4,128)(2,1)S(1)} %get-tuple-element.31), channel_id=1, source_target_pairs={{4,16},{0,20},{12,24},{8,28},{20,0},{16,4},{28,8},{24,12},{5,17},{... | collective-permute-start | bytes 49160 | tf_op jit(solution)/shard_map/ppermute | solution.py:41

commit v8 on v7

--- a/solution.py
+++ b/solution.py
@@ -55,7 +55,7 @@
 def pack_kernel(dims, *refs):
     sections, tensors, rows, heads_dev, group, kv_dev = dims
     sources, refs = refs[:8], refs[8:]
-    packs, (h_ref, next_ref, lengths_ref) = refs[:tensors], refs[tensors : tensors + 3]
+    packs, (h_ref, next_ref, facts_ref) = refs[:tensors], refs[tensors : tensors + 3]
     ids, lengths, gains, biases, keys, values, sems = refs[tensors + 3 :]
     targets = (ids, lengths, keys, values, gains, biases, h_ref, next_ref)
     copies = [
@@ -68,17 +68,16 @@
     tenants = gains.shape[0]
     count = sections * rows
     spot = lax.broadcasted_iota(jnp.int32, (count, tenants), 0)
-    line = lax.broadcasted_iota(jnp.int32, lengths_ref.shape, 0)
+    lane = lax.broadcasted_iota(jnp.int32, facts_ref.shape, 1)
     wanted = jnp.zeros((count, tenants), jnp.int32)
-    kept = jnp.zeros(lengths_ref.shape, jnp.int32)
+    facts = jnp.zeros(facts_ref.shape, jnp.int32)
     copies[0].wait()
     copies[1].wait()
     for tick in range(sections):
         batch = batch_at(tick, sections)
-        kept = jnp.where(line == tick, lengths[batch], kept)
+        facts = jnp.where(lane == tick + 2, lengths[batch], facts)
         for i in range(rows):
             wanted = jnp.where(spot == tick * rows + i, ids[batch, i], wanted)
-    lengths_ref[...] = kept.astype(F32)
     wanted = wanted - at * tenants
     onehot = jnp.where(wanted == lax.broadcasted_iota(jnp.int32, (count, tenants), 1), 1.0, 0.0)
     onehot = onehot.astype(BF)
@@ -109,6 +108,9 @@
             for d in range(tensors):
                 packs[d][tick * blocks + j] = block
     copies[6].wait()
+    h = h_ref[...].astype(F32)
+    facts = jnp.where(lane == 0, jnp.sum(h, axis=-1, keepdims=True), facts.astype(F32))
+    facts_ref[...] = jnp.where(lane == 1, jnp.sum(h * h, axis=-1, keepdims=True), facts)
     copies[7].wait()
 
 
@@ -117,7 +119,7 @@
     pos = keys.shape[2]
     blocks = 2 * rows * gain.shape[1] // (pos * HD)
     out_shape = [shape((sections * (blocks + 2 * kv_dev), pos, HD))] * tensors
-    out_shape += [shape(h.shape), shape(following.shape), shape((sections, HD), F32)]
+    out_shape += [shape(h.shape), shape(following.shape), shape((rows, HD), F32)]
     operands = (tenant, lengths, keys, values, gain, bias, h, following)
     return pl.pallas_call(
         lambda *refs: pack_kernel(dims, *refs),
@@ -143,39 +145,38 @@
     dims = pieces[0].shape
     return pl.pallas_call(
         lambda *refs: join_kernel(count, first, refs),
-        out_shape=shape((count, dims[0] - first) + dims[1:]),
+        out_shape=shape((count, dims[0] - first) + dims[1:], pieces[0].dtype),
         in_specs=[VMEM] * count + [pl.BlockSpec(memory_space=pl.ANY)] * len(after),
         out_specs=VMEM,
         compiler_params=PARAMS,
     )(*pieces, *after)
 
 
-def hold_kernel(parts, after_ref, wq_ref, wo_ref, wq_out, wo_out, sems):
-    copies = []
-    for source, target in ((wq_ref, wq_out), (wo_ref, wo_out)):
-        rows = source.shape[0] // parts
-        for i in range(parts):
-            at = pl.ds(i * rows, rows)
-            copies.append(
-                pltpu.make_async_copy(source.at[at], target.at[at], sems.at[len(copies)])
-            )
+def hold_kernel(parts, after_ref, w_ref, out_ref, sems):
+    rows = w_ref.shape[0] // parts
+    copies = [
+        pltpu.make_async_copy(
+            w_ref.at[pl.ds(i * rows, rows)], out_ref.at[pl.ds(i * rows, rows)], sems.at[i]
+        )
+        for i in range(parts)
+    ]
     for copy in copies:
         copy.start()
     for copy in copies:
         copy.wait()
 
 
-def hold(wq, wo, after):
+def hold(w, after):
     parts = 8
     return pl.pallas_call(
         lambda *refs: hold_kernel(parts, *refs),
-        out_shape=[pltpu.VMEM(wq.shape, BF), pltpu.VMEM(wo.shape, BF)],
-        in_specs=[pl.BlockSpec(memory_space=pl.ANY), HBM, HBM],
-        out_specs=[VMEM] * 2,
-        scratch_shapes=[pltpu.SemaphoreType.DMA((2 * parts,))],
-        compiler_params=PARAMS,
-        cost_estimate=cost(0, 4 * wq.size),
-    )(after, in_hbm(wq), in_hbm(wo))
+        out_shape=pltpu.VMEM(w.shape, BF),
+        in_specs=[pl.BlockSpec(memory_space=pl.ANY), HBM],
+        out_specs=VMEM,
+        scratch_shapes=[pltpu.SemaphoreType.DMA((parts,))],
+        compiler_params=PARAMS,
+        cost_estimate=cost(0, 2 * w.size),
+    )(after, in_hbm(w))
 
 
 def tiles(w_ref):
@@ -189,15 +190,24 @@
     return [high, middle, x - high - middle]
 
 
-def query_sums(first_block, length, h, pieces, w_ref, out_ref):
-    rows, width = h.shape
+def affine_rows(first_block, rows, width, pieces):
     pos, lanes = pieces[0].shape[1:]
     per = pos // (2 * rows)
     cols = []
     for j in range(width // lanes // per):
         block = tree_sum([piece[first_block + j] for piece in pieces])
         cols += [block[k * 2 * rows : (k + 1) * 2 * rows] for k in range(per)]
-    affine = jnp.concatenate(cols, 1)
+    return jnp.concatenate(cols, 1)
+
+
+def scales(total, squares, width):
+    mean = total * (1.0 / width)
+    return mean, lax.rsqrt(squares * (1.0 / width) - mean * mean + 1e-05)
+
+
+def query_sums(first_block, h, pieces, w_ref, out_ref):
+    rows, width = h.shape
+    affine = affine_rows(first_block, rows, width, pieces)
     total = jnp.sum(h, axis=-1, keepdims=True)
     squares = jnp.sum(h * h, axis=-1, keepdims=True)
     centred = (h - total * (1.0 / width)) * affine[:rows]
@@ -209,27 +219,36 @@
             to = slice(k * count + at.start, k * count + at.stop)
             out_ref[:, to] = got[k * rows : (k + 1) * rows].astype(BF)
     lane = lax.broadcasted_iota(jnp.int32, (rows, HD), 1)
-    tail = jnp.broadcast_to(length, (rows, HD))
+    tail = jnp.zeros((rows, HD), F32)
     for i, term in enumerate(thirds(total) + thirds(squares)):
         tail = jnp.where(lane == i, term, tail)
     out_ref[:, 3 * count :] = tail.astype(BF)
 
 
-def first_kernel(tensors, lengths_ref, h_ref, *refs):
-    pieces, (w_ref, out_ref) = refs[:tensors], refs[tensors:]
-    query_sums(0, lengths_ref[0:1], h_ref[...].astype(F32), pieces, w_ref, out_ref)
-
-
-def first_sums(lengths, h, pieces, w):
+def first_kernel(tensors, h_ref, *refs):
+    pieces, facts, (w_ref, out_ref) = refs[:tensors], refs[tensors:-2], refs[-2:]
+    rows, width = h_ref.shape
+    facts = [ref[i] for ref in facts for i in range(ref.shape[0])]
+    facts = tree_sum(facts)
+    replicas = lax.axis_size("replica")
+    mean, rstd = scales(facts[:, 0:1], facts[:, 1:2], width * replicas)
+    affine = affine_rows(0, rows, width, pieces)
+    x = (h_ref[...].astype(F32) - mean) * rstd * affine[:rows] + affine[rows:]
+    x = x.astype(BF)
+    for at in tiles(w_ref):
+        out_ref[:, at] = jnp.dot(x, w_ref[:, at], preferred_element_type=F32).astype(BF)
+
+
+def first_sums(h, pieces, facts, w):
     tensors = len(pieces)
     return pl.pallas_call(
         lambda *refs: first_kernel(tensors, *refs),
-        out_shape=shape((h.shape[0], 3 * w.shape[1] + HD)),
-        in_specs=[VMEM] * (tensors + 3),
+        out_shape=shape((h.shape[0], w.shape[1])),
+        in_specs=[VMEM] * (tensors + len(facts) + 2),
         out_specs=VMEM,
         compiler_params=PARAMS,
         cost_estimate=cost(24 * w.size, 2 * w.size),
-    )(lengths, h, *pieces, w)
+    )(h, *pieces, *facts, w)
 
 
 def arrive(arrivals, following, tick):
@@ -248,7 +267,7 @@
     return h, jnp.where(section == 0, came, carried)
 
 
-def later_kernel(count, tick, lengths_ref, *refs):
+def later_kernel(count, tick, *refs):
     arrivals, next_ref = refs[:count], refs[count]
     pieces, (w_ref, out_ref, carry_ref) = refs[count + 1 : -3], refs[-3:]
     h, emitted = arrive(arrivals, next_ref, tick - 1)
@@ -260,20 +279,20 @@
         carry_ref[:, :width] = h.astype(BF)
         carry_ref[:, width:] = emitted.astype(BF)
     blocks = 2 * h.shape[0] * width // (pieces[0].shape[1] * HD)
-    query_sums(tick * blocks, lengths_ref[tick : tick + 1], h, pieces, w_ref, out_ref)
-
-
-def later_sums(tick, lengths, arrivals, following, pieces, w):
+    query_sums(tick * blocks, h, pieces, w_ref, out_ref)
+
+
+def later_sums(tick, arrivals, following, pieces, w):
     rows, width = following.shape[1:]
     parts = 1 if following.shape[0] == 2 else 2
     return pl.pallas_call(
         lambda *refs: later_kernel(len(arrivals), tick, *refs),
         out_shape=[shape((rows, 3 * w.shape[1] + HD)), shape((rows, width * parts))],
-        in_specs=[VMEM] * (len(arrivals) + len(pieces) + 3),
+        in_specs=[VMEM] * (len(arrivals) + len(pieces) + 2),
         out_specs=[VMEM] * 2,
         compiler_params=PARAMS,
         cost_estimate=cost(24 * w.size, 2 * w.size),
-    )(lengths, *arrivals, following, *pieces, w)
+    )(*arrivals, following, *pieces, w)
 
 
 def last_kernel(count, *refs):
@@ -297,26 +316,29 @@
     sections, tensors, rows, kv_dev = dims
     count = len(turns)
     pieces, (carry_ref, w_ref), refs = refs[:count], refs[count : count + 2], refs[count + 2 :]
-    caches, (out_ref, full_ref) = refs[:-2], refs[-2:]
+    (out_ref, full_ref), refs = refs[-2:], refs[:-2]
+    caches, facts = refs[: len(refs) // 2], refs[len(refs) // 2 :]
     each = caches[0].shape[0] // tensors
+    facts = [ref[i] for ref in facts for i in range(ref.shape[0])]
     span = w_ref.shape[0]
     width = w_ref.shape[1]
     batch = batch_at(tick, sections)
 
-    tails = [piece[:, 3 * span :].astype(F32) for piece in pieces]
-    totals = [tail[:, 0:1] + tail[:, 1:2] + tail[:, 2:3] for tail in tails]
-    squares = [tail[:, 3:4] + tail[:, 4:5] + tail[:, 5:6] for tail in tails]
-    scale = 1.0 / (width * count)
-    mean = tree_sum(totals) * scale
-    rstd = lax.rsqrt(tree_sum(squares) * scale - mean * mean + 1e-05)
-    query = tree_sum(
-        [
-            piece[:, :span].astype(F32)
-            + (total * (1.0 / width) - mean) * piece[:, span : 2 * span].astype(F32)
-            for piece, total in zip(pieces, totals)
-        ]
-    )
-    query = rstd * query + tree_sum([piece[:, 2 * span : 3 * span] for piece in pieces])
+    if tick == 0:
+        query = tree_sum([piece[...] for piece in pieces])
+    else:
+        tails = [piece[:, 3 * span :].astype(F32) for piece in pieces]
+        totals = [tail[:, 0:1] + tail[:, 1:2] + tail[:, 2:3] for tail in tails]
+        squares = [tail[:, 3:4] + tail[:, 4:5] + tail[:, 5:6] for tail in tails]
+        mean, rstd = scales(tree_sum(totals), tree_sum(squares), width * count)
+        query = tree_sum(
+            [
+                piece[:, :span].astype(F32)
+                + (total * (1.0 / width) - mean) * piece[:, span : 2 * span].astype(F32)
+                for piece, total in zip(pieces, totals)
+            ]
+        )
+        query = rstd * query + tree_sum([piece[:, 2 * span : 3 * span] for piece in pieces])
     query = query.astype(BF).astype(F32)
 
     pos = caches[0].shape[2]
@@ -326,13 +348,14 @@
     spots = jnp.bitwise_xor(cols // pos, tensor_at) * pos + cols % pos
     spots = spots.astype(F32)
     keep = []
-    for turn in turns:
-        valid = jnp.logical_and(row == jnp.bitwise_xor(replica_at, turn), spots < tails[turn][:, 6:7])
+    for turn, fact in zip(turns, facts):
+        length = fact[:, tick + 2 : tick + 3]
+        valid = jnp.logical_and(row == jnp.bitwise_xor(replica_at, turn), spots < length)
         keep.append(jnp.where(valid, 0.0, -1e30))
     per_kv = span // HD // kv_dev
     keep = jnp.concatenate([jnp.concatenate(keep, 1)] * per_kv, 0)
 
-    sums = [0.0] * len(tiles(w_ref))
+    att = []
     for g in range(kv_dev):
         mine = jnp.concatenate(
             [query[:, h * HD : (h + 1) * HD] for h in range(g * per_kv, (g + 1) * per_kv)], 0
@@ -353,27 +376,25 @@
         probs = jnp.exp(scores - jnp.max(scores, axis=-1, keepdims=True))
         total = jnp.sum(probs, axis=-1, keepdims=True)
         got = jnp.dot(probs.astype(BF), values, preferred_element_type=F32) / total
-        att = jnp.concatenate([got[h * rows : (h + 1) * rows] for h in range(per_kv)], 1)
-        att = att.astype(BF)
-        depth = slice(g * per_kv * HD, (g + 1) * per_kv * HD)
-        for i, at in enumerate(tiles(w_ref)):
-            sums[i] += jnp.dot(att, w_ref[depth, at], preferred_element_type=F32)
-    for got, at in zip(sums, tiles(w_ref)):
-        out_ref[:, at] = got.astype(BF)
-        full_ref[:, at] = got.astype(BF)
+        att += [got[h * rows : (h + 1) * rows] for h in range(per_kv)]
+    att = jnp.concatenate(att, 1).astype(BF)
+    for at in tiles(w_ref):
+        got = jnp.dot(att, w_ref[:, at], preferred_element_type=F32).astype(BF)
+        out_ref[:, at] = got
+        full_ref[:, at] = got
     full_ref[:, width:] = carry_ref[...]
 
 
-def attend(dims, turns, tick, pieces, caches, carry, w):
+def attend(dims, turns, tick, pieces, caches, facts, carry, w):
     rows, width = carry.shape[0], w.shape[1]
     return pl.pallas_call(
         lambda *refs: attend_kernel(dims, turns, tick, *refs),
         out_shape=[shape((rows, width)), shape((rows, width + carry.shape[1]))],
-        in_specs=[VMEM] * (len(pieces) + len(caches) + 2),
+        in_specs=[VMEM] * (len(pieces) + len(caches) + len(facts) + 2),
         out_specs=[VMEM] * 2,
         compiler_params=PARAMS,
         cost_estimate=cost(8 * w.size, 2 * w.size),
-    )(*pieces, carry, w, *caches)
+    )(*pieces, carry, w, *caches, *facts)
 
 
 def on_device(state, next_embed, tenant, lengths, gain, bias, wq, wo, keys, values):
@@ -387,7 +408,7 @@
     pos = keys.shape[4]
     dims = (sections, tensors, rows, heads_dev, group, kv_dev)
 
-    *packs, carry, following, lengths = pack(
+    *packs, carry, following, facts = pack(
         dims,
         tenant,
         lengths.reshape(-1),
@@ -399,10 +420,21 @@
         next_embed,
     )
     got = [packs[0]] + [swapped(packs[d], "tensor", d) for d in range(1, tensors)]
-    wq_held, wo_held = hold(wq[0], wo[0], packs[0])
+    wq_held = hold(wq[0], packs[0])
+
+    facts = [facts[None]]
+    bit = replicas // 2
+    while bit:
+        if len(facts) > 1:
+            both = join(facts, 0, [wq_held])
+            facts = [both.reshape((-1,) + both.shape[2:])]
+        facts = [facts[0], swapped(facts[0], "replica", bit)]
+        bit //= 2
+
+    wo_held = hold(wo[0], facts[0])
 
     blocks = 2 * rows * width // (pos * HD)
-    kv = join(got, sections * blocks, [wq_held, wo_held])
+    kv = join(got, sections * blocks, [wo_held, facts[-1]])
     turns, bit = [0], replicas // 2
     caches, waiting = [kv], None
     if bit:
@@ -410,9 +442,9 @@
     arrivals = None
     for tick in range(sections):
         if tick == 0:
-            sums = first_sums(lengths, carry, got, wq_held)
+            sums = first_sums(carry, got, facts, wq_held)
         else:
-            sums, carry = later_sums(tick, lengths, arrivals, following, got, wq_held)
+            sums, carry = later_sums(tick, arrivals, following, got, wq_held)
         pieces = [sums] + [swapped(sums, "replica", d) for d in range(1, replicas)]
         if tick == 0:
             while bit:
@@ -423,7 +455,7 @@
                     kv = both.reshape((-1,) + both.shape[2:])
                     waiting = swapped(kv, "replica", bit)
         out, full = attend(
-            (sections, tensors, rows, kv_dev), turns, tick, pieces, caches, carry, wo_held
+            (sections, tensors, rows, kv_dev), turns, tick, pieces, caches, facts, carry, wo_held
         )
         arrivals = [from_behind(full, 0)] + [from_behind(out, d) for d in range(1, tensors)]
     return tuple(last(arrivals, following))

time: 55.2 us -> 55.4 us (level)
  waiting for transfers between devices: 16 us -> 13.4 us
  starting transfers between devices: 23.8 us -> 25.7 us
  Pallas kernels: 14.6 us -> 15.4 us
    ppermute x11 -> x13, waiting for transfers between devices: 9.86 us -> 7.25 us  [swapped(): return lax.ppermute(block, axis, route)]
    ppermute x11 -> x13, starting transfers between devices: 10.3 us -> 12.1 us  [swapped(): return lax.ppermute(block, axis, route)]
    pallas_call x1 -> x2, Pallas kernels: 5.93 us -> 6.95 us  [hold(): pl.pallas_call(lambda *refs: hold_kernel(parts, *refs), out_shape=pltpu.V...]
  transfers between devices with their start and end apart: 19 -> 21, of which waited for: 11 -> 10; matrix products, arithmetic and copies ran while one was open for 0% -> 0% of each run, Pallas kernels for 13% -> 15%
where the time goes in v8:
time: 55.4 us; the launch traced here: 55.2 us
  starting transfers between devices  25.7 us (46%)
  Pallas kernels  15.4 us (28%)
  waiting for transfers between devices  13.4 us (24%)
  between operations  0.75 us (1%)
    ppermute x8, starting transfers between devices, from_behind(): return lax.ppermute(block, ('section', 'tensor'), route)  13.5 us
    ppermute x13, starting transfers between devices, swapped(): return lax.ppermute(block, axis, route)  12.1 us
    ppermute x13, waiting for transfers between devices, swapped(): return lax.ppermute(block, axis, route)  7.25 us
    pallas_call x2, Pallas kernels, hold(): pl.pallas_call(lambda *refs: hold_kernel(parts, *refs), out_shape=pltpu.V...  6.95 us
    ppermute x8, waiting for transfers between devices, from_behind(): return lax.ppermute(block, ('section', 'tensor'), route)  6.16 us
    pallas_call x2, Pallas kernels, attend(): pl.pallas_call(lambda *refs: attend_kernel(dims, turns, tick, *refs), out...  3.52 us
    pallas_call x1, Pallas kernels, pack(): pl.pallas_call(lambda *refs: pack_kernel(dims, *refs), out_shape=out_shap...  1.62 us
    pallas_call x1, Pallas kernels, first_sums(): pl.pallas_call(lambda *refs: first_kernel(tensors, *refs), out_shape=shap...  1.31 us
  transfers between devices with their start and end apart: 21, of which 10 were waited for; matrix products, arithmetic and copies ran while one was open for 0% of the time, Pallas kernels for 15%

profile of v8, /device:TPU:0, one launch (start us, length us, event | category | flops | bytes accessed | tf_op | source)
XLA Modules:
  0.0 55.2 jit_solution(18121566222810410596)
XLA Ops:
  0.6 1.6 %shard_map.113 = (bf16[24,16,128]{2,1,0:T(8,128)(2,1)S(1)}, bf16[24,16,128]{2,1,0:T(8,128)(2,1)S(1)}, bf16[24,16,128]{2,1,0:T(8,128)(2,1)S(1)}, bf16[24,16,128]{...) custom-call(s32[2,4]{1,0:T(2,128)} %refs_0_.1, ...), custom_call_target="tpu_custom_call" | custom-call | bytes 819200 | tf_op jit(solution)/shard_map/pallas_call | solution.py:124
  2.3 3.1 %collective-permute-start = (bf16[24,16,128]{2,1,0:T(8,128)(2,1)S(1)}, bf16[24,16,128]{2,1,0:T(8,128)(2,1)S(1)}, u32[]{:S(2)}, u32[]{:S(2)}) collective-permute-start(bf16[24,16,128]{2,1,0:T(8,128)(2,1)S(1)} %get-tuple-element.17), channel_id=1, source_target_pairs={{0,4},{4,0},{8,12},{12,8},{1,5},{5,1},{9,13},{13,9},{2,6},{6,2},{1... | collective-permute-start | bytes 294920 | tf_op jit(solution)/shard_map/ppermute | solution.py:31
  5.4 2.6 %collective-permute-start.1 = (bf16[24,16,128]{2,1,0:T(8,128)(2,1)S(1)}, bf16[24,16,128]{2,1,0:T(8,128)(2,1)S(1)}, u32[]{:S(2)}, u32[]{:S(2)}) collective-permute-start(bf16[24,16,128]{2,1,0:T(8,128)(2,1)S(1)} %get-tuple-element.18), channel_id=1, source_target_pairs={{0,8},{4,12},{8,0},{12,4},{1,9},{5,13},{9,1},{13,5},{2,10},{6,14},... | collective-permute-start | bytes 294920 | tf_op jit(solution)/shard_map/ppermute | solution.py:31
  7.9 0.0 collective-permute-start.2
  7.9 1.7 %collective-permute-start.3 = (f32[1,4,128]{2,1,0:T(4,128)S(1)}, f32[1,4,128]{2,1,0:T(4,128)S(1)}, u32[]{:S(2)}, u32[]{:S(2)}) collective-permute-start(f32[1,4,128]{2,1,0:T(4,128)S(1)} %bitcast.19), channel_id=1, source_target_pairs={{0,2},{1,3},{2,0},{3,1},{4,6},{5,7},{6,4},{7,5},{8,10},{9,11},{10,... | collective-permute-start | bytes 6152 | tf_op jit(solution)/shard_map/ppermute | solution.py:31
  9.7 3.5 %shard_map.114.refs_2_.refs_7_.refs_9_ = bf16[2048,2048]{1,0:T(8,128)(2,1)S(1)} custom-call(bf16[24,16,128]{2,1,0:T(8,128)(2,1)S(1)} %get-tuple-element.16.refs_0_.refs_1_.refs_5_, bf16[2048,2048]{1,0:T(8,128)(2,1)} %bitcast.22), custom_call_target="tpu_custom_call" | custom-call | bytes 8388608 | tf_op jit(solution)/shard_map/pallas_call | solution.py:171
  13.2 0.0 collective-permute-done.3.refs_1_
  13.2 0.1 collective-permute-start.4
  13.3 3.5 %shard_map.117.refs_4_.refs_5_ = bf16[2048,2048]{1,0:T(8,128)(2,1)S(1)} custom-call(f32[2,4,128]{2,1,0:T(4,128)S(1)} %bitcast.15, bf16[2048,2048]{1,0:T(8,128)(2,1)} %bitcast.21), custom_call_target="tpu_custom_call" | custom-call | bytes 8388608 | tf_op jit(solution)/shard_map/pallas_call | solution.py:171
  16.7 0.0 collective-permute-done.4.refs_6_.refs_5_.refs_9_
  16.8 0.0 collective-permute-done.refs_2_.refs_1_.refs_6_
  16.8 0.0 collective-permute-done.1.refs_3_.refs_2_.refs_7_
  16.8 0.0 collective-permute-done.2.refs_4_.refs_3_.refs_8_
  16.8 0.6 %collective-permute-start.8 = (bf16[4,8,16,128]{3,2,1,0:T(8,128)(2,1)S(1)}, bf16[4,8,16,128]{3,2,1,0:T(8,128)(2,1)S(1)}, u32[]{:S(2)}, u32[]{:S(2)}) collective-permute-start(bf16[4,8,16,128]{3,2,1,0:T(8,128)(2,1)S(1)} %shard_map.118.refs_0_), channel_id=1, source_target_pairs={{0,2},{1,3},{2,0},{3,1},{4,6},{5,7},{6,4},{7,5},{8,10},{9,11},{10,... | collective-permute-start | bytes 393224 | tf_op jit(solution)/shard_map/ppermute | solution.py:31
  17.4 1.3 %shard_map.116.refs_0_ = bf16[4,2048]{1,0:T(4,128)(2,1)S(1)} custom-call(bf16[4,2048]{1,0:T(4,128)(2,1)S(1)} %get-tuple-element.15.refs_0_.refs_4_, bf16[24,16,128]{2,1,0:T(8,128)(2,1)S(1)} %get-tuple-element.16.refs_0_.refs_1_.refs_5_, bf16[24,16,128]{2,1,0:T(8,128)(2,1)S(1)} %collective-permute-done.refs_2_.refs_1_.refs_6_, ...), custom_call_target="tpu_custom_call" | custom-call | flops 100663296 | bytes 8388608 | tf_op jit(solution)/shard_map/pallas_call | solution.py:244
  18.7 1.4 %collective-permute-start.7 = (bf16[4,2048]{1,0:T(4,128)(2,1)S(1)}, bf16[4,2048]{1,0:T(4,128)(2,1)S(1)}, u32[]{:S(2)}, u32[]{:S(2)}) collective-permute-start(bf16[4,2048]{1,0:T(4,128)(2,1)S(1)} %shard_map.116.refs_0_), channel_id=1, source_target_pairs={{0,3},{1,2},{2,1},{3,0},{4,7},{5,6},{6,5},{7,4},{8,11},{9,10},{10,... | collective-permute-start | bytes 49160 | tf_op jit(solution)/shard_map/ppermute | solution.py:31
  20.0 0.3 collective-permute-start.6
  20.3 2.4 %collective-permute-done.7.refs_3_ = bf16[4,2048]{1,0:T(4,128)(2,1)S(1)} collective-permute-done((bf16[4,2048]{1,0:T(4,128)(2,1)S(1)}, bf16[4,2048]{1,0:T(4,128)(2,1)S(1)}, u32[]{:S(2)}, u32[]{:S(2)}) %collective-permute-start.7) | collective-permute-done | bytes 16416 | tf_op jit(solution)/shard_map/ppermute | solution.py:31
  22.7 1.1 %collective-permute-done.6.refs_2_ = bf16[4,2048]{1,0:T(4,128)(2,1)S(1)} collective-permute-done((bf16[4,2048]{1,0:T(4,128)(2,1)S(1)}, bf16[4,2048]{1,0:T(4,128)(2,1)S(1)}, u32[]{:S(2)}, u32[]{:S(2)}) %collective-permute-start.6) | collective-permute-done | bytes 16416 | tf_op jit(solution)/shard_map/ppermute | solution.py:31
  23.8 0.0 collective-permute-done.8.refs_1_
  23.8 0.1 collective-permute-start.9
  23.9 0.5 collective-permute-start.5
  24.4 1.0 %collective-permute-done.5.refs_1_ = bf16[4,2048]{1,0:T(4,128)(2,1)S(1)} collective-permute-done((bf16[4,2048]{1,0:T(4,128)(2,1)S(1)}, bf16[4,2048]{1,0:T(4,128)(2,1)S(1)}, u32[]{:S(2)}, u32[]{:S(2)}) %collective-permute-start.5) | collective-permute-done | bytes 16416 | tf_op jit(solution)/shard_map/ppermute | solution.py:31
  25.4 0.0 collective-permute-done.9.refs_7_
  25.4 1.7 %shard_map.120 = (bf16[4,2048]{1,0:T(4,128)(2,1)S(1)}, bf16[4,4096]{1,0:T(4,128)(2,1)S(1)}) custom-call(bf16[4,2048]{1,0:T(4,128)(2,1)S(1)} %shard_map.116.refs_0_, bf16[4,2048]{1,0:T(4,128)(2,1)S(1)} %collective-permute-done.5.refs_1_, bf16[4,2048]{1,0:T(4,128)(2,1)S(1)} %collective-permute-done.6.refs_2_, ...), custom_call_target="tpu_custom_call" | custom-call | flops 33554432 | bytes 8388608 | tf_op jit(solution)/shard_map/pallas_call | solution.py:390
  27.1 1.5 %collective-permute-start.10 = (bf16[4,4096]{1,0:T(4,128)(2,1)S(1)}, bf16[4,4096]{1,0:T(4,128)(2,1)S(1)}, u32[]{:S(2)}, u32[]{:S(2)}) collective-permute-start(bf16[4,4096]{1,0:T(4,128)(2,1)S(1)} %get-tuple-element.21), channel_id=1, source_target_pairs={{0,16},{4,20},{8,24},{12,28},{16,0},{20,4},{24,8},{28,12},{1,17},{... | collective-permute-start | bytes 98312 | tf_op jit(solution)/shard_map/ppermute | solution.py:41
  28.6 3.6 %collective-permute-start.13 = (bf16[4,2048]{1,0:T(4,128)(2,1)S(1)}, bf16[4,2048]{1,0:T(4,128)(2,1)S(1)}, u32[]{:S(2)}, u32[]{:S(2)}) collective-permute-start(bf16[4,2048]{1,0:T(4,128)(2,1)S(1)} %get-tuple-element.22), channel_id=1, source_target_pairs={{12,16},{8,20},{4,24},{0,28},{28,0},{24,4},{20,8},{16,12},{13,17},... | collective-permute-start | bytes 49160 | tf_op jit(solution)/shard_map/ppermute | solution.py:41
  32.2 0.0 collective-permute-start.12
  32.2 1.7 %collective-permute-start.11 = (bf16[4,2048]{1,0:T(4,128)(2,1)S(1)}, bf16[4,2048]{1,0:T(4,128)(2,1)S(1)}, u32[]{:S(2)}, u32[]{:S(2)}) collective-permute-start(bf16[4,2048]{1,0:T(4,128)(2,1)S(1)} %get-tuple-element.22), channel_id=1, source_target_pairs={{4,16},{0,20},{12,24},{8,28},{20,0},{16,4},{28,8},{24,12},{5,17},{... | collective-permute-start | bytes 49160 | tf_op jit(solution)/shard_map/ppermute | solution.py:41
  33.9 1.2 %collective-permute-done.13.refs_3_ = bf16[4,2048]{1,0:T(4,128)(2,1)S(1)} collective-permute-done((bf16[4,2048]{1,0:T(4,128)(2,1)S(1)}, bf16[4,2048]{1,0:T(4,128)(2,1)S(1)}, u32[]{:S(2)}, u32[]{:S(2)}) %collective-permute-start.13) | collective-permute-done | bytes 16416 | tf_op jit(solution)/shard_map/ppermute | solution.py:41
  35.0 2.7 %collective-permute-done.12.refs_2_ = bf16[4,2048]{1,0:T(4,128)(2,1)S(1)} collective-permute-done((bf16[4,2048]{1,0:T(4,128)(2,1)S(1)}, bf16[4,2048]{1,0:T(4,128)(2,1)S(1)}, u32[]{:S(2)}, u32[]{:S(2)}) %collective-permute-start.12) | collective-permute-done | bytes 16416 | tf_op jit(solution)/shard_map/ppermute | solution.py:41
  37.7 0.0 collective-permute-done.11.refs_1_
  37.7 0.0 collective-permute-done.10.refs_0_
  37.7 1.3 %shard_map.121 = (bf16[4,6272]{1,0:T(4,128)(2,1)S(1)}, bf16[4,2048]{1,0:T(4,128)(2,1)S(1)}) custom-call(bf16[4,4096]{1,0:T(4,128)(2,1)S(1)} %collective-permute-done.10.refs_0_, bf16[4,2048]{1,0:T(4,128)(2,1)S(1)} %collective-permute-done.11.refs_1_, bf16[4,2048]{1,0:T(4,128)(2,1)S(1)} %collective-permute-done.12.refs_2_, ...), custom_call_target="tpu_custom_call" | custom-call | flops 100663296 | bytes 8388608 | tf_op jit(solution)/shard_map/pallas_call | solution.py:288
  39.0 0.6 %collective-permute-start.15 = (bf16[4,6272]{1,0:T(4,128)(2,1)S(1)}, bf16[4,6272]{1,0:T(4,128)(2,1)S(1)}, u32[]{:S(2)}, u32[]{:S(2)}) collective-permute-start(bf16[4,6272]{1,0:T(4,128)(2,1)S(1)} %get-tuple-element.24.refs_0_), channel_id=1, source_target_pairs={{0,2},{1,3},{2,0},{3,1},{4,6},{5,7},{6,4},{7,5},{8,10},{9,11},{10,... | collective-permute-start | bytes 150536 | tf_op jit(solution)/shard_map/ppermute | solution.py:31
  39.6 1.3 %collective-permute-start.14 = (bf16[4,6272]{1,0:T(4,128)(2,1)S(1)}, bf16[4,6272]{1,0:T(4,128)(2,1)S(1)}, u32[]{:S(2)}, u32[]{:S(2)}) collective-permute-start(bf16[4,6272]{1,0:T(4,128)(2,1)S(1)} %get-tuple-element.24.refs_0_), channel_id=1, source_target_pairs={{0,1},{1,0},{2,3},{3,2},{4,5},{5,4},{6,7},{7,6},{8,9},{9,8},{10,11... | collective-permute-start | bytes 150536 | tf_op jit(solution)/shard_map/ppermute | solution.py:31
  40.9 1.7 %collective-permute-done.16.refs_3_ = bf16[4,6272]{1,0:T(4,128)(2,1)S(1)} collective-permute-done((bf16[4,6272]{1,0:T(4,128)(2,1)S(1)}, bf16[4,6272]{1,0:T(4,128)(2,1)S(1)}, u32[]{:S(2)}, u32[]{:S(2)}) %collective-permute-start.16) | collective-permute-done | bytes 50208 | tf_op jit(solution)/shard_map/ppermute | solution.py:31
  42.5 1.1 %collective-permute-done.15.refs_2_ = bf16[4,6272]{1,0:T(4,128)(2,1)S(1)} collective-permute-done((bf16[4,6272]{1,0:T(4,128)(2,1)S(1)}, bf16[4,6272]{1,0:T(4,128)(2,1)S(1)}, u32[]{:S(2)}, u32[]{:S(2)}) %collective-permute-start.15) | collective-permute-done | bytes 50208 | tf_op jit(solution)/shard_map/ppermute | solution.py:31
  43.6 0.0 collective-permute-done.14.refs_1_
  43.6 1.9 %shard_map.122 = (bf16[4,2048]{1,0:T(4,128)(2,1)S(1)}, bf16[4,4096]{1,0:T(4,128)(2,1)S(1)}) custom-call(bf16[4,6272]{1,0:T(4,128)(2,1)S(1)} %get-tuple-element.24.refs_0_, bf16[4,6272]{1,0:T(4,128)(2,1)S(1)} %collective-permute-done.14.refs_1_, bf16[4,6272]{1,0:T(4,128)(2,1)S(1)} %collective-permute-done.15.refs_2_, ...), custom_call_target="tpu_custom_call" | custom-call | flops 33554432 | bytes 8388608 | tf_op jit(solution)/shard_map/pallas_call | solution.py:390
  45.5 1.5 %collective-permute-start.17 = (bf16[4,4096]{1,0:T(4,128)(2,1)S(1)}, bf16[4,4096]{1,0:T(4,128)(2,1)S(1)}, u32[]{:S(2)}, u32[]{:S(2)}) collective-permute-start(bf16[4,4096]{1,0:T(4,128)(2,1)S(1)} %get-tuple-element.26), channel_id=1, source_target_pairs={{0,16},{4,20},{8,24},{12,28},{16,0},{20,4},{24,8},{28,12},{1,17},{... | collective-permute-start | bytes 98312 | tf_op jit(solution)/shard_map/ppermute | solution.py:41
  47.0 1.4 %collective-permute-start.20 = (bf16[4,2048]{1,0:T(4,128)(2,1)S(1)}, bf16[4,2048]{1,0:T(4,128)(2,1)S(1)}, u32[]{:S(2)}, u32[]{:S(2)}) collective-permute-start(bf16[4,2048]{1,0:T(4,128)(2,1)S(1)} %get-tuple-element.27), channel_id=1, source_target_pairs={{12,16},{8,20},{4,24},{0,28},{28,0},{24,4},{20,8},{16,12},{13,17},... | collective-permute-start | bytes 49160 | tf_op jit(solution)/shard_map/ppermute | solution.py:41
  48.4 1.5 %collective-permute-start.19 = (bf16[4,2048]{1,0:T(4,128)(2,1)S(1)}, bf16[4,2048]{1,0:T(4,128)(2,1)S(1)}, u32[]{:S(2)}, u32[]{:S(2)}) collective-permute-start(bf16[4,2048]{1,0:T(4,128)(2,1)S(1)} %get-tuple-element.27), channel_id=1, source_target_pairs={{8,16},{12,20},{0,24},{4,28},{24,0},{28,4},{16,8},{20,12},{9,17},{... | collective-permute-start | bytes 49160 | tf_op jit(solution)/shard_map/ppermute | solution.py:41
  49.9 2.3 %collective-permute-start.18 = (bf16[4,2048]{1,0:T(4,128)(2,1)S(1)}, bf16[4,2048]{1,0:T(4,128)(2,1)S(1)}, u32[]{:S(2)}, u32[]{:S(2)}) collective-permute-start(bf16[4,2048]{1,0:T(4,128)(2,1)S(1)} %get-tuple-element.27), channel_id=1, source_target_pairs={{4,16},{0,20},{12,24},{8,28},{20,0},{16,4},{28,8},{24,12},{5,17},{... | collective-permute-start | bytes 49160 | tf_op jit(solution)/shard_map/ppermute | solution.py:41
  52.2 1.2 %collective-permute-done.20.refs_3_ = bf16[4,2048]{1,0:T(4,128)(2,1)S(1)} collective-permute-done((bf16[4,2048]{1,0:T(4,128)(2,1)S(1)}, bf16[4,2048]{1,0:T(4,128)(2,1)S(1)}, u32[]{:S(2)}, u32[]{:S(2)}) %collective-permute-start.20) | collective-permute-done | bytes 16416 | tf_op jit(solution)/shard_map/ppermute | solution.py:41
  53.4 0.7 %collective-permute-done.19.refs_2_ = bf16[4,2048]{1,0:T(4,128)(2,1)S(1)} collective-permute-done((bf16[4,2048]{1,0:T(4,128)(2,1)S(1)}, bf16[4,2048]{1,0:T(4,128)(2,1)S(1)}, u32[]{:S(2)}, u32[]{:S(2)}) %collective-permute-start.19) | collective-permute-done | bytes 16416 | tf_op jit(solution)/shard_map/ppermute | solution.py:41
  54.1 0.4 collective-permute-done.18.refs_1_
  54.6 0.6 %shard_map.123 = (bf16[1,4,2048]{2,1,0:T(4,128)(2,1)}, bf16[1,4,2048]{2,1,0:T(4,128)(2,1)}) custom-call(bf16[4,4096]{1,0:T(4,128)(2,1)S(1)} %collective-permute-done.17.refs_0_, bf16[4,2048]{1,0:T(4,128)(2,1)S(1)} %collective-permute-done.18.refs_1_, bf16[4,2048]{1,0:T(4,128)(2,1)S(1)} %collective-permute-done.19.refs_2_, ...), custom_call_target="tpu_custom_call" | custom-call | tf_op jit(solution)/shard_map/pallas_call | solution.py:306
  (5 shorter events, 0.0 us)
Async XLA Ops:
  2.3 14.5 %collective-permute-start = (bf16[24,16,128]{2,1,0:T(8,128)(2,1)S(1)}, bf16[24,16,128]{2,1,0:T(8,128)(2,1)S(1)}, u32[]{:S(2)}, u32[]{:S(2)}) collective-permute-start(bf16[24,16,128]{2,1,0:T(8,128)(2,1)S(1)} %get-tuple-element.17), channel_id=1, source_target_pairs={{0,4},{4,0},{8,12},{12,8},{1,5},{5,1},{9,13},{13,9},{2,6},{6,2},{1... | collective-permute-start | bytes 294920 | tf_op jit(solution)/shard_map/ppermute | solution.py:31
  5.4 11.4 %collective-permute-start.1 = (bf16[24,16,128]{2,1,0:T(8,128)(2,1)S(1)}, bf16[24,16,128]{2,1,0:T(8,128)(2,1)S(1)}, u32[]{:S(2)}, u32[]{:S(2)}) collective-permute-start(bf16[24,16,128]{2,1,0:T(8,128)(2,1)S(1)} %get-tuple-element.18), channel_id=1, source_target_pairs={{0,8},{4,12},{8,0},{12,4},{1,9},{5,13},{9,1},{13,5},{2,10},{6,14},... | collective-permute-start | bytes 294920 | tf_op jit(solution)/shard_map/ppermute | solution.py:31
  7.9 8.8 %collective-permute-start.2 = (bf16[24,16,128]{2,1,0:T(8,128)(2,1)S(1)}, bf16[24,16,128]{2,1,0:T(8,128)(2,1)S(1)}, u32[]{:S(2)}, u32[]{:S(2)}) collective-permute-start(bf16[24,16,128]{2,1,0:T(8,128)(2,1)S(1)} %get-tuple-element.19), channel_id=1, source_target_pairs={{0,12},{4,8},{8,4},{12,0},{1,13},{5,9},{9,5},{13,1},{2,14},{6,10},... | collective-permute-start | bytes 294920 | tf_op jit(solution)/shard_map/ppermute | solution.py:31
  7.9 5.2 %collective-permute-start.3 = (f32[1,4,128]{2,1,0:T(4,128)S(1)}, f32[1,4,128]{2,1,0:T(4,128)S(1)}, u32[]{:S(2)}, u32[]{:S(2)}) collective-permute-start(f32[1,4,128]{2,1,0:T(4,128)S(1)} %bitcast.19), channel_id=1, source_target_pairs={{0,2},{1,3},{2,0},{3,1},{4,6},{5,7},{6,4},{7,5},{8,10},{9,11},{10,... | collective-permute-start | bytes 6152 | tf_op jit(solution)/shard_map/ppermute | solution.py:31
  13.2 3.6 %collective-permute-start.4 = (f32[2,4,128]{2,1,0:T(4,128)S(1)}, f32[2,4,128]{2,1,0:T(4,128)S(1)}, u32[]{:S(2)}, u32[]{:S(2)}) collective-permute-start(f32[2,4,128]{2,1,0:T(4,128)S(1)} %bitcast.14), channel_id=1, source_target_pairs={{0,1},{1,0},{2,3},{3,2},{4,5},{5,4},{6,7},{7,6},{8,9},{9,8},{10,11... | collective-permute-start | bytes 12296 | tf_op jit(solution)/shard_map/ppermute | solution.py:31
  16.8 7.0 %collective-permute-start.8 = (bf16[4,8,16,128]{3,2,1,0:T(8,128)(2,1)S(1)}, bf16[4,8,16,128]{3,2,1,0:T(8,128)(2,1)S(1)}, u32[]{:S(2)}, u32[]{:S(2)}) collective-permute-start(bf16[4,8,16,128]{3,2,1,0:T(8,128)(2,1)S(1)} %shard_map.118.refs_0_), channel_id=1, source_target_pairs={{0,2},{1,3},{2,0},{3,1},{4,6},{5,7},{6,4},{7,5},{8,10},{9,11},{10,... | collective-permute-start | bytes 393224 | tf_op jit(solution)/shard_map/ppermute | solution.py:31
  18.7 4.0 %collective-permute-start.7 = (bf16[4,2048]{1,0:T(4,128)(2,1)S(1)}, bf16[4,2048]{1,0:T(4,128)(2,1)S(1)}, u32[]{:S(2)}, u32[]{:S(2)}) collective-permute-start(bf16[4,2048]{1,0:T(4,128)(2,1)S(1)} %shard_map.116.refs_0_), channel_id=1, source_target_pairs={{0,3},{1,2},{2,1},{3,0},{4,7},{5,6},{6,5},{7,4},{8,11},{9,10},{10,... | collective-permute-start | bytes 49160 | tf_op jit(solution)/shard_map/ppermute | solution.py:31
  20.0 3.7 %collective-permute-start.6 = (bf16[4,2048]{1,0:T(4,128)(2,1)S(1)}, bf16[4,2048]{1,0:T(4,128)(2,1)S(1)}, u32[]{:S(2)}, u32[]{:S(2)}) collective-permute-start(bf16[4,2048]{1,0:T(4,128)(2,1)S(1)} %shard_map.116.refs_0_), channel_id=1, source_target_pairs={{0,2},{1,3},{2,0},{3,1},{4,6},{5,7},{6,4},{7,5},{8,10},{9,11},{10,... | collective-permute-start | bytes 49160 | tf_op jit(solution)/shard_map/ppermute | solution.py:31
  23.8 1.6 %collective-permute-start.9 = (bf16[8,8,16,128]{3,2,1,0:T(8,128)(2,1)S(1)}, bf16[8,8,16,128]{3,2,1,0:T(8,128)(2,1)S(1)}, u32[]{:S(2)}, u32[]{:S(2)}) collective-permute-start(bf16[8,8,16,128]{3,2,1,0:T(8,128)(2,1)S(1)} %bitcast.11), channel_id=1, source_target_pairs={{0,1},{1,0},{2,3},{3,2},{4,5},{5,4},{6,7},{7,6},{8,9},{9,8},{10,11... | collective-permute-start | bytes 786440 | tf_op jit(solution)/shard_map/ppermute | solution.py:31
  23.9 1.5 %collective-permute-start.5 = (bf16[4,2048]{1,0:T(4,128)(2,1)S(1)}, bf16[4,2048]{1,0:T(4,128)(2,1)S(1)}, u32[]{:S(2)}, u32[]{:S(2)}) collective-permute-start(bf16[4,2048]{1,0:T(4,128)(2,1)S(1)} %shard_map.116.refs_0_), channel_id=1, source_target_pairs={{0,1},{1,0},{2,3},{3,2},{4,5},{5,4},{6,7},{7,6},{8,9},{9,8},{10,11... | collective-permute-start | bytes 49160 | tf_op jit(solution)/shard_map/ppermute | solution.py:31
  27.1 10.6 %collective-permute-start.10 = (bf16[4,4096]{1,0:T(4,128)(2,1)S(1)}, bf16[4,4096]{1,0:T(4,128)(2,1)S(1)}, u32[]{:S(2)}, u32[]{:S(2)}) collective-permute-start(bf16[4,4096]{1,0:T(4,128)(2,1)S(1)} %get-tuple-element.21), channel_id=1, source_target_pairs={{0,16},{4,20},{8,24},{12,28},{16,0},{20,4},{24,8},{28,12},{1,17},{... | collective-permute-start | bytes 98312 | tf_op jit(solution)/shard_map/ppermute | solution.py:41
  28.6 6.4 %collective-permute-start.13 = (bf16[4,2048]{1,0:T(4,128)(2,1)S(1)}, bf16[4,2048]{1,0:T(4,128)(2,1)S(1)}, u32[]{:S(2)}, u32[]{:S(2)}) collective-permute-start(bf16[4,2048]{1,0:T(4,128)(2,1)S(1)} %get-tuple-element.22), channel_id=1, source_target_pairs={{12,16},{8,20},{4,24},{0,28},{28,0},{24,4},{20,8},{16,12},{13,17},... | collective-permute-start | bytes 49160 | tf_op jit(solution)/shard_map/ppermute | solution.py:41
  32.2 5.5 %collective-permute-start.12 = (bf16[4,2048]{1,0:T(4,128)(2,1)S(1)}, bf16[4,2048]{1,0:T(4,128)(2,1)S(1)}, u32[]{:S(2)}, u32[]{:S(2)}) collective-permute-start(bf16[4,2048]{1,0:T(4,128)(2,1)S(1)} %get-tuple-element.22), channel_id=1, source_target_pairs={{8,16},{12,20},{0,24},{4,28},{24,0},{28,4},{16,8},{20,12},{9,17},{... | collective-permute-start | bytes 49160 | tf_op jit(solution)/shard_map/ppermute | solution.py:41
  32.2 5.5 %collective-permute-start.11 = (bf16[4,2048]{1,0:T(4,128)(2,1)S(1)}, bf16[4,2048]{1,0:T(4,128)(2,1)S(1)}, u32[]{:S(2)}, u32[]{:S(2)}) collective-permute-start(bf16[4,2048]{1,0:T(4,128)(2,1)S(1)} %get-tuple-element.22), channel_id=1, source_target_pairs={{4,16},{0,20},{12,24},{8,28},{20,0},{16,4},{28,8},{24,12},{5,17},{... | collective-permute-start | bytes 49160 | tf_op jit(solution)/shard_map/ppermute | solution.py:41
  39.0 3.5 %collective-permute-start.16 = (bf16[4,6272]{1,0:T(4,128)(2,1)S(1)}, bf16[4,6272]{1,0:T(4,128)(2,1)S(1)}, u32[]{:S(2)}, u32[]{:S(2)}) collective-permute-start(bf16[4,6272]{1,0:T(4,128)(2,1)S(1)} %get-tuple-element.24.refs_0_), channel_id=1, source_target_pairs={{0,3},{1,2},{2,1},{3,0},{4,7},{5,6},{6,5},{7,4},{8,11},{9,10},{10,... | collective-permute-start | bytes 150536 | tf_op jit(solution)/shard_map/ppermute | solution.py:31
  39.0 4.6 %collective-permute-start.15 = (bf16[4,6272]{1,0:T(4,128)(2,1)S(1)}, bf16[4,6272]{1,0:T(4,128)(2,1)S(1)}, u32[]{:S(2)}, u32[]{:S(2)}) collective-permute-start(bf16[4,6272]{1,0:T(4,128)(2,1)S(1)} %get-tuple-element.24.refs_0_), channel_id=1, source_target_pairs={{0,2},{1,3},{2,0},{3,1},{4,6},{5,7},{6,4},{7,5},{8,10},{9,11},{10,... | collective-permute-start | bytes 150536 | tf_op jit(solution)/shard_map/ppermute | solution.py:31
  39.6 4.1 %collective-permute-start.14 = (bf16[4,6272]{1,0:T(4,128)(2,1)S(1)}, bf16[4,6272]{1,0:T(4,128)(2,1)S(1)}, u32[]{:S(2)}, u32[]{:S(2)}) collective-permute-start(bf16[4,6272]{1,0:T(4,128)(2,1)S(1)} %get-tuple-element.24.refs_0_), channel_id=1, source_target_pairs={{0,1},{1,0},{2,3},{3,2},{4,5},{5,4},{6,7},{7,6},{8,9},{9,8},{10,11... | collective-permute-start | bytes 150536 | tf_op jit(solution)/shard_map/ppermute | solution.py:31
  45.5 9.1 %collective-permute-start.17 = (bf16[4,4096]{1,0:T(4,128)(2,1)S(1)}, bf16[4,4096]{1,0:T(4,128)(2,1)S(1)}, u32[]{:S(2)}, u32[]{:S(2)}) collective-permute-start(bf16[4,4096]{1,0:T(4,128)(2,1)S(1)} %get-tuple-element.26), channel_id=1, source_target_pairs={{0,16},{4,20},{8,24},{12,28},{16,0},{20,4},{24,8},{28,12},{1,17},{... | collective-permute-start | bytes 98312 | tf_op jit(solution)/shard_map/ppermute | solution.py:41
  47.0 6.4 %collective-permute-start.20 = (bf16[4,2048]{1,0:T(4,128)(2,1)S(1)}, bf16[4,2048]{1,0:T(4,128)(2,1)S(1)}, u32[]{:S(2)}, u32[]{:S(2)}) collective-permute-start(bf16[4,2048]{1,0:T(4,128)(2,1)S(1)} %get-tuple-element.27), channel_id=1, source_target_pairs={{12,16},{8,20},{4,24},{0,28},{28,0},{24,4},{20,8},{16,12},{13,17},... | collective-permute-start | bytes 49160 | tf_op jit(solution)/shard_map/ppermute | solution.py:41
  48.4 5.7 %collective-permute-start.19 = (bf16[4,2048]{1,0:T(4,128)(2,1)S(1)}, bf16[4,2048]{1,0:T(4,128)(2,1)S(1)}, u32[]{:S(2)}, u32[]{:S(2)}) collective-permute-start(bf16[4,2048]{1,0:T(4,128)(2,1)S(1)} %get-tuple-element.27), channel_id=1, source_target_pairs={{8,16},{12,20},{0,24},{4,28},{24,0},{28,4},{16,8},{20,12},{9,17},{... | collective-permute-start | bytes 49160 | tf_op jit(solution)/shard_map/ppermute | solution.py:41
  49.9 4.6 %collective-permute-start.18 = (bf16[4,2048]{1,0:T(4,128)(2,1)S(1)}, bf16[4,2048]{1,0:T(4,128)(2,1)S(1)}, u32[]{:S(2)}, u32[]{:S(2)}) collective-permute-start(bf16[4,2048]{1,0:T(4,128)(2,1)S(1)} %get-tuple-element.27), channel_id=1, source_target_pairs={{4,16},{0,20},{12,24},{8,28},{20,0},{16,4},{28,8},{24,12},{5,17},{... | collective-permute-start | bytes 49160 | tf_op jit(solution)/shard_map/ppermute | solution.py:41

commit v9 on v7

--- a/solution.py
+++ b/solution.py
@@ -6,6 +6,7 @@
 from jax.sharding import PartitionSpec as P
 
 HD = 128
+NEAR = 2
 BF = jnp.bfloat16
 F32 = jnp.float32
 VMEM = pl.BlockSpec(memory_space=pltpu.VMEM)
@@ -55,8 +56,9 @@
 def pack_kernel(dims, *refs):
     sections, tensors, rows, heads_dev, group, kv_dev = dims
     sources, refs = refs[:8], refs[8:]
-    packs, (h_ref, next_ref, lengths_ref) = refs[:tensors], refs[tensors : tensors + 3]
-    ids, lengths, gains, biases, keys, values, sems = refs[tensors + 3 :]
+    packs, (far_ref, h_ref, next_ref, lengths_ref) = refs[:tensors], refs[tensors : tensors + 4]
+    ids, lengths, gains, biases, keys, values, sems = refs[tensors + 4 :]
+    held = 2 * sections * kv_dev
     targets = (ids, lengths, keys, values, gains, biases, h_ref, next_ref)
     copies = [
         pltpu.make_async_copy(source, target, sems.at[i])
@@ -93,7 +95,7 @@
         for which, cache in enumerate((keys, values)):
             for b in range(sections):
                 for g in range(kv_dev):
-                    to = sections * blocks + (which * sections + b) * kv_dev + g
+                    to = (which * sections + b) * kv_dev + g
                     packs[d][to] = cache[b, start + g]
     copies[4].wait()
     gain_rows = jnp.dot(onehot, gains[...], preferred_element_type=F32)
@@ -106,8 +108,10 @@
             block = jnp.concatenate(
                 [both[:, (j * per + k) * lanes : (j * per + k + 1) * lanes] for k in range(per)], 0
             ).astype(BF)
-            for d in range(tensors):
-                packs[d][tick * blocks + j] = block
+            for d in range(tensors if tick == 0 else min(tensors, NEAR)):
+                packs[d][held + tick * blocks + j] = block
+            if tick > 0:
+                far_ref[(tick - 1) * blocks + j] = block
     copies[6].wait()
     copies[7].wait()
 
@@ -116,7 +120,11 @@
     sections, tensors, rows, heads_dev, group, kv_dev = dims
     pos = keys.shape[2]
     blocks = 2 * rows * gain.shape[1] // (pos * HD)
-    out_shape = [shape((sections * (blocks + 2 * kv_dev), pos, HD))] * tensors
+    held, later = 2 * sections * kv_dev, (sections - 1) * blocks
+    out_shape = [
+        shape((held + blocks + (later if d < NEAR else 0), pos, HD)) for d in range(tensors)
+    ]
+    out_shape += [shape((later, pos, HD))]
     out_shape += [shape(h.shape), shape(following.shape), shape((sections, HD), F32)]
     operands = (tenant, lengths, keys, values, gain, bias, h, following)
     return pl.pallas_call(
@@ -132,18 +140,18 @@
     )(*[in_hbm(x) for x in operands])
 
 
-def join_kernel(count, first, refs):
+def join_kernel(count, size, refs):
     out_ref = refs[-1]
     for i in range(count):
-        out_ref[i] = refs[i][first:]
-
-
-def join(pieces, first, after):
+        out_ref[i] = refs[i][:size]
+
+
+def join(pieces, size, after):
     count = len(pieces)
     dims = pieces[0].shape
     return pl.pallas_call(
-        lambda *refs: join_kernel(count, first, refs),
-        out_shape=shape((count, dims[0] - first) + dims[1:]),
+        lambda *refs: join_kernel(count, size, refs),
+        out_shape=shape((count, size) + dims[1:]),
         in_specs=[VMEM] * count + [pl.BlockSpec(memory_space=pl.ANY)] * len(after),
         out_specs=VMEM,
         compiler_params=PARAMS,
@@ -189,13 +197,13 @@
     return [high, middle, x - high - middle]
 
 
-def query_sums(first_block, length, h, pieces, w_ref, out_ref):
+def query_sums(first_blocks, length, h, pieces, w_ref, out_ref):
     rows, width = h.shape
     pos, lanes = pieces[0].shape[1:]
     per = pos // (2 * rows)
     cols = []
     for j in range(width // lanes // per):
-        block = tree_sum([piece[first_block + j] for piece in pieces])
+        block = tree_sum([piece[first + j] for first, piece in zip(first_blocks, pieces)])
         cols += [block[k * 2 * rows : (k + 1) * 2 * rows] for k in range(per)]
     affine = jnp.concatenate(cols, 1)
     total = jnp.sum(h, axis=-1, keepdims=True)
@@ -215,15 +223,15 @@
     out_ref[:, 3 * count :] = tail.astype(BF)
 
 
-def first_kernel(tensors, lengths_ref, h_ref, *refs):
+def first_kernel(tensors, held, lengths_ref, h_ref, *refs):
     pieces, (w_ref, out_ref) = refs[:tensors], refs[tensors:]
-    query_sums(0, lengths_ref[0:1], h_ref[...].astype(F32), pieces, w_ref, out_ref)
-
-
-def first_sums(lengths, h, pieces, w):
+    query_sums([held] * tensors, lengths_ref[0:1], h_ref[...].astype(F32), pieces, w_ref, out_ref)
+
+
+def first_sums(held, lengths, h, pieces, w):
     tensors = len(pieces)
     return pl.pallas_call(
-        lambda *refs: first_kernel(tensors, *refs),
+        lambda *refs: first_kernel(tensors, held, *refs),
         out_shape=shape((h.shape[0], 3 * w.shape[1] + HD)),
         in_specs=[VMEM] * (tensors + 3),
         out_specs=VMEM,
@@ -248,7 +256,7 @@
     return h, jnp.where(section == 0, came, carried)
 
 
-def later_kernel(count, tick, lengths_ref, *refs):
+def later_kernel(count, tick, held, lengths_ref, *refs):
     arrivals, next_ref = refs[:count], refs[count]
     pieces, (w_ref, out_ref, carry_ref) = refs[count + 1 : -3], refs[-3:]
     h, emitted = arrive(arrivals, next_ref, tick - 1)
@@ -260,14 +268,15 @@
         carry_ref[:, :width] = h.astype(BF)
         carry_ref[:, width:] = emitted.astype(BF)
     blocks = 2 * h.shape[0] * width // (pieces[0].shape[1] * HD)
-    query_sums(tick * blocks, lengths_ref[tick : tick + 1], h, pieces, w_ref, out_ref)
-
-
-def later_sums(tick, lengths, arrivals, following, pieces, w):
+    firsts = [held + tick * blocks if d < NEAR else (tick - 1) * blocks for d in range(len(pieces))]
+    query_sums(firsts, lengths_ref[tick : tick + 1], h, pieces, w_ref, out_ref)
+
+
+def later_sums(tick, held, lengths, arrivals, following, pieces, w):
     rows, width = following.shape[1:]
     parts = 1 if following.shape[0] == 2 else 2
     return pl.pallas_call(
-        lambda *refs: later_kernel(len(arrivals), tick, *refs),
+        lambda *refs: later_kernel(len(arrivals), tick, held, *refs),
         out_shape=[shape((rows, 3 * w.shape[1] + HD)), shape((rows, width * parts))],
         in_specs=[VMEM] * (len(arrivals) + len(pieces) + 3),
         out_specs=[VMEM] * 2,
@@ -332,7 +341,7 @@
     per_kv = span // HD // kv_dev
     keep = jnp.concatenate([jnp.concatenate(keep, 1)] * per_kv, 0)
 
-    sums = [0.0] * len(tiles(w_ref))
+    att = []
     for g in range(kv_dev):
         mine = jnp.concatenate(
             [query[:, h * HD : (h + 1) * HD] for h in range(g * per_kv, (g + 1) * per_kv)], 0
@@ -353,14 +362,12 @@
         probs = jnp.exp(scores - jnp.max(scores, axis=-1, keepdims=True))
         total = jnp.sum(probs, axis=-1, keepdims=True)
         got = jnp.dot(probs.astype(BF), values, preferred_element_type=F32) / total
-        att = jnp.concatenate([got[h * rows : (h + 1) * rows] for h in range(per_kv)], 1)
-        att = att.astype(BF)
-        depth = slice(g * per_kv * HD, (g + 1) * per_kv * HD)
-        for i, at in enumerate(tiles(w_ref)):
-            sums[i] += jnp.dot(att, w_ref[depth, at], preferred_element_type=F32)
-    for got, at in zip(sums, tiles(w_ref)):
-        out_ref[:, at] = got.astype(BF)
-        full_ref[:, at] = got.astype(BF)
+        att += [got[h * rows : (h + 1) * rows] for h in range(per_kv)]
+    att = jnp.concatenate(att, 1).astype(BF)
+    for at in tiles(w_ref):
+        got = jnp.dot(att, w_ref[:, at], preferred_element_type=F32).astype(BF)
+        out_ref[:, at] = got
+        full_ref[:, at] = got
     full_ref[:, width:] = carry_ref[...]
 
 
@@ -384,10 +391,9 @@
     heads_dev = wq.shape[2] // HD
     group = heads_dev * tensors // keys.shape[3]
     kv_dev = max(1, heads_dev // group)
-    pos = keys.shape[4]
     dims = (sections, tensors, rows, heads_dev, group, kv_dev)
 
-    *packs, carry, following, lengths = pack(
+    *packs, far, carry, following, lengths = pack(
         dims,
         tenant,
         lengths.reshape(-1),
@@ -399,10 +405,11 @@
         next_embed,
     )
     got = [packs[0]] + [swapped(packs[d], "tensor", d) for d in range(1, tensors)]
+    later = got[:NEAR] + [swapped(far, "tensor", d) for d in range(NEAR, tensors)]
     wq_held, wo_held = hold(wq[0], wo[0], packs[0])
 
-    blocks = 2 * rows * width // (pos * HD)
-    kv = join(got, sections * blocks, [wq_held, wo_held])
+    held = 2 * sections * kv_dev
+    kv = join(got, held, [wq_held, wo_held])
     turns, bit = [0], replicas // 2
     caches, waiting = [kv], None
     if bit:
@@ -410,16 +417,16 @@
     arrivals = None
     for tick in range(sections):
         if tick == 0:
-            sums = first_sums(lengths, carry, got, wq_held)
+            sums = first_sums(held, lengths, carry, got, wq_held)
         else:
-            sums, carry = later_sums(tick, lengths, arrivals, following, got, wq_held)
+            sums, carry = later_sums(tick, held, lengths, arrivals, following, later, wq_held)
         pieces = [sums] + [swapped(sums, "replica", d) for d in range(1, replicas)]
         if tick == 0:
             while bit:
                 turns = turns + [turn ^ bit for turn in turns]
                 caches, bit = [kv, waiting], bit // 2
                 if bit:
-                    both = join(caches, 0, pieces[2:])
+                    both = join(caches, kv.shape[0], pieces[2:])
                     kv = both.reshape((-1,) + both.shape[2:])
                     waiting = swapped(kv, "replica", bit)
         out, full = attend(

time: 55.2 us -> 57.8 us (1.047)
  starting transfers between devices: 23.8 us -> 26.5 us
    ppermute x11 -> x13, starting transfers between devices: 10.3 us -> 13.9 us  [swapped(): return lax.ppermute(block, axis, route)]
    ppermute x8, waiting for transfers between devices: 6.18 us -> 8.71 us  [from_behind(): return lax.ppermute(block, ('section', 'tensor'), route)]
    ppermute x11 -> x13, waiting for transfers between devices: 9.86 us -> 7.36 us  [swapped(): return lax.ppermute(block, axis, route)]
    ppermute x8, starting transfers between devices: 13.5 us -> 12.6 us  [from_behind(): return lax.ppermute(block, ('section', 'tensor'), route)]
  transfers between devices with their start and end apart: 19 -> 21, of which waited for: 11 -> 9; matrix products, arithmetic and copies ran while one was open for 0% -> 0% of each run, Pallas kernels for 13% -> 16%
where the time goes in v9:
time: 57.8 us; the launch traced here: 57.6 us
  starting transfers between devices  26.5 us (46%)
  waiting for transfers between devices  16.1 us (28%)
  Pallas kernels  14.4 us (25%)
  between operations  0.69 us (1%)
    ppermute x13, starting transfers between devices, swapped(): return lax.ppermute(block, axis, route)  13.9 us
    ppermute x8, starting transfers between devices, from_behind(): return lax.ppermute(block, ('section', 'tensor'), route)  12.6 us
    ppermute x8, waiting for transfers between devices, from_behind(): return lax.ppermute(block, ('section', 'tensor'), route)  8.71 us
    ppermute x13, waiting for transfers between devices, swapped(): return lax.ppermute(block, axis, route)  7.36 us
    pallas_call x1, Pallas kernels, hold(): pl.pallas_call(lambda *refs: hold_kernel(parts, *refs), out_shape=[pltpu....  5.93 us
    pallas_call x2, Pallas kernels, attend(): pl.pallas_call(lambda *refs: attend_kernel(dims, turns, tick, *refs), out...  3.71 us
    pallas_call x1, Pallas kernels, pack(): pl.pallas_call(lambda *refs: pack_kernel(dims, *refs), out_shape=out_shap...  1.52 us
    pallas_call x1, Pallas kernels, later_sums(): pl.pallas_call(lambda *refs: later_kernel(len(arrivals), tick, held, *ref...  1.28 us
  transfers between devices with their start and end apart: 21, of which 9 were waited for; matrix products, arithmetic and copies ran while one was open for 0% of the time, Pallas kernels for 16%

profile of v9, /device:TPU:0, one launch (start us, length us, event | category | flops | bytes accessed | tf_op | source)
XLA Modules:
  0.0 57.6 jit_solution(12710562142834362020)
XLA Ops:
  0.6 1.5 %shard_map.113 = (bf16[24,16,128]{2,1,0:T(8,128)(2,1)S(1)}, bf16[24,16,128]{2,1,0:T(8,128)(2,1)S(1)}, bf16[16,16,128]{2,1,0:T(8,128)(2,1)S(1)}, bf16[16,16,128]{...) custom-call(s32[2,4]{1,0:T(2,128)} %refs_0_.1, ...), custom_call_target="tpu_custom_call" | custom-call | bytes 819200 | tf_op jit(solution)/shard_map/pallas_call | solution.py:130
  2.2 3.1 %collective-permute-start = (bf16[24,16,128]{2,1,0:T(8,128)(2,1)S(1)}, bf16[24,16,128]{2,1,0:T(8,128)(2,1)S(1)}, u32[]{:S(2)}, u32[]{:S(2)}) collective-permute-start(bf16[24,16,128]{2,1,0:T(8,128)(2,1)S(1)} %get-tuple-element.21), channel_id=1, source_target_pairs={{0,4},{4,0},{8,12},{12,8},{1,5},{5,1},{9,13},{13,9},{2,6},{6,2},{1... | collective-permute-start | bytes 294920 | tf_op jit(solution)/shard_map/ppermute | solution.py:32
  5.3 2.6 %collective-permute-start.1 = (bf16[16,16,128]{2,1,0:T(8,128)(2,1)S(1)}, bf16[16,16,128]{2,1,0:T(8,128)(2,1)S(1)}, u32[]{:S(2)}, u32[]{:S(2)}) collective-permute-start(bf16[16,16,128]{2,1,0:T(8,128)(2,1)S(1)} %get-tuple-element.22), channel_id=1, source_target_pairs={{0,8},{4,12},{8,0},{12,4},{1,9},{5,13},{9,1},{13,5},{2,10},{6,14},... | collective-permute-start | bytes 196616 | tf_op jit(solution)/shard_map/ppermute | solution.py:32
  7.8 0.0 collective-permute-start.2
  7.8 5.9 %shard_map.114 = (bf16[2048,2048]{1,0:T(8,128)(2,1)S(1)}, bf16[2048,2048]{1,0:T(8,128)(2,1)S(1)}) custom-call(bf16[24,16,128]{2,1,0:T(8,128)(2,1)S(1)} %get-tuple-element.20.refs_0_.refs_2_.refs_6_, bf16[2048,2048]{1,0:T(8,128)(2,1)} %bitcast.12, bf16[2048,2048]{1,0:T(8,128)(2,1)} %bitcast.13), custom_call_target="tpu_custom_call" | custom-call | bytes 16777216 | tf_op jit(solution)/shard_map/pallas_call | solution.py:178
  13.8 0.0 collective-permute-done.1.refs_4_.refs_2_
  13.8 0.2 collective-permute-done.2.refs_5_.refs_3_
  14.0 0.0 collective-permute-done.refs_3_.refs_1_.refs_7_
  14.0 1.6 %collective-permute-start.6 = (bf16[4,8,16,128]{3,2,1,0:T(8,128)(2,1)S(1)}, bf16[4,8,16,128]{3,2,1,0:T(8,128)(2,1)S(1)}, u32[]{:S(2)}, u32[]{:S(2)}) collective-permute-start(bf16[4,8,16,128]{3,2,1,0:T(8,128)(2,1)S(1)} %shard_map.116.refs_0_), channel_id=1, source_target_pairs={{0,2},{1,3},{2,0},{3,1},{4,6},{5,7},{6,4},{7,5},{8,10},{9,11},{10,... | collective-permute-start | bytes 393224 | tf_op jit(solution)/shard_map/ppermute | solution.py:32
  15.6 1.3 %shard_map.115.refs_0_ = bf16[4,6272]{1,0:T(4,128)(2,1)S(1)} custom-call(f32[2,128]{1,0:T(2,128)S(1)} %get-tuple-element.18.refs_0_, bf16[4,2048]{1,0:T(4,128)(2,1)S(1)} %get-tuple-element.19.refs_1_.refs_4_, bf16[24,16,128]{2,1,0:T(8,128)(2,1)S(1)} %get-tuple-element.20.refs_0_.refs_2_.refs_6_, ...), custom_call_target="tpu_custom_call" | custom-call | flops 100663296 | bytes 8388608 | tf_op jit(solution)/shard_map/pallas_call | solution.py:233
  16.9 0.5 collective-permute-start.4
  17.4 0.0 collective-permute-start.5
  17.4 4.1 %collective-permute-done.4.refs_2_ = bf16[4,6272]{1,0:T(4,128)(2,1)S(1)} collective-permute-done((bf16[4,6272]{1,0:T(4,128)(2,1)S(1)}, bf16[4,6272]{1,0:T(4,128)(2,1)S(1)}, u32[]{:S(2)}, u32[]{:S(2)}) %collective-permute-start.4) | collective-permute-done | bytes 50208 | tf_op jit(solution)/shard_map/ppermute | solution.py:32
  21.5 0.0 collective-permute-done.5.refs_3_
  21.5 0.0 collective-permute-done.6.refs_1_
  21.5 0.4 collective-permute-start.7
  21.9 0.2 collective-permute-start.3
  22.1 1.7 %collective-permute-start.12 = (bf16[8,16,128]{2,1,0:T(8,128)(2,1)S(1)}, bf16[8,16,128]{2,1,0:T(8,128)(2,1)S(1)}, u32[]{:S(2)}, u32[]{:S(2)}) collective-permute-start(bf16[8,16,128]{2,1,0:T(8,128)(2,1)S(1)} %get-tuple-element.29), channel_id=1, source_target_pairs={{0,8},{4,12},{8,0},{12,4},{1,9},{5,13},{9,1},{13,5},{2,10},{6,14},... | collective-permute-start | bytes 98312 | tf_op jit(solution)/shard_map/ppermute | solution.py:32
  23.8 1.9 %collective-permute-start.13 = (bf16[8,16,128]{2,1,0:T(8,128)(2,1)S(1)}, bf16[8,16,128]{2,1,0:T(8,128)(2,1)S(1)}, u32[]{:S(2)}, u32[]{:S(2)}) collective-permute-start(bf16[8,16,128]{2,1,0:T(8,128)(2,1)S(1)} %get-tuple-element.29), channel_id=1, source_target_pairs={{0,12},{4,8},{8,4},{12,0},{1,13},{5,9},{9,5},{13,1},{2,14},{6,10},... | collective-permute-start | bytes 98312 | tf_op jit(solution)/shard_map/ppermute | solution.py:32
  25.7 0.0 collective-permute-done.3.refs_1_
  25.7 0.0 collective-permute-done.7.refs_7_
  25.7 1.9 %shard_map.118 = (bf16[4,2048]{1,0:T(4,128)(2,1)S(1)}, bf16[4,4096]{1,0:T(4,128)(2,1)S(1)}) custom-call(bf16[4,6272]{1,0:T(4,128)(2,1)S(1)} %shard_map.115.refs_0_, bf16[4,6272]{1,0:T(4,128)(2,1)S(1)} %collective-permute-done.3.refs_1_, bf16[4,6272]{1,0:T(4,128)(2,1)S(1)} %collective-permute-done.4.refs_2_, ...), custom_call_target="tpu_custom_call" | custom-call | flops 33554432 | bytes 8388608 | tf_op jit(solution)/shard_map/pallas_call | solution.py:376
  27.6 1.5 %collective-permute-start.8 = (bf16[4,4096]{1,0:T(4,128)(2,1)S(1)}, bf16[4,4096]{1,0:T(4,128)(2,1)S(1)}, u32[]{:S(2)}, u32[]{:S(2)}) collective-permute-start(bf16[4,4096]{1,0:T(4,128)(2,1)S(1)} %get-tuple-element.26), channel_id=1, source_target_pairs={{0,16},{4,20},{8,24},{12,28},{16,0},{20,4},{24,8},{28,12},{1,17},{... | collective-permute-start | bytes 98312 | tf_op jit(solution)/shard_map/ppermute | solution.py:42
  29.1 2.0 %collective-permute-start.10 = (bf16[4,2048]{1,0:T(4,128)(2,1)S(1)}, bf16[4,2048]{1,0:T(4,128)(2,1)S(1)}, u32[]{:S(2)}, u32[]{:S(2)}) collective-permute-start(bf16[4,2048]{1,0:T(4,128)(2,1)S(1)} %get-tuple-element.27), channel_id=1, source_target_pairs={{8,16},{12,20},{0,24},{4,28},{24,0},{28,4},{16,8},{20,12},{9,17},{... | collective-permute-start | bytes 49160 | tf_op jit(solution)/shard_map/ppermute | solution.py:42
  31.1 1.8 %collective-permute-start.11 = (bf16[4,2048]{1,0:T(4,128)(2,1)S(1)}, bf16[4,2048]{1,0:T(4,128)(2,1)S(1)}, u32[]{:S(2)}, u32[]{:S(2)}) collective-permute-start(bf16[4,2048]{1,0:T(4,128)(2,1)S(1)} %get-tuple-element.27), channel_id=1, source_target_pairs={{12,16},{8,20},{4,24},{0,28},{28,0},{24,4},{20,8},{16,12},{13,17},... | collective-permute-start | bytes 49160 | tf_op jit(solution)/shard_map/ppermute | solution.py:42
  32.9 0.5 collective-permute-start.9
  33.4 0.0 collective-permute-done.13.refs_9_
  33.4 1.3 %collective-permute-done.10.refs_3_ = bf16[4,2048]{1,0:T(4,128)(2,1)S(1)} collective-permute-done((bf16[4,2048]{1,0:T(4,128)(2,1)S(1)}, bf16[4,2048]{1,0:T(4,128)(2,1)S(1)}, u32[]{:S(2)}, u32[]{:S(2)}) %collective-permute-start.10) | collective-permute-done | bytes 16416 | tf_op jit(solution)/shard_map/ppermute | solution.py:42
  34.8 2.7 %collective-permute-done.11.refs_4_ = bf16[4,2048]{1,0:T(4,128)(2,1)S(1)} collective-permute-done((bf16[4,2048]{1,0:T(4,128)(2,1)S(1)}, bf16[4,2048]{1,0:T(4,128)(2,1)S(1)}, u32[]{:S(2)}, u32[]{:S(2)}) %collective-permute-start.11) | collective-permute-done | bytes 16416 | tf_op jit(solution)/shard_map/ppermute | solution.py:42
  37.5 0.2 collective-permute-done.9.refs_2_
  37.7 0.0 collective-permute-done.8.refs_1_
  37.7 1.3 %shard_map.119 = (bf16[4,6272]{1,0:T(4,128)(2,1)S(1)}, bf16[4,2048]{1,0:T(4,128)(2,1)S(1)}) custom-call(f32[2,128]{1,0:T(2,128)S(1)} %get-tuple-element.18.refs_0_, bf16[4,4096]{1,0:T(4,128)(2,1)S(1)} %collective-permute-done.8.refs_1_, bf16[4,2048]{1,0:T(4,128)(2,1)S(1)} %collective-permute-done.9.refs_2_, ...), custom_call_target="tpu_custom_call" | custom-call | flops 100663296 | bytes 8388608 | tf_op jit(solution)/shard_map/pallas_call | solution.py:278
  39.0 0.0 collective-permute-start.14
  39.0 1.2 %collective-permute-start.15 = (bf16[4,6272]{1,0:T(4,128)(2,1)S(1)}, bf16[4,6272]{1,0:T(4,128)(2,1)S(1)}, u32[]{:S(2)}, u32[]{:S(2)}) collective-permute-start(bf16[4,6272]{1,0:T(4,128)(2,1)S(1)} %get-tuple-element.30.refs_0_), channel_id=1, source_target_pairs={{0,2},{1,3},{2,0},{3,1},{4,6},{5,7},{6,4},{7,5},{8,10},{9,11},{10,... | collective-permute-start | bytes 150536 | tf_op jit(solution)/shard_map/ppermute | solution.py:32
  40.1 0.7 %collective-permute-start.16 = (bf16[4,6272]{1,0:T(4,128)(2,1)S(1)}, bf16[4,6272]{1,0:T(4,128)(2,1)S(1)}, u32[]{:S(2)}, u32[]{:S(2)}) collective-permute-start(bf16[4,6272]{1,0:T(4,128)(2,1)S(1)} %get-tuple-element.30.refs_0_), channel_id=1, source_target_pairs={{0,3},{1,2},{2,1},{3,0},{4,7},{5,6},{6,5},{7,4},{8,11},{9,10},{10,... | collective-permute-start | bytes 150536 | tf_op jit(solution)/shard_map/ppermute | solution.py:32
  40.8 0.0 collective-permute-done.14.refs_1_
  40.8 2.4 %collective-permute-done.15.refs_2_ = bf16[4,6272]{1,0:T(4,128)(2,1)S(1)} collective-permute-done((bf16[4,6272]{1,0:T(4,128)(2,1)S(1)}, bf16[4,6272]{1,0:T(4,128)(2,1)S(1)}, u32[]{:S(2)}, u32[]{:S(2)}) %collective-permute-start.15) | collective-permute-done | bytes 50208 | tf_op jit(solution)/shard_map/ppermute | solution.py:32
  43.2 0.6 %collective-permute-done.16.refs_3_ = bf16[4,6272]{1,0:T(4,128)(2,1)S(1)} collective-permute-done((bf16[4,6272]{1,0:T(4,128)(2,1)S(1)}, bf16[4,6272]{1,0:T(4,128)(2,1)S(1)}, u32[]{:S(2)}, u32[]{:S(2)}) %collective-permute-start.16) | collective-permute-done | bytes 50208 | tf_op jit(solution)/shard_map/ppermute | solution.py:32
  43.9 1.9 %shard_map.120 = (bf16[4,2048]{1,0:T(4,128)(2,1)S(1)}, bf16[4,4096]{1,0:T(4,128)(2,1)S(1)}) custom-call(bf16[4,6272]{1,0:T(4,128)(2,1)S(1)} %get-tuple-element.30.refs_0_, bf16[4,6272]{1,0:T(4,128)(2,1)S(1)} %collective-permute-done.14.refs_1_, bf16[4,6272]{1,0:T(4,128)(2,1)S(1)} %collective-permute-done.15.refs_2_, ...), custom_call_target="tpu_custom_call" | custom-call | flops 33554432 | bytes 8388608 | tf_op jit(solution)/shard_map/pallas_call | solution.py:376
  45.7 1.3 %collective-permute-start.17 = (bf16[4,4096]{1,0:T(4,128)(2,1)S(1)}, bf16[4,4096]{1,0:T(4,128)(2,1)S(1)}, u32[]{:S(2)}, u32[]{:S(2)}) collective-permute-start(bf16[4,4096]{1,0:T(4,128)(2,1)S(1)} %get-tuple-element.32), channel_id=1, source_target_pairs={{0,16},{4,20},{8,24},{12,28},{16,0},{20,4},{24,8},{28,12},{1,17},{... | collective-permute-start | bytes 98312 | tf_op jit(solution)/shard_map/ppermute | solution.py:42
  47.1 0.6 collective-permute-start.18
  47.6 2.9 %collective-permute-start.19 = (bf16[4,2048]{1,0:T(4,128)(2,1)S(1)}, bf16[4,2048]{1,0:T(4,128)(2,1)S(1)}, u32[]{:S(2)}, u32[]{:S(2)}) collective-permute-start(bf16[4,2048]{1,0:T(4,128)(2,1)S(1)} %get-tuple-element.33), channel_id=1, source_target_pairs={{8,16},{12,20},{0,24},{4,28},{24,0},{28,4},{16,8},{20,12},{9,17},{... | collective-permute-start | bytes 49160 | tf_op jit(solution)/shard_map/ppermute | solution.py:42
  50.5 2.0 %collective-permute-start.20 = (bf16[4,2048]{1,0:T(4,128)(2,1)S(1)}, bf16[4,2048]{1,0:T(4,128)(2,1)S(1)}, u32[]{:S(2)}, u32[]{:S(2)}) collective-permute-start(bf16[4,2048]{1,0:T(4,128)(2,1)S(1)} %get-tuple-element.33), channel_id=1, source_target_pairs={{12,16},{8,20},{4,24},{0,28},{28,0},{24,4},{20,8},{16,12},{13,17},... | collective-permute-start | bytes 49160 | tf_op jit(solution)/shard_map/ppermute | solution.py:42
  52.5 0.0 collective-permute-done.18.refs_1_
  52.5 0.8 %collective-permute-done.19.refs_2_ = bf16[4,2048]{1,0:T(4,128)(2,1)S(1)} collective-permute-done((bf16[4,2048]{1,0:T(4,128)(2,1)S(1)}, bf16[4,2048]{1,0:T(4,128)(2,1)S(1)}, u32[]{:S(2)}, u32[]{:S(2)}) %collective-permute-start.19) | collective-permute-done | bytes 16416 | tf_op jit(solution)/shard_map/ppermute | solution.py:42
  53.3 3.7 %collective-permute-done.20.refs_3_ = bf16[4,2048]{1,0:T(4,128)(2,1)S(1)} collective-permute-done((bf16[4,2048]{1,0:T(4,128)(2,1)S(1)}, bf16[4,2048]{1,0:T(4,128)(2,1)S(1)}, u32[]{:S(2)}, u32[]{:S(2)}) %collective-permute-start.20) | collective-permute-done | bytes 16416 | tf_op jit(solution)/shard_map/ppermute | solution.py:42
  57.0 0.0 collective-permute-done.17.refs_0_
  57.0 0.6 %shard_map.121 = (bf16[1,4,2048]{2,1,0:T(4,128)(2,1)}, bf16[1,4,2048]{2,1,0:T(4,128)(2,1)}) custom-call(bf16[4,4096]{1,0:T(4,128)(2,1)S(1)} %collective-permute-done.17.refs_0_, bf16[4,2048]{1,0:T(4,128)(2,1)S(1)} %collective-permute-done.18.refs_1_, bf16[4,2048]{1,0:T(4,128)(2,1)S(1)} %collective-permute-done.19.refs_2_, ...), custom_call_target="tpu_custom_call" | custom-call | tf_op jit(solution)/shard_map/pallas_call | solution.py:296
  (3 shorter events, 0.0 us)
Async XLA Ops:
  2.2 11.9 %collective-permute-start = (bf16[24,16,128]{2,1,0:T(8,128)(2,1)S(1)}, bf16[24,16,128]{2,1,0:T(8,128)(2,1)S(1)}, u32[]{:S(2)}, u32[]{:S(2)}) collective-permute-start(bf16[24,16,128]{2,1,0:T(8,128)(2,1)S(1)} %get-tuple-element.21), channel_id=1, source_target_pairs={{0,4},{4,0},{8,12},{12,8},{1,5},{5,1},{9,13},{13,9},{2,6},{6,2},{1... | collective-permute-start | bytes 294920 | tf_op jit(solution)/shard_map/ppermute | solution.py:32
  5.3 8.5 %collective-permute-start.1 = (bf16[16,16,128]{2,1,0:T(8,128)(2,1)S(1)}, bf16[16,16,128]{2,1,0:T(8,128)(2,1)S(1)}, u32[]{:S(2)}, u32[]{:S(2)}) collective-permute-start(bf16[16,16,128]{2,1,0:T(8,128)(2,1)S(1)} %get-tuple-element.22), channel_id=1, source_target_pairs={{0,8},{4,12},{8,0},{12,4},{1,9},{5,13},{9,1},{13,5},{2,10},{6,14},... | collective-permute-start | bytes 196616 | tf_op jit(solution)/shard_map/ppermute | solution.py:32
  7.8 6.2 %collective-permute-start.2 = (bf16[16,16,128]{2,1,0:T(8,128)(2,1)S(1)}, bf16[16,16,128]{2,1,0:T(8,128)(2,1)S(1)}, u32[]{:S(2)}, u32[]{:S(2)}) collective-permute-start(bf16[16,16,128]{2,1,0:T(8,128)(2,1)S(1)} %get-tuple-element.23), channel_id=1, source_target_pairs={{0,12},{4,8},{8,4},{12,0},{1,13},{5,9},{9,5},{13,1},{2,14},{6,10},... | collective-permute-start | bytes 196616 | tf_op jit(solution)/shard_map/ppermute | solution.py:32
  14.0 7.4 %collective-permute-start.6 = (bf16[4,8,16,128]{3,2,1,0:T(8,128)(2,1)S(1)}, bf16[4,8,16,128]{3,2,1,0:T(8,128)(2,1)S(1)}, u32[]{:S(2)}, u32[]{:S(2)}) collective-permute-start(bf16[4,8,16,128]{3,2,1,0:T(8,128)(2,1)S(1)} %shard_map.116.refs_0_), channel_id=1, source_target_pairs={{0,2},{1,3},{2,0},{3,1},{4,6},{5,7},{6,4},{7,5},{8,10},{9,11},{10,... | collective-permute-start | bytes 393224 | tf_op jit(solution)/shard_map/ppermute | solution.py:32
  16.9 4.6 %collective-permute-start.4 = (bf16[4,6272]{1,0:T(4,128)(2,1)S(1)}, bf16[4,6272]{1,0:T(4,128)(2,1)S(1)}, u32[]{:S(2)}, u32[]{:S(2)}) collective-permute-start(bf16[4,6272]{1,0:T(4,128)(2,1)S(1)} %shard_map.115.refs_0_), channel_id=1, source_target_pairs={{0,2},{1,3},{2,0},{3,1},{4,6},{5,7},{6,4},{7,5},{8,10},{9,11},{10,... | collective-permute-start | bytes 150536 | tf_op jit(solution)/shard_map/ppermute | solution.py:32
  17.4 4.1 %collective-permute-start.5 = (bf16[4,6272]{1,0:T(4,128)(2,1)S(1)}, bf16[4,6272]{1,0:T(4,128)(2,1)S(1)}, u32[]{:S(2)}, u32[]{:S(2)}) collective-permute-start(bf16[4,6272]{1,0:T(4,128)(2,1)S(1)} %shard_map.115.refs_0_), channel_id=1, source_target_pairs={{0,3},{1,2},{2,1},{3,0},{4,7},{5,6},{6,5},{7,4},{8,11},{9,10},{10,... | collective-permute-start | bytes 150536 | tf_op jit(solution)/shard_map/ppermute | solution.py:32
  21.5 4.2 %collective-permute-start.7 = (bf16[8,8,16,128]{3,2,1,0:T(8,128)(2,1)S(1)}, bf16[8,8,16,128]{3,2,1,0:T(8,128)(2,1)S(1)}, u32[]{:S(2)}, u32[]{:S(2)}) collective-permute-start(bf16[8,8,16,128]{3,2,1,0:T(8,128)(2,1)S(1)} %bitcast.9), channel_id=1, source_target_pairs={{0,1},{1,0},{2,3},{3,2},{4,5},{5,4},{6,7},{7,6},{8,9},{9,8},{10,11... | collective-permute-start | bytes 786440 | tf_op jit(solution)/shard_map/ppermute | solution.py:32
  21.9 3.8 %collective-permute-start.3 = (bf16[4,6272]{1,0:T(4,128)(2,1)S(1)}, bf16[4,6272]{1,0:T(4,128)(2,1)S(1)}, u32[]{:S(2)}, u32[]{:S(2)}) collective-permute-start(bf16[4,6272]{1,0:T(4,128)(2,1)S(1)} %shard_map.115.refs_0_), channel_id=1, source_target_pairs={{0,1},{1,0},{2,3},{3,2},{4,5},{5,4},{6,7},{7,6},{8,9},{9,8},{10,11... | collective-permute-start | bytes 150536 | tf_op jit(solution)/shard_map/ppermute | solution.py:32
  22.1 10.8 %collective-permute-start.12 = (bf16[8,16,128]{2,1,0:T(8,128)(2,1)S(1)}, bf16[8,16,128]{2,1,0:T(8,128)(2,1)S(1)}, u32[]{:S(2)}, u32[]{:S(2)}) collective-permute-start(bf16[8,16,128]{2,1,0:T(8,128)(2,1)S(1)} %get-tuple-element.29), channel_id=1, source_target_pairs={{0,8},{4,12},{8,0},{12,4},{1,9},{5,13},{9,1},{13,5},{2,10},{6,14},... | collective-permute-start | bytes 98312 | tf_op jit(solution)/shard_map/ppermute | solution.py:32
  23.8 9.7 %collective-permute-start.13 = (bf16[8,16,128]{2,1,0:T(8,128)(2,1)S(1)}, bf16[8,16,128]{2,1,0:T(8,128)(2,1)S(1)}, u32[]{:S(2)}, u32[]{:S(2)}) collective-permute-start(bf16[8,16,128]{2,1,0:T(8,128)(2,1)S(1)} %get-tuple-element.29), channel_id=1, source_target_pairs={{0,12},{4,8},{8,4},{12,0},{1,13},{5,9},{9,5},{13,1},{2,14},{6,10},... | collective-permute-start | bytes 98312 | tf_op jit(solution)/shard_map/ppermute | solution.py:32
  27.6 10.1 %collective-permute-start.8 = (bf16[4,4096]{1,0:T(4,128)(2,1)S(1)}, bf16[4,4096]{1,0:T(4,128)(2,1)S(1)}, u32[]{:S(2)}, u32[]{:S(2)}) collective-permute-start(bf16[4,4096]{1,0:T(4,128)(2,1)S(1)} %get-tuple-element.26), channel_id=1, source_target_pairs={{0,16},{4,20},{8,24},{12,28},{16,0},{20,4},{24,8},{28,12},{1,17},{... | collective-permute-start | bytes 98312 | tf_op jit(solution)/shard_map/ppermute | solution.py:42
  29.1 5.7 %collective-permute-start.10 = (bf16[4,2048]{1,0:T(4,128)(2,1)S(1)}, bf16[4,2048]{1,0:T(4,128)(2,1)S(1)}, u32[]{:S(2)}, u32[]{:S(2)}) collective-permute-start(bf16[4,2048]{1,0:T(4,128)(2,1)S(1)} %get-tuple-element.27), channel_id=1, source_target_pairs={{8,16},{12,20},{0,24},{4,28},{24,0},{28,4},{16,8},{20,12},{9,17},{... | collective-permute-start | bytes 49160 | tf_op jit(solution)/shard_map/ppermute | solution.py:42
  31.1 6.4 %collective-permute-start.11 = (bf16[4,2048]{1,0:T(4,128)(2,1)S(1)}, bf16[4,2048]{1,0:T(4,128)(2,1)S(1)}, u32[]{:S(2)}, u32[]{:S(2)}) collective-permute-start(bf16[4,2048]{1,0:T(4,128)(2,1)S(1)} %get-tuple-element.27), channel_id=1, source_target_pairs={{12,16},{8,20},{4,24},{0,28},{28,0},{24,4},{20,8},{16,12},{13,17},... | collective-permute-start | bytes 49160 | tf_op jit(solution)/shard_map/ppermute | solution.py:42
  32.9 4.8 %collective-permute-start.9 = (bf16[4,2048]{1,0:T(4,128)(2,1)S(1)}, bf16[4,2048]{1,0:T(4,128)(2,1)S(1)}, u32[]{:S(2)}, u32[]{:S(2)}) collective-permute-start(bf16[4,2048]{1,0:T(4,128)(2,1)S(1)} %get-tuple-element.27), channel_id=1, source_target_pairs={{4,16},{0,20},{12,24},{8,28},{20,0},{16,4},{28,8},{24,12},{5,17},{... | collective-permute-start | bytes 49160 | tf_op jit(solution)/shard_map/ppermute | solution.py:42
  39.0 1.9 %collective-permute-start.14 = (bf16[4,6272]{1,0:T(4,128)(2,1)S(1)}, bf16[4,6272]{1,0:T(4,128)(2,1)S(1)}, u32[]{:S(2)}, u32[]{:S(2)}) collective-permute-start(bf16[4,6272]{1,0:T(4,128)(2,1)S(1)} %get-tuple-element.30.refs_0_), channel_id=1, source_target_pairs={{0,1},{1,0},{2,3},{3,2},{4,5},{5,4},{6,7},{7,6},{8,9},{9,8},{10,11... | collective-permute-start | bytes 150536 | tf_op jit(solution)/shard_map/ppermute | solution.py:32
  39.0 4.3 %collective-permute-start.15 = (bf16[4,6272]{1,0:T(4,128)(2,1)S(1)}, bf16[4,6272]{1,0:T(4,128)(2,1)S(1)}, u32[]{:S(2)}, u32[]{:S(2)}) collective-permute-start(bf16[4,6272]{1,0:T(4,128)(2,1)S(1)} %get-tuple-element.30.refs_0_), channel_id=1, source_target_pairs={{0,2},{1,3},{2,0},{3,1},{4,6},{5,7},{6,4},{7,5},{8,10},{9,11},{10,... | collective-permute-start | bytes 150536 | tf_op jit(solution)/shard_map/ppermute | solution.py:32
  40.1 3.8 %collective-permute-start.16 = (bf16[4,6272]{1,0:T(4,128)(2,1)S(1)}, bf16[4,6272]{1,0:T(4,128)(2,1)S(1)}, u32[]{:S(2)}, u32[]{:S(2)}) collective-permute-start(bf16[4,6272]{1,0:T(4,128)(2,1)S(1)} %get-tuple-element.30.refs_0_), channel_id=1, source_target_pairs={{0,3},{1,2},{2,1},{3,0},{4,7},{5,6},{6,5},{7,4},{8,11},{9,10},{10,... | collective-permute-start | bytes 150536 | tf_op jit(solution)/shard_map/ppermute | solution.py:32
  45.7 11.2 %collective-permute-start.17 = (bf16[4,4096]{1,0:T(4,128)(2,1)S(1)}, bf16[4,4096]{1,0:T(4,128)(2,1)S(1)}, u32[]{:S(2)}, u32[]{:S(2)}) collective-permute-start(bf16[4,4096]{1,0:T(4,128)(2,1)S(1)} %get-tuple-element.32), channel_id=1, source_target_pairs={{0,16},{4,20},{8,24},{12,28},{16,0},{20,4},{24,8},{28,12},{1,17},{... | collective-permute-start | bytes 98312 | tf_op jit(solution)/shard_map/ppermute | solution.py:42
  47.1 5.4 %collective-permute-start.18 = (bf16[4,2048]{1,0:T(4,128)(2,1)S(1)}, bf16[4,2048]{1,0:T(4,128)(2,1)S(1)}, u32[]{:S(2)}, u32[]{:S(2)}) collective-permute-start(bf16[4,2048]{1,0:T(4,128)(2,1)S(1)} %get-tuple-element.33), channel_id=1, source_target_pairs={{4,16},{0,20},{12,24},{8,28},{20,0},{16,4},{28,8},{24,12},{5,17},{... | collective-permute-start | bytes 49160 | tf_op jit(solution)/shard_map/ppermute | solution.py:42
  47.6 5.6 %collective-permute-start.19 = (bf16[4,2048]{1,0:T(4,128)(2,1)S(1)}, bf16[4,2048]{1,0:T(4,128)(2,1)S(1)}, u32[]{:S(2)}, u32[]{:S(2)}) collective-permute-start(bf16[4,2048]{1,0:T(4,128)(2,1)S(1)} %get-tuple-element.33), channel_id=1, source_target_pairs={{8,16},{12,20},{0,24},{4,28},{24,0},{28,4},{16,8},{20,12},{9,17},{... | collective-permute-start | bytes 49160 | tf_op jit(solution)/shard_map/ppermute | solution.py:42
  50.5 6.4 %collective-permute-start.20 = (bf16[4,2048]{1,0:T(4,128)(2,1)S(1)}, bf16[4,2048]{1,0:T(4,128)(2,1)S(1)}, u32[]{:S(2)}, u32[]{:S(2)}) collective-permute-start(bf16[4,2048]{1,0:T(4,128)(2,1)S(1)} %get-tuple-element.33), channel_id=1, source_target_pairs={{12,16},{8,20},{4,24},{0,28},{28,0},{24,4},{20,8},{16,12},{13,17},... | collective-permute-start | bytes 49160 | tf_op jit(solution)/shard_map/ppermute | solution.py:42

commit v10 on v9

--- a/solution.py
+++ b/solution.py
@@ -56,8 +56,8 @@
 def pack_kernel(dims, *refs):
     sections, tensors, rows, heads_dev, group, kv_dev = dims
     sources, refs = refs[:8], refs[8:]
-    packs, (far_ref, h_ref, next_ref, lengths_ref) = refs[:tensors], refs[tensors : tensors + 4]
-    ids, lengths, gains, biases, keys, values, sems = refs[tensors + 4 :]
+    packs, (h_ref, next_ref, lengths_ref) = refs[:tensors], refs[tensors : tensors + 3]
+    ids, lengths, gains, biases, keys, values, sems = refs[tensors + 3 :]
     held = 2 * sections * kv_dev
     targets = (ids, lengths, keys, values, gains, biases, h_ref, next_ref)
     copies = [
@@ -110,8 +110,6 @@
             ).astype(BF)
             for d in range(tensors if tick == 0 else min(tensors, NEAR)):
                 packs[d][held + tick * blocks + j] = block
-            if tick > 0:
-                far_ref[(tick - 1) * blocks + j] = block
     copies[6].wait()
     copies[7].wait()
 
@@ -124,7 +122,6 @@
     out_shape = [
         shape((held + blocks + (later if d < NEAR else 0), pos, HD)) for d in range(tensors)
     ]
-    out_shape += [shape((later, pos, HD))]
     out_shape += [shape(h.shape), shape(following.shape), shape((sections, HD), F32)]
     operands = (tenant, lengths, keys, values, gain, bias, h, following)
     return pl.pallas_call(
@@ -174,7 +171,7 @@
 
 
 def hold(wq, wo, after):
-    parts = 8
+    parts = 16
     return pl.pallas_call(
         lambda *refs: hold_kernel(parts, *refs),
         out_shape=[pltpu.VMEM(wq.shape, BF), pltpu.VMEM(wo.shape, BF)],
@@ -256,7 +253,7 @@
     return h, jnp.where(section == 0, came, carried)
 
 
-def later_kernel(count, tick, held, lengths_ref, *refs):
+def later_kernel(count, tick, lengths_ref, *refs):
     arrivals, next_ref = refs[:count], refs[count]
     pieces, (w_ref, out_ref, carry_ref) = refs[count + 1 : -3], refs[-3:]
     h, emitted = arrive(arrivals, next_ref, tick - 1)
@@ -268,15 +265,14 @@
         carry_ref[:, :width] = h.astype(BF)
         carry_ref[:, width:] = emitted.astype(BF)
     blocks = 2 * h.shape[0] * width // (pieces[0].shape[1] * HD)
-    firsts = [held + tick * blocks if d < NEAR else (tick - 1) * blocks for d in range(len(pieces))]
-    query_sums(firsts, lengths_ref[tick : tick + 1], h, pieces, w_ref, out_ref)
-
-
-def later_sums(tick, held, lengths, arrivals, following, pieces, w):
+    query_sums([(tick - 1) * blocks] * len(pieces), lengths_ref[tick : tick + 1], h, pieces, w_ref, out_ref)
+
+
+def later_sums(tick, lengths, arrivals, following, pieces, w):
     rows, width = following.shape[1:]
     parts = 1 if following.shape[0] == 2 else 2
     return pl.pallas_call(
-        lambda *refs: later_kernel(len(arrivals), tick, held, *refs),
+        lambda *refs: later_kernel(len(arrivals), tick, *refs),
         out_shape=[shape((rows, 3 * w.shape[1] + HD)), shape((rows, width * parts))],
         in_specs=[VMEM] * (len(arrivals) + len(pieces) + 3),
         out_specs=[VMEM] * 2,
@@ -393,7 +389,7 @@
     kv_dev = max(1, heads_dev // group)
     dims = (sections, tensors, rows, heads_dev, group, kv_dev)
 
-    *packs, far, carry, following, lengths = pack(
+    *packs, carry, following, lengths = pack(
         dims,
         tenant,
         lengths.reshape(-1),
@@ -405,11 +401,17 @@
         next_embed,
     )
     got = [packs[0]] + [swapped(packs[d], "tensor", d) for d in range(1, tensors)]
-    later = got[:NEAR] + [swapped(far, "tensor", d) for d in range(NEAR, tensors)]
     wq_held, wo_held = hold(wq[0], wo[0], packs[0])
 
     held = 2 * sections * kv_dev
     kv = join(got, held, [wq_held, wo_held])
+
+    later = [piece[held + 2 * rows * width // (keys.shape[4] * HD) :] for piece in got[:NEAR]]
+    bit = NEAR
+    while bit < tensors:
+        later = [sum(later)]
+        later = later + [swapped(later[0], "tensor", bit)]
+        bit *= 2
     turns, bit = [0], replicas // 2
     caches, waiting = [kv], None
     if bit:
@@ -419,7 +421,7 @@
         if tick == 0:
             sums = first_sums(held, lengths, carry, got, wq_held)
         else:
-            sums, carry = later_sums(tick, held, lengths, arrivals, following, later, wq_held)
+            sums, carry = later_sums(tick, lengths, arrivals, following, later, wq_held)
         pieces = [sums] + [swapped(sums, "replica", d) for d in range(1, replicas)]
         if tick == 0:
             while bit:

time: 57.8 us -> 53.9 us (0.933)
  waiting for transfers between devices: 16.1 us -> 13.1 us
  starting transfers between devices: 26.5 us -> 25.5 us
    ppermute x8, waiting for transfers between devices: 8.71 us -> 5.93 us  [from_behind(): return lax.ppermute(block, ('section', 'tensor'), route)]
    ppermute x13 -> x12, starting transfers between devices: 13.9 us -> 12 us  [swapped(): return lax.ppermute(block, axis, route)]
    ppermute x8, starting transfers between devices: 12.6 us -> 13.5 us  [from_behind(): return lax.ppermute(block, ('section', 'tensor'), route)]
    ppermute x13 -> x12, waiting for transfers between devices: 7.36 us -> 7.13 us  [swapped(): return lax.ppermute(block, axis, route)]
  transfers between devices with their start and end apart: 21 -> 20, of which waited for: 9 -> 11; matrix products, arithmetic and copies ran while one was open for 0% -> 0% of each run, Pallas kernels for 16% -> 17%
where the time goes in v10:
time: 53.9 us; the launch traced here: 53.7 us
  starting transfers between devices  25.5 us (47%)
  Pallas kernels  14.5 us (27%)
  waiting for transfers between devices  13.1 us (24%)
  between operations  0.69 us (1%)
    ppermute x8, starting transfers between devices, from_behind(): return lax.ppermute(block, ('section', 'tensor'), route)  13.5 us
    ppermute x12, starting transfers between devices, swapped(): return lax.ppermute(block, axis, route)  12 us
    ppermute x12, waiting for transfers between devices, swapped(): return lax.ppermute(block, axis, route)  7.13 us
    pallas_call x1, Pallas kernels, hold(): pl.pallas_call(lambda *refs: hold_kernel(parts, *refs), out_shape=[pltpu....  6.04 us
    ppermute x8, waiting for transfers between devices, from_behind(): return lax.ppermute(block, ('section', 'tensor'), route)  5.93 us
    pallas_call x2, Pallas kernels, attend(): pl.pallas_call(lambda *refs: attend_kernel(dims, turns, tick, *refs), out...  3.71 us
    pallas_call x1, Pallas kernels, pack(): pl.pallas_call(lambda *refs: pack_kernel(dims, *refs), out_shape=out_shap...  1.52 us
    pallas_call x1, Pallas kernels, later_sums(): pl.pallas_call(lambda *refs: later_kernel(len(arrivals), tick, *refs), ou...  1.28 us
  transfers between devices with their start and end apart: 20, of which 11 were waited for; matrix products, arithmetic and copies ran while one was open for 0% of the time, Pallas kernels for 17%

profile of v10, /device:TPU:0, one launch (start us, length us, event | category | flops | bytes accessed | tf_op | source)
XLA Modules:
  0.0 53.7 jit_solution(9409200239923583553)
XLA Ops:
  0.6 1.5 %shard_map.113 = (bf16[24,16,128]{2,1,0:T(8,128)(2,1)S(1)}, bf16[24,16,128]{2,1,0:T(8,128)(2,1)S(1)}, bf16[16,16,128]{2,1,0:T(8,128)(2,1)S(1)}, bf16[16,16,128]{...) custom-call(s32[2,4]{1,0:T(2,128)} %refs_0_.1, ...), custom_call_target="tpu_custom_call" | custom-call | bytes 819200 | tf_op jit(solution)/shard_map/pallas_call | solution.py:127
  2.2 3.1 %collective-permute-start = (bf16[24,16,128]{2,1,0:T(8,128)(2,1)S(1)}, bf16[24,16,128]{2,1,0:T(8,128)(2,1)S(1)}, u32[]{:S(2)}, u32[]{:S(2)}) collective-permute-start(bf16[24,16,128]{2,1,0:T(8,128)(2,1)S(1)} %get-tuple-element.20), channel_id=1, source_target_pairs={{0,4},{4,0},{8,12},{12,8},{1,5},{5,1},{9,13},{13,9},{2,6},{6,2},{1... | collective-permute-start | bytes 294920 | tf_op jit(solution)/shard_map/ppermute | solution.py:32
  5.3 2.6 %collective-permute-start.1 = (bf16[16,16,128]{2,1,0:T(8,128)(2,1)S(1)}, bf16[16,16,128]{2,1,0:T(8,128)(2,1)S(1)}, u32[]{:S(2)}, u32[]{:S(2)}) collective-permute-start(bf16[16,16,128]{2,1,0:T(8,128)(2,1)S(1)} %get-tuple-element.21), channel_id=1, source_target_pairs={{0,8},{4,12},{8,0},{12,4},{1,9},{5,13},{9,1},{13,5},{2,10},{6,14},... | collective-permute-start | bytes 196616 | tf_op jit(solution)/shard_map/ppermute | solution.py:32
  7.8 0.0 collective-permute-start.2
  7.8 6.0 %shard_map.114 = (bf16[2048,2048]{1,0:T(8,128)(2,1)S(1)}, bf16[2048,2048]{1,0:T(8,128)(2,1)S(1)}) custom-call(bf16[24,16,128]{2,1,0:T(8,128)(2,1)S(1)} %get-tuple-element.19.refs_0_.refs_2_, bf16[2048,2048]{1,0:T(8,128)(2,1)} %bitcast.12, bf16[2048,2048]{1,0:T(8,128)(2,1)} %bitcast.13), custom_call_target="tpu_custom_call" | custom-call | bytes 16777216 | tf_op jit(solution)/shard_map/pallas_call | solution.py:175
  13.9 0.0 collective-permute-done.1.refs_4_.refs_2_
  13.9 0.1 collective-permute-done.2.refs_5_.refs_3_
  14.0 0.0 collective-permute-done.refs_3_.refs_1_
  14.0 1.7 %collective-permute-start.6 = (bf16[4,8,16,128]{3,2,1,0:T(8,128)(2,1)S(1)}, bf16[4,8,16,128]{3,2,1,0:T(8,128)(2,1)S(1)}, u32[]{:S(2)}, u32[]{:S(2)}) collective-permute-start(bf16[4,8,16,128]{3,2,1,0:T(8,128)(2,1)S(1)} %shard_map.116.refs_0_), channel_id=1, source_target_pairs={{0,2},{1,3},{2,0},{3,1},{4,6},{5,7},{6,4},{7,5},{8,10},{9,11},{10,... | collective-permute-start | bytes 393224 | tf_op jit(solution)/shard_map/ppermute | solution.py:32
  15.7 1.3 %shard_map.115.refs_0_ = bf16[4,6272]{1,0:T(4,128)(2,1)S(1)} custom-call(f32[2,128]{1,0:T(2,128)S(1)} %get-tuple-element.17.refs_0_, bf16[4,2048]{1,0:T(4,128)(2,1)S(1)} %get-tuple-element.18.refs_1_.refs_4_, bf16[24,16,128]{2,1,0:T(8,128)(2,1)S(1)} %get-tuple-element.19.refs_0_.refs_2_, bf16[24,16,128]{2,1,0:T(8,128)(2,1)S(1)} %collective-permute-done.refs_3_.refs_1_, ...), custom_call_target="tpu_custom_call" | custom-call | flops 100663296 | bytes 8388608 | tf_op jit(solution)/shard_map/pallas_call | solution.py:230
  17.0 0.0 collective-permute-start.5
  17.0 0.4 collective-permute-start.4
  17.4 3.1 %collective-permute-done.5.refs_3_ = bf16[4,6272]{1,0:T(4,128)(2,1)S(1)} collective-permute-done((bf16[4,6272]{1,0:T(4,128)(2,1)S(1)}, bf16[4,6272]{1,0:T(4,128)(2,1)S(1)}, u32[]{:S(2)}, u32[]{:S(2)}) %collective-permute-start.5) | collective-permute-done | bytes 50208 | tf_op jit(solution)/shard_map/ppermute | solution.py:32
  20.5 1.1 %collective-permute-done.4.refs_2_ = bf16[4,6272]{1,0:T(4,128)(2,1)S(1)} collective-permute-done((bf16[4,6272]{1,0:T(4,128)(2,1)S(1)}, bf16[4,6272]{1,0:T(4,128)(2,1)S(1)}, u32[]{:S(2)}, u32[]{:S(2)}) %collective-permute-start.4) | collective-permute-done | bytes 50208 | tf_op jit(solution)/shard_map/ppermute | solution.py:32
  21.6 0.0 collective-permute-done.6.refs_1_
  21.6 0.1 collective-permute-start.7
  21.8 0.4 collective-permute-start.3
  22.2 1.7 %collective-permute-start.12 = (bf16[8,16,128]{2,1,0:T(8,128)(2,1)S(1)}, bf16[8,16,128]{2,1,0:T(8,128)(2,1)S(1)}, u32[]{:S(2)}, u32[]{:S(2)}) collective-permute-start(bf16[8,16,128]{2,1,0:T(8,128)(2,1)S(1)} %slice_add_fusion.refs_6_), channel_id=1, source_target_pairs={{0,8},{4,12},{8,0},{12,4},{1,9},{5,13},{9,1},{13,5},{2,10},{6,14},... | collective-permute-start | bytes 98312 | tf_op jit(solution)/shard_map/ppermute | solution.py:32
  23.9 0.0 collective-permute-done.3.refs_1_
  23.9 0.0 collective-permute-done.7.refs_7_
  23.9 1.9 %shard_map.118 = (bf16[4,2048]{1,0:T(4,128)(2,1)S(1)}, bf16[4,4096]{1,0:T(4,128)(2,1)S(1)}) custom-call(bf16[4,6272]{1,0:T(4,128)(2,1)S(1)} %shard_map.115.refs_0_, bf16[4,6272]{1,0:T(4,128)(2,1)S(1)} %collective-permute-done.3.refs_1_, bf16[4,6272]{1,0:T(4,128)(2,1)S(1)} %collective-permute-done.4.refs_2_, ...), custom_call_target="tpu_custom_call" | custom-call | flops 33554432 | bytes 8388608 | tf_op jit(solution)/shard_map/pallas_call | solution.py:372
  25.8 1.5 %collective-permute-start.8 = (bf16[4,4096]{1,0:T(4,128)(2,1)S(1)}, bf16[4,4096]{1,0:T(4,128)(2,1)S(1)}, u32[]{:S(2)}, u32[]{:S(2)}) collective-permute-start(bf16[4,4096]{1,0:T(4,128)(2,1)S(1)} %get-tuple-element.25), channel_id=1, source_target_pairs={{0,16},{4,20},{8,24},{12,28},{16,0},{20,4},{24,8},{28,12},{1,17},{... | collective-permute-start | bytes 98312 | tf_op jit(solution)/shard_map/ppermute | solution.py:42
  27.3 3.0 %collective-permute-start.11 = (bf16[4,2048]{1,0:T(4,128)(2,1)S(1)}, bf16[4,2048]{1,0:T(4,128)(2,1)S(1)}, u32[]{:S(2)}, u32[]{:S(2)}) collective-permute-start(bf16[4,2048]{1,0:T(4,128)(2,1)S(1)} %get-tuple-element.26), channel_id=1, source_target_pairs={{12,16},{8,20},{4,24},{0,28},{28,0},{24,4},{20,8},{16,12},{13,17},... | collective-permute-start | bytes 49160 | tf_op jit(solution)/shard_map/ppermute | solution.py:42
  30.3 1.9 %collective-permute-start.10 = (bf16[4,2048]{1,0:T(4,128)(2,1)S(1)}, bf16[4,2048]{1,0:T(4,128)(2,1)S(1)}, u32[]{:S(2)}, u32[]{:S(2)}) collective-permute-start(bf16[4,2048]{1,0:T(4,128)(2,1)S(1)} %get-tuple-element.26), channel_id=1, source_target_pairs={{8,16},{12,20},{0,24},{4,28},{24,0},{28,4},{16,8},{20,12},{9,17},{... | collective-permute-start | bytes 49160 | tf_op jit(solution)/shard_map/ppermute | solution.py:42
  32.1 0.4 collective-permute-start.9
  32.6 0.0 collective-permute-done.12.refs_7_
  32.6 1.2 %collective-permute-done.11.refs_4_ = bf16[4,2048]{1,0:T(4,128)(2,1)S(1)} collective-permute-done((bf16[4,2048]{1,0:T(4,128)(2,1)S(1)}, bf16[4,2048]{1,0:T(4,128)(2,1)S(1)}, u32[]{:S(2)}, u32[]{:S(2)}) %collective-permute-start.11) | collective-permute-done | bytes 16416 | tf_op jit(solution)/shard_map/ppermute | solution.py:42
  33.7 2.1 %collective-permute-done.10.refs_3_ = bf16[4,2048]{1,0:T(4,128)(2,1)S(1)} collective-permute-done((bf16[4,2048]{1,0:T(4,128)(2,1)S(1)}, bf16[4,2048]{1,0:T(4,128)(2,1)S(1)}, u32[]{:S(2)}, u32[]{:S(2)}) %collective-permute-start.10) | collective-permute-done | bytes 16416 | tf_op jit(solution)/shard_map/ppermute | solution.py:42
  35.8 1.0 %collective-permute-done.9.refs_2_ = bf16[4,2048]{1,0:T(4,128)(2,1)S(1)} collective-permute-done((bf16[4,2048]{1,0:T(4,128)(2,1)S(1)}, bf16[4,2048]{1,0:T(4,128)(2,1)S(1)}, u32[]{:S(2)}, u32[]{:S(2)}) %collective-permute-start.9) | collective-permute-done | bytes 16416 | tf_op jit(solution)/shard_map/ppermute | solution.py:42
  36.8 0.0 collective-permute-done.8.refs_1_
  36.8 1.3 %shard_map.119 = (bf16[4,6272]{1,0:T(4,128)(2,1)S(1)}, bf16[4,2048]{1,0:T(4,128)(2,1)S(1)}) custom-call(f32[2,128]{1,0:T(2,128)S(1)} %get-tuple-element.17.refs_0_, bf16[4,4096]{1,0:T(4,128)(2,1)S(1)} %collective-permute-done.8.refs_1_, bf16[4,2048]{1,0:T(4,128)(2,1)S(1)} %collective-permute-done.9.refs_2_, ...), custom_call_target="tpu_custom_call" | custom-call | flops 100663296 | bytes 8388608 | tf_op jit(solution)/shard_map/pallas_call | solution.py:274
  38.0 0.0 collective-permute-start.15
  38.1 1.3 %collective-permute-start.14 = (bf16[4,6272]{1,0:T(4,128)(2,1)S(1)}, bf16[4,6272]{1,0:T(4,128)(2,1)S(1)}, u32[]{:S(2)}, u32[]{:S(2)}) collective-permute-start(bf16[4,6272]{1,0:T(4,128)(2,1)S(1)} %get-tuple-element.28.refs_0_), channel_id=1, source_target_pairs={{0,2},{1,3},{2,0},{3,1},{4,6},{5,7},{6,4},{7,5},{8,10},{9,11},{10,... | collective-permute-start | bytes 150536 | tf_op jit(solution)/shard_map/ppermute | solution.py:32
  39.3 0.6 %collective-permute-start.13 = (bf16[4,6272]{1,0:T(4,128)(2,1)S(1)}, bf16[4,6272]{1,0:T(4,128)(2,1)S(1)}, u32[]{:S(2)}, u32[]{:S(2)}) collective-permute-start(bf16[4,6272]{1,0:T(4,128)(2,1)S(1)} %get-tuple-element.28.refs_0_), channel_id=1, source_target_pairs={{0,1},{1,0},{2,3},{3,2},{4,5},{5,4},{6,7},{7,6},{8,9},{9,8},{10,11... | collective-permute-start | bytes 150536 | tf_op jit(solution)/shard_map/ppermute | solution.py:32
  39.9 2.2 %collective-permute-done.15.refs_3_ = bf16[4,6272]{1,0:T(4,128)(2,1)S(1)} collective-permute-done((bf16[4,6272]{1,0:T(4,128)(2,1)S(1)}, bf16[4,6272]{1,0:T(4,128)(2,1)S(1)}, u32[]{:S(2)}, u32[]{:S(2)}) %collective-permute-start.15) | collective-permute-done | bytes 50208 | tf_op jit(solution)/shard_map/ppermute | solution.py:32
  42.1 0.6 %collective-permute-done.14.refs_2_ = bf16[4,6272]{1,0:T(4,128)(2,1)S(1)} collective-permute-done((bf16[4,6272]{1,0:T(4,128)(2,1)S(1)}, bf16[4,6272]{1,0:T(4,128)(2,1)S(1)}, u32[]{:S(2)}, u32[]{:S(2)}) %collective-permute-start.14) | collective-permute-done | bytes 50208 | tf_op jit(solution)/shard_map/ppermute | solution.py:32
  42.7 0.0 collective-permute-done.13.refs_1_
  42.7 1.9 %shard_map.120 = (bf16[4,2048]{1,0:T(4,128)(2,1)S(1)}, bf16[4,4096]{1,0:T(4,128)(2,1)S(1)}) custom-call(bf16[4,6272]{1,0:T(4,128)(2,1)S(1)} %get-tuple-element.28.refs_0_, bf16[4,6272]{1,0:T(4,128)(2,1)S(1)} %collective-permute-done.13.refs_1_, bf16[4,6272]{1,0:T(4,128)(2,1)S(1)} %collective-permute-done.14.refs_2_, ...), custom_call_target="tpu_custom_call" | custom-call | flops 33554432 | bytes 8388608 | tf_op jit(solution)/shard_map/pallas_call | solution.py:372
  44.6 0.7 %collective-permute-start.16 = (bf16[4,4096]{1,0:T(4,128)(2,1)S(1)}, bf16[4,4096]{1,0:T(4,128)(2,1)S(1)}, u32[]{:S(2)}, u32[]{:S(2)}) collective-permute-start(bf16[4,4096]{1,0:T(4,128)(2,1)S(1)} %get-tuple-element.30), channel_id=1, source_target_pairs={{0,16},{4,20},{8,24},{12,28},{16,0},{20,4},{24,8},{28,12},{1,17},{... | collective-permute-start | bytes 98312 | tf_op jit(solution)/shard_map/ppermute | solution.py:42
  45.3 1.3 %collective-permute-start.19 = (bf16[4,2048]{1,0:T(4,128)(2,1)S(1)}, bf16[4,2048]{1,0:T(4,128)(2,1)S(1)}, u32[]{:S(2)}, u32[]{:S(2)}) collective-permute-start(bf16[4,2048]{1,0:T(4,128)(2,1)S(1)} %get-tuple-element.31), channel_id=1, source_target_pairs={{12,16},{8,20},{4,24},{0,28},{28,0},{24,4},{20,8},{16,12},{13,17},... | collective-permute-start | bytes 49160 | tf_op jit(solution)/shard_map/ppermute | solution.py:42
  46.6 1.5 %collective-permute-start.18 = (bf16[4,2048]{1,0:T(4,128)(2,1)S(1)}, bf16[4,2048]{1,0:T(4,128)(2,1)S(1)}, u32[]{:S(2)}, u32[]{:S(2)}) collective-permute-start(bf16[4,2048]{1,0:T(4,128)(2,1)S(1)} %get-tuple-element.31), channel_id=1, source_target_pairs={{8,16},{12,20},{0,24},{4,28},{24,0},{28,4},{16,8},{20,12},{9,17},{... | collective-permute-start | bytes 49160 | tf_op jit(solution)/shard_map/ppermute | solution.py:42
  48.1 3.3 %collective-permute-start.17 = (bf16[4,2048]{1,0:T(4,128)(2,1)S(1)}, bf16[4,2048]{1,0:T(4,128)(2,1)S(1)}, u32[]{:S(2)}, u32[]{:S(2)}) collective-permute-start(bf16[4,2048]{1,0:T(4,128)(2,1)S(1)} %get-tuple-element.31), channel_id=1, source_target_pairs={{4,16},{0,20},{12,24},{8,28},{20,0},{16,4},{28,8},{24,12},{5,17},{... | collective-permute-start | bytes 49160 | tf_op jit(solution)/shard_map/ppermute | solution.py:42
  51.4 0.5 collective-permute-done.19.refs_3_
  51.8 0.3 collective-permute-done.18.refs_2_
  52.1 1.0 %collective-permute-done.17.refs_1_ = bf16[4,2048]{1,0:T(4,128)(2,1)S(1)} collective-permute-done((bf16[4,2048]{1,0:T(4,128)(2,1)S(1)}, bf16[4,2048]{1,0:T(4,128)(2,1)S(1)}, u32[]{:S(2)}, u32[]{:S(2)}) %collective-permute-start.17) | collective-permute-done | bytes 16416 | tf_op jit(solution)/shard_map/ppermute | solution.py:42
  53.1 0.0 collective-permute-done.16.refs_0_
  53.1 0.6 %shard_map.121 = (bf16[1,4,2048]{2,1,0:T(4,128)(2,1)}, bf16[1,4,2048]{2,1,0:T(4,128)(2,1)}) custom-call(bf16[4,4096]{1,0:T(4,128)(2,1)S(1)} %collective-permute-done.16.refs_0_, bf16[4,2048]{1,0:T(4,128)(2,1)S(1)} %collective-permute-done.17.refs_1_, bf16[4,2048]{1,0:T(4,128)(2,1)S(1)} %collective-permute-done.18.refs_2_, ...), custom_call_target="tpu_custom_call" | custom-call | tf_op jit(solution)/shard_map/pallas_call | solution.py:292
  (3 shorter events, 0.0 us)
Async XLA Ops:
  2.2 11.9 %collective-permute-start = (bf16[24,16,128]{2,1,0:T(8,128)(2,1)S(1)}, bf16[24,16,128]{2,1,0:T(8,128)(2,1)S(1)}, u32[]{:S(2)}, u32[]{:S(2)}) collective-permute-start(bf16[24,16,128]{2,1,0:T(8,128)(2,1)S(1)} %get-tuple-element.20), channel_id=1, source_target_pairs={{0,4},{4,0},{8,12},{12,8},{1,5},{5,1},{9,13},{13,9},{2,6},{6,2},{1... | collective-permute-start | bytes 294920 | tf_op jit(solution)/shard_map/ppermute | solution.py:32
  5.3 8.6 %collective-permute-start.1 = (bf16[16,16,128]{2,1,0:T(8,128)(2,1)S(1)}, bf16[16,16,128]{2,1,0:T(8,128)(2,1)S(1)}, u32[]{:S(2)}, u32[]{:S(2)}) collective-permute-start(bf16[16,16,128]{2,1,0:T(8,128)(2,1)S(1)} %get-tuple-element.21), channel_id=1, source_target_pairs={{0,8},{4,12},{8,0},{12,4},{1,9},{5,13},{9,1},{13,5},{2,10},{6,14},... | collective-permute-start | bytes 196616 | tf_op jit(solution)/shard_map/ppermute | solution.py:32
  7.8 6.2 %collective-permute-start.2 = (bf16[16,16,128]{2,1,0:T(8,128)(2,1)S(1)}, bf16[16,16,128]{2,1,0:T(8,128)(2,1)S(1)}, u32[]{:S(2)}, u32[]{:S(2)}) collective-permute-start(bf16[16,16,128]{2,1,0:T(8,128)(2,1)S(1)} %get-tuple-element.22), channel_id=1, source_target_pairs={{0,12},{4,8},{8,4},{12,0},{1,13},{5,9},{9,5},{13,1},{2,14},{6,10},... | collective-permute-start | bytes 196616 | tf_op jit(solution)/shard_map/ppermute | solution.py:32
  14.0 7.6 %collective-permute-start.6 = (bf16[4,8,16,128]{3,2,1,0:T(8,128)(2,1)S(1)}, bf16[4,8,16,128]{3,2,1,0:T(8,128)(2,1)S(1)}, u32[]{:S(2)}, u32[]{:S(2)}) collective-permute-start(bf16[4,8,16,128]{3,2,1,0:T(8,128)(2,1)S(1)} %shard_map.116.refs_0_), channel_id=1, source_target_pairs={{0,2},{1,3},{2,0},{3,1},{4,6},{5,7},{6,4},{7,5},{8,10},{9,11},{10,... | collective-permute-start | bytes 393224 | tf_op jit(solution)/shard_map/ppermute | solution.py:32
  17.0 3.5 %collective-permute-start.5 = (bf16[4,6272]{1,0:T(4,128)(2,1)S(1)}, bf16[4,6272]{1,0:T(4,128)(2,1)S(1)}, u32[]{:S(2)}, u32[]{:S(2)}) collective-permute-start(bf16[4,6272]{1,0:T(4,128)(2,1)S(1)} %shard_map.115.refs_0_), channel_id=1, source_target_pairs={{0,3},{1,2},{2,1},{3,0},{4,7},{5,6},{6,5},{7,4},{8,11},{9,10},{10,... | collective-permute-start | bytes 150536 | tf_op jit(solution)/shard_map/ppermute | solution.py:32
  17.0 4.6 %collective-permute-start.4 = (bf16[4,6272]{1,0:T(4,128)(2,1)S(1)}, bf16[4,6272]{1,0:T(4,128)(2,1)S(1)}, u32[]{:S(2)}, u32[]{:S(2)}) collective-permute-start(bf16[4,6272]{1,0:T(4,128)(2,1)S(1)} %shard_map.115.refs_0_), channel_id=1, source_target_pairs={{0,2},{1,3},{2,0},{3,1},{4,6},{5,7},{6,4},{7,5},{8,10},{9,11},{10,... | collective-permute-start | bytes 150536 | tf_op jit(solution)/shard_map/ppermute | solution.py:32
  21.6 2.3 %collective-permute-start.7 = (bf16[8,8,16,128]{3,2,1,0:T(8,128)(2,1)S(1)}, bf16[8,8,16,128]{3,2,1,0:T(8,128)(2,1)S(1)}, u32[]{:S(2)}, u32[]{:S(2)}) collective-permute-start(bf16[8,8,16,128]{3,2,1,0:T(8,128)(2,1)S(1)} %bitcast.9), channel_id=1, source_target_pairs={{0,1},{1,0},{2,3},{3,2},{4,5},{5,4},{6,7},{7,6},{8,9},{9,8},{10,11... | collective-permute-start | bytes 786440 | tf_op jit(solution)/shard_map/ppermute | solution.py:32
  21.8 2.1 %collective-permute-start.3 = (bf16[4,6272]{1,0:T(4,128)(2,1)S(1)}, bf16[4,6272]{1,0:T(4,128)(2,1)S(1)}, u32[]{:S(2)}, u32[]{:S(2)}) collective-permute-start(bf16[4,6272]{1,0:T(4,128)(2,1)S(1)} %shard_map.115.refs_0_), channel_id=1, source_target_pairs={{0,1},{1,0},{2,3},{3,2},{4,5},{5,4},{6,7},{7,6},{8,9},{9,8},{10,11... | collective-permute-start | bytes 150536 | tf_op jit(solution)/shard_map/ppermute | solution.py:32
  22.2 10.3 %collective-permute-start.12 = (bf16[8,16,128]{2,1,0:T(8,128)(2,1)S(1)}, bf16[8,16,128]{2,1,0:T(8,128)(2,1)S(1)}, u32[]{:S(2)}, u32[]{:S(2)}) collective-permute-start(bf16[8,16,128]{2,1,0:T(8,128)(2,1)S(1)} %slice_add_fusion.refs_6_), channel_id=1, source_target_pairs={{0,8},{4,12},{8,0},{12,4},{1,9},{5,13},{9,1},{13,5},{2,10},{6,14},... | collective-permute-start | bytes 98312 | tf_op jit(solution)/shard_map/ppermute | solution.py:32
  25.8 11.0 %collective-permute-start.8 = (bf16[4,4096]{1,0:T(4,128)(2,1)S(1)}, bf16[4,4096]{1,0:T(4,128)(2,1)S(1)}, u32[]{:S(2)}, u32[]{:S(2)}) collective-permute-start(bf16[4,4096]{1,0:T(4,128)(2,1)S(1)} %get-tuple-element.25), channel_id=1, source_target_pairs={{0,16},{4,20},{8,24},{12,28},{16,0},{20,4},{24,8},{28,12},{1,17},{... | collective-permute-start | bytes 98312 | tf_op jit(solution)/shard_map/ppermute | solution.py:42
  27.3 6.4 %collective-permute-start.11 = (bf16[4,2048]{1,0:T(4,128)(2,1)S(1)}, bf16[4,2048]{1,0:T(4,128)(2,1)S(1)}, u32[]{:S(2)}, u32[]{:S(2)}) collective-permute-start(bf16[4,2048]{1,0:T(4,128)(2,1)S(1)} %get-tuple-element.26), channel_id=1, source_target_pairs={{12,16},{8,20},{4,24},{0,28},{28,0},{24,4},{20,8},{16,12},{13,17},... | collective-permute-start | bytes 49160 | tf_op jit(solution)/shard_map/ppermute | solution.py:42
  30.3 5.5 %collective-permute-start.10 = (bf16[4,2048]{1,0:T(4,128)(2,1)S(1)}, bf16[4,2048]{1,0:T(4,128)(2,1)S(1)}, u32[]{:S(2)}, u32[]{:S(2)}) collective-permute-start(bf16[4,2048]{1,0:T(4,128)(2,1)S(1)} %get-tuple-element.26), channel_id=1, source_target_pairs={{8,16},{12,20},{0,24},{4,28},{24,0},{28,4},{16,8},{20,12},{9,17},{... | collective-permute-start | bytes 49160 | tf_op jit(solution)/shard_map/ppermute | solution.py:42
  32.1 4.6 %collective-permute-start.9 = (bf16[4,2048]{1,0:T(4,128)(2,1)S(1)}, bf16[4,2048]{1,0:T(4,128)(2,1)S(1)}, u32[]{:S(2)}, u32[]{:S(2)}) collective-permute-start(bf16[4,2048]{1,0:T(4,128)(2,1)S(1)} %get-tuple-element.26), channel_id=1, source_target_pairs={{4,16},{0,20},{12,24},{8,28},{20,0},{16,4},{28,8},{24,12},{5,17},{... | collective-permute-start | bytes 49160 | tf_op jit(solution)/shard_map/ppermute | solution.py:42
  38.0 4.0 %collective-permute-start.15 = (bf16[4,6272]{1,0:T(4,128)(2,1)S(1)}, bf16[4,6272]{1,0:T(4,128)(2,1)S(1)}, u32[]{:S(2)}, u32[]{:S(2)}) collective-permute-start(bf16[4,6272]{1,0:T(4,128)(2,1)S(1)} %get-tuple-element.28.refs_0_), channel_id=1, source_target_pairs={{0,3},{1,2},{2,1},{3,0},{4,7},{5,6},{6,5},{7,4},{8,11},{9,10},{10,... | collective-permute-start | bytes 150536 | tf_op jit(solution)/shard_map/ppermute | solution.py:32
  38.1 4.7 %collective-permute-start.14 = (bf16[4,6272]{1,0:T(4,128)(2,1)S(1)}, bf16[4,6272]{1,0:T(4,128)(2,1)S(1)}, u32[]{:S(2)}, u32[]{:S(2)}) collective-permute-start(bf16[4,6272]{1,0:T(4,128)(2,1)S(1)} %get-tuple-element.28.refs_0_), channel_id=1, source_target_pairs={{0,2},{1,3},{2,0},{3,1},{4,6},{5,7},{6,4},{7,5},{8,10},{9,11},{10,... | collective-permute-start | bytes 150536 | tf_op jit(solution)/shard_map/ppermute | solution.py:32
  39.3 3.4 %collective-permute-start.13 = (bf16[4,6272]{1,0:T(4,128)(2,1)S(1)}, bf16[4,6272]{1,0:T(4,128)(2,1)S(1)}, u32[]{:S(2)}, u32[]{:S(2)}) collective-permute-start(bf16[4,6272]{1,0:T(4,128)(2,1)S(1)} %get-tuple-element.28.refs_0_), channel_id=1, source_target_pairs={{0,1},{1,0},{2,3},{3,2},{4,5},{5,4},{6,7},{7,6},{8,9},{9,8},{10,11... | collective-permute-start | bytes 150536 | tf_op jit(solution)/shard_map/ppermute | solution.py:32
  44.6 8.5 %collective-permute-start.16 = (bf16[4,4096]{1,0:T(4,128)(2,1)S(1)}, bf16[4,4096]{1,0:T(4,128)(2,1)S(1)}, u32[]{:S(2)}, u32[]{:S(2)}) collective-permute-start(bf16[4,4096]{1,0:T(4,128)(2,1)S(1)} %get-tuple-element.30), channel_id=1, source_target_pairs={{0,16},{4,20},{8,24},{12,28},{16,0},{20,4},{24,8},{28,12},{1,17},{... | collective-permute-start | bytes 98312 | tf_op jit(solution)/shard_map/ppermute | solution.py:42
  45.3 6.5 %collective-permute-start.19 = (bf16[4,2048]{1,0:T(4,128)(2,1)S(1)}, bf16[4,2048]{1,0:T(4,128)(2,1)S(1)}, u32[]{:S(2)}, u32[]{:S(2)}) collective-permute-start(bf16[4,2048]{1,0:T(4,128)(2,1)S(1)} %get-tuple-element.31), channel_id=1, source_target_pairs={{12,16},{8,20},{4,24},{0,28},{28,0},{24,4},{20,8},{16,12},{13,17},... | collective-permute-start | bytes 49160 | tf_op jit(solution)/shard_map/ppermute | solution.py:42
  46.6 5.5 %collective-permute-start.18 = (bf16[4,2048]{1,0:T(4,128)(2,1)S(1)}, bf16[4,2048]{1,0:T(4,128)(2,1)S(1)}, u32[]{:S(2)}, u32[]{:S(2)}) collective-permute-start(bf16[4,2048]{1,0:T(4,128)(2,1)S(1)} %get-tuple-element.31), channel_id=1, source_target_pairs={{8,16},{12,20},{0,24},{4,28},{24,0},{28,4},{16,8},{20,12},{9,17},{... | collective-permute-start | bytes 49160 | tf_op jit(solution)/shard_map/ppermute | solution.py:42
  48.1 5.0 %collective-permute-start.17 = (bf16[4,2048]{1,0:T(4,128)(2,1)S(1)}, bf16[4,2048]{1,0:T(4,128)(2,1)S(1)}, u32[]{:S(2)}, u32[]{:S(2)}) collective-permute-start(bf16[4,2048]{1,0:T(4,128)(2,1)S(1)} %get-tuple-element.31), channel_id=1, source_target_pairs={{4,16},{0,20},{12,24},{8,28},{20,0},{16,4},{28,8},{24,12},{5,17},{... | collective-permute-start | bytes 49160 | tf_op jit(solution)/shard_map/ppermute | solution.py:42

commit v11 on v10

--- a/solution.py
+++ b/solution.py
@@ -221,20 +221,20 @@
 
 
 def first_kernel(tensors, held, lengths_ref, h_ref, *refs):
-    pieces, (w_ref, out_ref) = refs[:tensors], refs[tensors:]
+    pieces, (w_ref, _, out_ref) = refs[:tensors], refs[tensors:]
     query_sums([held] * tensors, lengths_ref[0:1], h_ref[...].astype(F32), pieces, w_ref, out_ref)
 
 
-def first_sums(held, lengths, h, pieces, w):
+def first_sums(held, lengths, h, pieces, w, after):
     tensors = len(pieces)
     return pl.pallas_call(
         lambda *refs: first_kernel(tensors, held, *refs),
         out_shape=shape((h.shape[0], 3 * w.shape[1] + HD)),
-        in_specs=[VMEM] * (tensors + 3),
+        in_specs=[VMEM] * (tensors + 3) + [pl.BlockSpec(memory_space=pl.ANY)],
         out_specs=VMEM,
         compiler_params=PARAMS,
         cost_estimate=cost(24 * w.size, 2 * w.size),
-    )(lengths, h, *pieces, w)
+    )(lengths, h, *pieces, w, after)
 
 
 def arrive(arrivals, following, tick):
@@ -419,7 +419,7 @@
     arrivals = None
     for tick in range(sections):
         if tick == 0:
-            sums = first_sums(held, lengths, carry, got, wq_held)
+            sums = first_sums(held, lengths, carry, got, wq_held, later[0] if later else kv)
         else:
             sums, carry = later_sums(tick, lengths, arrivals, following, later, wq_held)
         pieces = [sums] + [swapped(sums, "replica", d) for d in range(1, replicas)]
@@ -428,7 +428,7 @@
                 turns = turns + [turn ^ bit for turn in turns]
                 caches, bit = [kv, waiting], bit // 2
                 if bit:
-                    both = join(caches, kv.shape[0], pieces[2:])
+                    both = join(caches, kv.shape[0], pieces[2:] + later[-1:])
                     kv = both.reshape((-1,) + both.shape[2:])
                     waiting = swapped(kv, "replica", bit)
         out, full = attend(

time: 53.9 us -> 54.6 us (1.013)
  transfers between devices with their start and end apart: 20 -> 20, of which waited for: 11 -> 10; matrix products, arithmetic and copies ran while one was open for 0% -> 0% of each run, Pallas kernels for 17% -> 13%
where the time goes in v11:
time: 54.6 us; the launch traced here: 54.4 us
  starting transfers between devices  25.6 us (47%)
  Pallas kernels  14.5 us (27%)
  waiting for transfers between devices  13.6 us (25%)
  between operations  0.7 us (1%)
    ppermute x8, starting transfers between devices, from_behind(): return lax.ppermute(block, ('section', 'tensor'), route)  13.5 us
    ppermute x12, starting transfers between devices, swapped(): return lax.ppermute(block, axis, route)  12.1 us
    ppermute x12, waiting for transfers between devices, swapped(): return lax.ppermute(block, axis, route)  7.3 us
    ppermute x8, waiting for transfers between devices, from_behind(): return lax.ppermute(block, ('section', 'tensor'), route)  6.31 us
    pallas_call x1, Pallas kernels, hold(): pl.pallas_call(lambda *refs: hold_kernel(parts, *refs), out_shape=[pltpu....  6.04 us
    pallas_call x2, Pallas kernels, attend(): pl.pallas_call(lambda *refs: attend_kernel(dims, turns, tick, *refs), out...  3.71 us
    pallas_call x1, Pallas kernels, pack(): pl.pallas_call(lambda *refs: pack_kernel(dims, *refs), out_shape=out_shap...  1.52 us
    pallas_call x1, Pallas kernels, later_sums(): pl.pallas_call(lambda *refs: later_kernel(len(arrivals), tick, *refs), ou...  1.28 us
  transfers between devices with their start and end apart: 20, of which 10 were waited for; matrix products, arithmetic and copies ran while one was open for 0% of the time, Pallas kernels for 13%

profile of v11, /device:TPU:0, one launch (start us, length us, event | category | flops | bytes accessed | tf_op | source)
XLA Modules:
  0.0 54.4 jit_solution(12601337340570538174)
XLA Ops:
  0.6 1.5 %shard_map.113 = (bf16[24,16,128]{2,1,0:T(8,128)(2,1)S(1)}, bf16[24,16,128]{2,1,0:T(8,128)(2,1)S(1)}, bf16[16,16,128]{2,1,0:T(8,128)(2,1)S(1)}, bf16[16,16,128]{...) custom-call(s32[2,4]{1,0:T(2,128)} %refs_0_.1, ...), custom_call_target="tpu_custom_call" | custom-call | bytes 819200 | tf_op jit(solution)/shard_map/pallas_call | solution.py:127
  2.2 3.1 %collective-permute-start = (bf16[24,16,128]{2,1,0:T(8,128)(2,1)S(1)}, bf16[24,16,128]{2,1,0:T(8,128)(2,1)S(1)}, u32[]{:S(2)}, u32[]{:S(2)}) collective-permute-start(bf16[24,16,128]{2,1,0:T(8,128)(2,1)S(1)} %get-tuple-element.20), channel_id=1, source_target_pairs={{0,4},{4,0},{8,12},{12,8},{1,5},{5,1},{9,13},{13,9},{2,6},{6,2},{1... | collective-permute-start | bytes 294920 | tf_op jit(solution)/shard_map/ppermute | solution.py:32
  5.3 2.6 %collective-permute-start.1 = (bf16[16,16,128]{2,1,0:T(8,128)(2,1)S(1)}, bf16[16,16,128]{2,1,0:T(8,128)(2,1)S(1)}, u32[]{:S(2)}, u32[]{:S(2)}) collective-permute-start(bf16[16,16,128]{2,1,0:T(8,128)(2,1)S(1)} %get-tuple-element.21), channel_id=1, source_target_pairs={{0,8},{4,12},{8,0},{12,4},{1,9},{5,13},{9,1},{13,5},{2,10},{6,14},... | collective-permute-start | bytes 196616 | tf_op jit(solution)/shard_map/ppermute | solution.py:32
  7.8 0.0 collective-permute-start.2
  7.8 6.0 %shard_map.114 = (bf16[2048,2048]{1,0:T(8,128)(2,1)S(1)}, bf16[2048,2048]{1,0:T(8,128)(2,1)S(1)}) custom-call(bf16[24,16,128]{2,1,0:T(8,128)(2,1)S(1)} %get-tuple-element.19.refs_0_.refs_2_, bf16[2048,2048]{1,0:T(8,128)(2,1)} %bitcast.12, bf16[2048,2048]{1,0:T(8,128)(2,1)} %bitcast.13), custom_call_target="tpu_custom_call" | custom-call | bytes 16777216 | tf_op jit(solution)/shard_map/pallas_call | solution.py:175
  13.9 0.0 collective-permute-done.1.refs_4_.refs_2_
  13.9 0.1 collective-permute-done.2.refs_5_.refs_3_
  14.0 0.0 collective-permute-done.refs_3_.refs_1_
  14.0 1.7 %collective-permute-start.6 = (bf16[4,8,16,128]{3,2,1,0:T(8,128)(2,1)S(1)}, bf16[4,8,16,128]{3,2,1,0:T(8,128)(2,1)S(1)}, u32[]{:S(2)}, u32[]{:S(2)}) collective-permute-start(bf16[4,8,16,128]{3,2,1,0:T(8,128)(2,1)S(1)} %shard_map.116.refs_0_), channel_id=1, source_target_pairs={{0,2},{1,3},{2,0},{3,1},{4,6},{5,7},{6,4},{7,5},{8,10},{9,11},{10,... | collective-permute-start | bytes 393224 | tf_op jit(solution)/shard_map/ppermute | solution.py:32
  15.8 1.3 %shard_map.115.refs_0_ = bf16[4,6272]{1,0:T(4,128)(2,1)S(1)} custom-call(f32[2,128]{1,0:T(2,128)S(1)} %get-tuple-element.17.refs_0_, bf16[4,2048]{1,0:T(4,128)(2,1)S(1)} %get-tuple-element.18.refs_1_.refs_4_, bf16[24,16,128]{2,1,0:T(8,128)(2,1)S(1)} %get-tuple-element.19.refs_0_.refs_2_, bf16[24,16,128]{2,1,0:T(8,128)(2,1)S(1)} %collective-permute-done.refs_3_.refs_1_, ...), custom_call_target="tpu_custom_call" | custom-call | flops 100663296 | bytes 8388608 | tf_op jit(solution)/shard_map/pallas_call | solution.py:230
  17.0 0.0 collective-permute-start.5
  17.0 0.4 collective-permute-start.4
  17.4 1.8 %collective-permute-start.7 = (bf16[8,16,128]{2,1,0:T(8,128)(2,1)S(1)}, bf16[8,16,128]{2,1,0:T(8,128)(2,1)S(1)}, u32[]{:S(2)}, u32[]{:S(2)}) collective-permute-start(bf16[8,16,128]{2,1,0:T(8,128)(2,1)S(1)} %slice_add_fusion.refs_7_.refs_6_), channel_id=1, source_target_pairs={{0,8},{4,12},{8,0},{12,4},{1,9},{5,13},{9,1},{13,5},{2,10},{6,14},... | collective-permute-start | bytes 98312 | tf_op jit(solution)/shard_map/ppermute | solution.py:32
  19.3 3.0 %collective-permute-done.7.refs_4_.refs_7_ = bf16[8,16,128]{2,1,0:T(8,128)(2,1)S(1)} collective-permute-done((bf16[8,16,128]{2,1,0:T(8,128)(2,1)S(1)}, bf16[8,16,128]{2,1,0:T(8,128)(2,1)S(1)}, u32[]{:S(2)}, u32[]{:S(2)}) %collective-permute-start.7) | collective-permute-done | bytes 32800 | tf_op jit(solution)/shard_map/ppermute | solution.py:32
  22.3 0.0 collective-permute-done.5.refs_3_
  22.3 0.0 collective-permute-done.4.refs_2_
  22.3 0.0 collective-permute-done.6.refs_1_
  22.3 0.4 collective-permute-start.8
  22.7 0.2 collective-permute-start.3
  22.9 1.1 %collective-permute-done.3.refs_1_ = bf16[4,6272]{1,0:T(4,128)(2,1)S(1)} collective-permute-done((bf16[4,6272]{1,0:T(4,128)(2,1)S(1)}, bf16[4,6272]{1,0:T(4,128)(2,1)S(1)}, u32[]{:S(2)}, u32[]{:S(2)}) %collective-permute-start.3) | collective-permute-done | bytes 50208 | tf_op jit(solution)/shard_map/ppermute | solution.py:32
  24.0 0.0 collective-permute-done.8.refs_7_
  24.0 1.9 %shard_map.118 = (bf16[4,2048]{1,0:T(4,128)(2,1)S(1)}, bf16[4,4096]{1,0:T(4,128)(2,1)S(1)}) custom-call(bf16[4,6272]{1,0:T(4,128)(2,1)S(1)} %shard_map.115.refs_0_, bf16[4,6272]{1,0:T(4,128)(2,1)S(1)} %collective-permute-done.3.refs_1_, bf16[4,6272]{1,0:T(4,128)(2,1)S(1)} %collective-permute-done.4.refs_2_, ...), custom_call_target="tpu_custom_call" | custom-call | flops 33554432 | bytes 8388608 | tf_op jit(solution)/shard_map/pallas_call | solution.py:372
  25.8 1.7 %collective-permute-start.9 = (bf16[4,4096]{1,0:T(4,128)(2,1)S(1)}, bf16[4,4096]{1,0:T(4,128)(2,1)S(1)}, u32[]{:S(2)}, u32[]{:S(2)}) collective-permute-start(bf16[4,4096]{1,0:T(4,128)(2,1)S(1)} %get-tuple-element.25), channel_id=1, source_target_pairs={{0,16},{4,20},{8,24},{12,28},{16,0},{20,4},{24,8},{28,12},{1,17},{... | collective-permute-start | bytes 98312 | tf_op jit(solution)/shard_map/ppermute | solution.py:42
  27.5 3.6 %collective-permute-start.12 = (bf16[4,2048]{1,0:T(4,128)(2,1)S(1)}, bf16[4,2048]{1,0:T(4,128)(2,1)S(1)}, u32[]{:S(2)}, u32[]{:S(2)}) collective-permute-start(bf16[4,2048]{1,0:T(4,128)(2,1)S(1)} %get-tuple-element.26), channel_id=1, source_target_pairs={{12,16},{8,20},{4,24},{0,28},{28,0},{24,4},{20,8},{16,12},{13,17},... | collective-permute-start | bytes 49160 | tf_op jit(solution)/shard_map/ppermute | solution.py:42
  31.1 0.1 collective-permute-start.11
  31.2 1.4 %collective-permute-start.10 = (bf16[4,2048]{1,0:T(4,128)(2,1)S(1)}, bf16[4,2048]{1,0:T(4,128)(2,1)S(1)}, u32[]{:S(2)}, u32[]{:S(2)}) collective-permute-start(bf16[4,2048]{1,0:T(4,128)(2,1)S(1)} %get-tuple-element.26), channel_id=1, source_target_pairs={{4,16},{0,20},{12,24},{8,28},{20,0},{16,4},{28,8},{24,12},{5,17},{... | collective-permute-start | bytes 49160 | tf_op jit(solution)/shard_map/ppermute | solution.py:42
  32.6 1.3 %collective-permute-done.12.refs_4_ = bf16[4,2048]{1,0:T(4,128)(2,1)S(1)} collective-permute-done((bf16[4,2048]{1,0:T(4,128)(2,1)S(1)}, bf16[4,2048]{1,0:T(4,128)(2,1)S(1)}, u32[]{:S(2)}, u32[]{:S(2)}) %collective-permute-start.12) | collective-permute-done | bytes 16416 | tf_op jit(solution)/shard_map/ppermute | solution.py:42
  33.9 2.7 %collective-permute-done.11.refs_3_ = bf16[4,2048]{1,0:T(4,128)(2,1)S(1)} collective-permute-done((bf16[4,2048]{1,0:T(4,128)(2,1)S(1)}, bf16[4,2048]{1,0:T(4,128)(2,1)S(1)}, u32[]{:S(2)}, u32[]{:S(2)}) %collective-permute-start.11) | collective-permute-done | bytes 16416 | tf_op jit(solution)/shard_map/ppermute | solution.py:42
  36.6 0.0 collective-permute-done.10.refs_2_
  36.6 0.0 collective-permute-done.9.refs_1_
  36.6 1.3 %shard_map.119 = (bf16[4,6272]{1,0:T(4,128)(2,1)S(1)}, bf16[4,2048]{1,0:T(4,128)(2,1)S(1)}) custom-call(f32[2,128]{1,0:T(2,128)S(1)} %get-tuple-element.17.refs_0_, bf16[4,4096]{1,0:T(4,128)(2,1)S(1)} %collective-permute-done.9.refs_1_, bf16[4,2048]{1,0:T(4,128)(2,1)S(1)} %collective-permute-done.10.refs_2_, ...), custom_call_target="tpu_custom_call" | custom-call | flops 100663296 | bytes 8388608 | tf_op jit(solution)/shard_map/pallas_call | solution.py:274
  37.9 0.0 collective-permute-start.15
  37.9 1.6 %collective-permute-start.14 = (bf16[4,6272]{1,0:T(4,128)(2,1)S(1)}, bf16[4,6272]{1,0:T(4,128)(2,1)S(1)}, u32[]{:S(2)}, u32[]{:S(2)}) collective-permute-start(bf16[4,6272]{1,0:T(4,128)(2,1)S(1)} %get-tuple-element.28.refs_0_), channel_id=1, source_target_pairs={{0,2},{1,3},{2,0},{3,1},{4,6},{5,7},{6,4},{7,5},{8,10},{9,11},{10,... | collective-permute-start | bytes 150536 | tf_op jit(solution)/shard_map/ppermute | solution.py:32
  39.4 0.3 collective-permute-start.13
  39.8 2.1 %collective-permute-done.15.refs_3_ = bf16[4,6272]{1,0:T(4,128)(2,1)S(1)} collective-permute-done((bf16[4,6272]{1,0:T(4,128)(2,1)S(1)}, bf16[4,6272]{1,0:T(4,128)(2,1)S(1)}, u32[]{:S(2)}, u32[]{:S(2)}) %collective-permute-start.15) | collective-permute-done | bytes 50208 | tf_op jit(solution)/shard_map/ppermute | solution.py:32
  41.9 1.0 %collective-permute-done.14.refs_2_ = bf16[4,6272]{1,0:T(4,128)(2,1)S(1)} collective-permute-done((bf16[4,6272]{1,0:T(4,128)(2,1)S(1)}, bf16[4,6272]{1,0:T(4,128)(2,1)S(1)}, u32[]{:S(2)}, u32[]{:S(2)}) %collective-permute-start.14) | collective-permute-done | bytes 50208 | tf_op jit(solution)/shard_map/ppermute | solution.py:32
  42.8 0.0 collective-permute-done.13.refs_1_
  42.9 1.9 %shard_map.120 = (bf16[4,2048]{1,0:T(4,128)(2,1)S(1)}, bf16[4,4096]{1,0:T(4,128)(2,1)S(1)}) custom-call(bf16[4,6272]{1,0:T(4,128)(2,1)S(1)} %get-tuple-element.28.refs_0_, bf16[4,6272]{1,0:T(4,128)(2,1)S(1)} %collective-permute-done.13.refs_1_, bf16[4,6272]{1,0:T(4,128)(2,1)S(1)} %collective-permute-done.14.refs_2_, ...), custom_call_target="tpu_custom_call" | custom-call | flops 33554432 | bytes 8388608 | tf_op jit(solution)/shard_map/pallas_call | solution.py:372
  44.7 1.5 %collective-permute-start.16 = (bf16[4,4096]{1,0:T(4,128)(2,1)S(1)}, bf16[4,4096]{1,0:T(4,128)(2,1)S(1)}, u32[]{:S(2)}, u32[]{:S(2)}) collective-permute-start(bf16[4,4096]{1,0:T(4,128)(2,1)S(1)} %get-tuple-element.30), channel_id=1, source_target_pairs={{0,16},{4,20},{8,24},{12,28},{16,0},{20,4},{24,8},{28,12},{1,17},{... | collective-permute-start | bytes 98312 | tf_op jit(solution)/shard_map/ppermute | solution.py:42
  46.2 1.4 %collective-permute-start.19 = (bf16[4,2048]{1,0:T(4,128)(2,1)S(1)}, bf16[4,2048]{1,0:T(4,128)(2,1)S(1)}, u32[]{:S(2)}, u32[]{:S(2)}) collective-permute-start(bf16[4,2048]{1,0:T(4,128)(2,1)S(1)} %get-tuple-element.31), channel_id=1, source_target_pairs={{12,16},{8,20},{4,24},{0,28},{28,0},{24,4},{20,8},{16,12},{13,17},... | collective-permute-start | bytes 49160 | tf_op jit(solution)/shard_map/ppermute | solution.py:42
  47.6 1.5 %collective-permute-start.18 = (bf16[4,2048]{1,0:T(4,128)(2,1)S(1)}, bf16[4,2048]{1,0:T(4,128)(2,1)S(1)}, u32[]{:S(2)}, u32[]{:S(2)}) collective-permute-start(bf16[4,2048]{1,0:T(4,128)(2,1)S(1)} %get-tuple-element.31), channel_id=1, source_target_pairs={{8,16},{12,20},{0,24},{4,28},{24,0},{28,4},{16,8},{20,12},{9,17},{... | collective-permute-start | bytes 49160 | tf_op jit(solution)/shard_map/ppermute | solution.py:42
  49.1 2.3 %collective-permute-start.17 = (bf16[4,2048]{1,0:T(4,128)(2,1)S(1)}, bf16[4,2048]{1,0:T(4,128)(2,1)S(1)}, u32[]{:S(2)}, u32[]{:S(2)}) collective-permute-start(bf16[4,2048]{1,0:T(4,128)(2,1)S(1)} %get-tuple-element.31), channel_id=1, source_target_pairs={{4,16},{0,20},{12,24},{8,28},{20,0},{16,4},{28,8},{24,12},{5,17},{... | collective-permute-start | bytes 49160 | tf_op jit(solution)/shard_map/ppermute | solution.py:42
  51.5 1.2 %collective-permute-done.19.refs_3_ = bf16[4,2048]{1,0:T(4,128)(2,1)S(1)} collective-permute-done((bf16[4,2048]{1,0:T(4,128)(2,1)S(1)}, bf16[4,2048]{1,0:T(4,128)(2,1)S(1)}, u32[]{:S(2)}, u32[]{:S(2)}) %collective-permute-start.19) | collective-permute-done | bytes 16416 | tf_op jit(solution)/shard_map/ppermute | solution.py:42
  52.7 0.5 collective-permute-done.18.refs_2_
  53.2 0.6 %collective-permute-done.17.refs_1_ = bf16[4,2048]{1,0:T(4,128)(2,1)S(1)} collective-permute-done((bf16[4,2048]{1,0:T(4,128)(2,1)S(1)}, bf16[4,2048]{1,0:T(4,128)(2,1)S(1)}, u32[]{:S(2)}, u32[]{:S(2)}) %collective-permute-start.17) | collective-permute-done | bytes 16416 | tf_op jit(solution)/shard_map/ppermute | solution.py:42
  53.8 0.0 collective-permute-done.16.refs_0_
  53.8 0.6 %shard_map.121 = (bf16[1,4,2048]{2,1,0:T(4,128)(2,1)}, bf16[1,4,2048]{2,1,0:T(4,128)(2,1)}) custom-call(bf16[4,4096]{1,0:T(4,128)(2,1)S(1)} %collective-permute-done.16.refs_0_, bf16[4,2048]{1,0:T(4,128)(2,1)S(1)} %collective-permute-done.17.refs_1_, bf16[4,2048]{1,0:T(4,128)(2,1)S(1)} %collective-permute-done.18.refs_2_, ...), custom_call_target="tpu_custom_call" | custom-call | tf_op jit(solution)/shard_map/pallas_call | solution.py:292
  (3 shorter events, 0.0 us)
Async XLA Ops:
  2.2 11.9 %collective-permute-start = (bf16[24,16,128]{2,1,0:T(8,128)(2,1)S(1)}, bf16[24,16,128]{2,1,0:T(8,128)(2,1)S(1)}, u32[]{:S(2)}, u32[]{:S(2)}) collective-permute-start(bf16[24,16,128]{2,1,0:T(8,128)(2,1)S(1)} %get-tuple-element.20), channel_id=1, source_target_pairs={{0,4},{4,0},{8,12},{12,8},{1,5},{5,1},{9,13},{13,9},{2,6},{6,2},{1... | collective-permute-start | bytes 294920 | tf_op jit(solution)/shard_map/ppermute | solution.py:32
  5.3 8.6 %collective-permute-start.1 = (bf16[16,16,128]{2,1,0:T(8,128)(2,1)S(1)}, bf16[16,16,128]{2,1,0:T(8,128)(2,1)S(1)}, u32[]{:S(2)}, u32[]{:S(2)}) collective-permute-start(bf16[16,16,128]{2,1,0:T(8,128)(2,1)S(1)} %get-tuple-element.21), channel_id=1, source_target_pairs={{0,8},{4,12},{8,0},{12,4},{1,9},{5,13},{9,1},{13,5},{2,10},{6,14},... | collective-permute-start | bytes 196616 | tf_op jit(solution)/shard_map/ppermute | solution.py:32
  7.8 6.2 %collective-permute-start.2 = (bf16[16,16,128]{2,1,0:T(8,128)(2,1)S(1)}, bf16[16,16,128]{2,1,0:T(8,128)(2,1)S(1)}, u32[]{:S(2)}, u32[]{:S(2)}) collective-permute-start(bf16[16,16,128]{2,1,0:T(8,128)(2,1)S(1)} %get-tuple-element.22), channel_id=1, source_target_pairs={{0,12},{4,8},{8,4},{12,0},{1,13},{5,9},{9,5},{13,1},{2,14},{6,10},... | collective-permute-start | bytes 196616 | tf_op jit(solution)/shard_map/ppermute | solution.py:32
  14.0 8.2 %collective-permute-start.6 = (bf16[4,8,16,128]{3,2,1,0:T(8,128)(2,1)S(1)}, bf16[4,8,16,128]{3,2,1,0:T(8,128)(2,1)S(1)}, u32[]{:S(2)}, u32[]{:S(2)}) collective-permute-start(bf16[4,8,16,128]{3,2,1,0:T(8,128)(2,1)S(1)} %shard_map.116.refs_0_), channel_id=1, source_target_pairs={{0,2},{1,3},{2,0},{3,1},{4,6},{5,7},{6,4},{7,5},{8,10},{9,11},{10,... | collective-permute-start | bytes 393224 | tf_op jit(solution)/shard_map/ppermute | solution.py:32
  17.0 5.2 %collective-permute-start.5 = (bf16[4,6272]{1,0:T(4,128)(2,1)S(1)}, bf16[4,6272]{1,0:T(4,128)(2,1)S(1)}, u32[]{:S(2)}, u32[]{:S(2)}) collective-permute-start(bf16[4,6272]{1,0:T(4,128)(2,1)S(1)} %shard_map.115.refs_0_), channel_id=1, source_target_pairs={{0,3},{1,2},{2,1},{3,0},{4,7},{5,6},{6,5},{7,4},{8,11},{9,10},{10,... | collective-permute-start | bytes 150536 | tf_op jit(solution)/shard_map/ppermute | solution.py:32
  17.0 5.2 %collective-permute-start.4 = (bf16[4,6272]{1,0:T(4,128)(2,1)S(1)}, bf16[4,6272]{1,0:T(4,128)(2,1)S(1)}, u32[]{:S(2)}, u32[]{:S(2)}) collective-permute-start(bf16[4,6272]{1,0:T(4,128)(2,1)S(1)} %shard_map.115.refs_0_), channel_id=1, source_target_pairs={{0,2},{1,3},{2,0},{3,1},{4,6},{5,7},{6,4},{7,5},{8,10},{9,11},{10,... | collective-permute-start | bytes 150536 | tf_op jit(solution)/shard_map/ppermute | solution.py:32
  17.4 4.8 %collective-permute-start.7 = (bf16[8,16,128]{2,1,0:T(8,128)(2,1)S(1)}, bf16[8,16,128]{2,1,0:T(8,128)(2,1)S(1)}, u32[]{:S(2)}, u32[]{:S(2)}) collective-permute-start(bf16[8,16,128]{2,1,0:T(8,128)(2,1)S(1)} %slice_add_fusion.refs_7_.refs_6_), channel_id=1, source_target_pairs={{0,8},{4,12},{8,0},{12,4},{1,9},{5,13},{9,1},{13,5},{2,10},{6,14},... | collective-permute-start | bytes 98312 | tf_op jit(solution)/shard_map/ppermute | solution.py:32
  22.3 1.7 %collective-permute-start.8 = (bf16[8,8,16,128]{3,2,1,0:T(8,128)(2,1)S(1)}, bf16[8,8,16,128]{3,2,1,0:T(8,128)(2,1)S(1)}, u32[]{:S(2)}, u32[]{:S(2)}) collective-permute-start(bf16[8,8,16,128]{3,2,1,0:T(8,128)(2,1)S(1)} %bitcast.9), channel_id=1, source_target_pairs={{0,1},{1,0},{2,3},{3,2},{4,5},{5,4},{6,7},{7,6},{8,9},{9,8},{10,11... | collective-permute-start | bytes 786440 | tf_op jit(solution)/shard_map/ppermute | solution.py:32
  22.7 1.3 %collective-permute-start.3 = (bf16[4,6272]{1,0:T(4,128)(2,1)S(1)}, bf16[4,6272]{1,0:T(4,128)(2,1)S(1)}, u32[]{:S(2)}, u32[]{:S(2)}) collective-permute-start(bf16[4,6272]{1,0:T(4,128)(2,1)S(1)} %shard_map.115.refs_0_), channel_id=1, source_target_pairs={{0,1},{1,0},{2,3},{3,2},{4,5},{5,4},{6,7},{7,6},{8,9},{9,8},{10,11... | collective-permute-start | bytes 150536 | tf_op jit(solution)/shard_map/ppermute | solution.py:32
  25.8 10.8 %collective-permute-start.9 = (bf16[4,4096]{1,0:T(4,128)(2,1)S(1)}, bf16[4,4096]{1,0:T(4,128)(2,1)S(1)}, u32[]{:S(2)}, u32[]{:S(2)}) collective-permute-start(bf16[4,4096]{1,0:T(4,128)(2,1)S(1)} %get-tuple-element.25), channel_id=1, source_target_pairs={{0,16},{4,20},{8,24},{12,28},{16,0},{20,4},{24,8},{28,12},{1,17},{... | collective-permute-start | bytes 98312 | tf_op jit(solution)/shard_map/ppermute | solution.py:42
  27.5 6.4 %collective-permute-start.12 = (bf16[4,2048]{1,0:T(4,128)(2,1)S(1)}, bf16[4,2048]{1,0:T(4,128)(2,1)S(1)}, u32[]{:S(2)}, u32[]{:S(2)}) collective-permute-start(bf16[4,2048]{1,0:T(4,128)(2,1)S(1)} %get-tuple-element.26), channel_id=1, source_target_pairs={{12,16},{8,20},{4,24},{0,28},{28,0},{24,4},{20,8},{16,12},{13,17},... | collective-permute-start | bytes 49160 | tf_op jit(solution)/shard_map/ppermute | solution.py:42
  31.1 5.5 %collective-permute-start.11 = (bf16[4,2048]{1,0:T(4,128)(2,1)S(1)}, bf16[4,2048]{1,0:T(4,128)(2,1)S(1)}, u32[]{:S(2)}, u32[]{:S(2)}) collective-permute-start(bf16[4,2048]{1,0:T(4,128)(2,1)S(1)} %get-tuple-element.26), channel_id=1, source_target_pairs={{8,16},{12,20},{0,24},{4,28},{24,0},{28,4},{16,8},{20,12},{9,17},{... | collective-permute-start | bytes 49160 | tf_op jit(solution)/shard_map/ppermute | solution.py:42
  31.2 5.4 %collective-permute-start.10 = (bf16[4,2048]{1,0:T(4,128)(2,1)S(1)}, bf16[4,2048]{1,0:T(4,128)(2,1)S(1)}, u32[]{:S(2)}, u32[]{:S(2)}) collective-permute-start(bf16[4,2048]{1,0:T(4,128)(2,1)S(1)} %get-tuple-element.26), channel_id=1, source_target_pairs={{4,16},{0,20},{12,24},{8,28},{20,0},{16,4},{28,8},{24,12},{5,17},{... | collective-permute-start | bytes 49160 | tf_op jit(solution)/shard_map/ppermute | solution.py:42
  37.9 4.0 %collective-permute-start.15 = (bf16[4,6272]{1,0:T(4,128)(2,1)S(1)}, bf16[4,6272]{1,0:T(4,128)(2,1)S(1)}, u32[]{:S(2)}, u32[]{:S(2)}) collective-permute-start(bf16[4,6272]{1,0:T(4,128)(2,1)S(1)} %get-tuple-element.28.refs_0_), channel_id=1, source_target_pairs={{0,3},{1,2},{2,1},{3,0},{4,7},{5,6},{6,5},{7,4},{8,11},{9,10},{10,... | collective-permute-start | bytes 150536 | tf_op jit(solution)/shard_map/ppermute | solution.py:32
  37.9 5.0 %collective-permute-start.14 = (bf16[4,6272]{1,0:T(4,128)(2,1)S(1)}, bf16[4,6272]{1,0:T(4,128)(2,1)S(1)}, u32[]{:S(2)}, u32[]{:S(2)}) collective-permute-start(bf16[4,6272]{1,0:T(4,128)(2,1)S(1)} %get-tuple-element.28.refs_0_), channel_id=1, source_target_pairs={{0,2},{1,3},{2,0},{3,1},{4,6},{5,7},{6,4},{7,5},{8,10},{9,11},{10,... | collective-permute-start | bytes 150536 | tf_op jit(solution)/shard_map/ppermute | solution.py:32
  39.4 3.4 %collective-permute-start.13 = (bf16[4,6272]{1,0:T(4,128)(2,1)S(1)}, bf16[4,6272]{1,0:T(4,128)(2,1)S(1)}, u32[]{:S(2)}, u32[]{:S(2)}) collective-permute-start(bf16[4,6272]{1,0:T(4,128)(2,1)S(1)} %get-tuple-element.28.refs_0_), channel_id=1, source_target_pairs={{0,1},{1,0},{2,3},{3,2},{4,5},{5,4},{6,7},{7,6},{8,9},{9,8},{10,11... | collective-permute-start | bytes 150536 | tf_op jit(solution)/shard_map/ppermute | solution.py:32
  44.7 9.1 %collective-permute-start.16 = (bf16[4,4096]{1,0:T(4,128)(2,1)S(1)}, bf16[4,4096]{1,0:T(4,128)(2,1)S(1)}, u32[]{:S(2)}, u32[]{:S(2)}) collective-permute-start(bf16[4,4096]{1,0:T(4,128)(2,1)S(1)} %get-tuple-element.30), channel_id=1, source_target_pairs={{0,16},{4,20},{8,24},{12,28},{16,0},{20,4},{24,8},{28,12},{1,17},{... | collective-permute-start | bytes 98312 | tf_op jit(solution)/shard_map/ppermute | solution.py:42
  46.2 6.4 %collective-permute-start.19 = (bf16[4,2048]{1,0:T(4,128)(2,1)S(1)}, bf16[4,2048]{1,0:T(4,128)(2,1)S(1)}, u32[]{:S(2)}, u32[]{:S(2)}) collective-permute-start(bf16[4,2048]{1,0:T(4,128)(2,1)S(1)} %get-tuple-element.31), channel_id=1, source_target_pairs={{12,16},{8,20},{4,24},{0,28},{28,0},{24,4},{20,8},{16,12},{13,17},... | collective-permute-start | bytes 49160 | tf_op jit(solution)/shard_map/ppermute | solution.py:42
  47.6 5.5 %collective-permute-start.18 = (bf16[4,2048]{1,0:T(4,128)(2,1)S(1)}, bf16[4,2048]{1,0:T(4,128)(2,1)S(1)}, u32[]{:S(2)}, u32[]{:S(2)}) collective-permute-start(bf16[4,2048]{1,0:T(4,128)(2,1)S(1)} %get-tuple-element.31), channel_id=1, source_target_pairs={{8,16},{12,20},{0,24},{4,28},{24,0},{28,4},{16,8},{20,12},{9,17},{... | collective-permute-start | bytes 49160 | tf_op jit(solution)/shard_map/ppermute | solution.py:42
  49.1 4.6 %collective-permute-start.17 = (bf16[4,2048]{1,0:T(4,128)(2,1)S(1)}, bf16[4,2048]{1,0:T(4,128)(2,1)S(1)}, u32[]{:S(2)}, u32[]{:S(2)}) collective-permute-start(bf16[4,2048]{1,0:T(4,128)(2,1)S(1)} %get-tuple-element.31), channel_id=1, source_target_pairs={{4,16},{0,20},{12,24},{8,28},{20,0},{16,4},{28,8},{24,12},{5,17},{... | collective-permute-start | bytes 49160 | tf_op jit(solution)/shard_map/ppermute | solution.py:42

commit v12 on v10

--- a/solution.py
+++ b/solution.py
@@ -155,14 +155,18 @@
     )(*pieces, *after)
 
 
-def hold_kernel(parts, after_ref, wq_ref, wo_ref, wq_out, wo_out, sems):
+def hold_kernel(parts, columns, after_ref, *refs):
+    count = len(columns)
     copies = []
-    for source, target in ((wq_ref, wq_out), (wo_ref, wo_out)):
+    sems = refs[-1]
+    for source, target, (first, size) in zip(refs[:count], refs[count:-1], columns):
         rows = source.shape[0] // parts
         for i in range(parts):
             at = pl.ds(i * rows, rows)
             copies.append(
-                pltpu.make_async_copy(source.at[at], target.at[at], sems.at[len(copies)])
+                pltpu.make_async_copy(
+                    source.at[at, pl.ds(first, size)], target.at[at], sems.at[len(copies)]
+                )
             )
     for copy in copies:
         copy.start()
@@ -170,17 +174,18 @@
         copy.wait()
 
 
-def hold(wq, wo, after):
-    parts = 16
-    return pl.pallas_call(
-        lambda *refs: hold_kernel(parts, *refs),
-        out_shape=[pltpu.VMEM(wq.shape, BF), pltpu.VMEM(wo.shape, BF)],
-        in_specs=[pl.BlockSpec(memory_space=pl.ANY), HBM, HBM],
-        out_specs=[VMEM] * 2,
-        scratch_shapes=[pltpu.SemaphoreType.DMA((2 * parts,))],
-        compiler_params=PARAMS,
-        cost_estimate=cost(0, 4 * wq.size),
-    )(after, in_hbm(wq), in_hbm(wo))
+def hold(weights, columns, after):
+    parts = 8
+    total = sum(w.shape[0] * size for w, (_, size) in zip(weights, columns))
+    return pl.pallas_call(
+        lambda *refs: hold_kernel(parts, columns, *refs),
+        out_shape=[pltpu.VMEM((w.shape[0], size), BF) for w, (_, size) in zip(weights, columns)],
+        in_specs=[pl.BlockSpec(memory_space=pl.ANY)] + [HBM] * len(weights),
+        out_specs=[VMEM] * len(weights),
+        scratch_shapes=[pltpu.SemaphoreType.DMA((len(weights) * parts,))],
+        compiler_params=PARAMS,
+        cost_estimate=cost(0, 2 * total),
+    )(after, *[in_hbm(w) for w in weights])
 
 
 def tiles(w_ref):
@@ -301,11 +306,12 @@
 def attend_kernel(dims, turns, tick, *refs):
     sections, tensors, rows, kv_dev = dims
     count = len(turns)
-    pieces, (carry_ref, w_ref), refs = refs[:count], refs[count : count + 2], refs[count + 2 :]
+    pieces, (carry_ref, *w_refs), refs = refs[:count], refs[count : count + 3], refs[count + 3 :]
     caches, (out_ref, full_ref) = refs[:-2], refs[-2:]
     each = caches[0].shape[0] // tensors
-    span = w_ref.shape[0]
-    width = w_ref.shape[1]
+    span = w_refs[0].shape[0]
+    half = w_refs[0].shape[1]
+    width = 2 * half
     batch = batch_at(tick, sections)
 
     tails = [piece[:, 3 * span :].astype(F32) for piece in pieces]
@@ -360,23 +366,25 @@
         got = jnp.dot(probs.astype(BF), values, preferred_element_type=F32) / total
         att += [got[h * rows : (h + 1) * rows] for h in range(per_kv)]
     att = jnp.concatenate(att, 1).astype(BF)
-    for at in tiles(w_ref):
-        got = jnp.dot(att, w_ref[:, at], preferred_element_type=F32).astype(BF)
-        out_ref[:, at] = got
-        full_ref[:, at] = got
+    for i, w_ref in enumerate(w_refs):
+        for at in tiles(w_ref):
+            got = jnp.dot(att, w_ref[:, at], preferred_element_type=F32).astype(BF)
+            to = slice(i * half + at.start, i * half + at.stop)
+            out_ref[:, to] = got
+            full_ref[:, to] = got
     full_ref[:, width:] = carry_ref[...]
 
 
-def attend(dims, turns, tick, pieces, caches, carry, w):
-    rows, width = carry.shape[0], w.shape[1]
+def attend(dims, turns, tick, pieces, caches, carry, left, right):
+    rows, width = carry.shape[0], left.shape[1] + right.shape[1]
     return pl.pallas_call(
         lambda *refs: attend_kernel(dims, turns, tick, *refs),
         out_shape=[shape((rows, width)), shape((rows, width + carry.shape[1]))],
-        in_specs=[VMEM] * (len(pieces) + len(caches) + 2),
+        in_specs=[VMEM] * (len(pieces) + len(caches) + 3),
         out_specs=[VMEM] * 2,
         compiler_params=PARAMS,
-        cost_estimate=cost(8 * w.size, 2 * w.size),
-    )(*pieces, carry, w, *caches)
+        cost_estimate=cost(16 * left.size, 4 * left.size),
+    )(*pieces, carry, left, right, *caches)
 
 
 def on_device(state, next_embed, tenant, lengths, gain, bias, wq, wo, keys, values):
@@ -401,10 +409,11 @@
         next_embed,
     )
     got = [packs[0]] + [swapped(packs[d], "tensor", d) for d in range(1, tensors)]
-    wq_held, wo_held = hold(wq[0], wo[0], packs[0])
+    half = width // 2
+    wq_held, wo_left = hold([wq[0], wo[0]], [(0, wq.shape[2]), (0, half)], packs[0])
 
     held = 2 * sections * kv_dev
-    kv = join(got, held, [wq_held, wo_held])
+    kv = join(got, held, [wq_held, wo_left])
 
     later = [piece[held + 2 * rows * width // (keys.shape[4] * HD) :] for piece in got[:NEAR]]
     bit = NEAR
@@ -424,15 +433,16 @@
             sums, carry = later_sums(tick, lengths, arrivals, following, later, wq_held)
         pieces = [sums] + [swapped(sums, "replica", d) for d in range(1, replicas)]
         if tick == 0:
+            (wo_right,) = hold([wo[0]], [(half, half)], sums)
             while bit:
                 turns = turns + [turn ^ bit for turn in turns]
                 caches, bit = [kv, waiting], bit // 2
                 if bit:
-                    both = join(caches, kv.shape[0], pieces[2:])
+                    both = join(caches, kv.shape[0], pieces[2:] + [wo_right])
                     kv = both.reshape((-1,) + both.shape[2:])
                     waiting = swapped(kv, "replica", bit)
         out, full = attend(
-            (sections, tensors, rows, kv_dev), turns, tick, pieces, caches, carry, wo_held
+            (sections, tensors, rows, kv_dev), turns, tick, pieces, caches, carry, wo_left, wo_right
         )
         arrivals = [from_behind(full, 0)] + [from_behind(out, d) for d in range(1, tensors)]
     return tuple(last(arrivals, following))

time: 53.9 us -> 53.1 us (0.985)
  waiting for transfers between devices: 13.1 us -> 11.6 us
  Pallas kernels: 14.5 us -> 15.4 us
    ppermute x12, waiting for transfers between devices: 7.13 us -> 6.12 us  [swapped(): return lax.ppermute(block, axis, route)]
    pallas_call x1 -> x2, Pallas kernels: 6.04 us -> 6.91 us  [hold(): pl.pallas_call(lambda *refs: hold_kernel(parts, columns, *refs), out_shap...]
  transfers between devices with their start and end apart: 20 -> 20, of which waited for: 11 -> 12; matrix products, arithmetic and copies ran while one was open for 0% -> 0% of each run, Pallas kernels for 17% -> 19%
where the time goes in v12:
time: 53.1 us; the launch traced here: 52.9 us
  starting transfers between devices  25.3 us (48%)
  Pallas kernels  15.4 us (29%)
  waiting for transfers between devices  11.6 us (22%)
  between operations  0.69 us (1%)
    ppermute x8, starting transfers between devices, from_behind(): return lax.ppermute(block, ('section', 'tensor'), route)  13.5 us
    ppermute x12, starting transfers between devices, swapped(): return lax.ppermute(block, axis, route)  11.8 us
    pallas_call x2, Pallas kernels, hold(): pl.pallas_call(lambda *refs: hold_kernel(parts, columns, *refs), out_shap...  6.91 us
    ppermute x12, waiting for transfers between devices, swapped(): return lax.ppermute(block, axis, route)  6.12 us
    ppermute x8, waiting for transfers between devices, from_behind(): return lax.ppermute(block, ('section', 'tensor'), route)  5.45 us
    pallas_call x2, Pallas kernels, attend(): pl.pallas_call(lambda *refs: attend_kernel(dims, turns, tick, *refs), out...  3.71 us
    pallas_call x1, Pallas kernels, pack(): pl.pallas_call(lambda *refs: pack_kernel(dims, *refs), out_shape=out_shap...  1.52 us
    pallas_call x1, Pallas kernels, later_sums(): pl.pallas_call(lambda *refs: later_kernel(len(arrivals), tick, *refs), ou...  1.28 us
  transfers between devices with their start and end apart: 20, of which 12 were waited for; matrix products, arithmetic and copies ran while one was open for 0% of the time, Pallas kernels for 19%

profile of v12, /device:TPU:0, one launch (start us, length us, event | category | flops | bytes accessed | tf_op | source)
XLA Modules:
  0.0 52.9 jit_solution(17142470483169878898)
XLA Ops:
  0.6 1.5 %shard_map.113 = (bf16[24,16,128]{2,1,0:T(8,128)(2,1)S(1)}, bf16[24,16,128]{2,1,0:T(8,128)(2,1)S(1)}, bf16[16,16,128]{2,1,0:T(8,128)(2,1)S(1)}, bf16[16,16,128]{...) custom-call(s32[2,4]{1,0:T(2,128)} %refs_0_.1, ...), custom_call_target="tpu_custom_call" | custom-call | bytes 819200 | tf_op jit(solution)/shard_map/pallas_call | solution.py:127
  2.2 3.1 %collective-permute-start = (bf16[24,16,128]{2,1,0:T(8,128)(2,1)S(1)}, bf16[24,16,128]{2,1,0:T(8,128)(2,1)S(1)}, u32[]{:S(2)}, u32[]{:S(2)}) collective-permute-start(bf16[24,16,128]{2,1,0:T(8,128)(2,1)S(1)} %get-tuple-element.20), channel_id=1, source_target_pairs={{0,4},{4,0},{8,12},{12,8},{1,5},{5,1},{9,13},{13,9},{2,6},{6,2},{1... | collective-permute-start | bytes 294920 | tf_op jit(solution)/shard_map/ppermute | solution.py:32
  5.3 2.6 %collective-permute-start.1 = (bf16[16,16,128]{2,1,0:T(8,128)(2,1)S(1)}, bf16[16,16,128]{2,1,0:T(8,128)(2,1)S(1)}, u32[]{:S(2)}, u32[]{:S(2)}) collective-permute-start(bf16[16,16,128]{2,1,0:T(8,128)(2,1)S(1)} %get-tuple-element.21), channel_id=1, source_target_pairs={{0,8},{4,12},{8,0},{12,4},{1,9},{5,13},{9,1},{13,5},{2,10},{6,14},... | collective-permute-start | bytes 196616 | tf_op jit(solution)/shard_map/ppermute | solution.py:32
  7.8 0.0 collective-permute-start.2
  7.8 4.7 %shard_map.114 = (bf16[2048,2048]{1,0:T(8,128)(2,1)S(1)}, bf16[2048,1024]{1,0:T(8,128)(2,1)S(1)}) custom-call(bf16[24,16,128]{2,1,0:T(8,128)(2,1)S(1)} %get-tuple-element.19.refs_0_.refs_2_, bf16[2048,2048]{1,0:T(8,128)(2,1)} %bitcast.14, bf16[2048,2048]{1,0:T(8,128)(2,1)} %bitcast.12), custom_call_target="tpu_custom_call" | custom-call | bytes 12582912 | tf_op jit(solution)/shard_map/pallas_call | solution.py:180
  12.5 0.3 collective-permute-done.1.refs_4_.refs_2_
  12.9 1.2 %collective-permute-done.2.refs_5_.refs_3_ = bf16[16,16,128]{2,1,0:T(8,128)(2,1)S(1)} collective-permute-done((bf16[16,16,128]{2,1,0:T(8,128)(2,1)S(1)}, bf16[16,16,128]{2,1,0:T(8,128)(2,1)S(1)}, u32[]{:S(2)}, u32[]{:S(2)}) %collective-permute-start.2) | collective-permute-done | bytes 65568 | tf_op jit(solution)/shard_map/ppermute | solution.py:32
  14.0 0.0 collective-permute-done.refs_3_.refs_1_
  14.0 1.6 %collective-permute-start.6 = (bf16[4,8,16,128]{3,2,1,0:T(8,128)(2,1)S(1)}, bf16[4,8,16,128]{3,2,1,0:T(8,128)(2,1)S(1)}, u32[]{:S(2)}, u32[]{:S(2)}) collective-permute-start(bf16[4,8,16,128]{3,2,1,0:T(8,128)(2,1)S(1)} %shard_map.117.refs_0_), channel_id=1, source_target_pairs={{0,2},{1,3},{2,0},{3,1},{4,6},{5,7},{6,4},{7,5},{8,10},{9,11},{10,... | collective-permute-start | bytes 393224 | tf_op jit(solution)/shard_map/ppermute | solution.py:32
  15.6 1.3 %shard_map.115.refs_0_ = bf16[4,6272]{1,0:T(4,128)(2,1)S(1)} custom-call(f32[2,128]{1,0:T(2,128)S(1)} %get-tuple-element.17.refs_0_, bf16[4,2048]{1,0:T(4,128)(2,1)S(1)} %get-tuple-element.18.refs_1_.refs_4_, bf16[24,16,128]{2,1,0:T(8,128)(2,1)S(1)} %get-tuple-element.19.refs_0_.refs_2_, bf16[24,16,128]{2,1,0:T(8,128)(2,1)S(1)} %collective-permute-done.refs_3_.refs_1_, ...), custom_call_target="tpu_custom_call" | custom-call | flops 100663296 | bytes 8388608 | tf_op jit(solution)/shard_map/pallas_call | solution.py:235
  16.9 0.0 collective-permute-start.5
  16.9 0.6 %collective-permute-start.4 = (bf16[4,6272]{1,0:T(4,128)(2,1)S(1)}, bf16[4,6272]{1,0:T(4,128)(2,1)S(1)}, u32[]{:S(2)}, u32[]{:S(2)}) collective-permute-start(bf16[4,6272]{1,0:T(4,128)(2,1)S(1)} %shard_map.115.refs_0_), channel_id=1, source_target_pairs={{0,2},{1,3},{2,0},{3,1},{4,6},{5,7},{6,4},{7,5},{8,10},{9,11},{10,... | collective-permute-start | bytes 150536 | tf_op jit(solution)/shard_map/ppermute | solution.py:32
  17.4 2.2 %shard_map.116.refs_4_.refs_6_ = bf16[2048,1024]{1,0:T(8,128)(2,1)S(1)} custom-call(bf16[4,6272]{1,0:T(4,128)(2,1)S(1)} %shard_map.115.refs_0_, bf16[2048,2048]{1,0:T(8,128)(2,1)} %bitcast.13), custom_call_target="tpu_custom_call" | custom-call | bytes 4194304 | tf_op jit(solution)/shard_map/pallas_call | solution.py:180
  19.7 0.8 %collective-permute-done.5.refs_3_ = bf16[4,6272]{1,0:T(4,128)(2,1)S(1)} collective-permute-done((bf16[4,6272]{1,0:T(4,128)(2,1)S(1)}, bf16[4,6272]{1,0:T(4,128)(2,1)S(1)}, u32[]{:S(2)}, u32[]{:S(2)}) %collective-permute-start.5) | collective-permute-done | bytes 50208 | tf_op jit(solution)/shard_map/ppermute | solution.py:32
  20.4 1.1 %collective-permute-done.4.refs_2_ = bf16[4,6272]{1,0:T(4,128)(2,1)S(1)} collective-permute-done((bf16[4,6272]{1,0:T(4,128)(2,1)S(1)}, bf16[4,6272]{1,0:T(4,128)(2,1)S(1)}, u32[]{:S(2)}, u32[]{:S(2)}) %collective-permute-start.4) | collective-permute-done | bytes 50208 | tf_op jit(solution)/shard_map/ppermute | solution.py:32
  21.5 0.0 collective-permute-done.6.refs_1_
  21.5 0.1 collective-permute-start.7
  21.7 0.4 collective-permute-start.3
  22.1 1.5 %collective-permute-start.12 = (bf16[8,16,128]{2,1,0:T(8,128)(2,1)S(1)}, bf16[8,16,128]{2,1,0:T(8,128)(2,1)S(1)}, u32[]{:S(2)}, u32[]{:S(2)}) collective-permute-start(bf16[8,16,128]{2,1,0:T(8,128)(2,1)S(1)} %slice_add_fusion.refs_6_), channel_id=1, source_target_pairs={{0,8},{4,12},{8,0},{12,4},{1,9},{5,13},{9,1},{13,5},{2,10},{6,14},... | collective-permute-start | bytes 98312 | tf_op jit(solution)/shard_map/ppermute | solution.py:32
  23.6 0.0 collective-permute-done.3.refs_1_
  23.6 0.0 collective-permute-done.7.refs_8_
  23.6 1.9 %shard_map.119 = (bf16[4,2048]{1,0:T(4,128)(2,1)S(1)}, bf16[4,4096]{1,0:T(4,128)(2,1)S(1)}) custom-call(bf16[4,6272]{1,0:T(4,128)(2,1)S(1)} %shard_map.115.refs_0_, bf16[4,6272]{1,0:T(4,128)(2,1)S(1)} %collective-permute-done.3.refs_1_, bf16[4,6272]{1,0:T(4,128)(2,1)S(1)} %collective-permute-done.4.refs_2_, ...), custom_call_target="tpu_custom_call" | custom-call | flops 33554432 | bytes 8388608 | tf_op jit(solution)/shard_map/pallas_call | solution.py:380
  25.4 1.5 %collective-permute-start.8 = (bf16[4,4096]{1,0:T(4,128)(2,1)S(1)}, bf16[4,4096]{1,0:T(4,128)(2,1)S(1)}, u32[]{:S(2)}, u32[]{:S(2)}) collective-permute-start(bf16[4,4096]{1,0:T(4,128)(2,1)S(1)} %get-tuple-element.25), channel_id=1, source_target_pairs={{0,16},{4,20},{8,24},{12,28},{16,0},{20,4},{24,8},{28,12},{1,17},{... | collective-permute-start | bytes 98312 | tf_op jit(solution)/shard_map/ppermute | solution.py:42
  26.9 2.0 %collective-permute-start.11 = (bf16[4,2048]{1,0:T(4,128)(2,1)S(1)}, bf16[4,2048]{1,0:T(4,128)(2,1)S(1)}, u32[]{:S(2)}, u32[]{:S(2)}) collective-permute-start(bf16[4,2048]{1,0:T(4,128)(2,1)S(1)} %get-tuple-element.26), channel_id=1, source_target_pairs={{12,16},{8,20},{4,24},{0,28},{28,0},{24,4},{20,8},{16,12},{13,17},... | collective-permute-start | bytes 49160 | tf_op jit(solution)/shard_map/ppermute | solution.py:42
  28.9 1.9 %collective-permute-start.10 = (bf16[4,2048]{1,0:T(4,128)(2,1)S(1)}, bf16[4,2048]{1,0:T(4,128)(2,1)S(1)}, u32[]{:S(2)}, u32[]{:S(2)}) collective-permute-start(bf16[4,2048]{1,0:T(4,128)(2,1)S(1)} %get-tuple-element.26), channel_id=1, source_target_pairs={{8,16},{12,20},{0,24},{4,28},{24,0},{28,4},{16,8},{20,12},{9,17},{... | collective-permute-start | bytes 49160 | tf_op jit(solution)/shard_map/ppermute | solution.py:42
  30.8 1.4 %collective-permute-start.9 = (bf16[4,2048]{1,0:T(4,128)(2,1)S(1)}, bf16[4,2048]{1,0:T(4,128)(2,1)S(1)}, u32[]{:S(2)}, u32[]{:S(2)}) collective-permute-start(bf16[4,2048]{1,0:T(4,128)(2,1)S(1)} %get-tuple-element.26), channel_id=1, source_target_pairs={{4,16},{0,20},{12,24},{8,28},{20,0},{16,4},{28,8},{24,12},{5,17},{... | collective-permute-start | bytes 49160 | tf_op jit(solution)/shard_map/ppermute | solution.py:42
  32.2 0.0 collective-permute-done.12.refs_7_
  32.2 1.2 %collective-permute-done.11.refs_4_ = bf16[4,2048]{1,0:T(4,128)(2,1)S(1)} collective-permute-done((bf16[4,2048]{1,0:T(4,128)(2,1)S(1)}, bf16[4,2048]{1,0:T(4,128)(2,1)S(1)}, u32[]{:S(2)}, u32[]{:S(2)}) %collective-permute-start.11) | collective-permute-done | bytes 16416 | tf_op jit(solution)/shard_map/ppermute | solution.py:42
  33.4 1.1 %collective-permute-done.10.refs_3_ = bf16[4,2048]{1,0:T(4,128)(2,1)S(1)} collective-permute-done((bf16[4,2048]{1,0:T(4,128)(2,1)S(1)}, bf16[4,2048]{1,0:T(4,128)(2,1)S(1)}, u32[]{:S(2)}, u32[]{:S(2)}) %collective-permute-start.10) | collective-permute-done | bytes 16416 | tf_op jit(solution)/shard_map/ppermute | solution.py:42
  34.5 1.0 %collective-permute-done.9.refs_2_ = bf16[4,2048]{1,0:T(4,128)(2,1)S(1)} collective-permute-done((bf16[4,2048]{1,0:T(4,128)(2,1)S(1)}, bf16[4,2048]{1,0:T(4,128)(2,1)S(1)}, u32[]{:S(2)}, u32[]{:S(2)}) %collective-permute-start.9) | collective-permute-done | bytes 16416 | tf_op jit(solution)/shard_map/ppermute | solution.py:42
  35.4 0.0 collective-permute-done.8.refs_1_
  35.4 1.3 %shard_map.120 = (bf16[4,6272]{1,0:T(4,128)(2,1)S(1)}, bf16[4,2048]{1,0:T(4,128)(2,1)S(1)}) custom-call(f32[2,128]{1,0:T(2,128)S(1)} %get-tuple-element.17.refs_0_, bf16[4,4096]{1,0:T(4,128)(2,1)S(1)} %collective-permute-done.8.refs_1_, bf16[4,2048]{1,0:T(4,128)(2,1)S(1)} %collective-permute-done.9.refs_2_, ...), custom_call_target="tpu_custom_call" | custom-call | flops 100663296 | bytes 8388608 | tf_op jit(solution)/shard_map/pallas_call | solution.py:279
  36.7 0.0 collective-permute-start.15
  36.7 1.3 %collective-permute-start.14 = (bf16[4,6272]{1,0:T(4,128)(2,1)S(1)}, bf16[4,6272]{1,0:T(4,128)(2,1)S(1)}, u32[]{:S(2)}, u32[]{:S(2)}) collective-permute-start(bf16[4,6272]{1,0:T(4,128)(2,1)S(1)} %get-tuple-element.28.refs_0_), channel_id=1, source_target_pairs={{0,2},{1,3},{2,0},{3,1},{4,6},{5,7},{6,4},{7,5},{8,10},{9,11},{10,... | collective-permute-start | bytes 150536 | tf_op jit(solution)/shard_map/ppermute | solution.py:32
  38.0 0.6 %collective-permute-start.13 = (bf16[4,6272]{1,0:T(4,128)(2,1)S(1)}, bf16[4,6272]{1,0:T(4,128)(2,1)S(1)}, u32[]{:S(2)}, u32[]{:S(2)}) collective-permute-start(bf16[4,6272]{1,0:T(4,128)(2,1)S(1)} %get-tuple-element.28.refs_0_), channel_id=1, source_target_pairs={{0,1},{1,0},{2,3},{3,2},{4,5},{5,4},{6,7},{7,6},{8,9},{9,8},{10,11... | collective-permute-start | bytes 150536 | tf_op jit(solution)/shard_map/ppermute | solution.py:32
  38.6 2.2 %collective-permute-done.15.refs_3_ = bf16[4,6272]{1,0:T(4,128)(2,1)S(1)} collective-permute-done((bf16[4,6272]{1,0:T(4,128)(2,1)S(1)}, bf16[4,6272]{1,0:T(4,128)(2,1)S(1)}, u32[]{:S(2)}, u32[]{:S(2)}) %collective-permute-start.15) | collective-permute-done | bytes 50208 | tf_op jit(solution)/shard_map/ppermute | solution.py:32
  40.8 0.6 %collective-permute-done.14.refs_2_ = bf16[4,6272]{1,0:T(4,128)(2,1)S(1)} collective-permute-done((bf16[4,6272]{1,0:T(4,128)(2,1)S(1)}, bf16[4,6272]{1,0:T(4,128)(2,1)S(1)}, u32[]{:S(2)}, u32[]{:S(2)}) %collective-permute-start.14) | collective-permute-done | bytes 50208 | tf_op jit(solution)/shard_map/ppermute | solution.py:32
  41.4 0.0 collective-permute-done.13.refs_1_
  41.4 1.9 %shard_map.121 = (bf16[4,2048]{1,0:T(4,128)(2,1)S(1)}, bf16[4,4096]{1,0:T(4,128)(2,1)S(1)}) custom-call(bf16[4,6272]{1,0:T(4,128)(2,1)S(1)} %get-tuple-element.28.refs_0_, bf16[4,6272]{1,0:T(4,128)(2,1)S(1)} %collective-permute-done.13.refs_1_, bf16[4,6272]{1,0:T(4,128)(2,1)S(1)} %collective-permute-done.14.refs_2_, ...), custom_call_target="tpu_custom_call" | custom-call | flops 33554432 | bytes 8388608 | tf_op jit(solution)/shard_map/pallas_call | solution.py:380
  43.3 0.7 %collective-permute-start.16 = (bf16[4,4096]{1,0:T(4,128)(2,1)S(1)}, bf16[4,4096]{1,0:T(4,128)(2,1)S(1)}, u32[]{:S(2)}, u32[]{:S(2)}) collective-permute-start(bf16[4,4096]{1,0:T(4,128)(2,1)S(1)} %get-tuple-element.30), channel_id=1, source_target_pairs={{0,16},{4,20},{8,24},{12,28},{16,0},{20,4},{24,8},{28,12},{1,17},{... | collective-permute-start | bytes 98312 | tf_op jit(solution)/shard_map/ppermute | solution.py:42
  44.0 2.2 %collective-permute-start.19 = (bf16[4,2048]{1,0:T(4,128)(2,1)S(1)}, bf16[4,2048]{1,0:T(4,128)(2,1)S(1)}, u32[]{:S(2)}, u32[]{:S(2)}) collective-permute-start(bf16[4,2048]{1,0:T(4,128)(2,1)S(1)} %get-tuple-element.31), channel_id=1, source_target_pairs={{12,16},{8,20},{4,24},{0,28},{28,0},{24,4},{20,8},{16,12},{13,17},... | collective-permute-start | bytes 49160 | tf_op jit(solution)/shard_map/ppermute | solution.py:42
  46.2 1.5 %collective-permute-start.18 = (bf16[4,2048]{1,0:T(4,128)(2,1)S(1)}, bf16[4,2048]{1,0:T(4,128)(2,1)S(1)}, u32[]{:S(2)}, u32[]{:S(2)}) collective-permute-start(bf16[4,2048]{1,0:T(4,128)(2,1)S(1)} %get-tuple-element.31), channel_id=1, source_target_pairs={{8,16},{12,20},{0,24},{4,28},{24,0},{28,4},{16,8},{20,12},{9,17},{... | collective-permute-start | bytes 49160 | tf_op jit(solution)/shard_map/ppermute | solution.py:42
  47.6 2.4 %collective-permute-start.17 = (bf16[4,2048]{1,0:T(4,128)(2,1)S(1)}, bf16[4,2048]{1,0:T(4,128)(2,1)S(1)}, u32[]{:S(2)}, u32[]{:S(2)}) collective-permute-start(bf16[4,2048]{1,0:T(4,128)(2,1)S(1)} %get-tuple-element.31), channel_id=1, source_target_pairs={{4,16},{0,20},{12,24},{8,28},{20,0},{16,4},{28,8},{24,12},{5,17},{... | collective-permute-start | bytes 49160 | tf_op jit(solution)/shard_map/ppermute | solution.py:42
  50.0 0.4 collective-permute-done.19.refs_3_
  50.5 1.2 %collective-permute-done.18.refs_2_ = bf16[4,2048]{1,0:T(4,128)(2,1)S(1)} collective-permute-done((bf16[4,2048]{1,0:T(4,128)(2,1)S(1)}, bf16[4,2048]{1,0:T(4,128)(2,1)S(1)}, u32[]{:S(2)}, u32[]{:S(2)}) %collective-permute-start.18) | collective-permute-done | bytes 16416 | tf_op jit(solution)/shard_map/ppermute | solution.py:42
  51.7 0.6 %collective-permute-done.17.refs_1_ = bf16[4,2048]{1,0:T(4,128)(2,1)S(1)} collective-permute-done((bf16[4,2048]{1,0:T(4,128)(2,1)S(1)}, bf16[4,2048]{1,0:T(4,128)(2,1)S(1)}, u32[]{:S(2)}, u32[]{:S(2)}) %collective-permute-start.17) | collective-permute-done | bytes 16416 | tf_op jit(solution)/shard_map/ppermute | solution.py:42
  52.3 0.0 collective-permute-done.16.refs_0_
  52.3 0.6 %shard_map.122 = (bf16[1,4,2048]{2,1,0:T(4,128)(2,1)}, bf16[1,4,2048]{2,1,0:T(4,128)(2,1)}) custom-call(bf16[4,4096]{1,0:T(4,128)(2,1)S(1)} %collective-permute-done.16.refs_0_, bf16[4,2048]{1,0:T(4,128)(2,1)S(1)} %collective-permute-done.17.refs_1_, bf16[4,2048]{1,0:T(4,128)(2,1)S(1)} %collective-permute-done.18.refs_2_, ...), custom_call_target="tpu_custom_call" | custom-call | tf_op jit(solution)/shard_map/pallas_call | solution.py:297
  (3 shorter events, 0.0 us)
Async XLA Ops:
  2.2 11.9 %collective-permute-start = (bf16[24,16,128]{2,1,0:T(8,128)(2,1)S(1)}, bf16[24,16,128]{2,1,0:T(8,128)(2,1)S(1)}, u32[]{:S(2)}, u32[]{:S(2)}) collective-permute-start(bf16[24,16,128]{2,1,0:T(8,128)(2,1)S(1)} %get-tuple-element.20), channel_id=1, source_target_pairs={{0,4},{4,0},{8,12},{12,8},{1,5},{5,1},{9,13},{13,9},{2,6},{6,2},{1... | collective-permute-start | bytes 294920 | tf_op jit(solution)/shard_map/ppermute | solution.py:32
  5.3 7.6 %collective-permute-start.1 = (bf16[16,16,128]{2,1,0:T(8,128)(2,1)S(1)}, bf16[16,16,128]{2,1,0:T(8,128)(2,1)S(1)}, u32[]{:S(2)}, u32[]{:S(2)}) collective-permute-start(bf16[16,16,128]{2,1,0:T(8,128)(2,1)S(1)} %get-tuple-element.21), channel_id=1, source_target_pairs={{0,8},{4,12},{8,0},{12,4},{1,9},{5,13},{9,1},{13,5},{2,10},{6,14},... | collective-permute-start | bytes 196616 | tf_op jit(solution)/shard_map/ppermute | solution.py:32
  7.8 6.2 %collective-permute-start.2 = (bf16[16,16,128]{2,1,0:T(8,128)(2,1)S(1)}, bf16[16,16,128]{2,1,0:T(8,128)(2,1)S(1)}, u32[]{:S(2)}, u32[]{:S(2)}) collective-permute-start(bf16[16,16,128]{2,1,0:T(8,128)(2,1)S(1)} %get-tuple-element.22), channel_id=1, source_target_pairs={{0,12},{4,8},{8,4},{12,0},{1,13},{5,9},{9,5},{13,1},{2,14},{6,10},... | collective-permute-start | bytes 196616 | tf_op jit(solution)/shard_map/ppermute | solution.py:32
  14.0 7.5 %collective-permute-start.6 = (bf16[4,8,16,128]{3,2,1,0:T(8,128)(2,1)S(1)}, bf16[4,8,16,128]{3,2,1,0:T(8,128)(2,1)S(1)}, u32[]{:S(2)}, u32[]{:S(2)}) collective-permute-start(bf16[4,8,16,128]{3,2,1,0:T(8,128)(2,1)S(1)} %shard_map.117.refs_0_), channel_id=1, source_target_pairs={{0,2},{1,3},{2,0},{3,1},{4,6},{5,7},{6,4},{7,5},{8,10},{9,11},{10,... | collective-permute-start | bytes 393224 | tf_op jit(solution)/shard_map/ppermute | solution.py:32
  16.9 3.5 %collective-permute-start.5 = (bf16[4,6272]{1,0:T(4,128)(2,1)S(1)}, bf16[4,6272]{1,0:T(4,128)(2,1)S(1)}, u32[]{:S(2)}, u32[]{:S(2)}) collective-permute-start(bf16[4,6272]{1,0:T(4,128)(2,1)S(1)} %shard_map.115.refs_0_), channel_id=1, source_target_pairs={{0,3},{1,2},{2,1},{3,0},{4,7},{5,6},{6,5},{7,4},{8,11},{9,10},{10,... | collective-permute-start | bytes 150536 | tf_op jit(solution)/shard_map/ppermute | solution.py:32
  16.9 4.6 %collective-permute-start.4 = (bf16[4,6272]{1,0:T(4,128)(2,1)S(1)}, bf16[4,6272]{1,0:T(4,128)(2,1)S(1)}, u32[]{:S(2)}, u32[]{:S(2)}) collective-permute-start(bf16[4,6272]{1,0:T(4,128)(2,1)S(1)} %shard_map.115.refs_0_), channel_id=1, source_target_pairs={{0,2},{1,3},{2,0},{3,1},{4,6},{5,7},{6,4},{7,5},{8,10},{9,11},{10,... | collective-permute-start | bytes 150536 | tf_op jit(solution)/shard_map/ppermute | solution.py:32
  21.5 2.1 %collective-permute-start.7 = (bf16[8,8,16,128]{3,2,1,0:T(8,128)(2,1)S(1)}, bf16[8,8,16,128]{3,2,1,0:T(8,128)(2,1)S(1)}, u32[]{:S(2)}, u32[]{:S(2)}) collective-permute-start(bf16[8,8,16,128]{3,2,1,0:T(8,128)(2,1)S(1)} %bitcast.9), channel_id=1, source_target_pairs={{0,1},{1,0},{2,3},{3,2},{4,5},{5,4},{6,7},{7,6},{8,9},{9,8},{10,11... | collective-permute-start | bytes 786440 | tf_op jit(solution)/shard_map/ppermute | solution.py:32
  21.7 1.9 %collective-permute-start.3 = (bf16[4,6272]{1,0:T(4,128)(2,1)S(1)}, bf16[4,6272]{1,0:T(4,128)(2,1)S(1)}, u32[]{:S(2)}, u32[]{:S(2)}) collective-permute-start(bf16[4,6272]{1,0:T(4,128)(2,1)S(1)} %shard_map.115.refs_0_), channel_id=1, source_target_pairs={{0,1},{1,0},{2,3},{3,2},{4,5},{5,4},{6,7},{7,6},{8,9},{9,8},{10,11... | collective-permute-start | bytes 150536 | tf_op jit(solution)/shard_map/ppermute | solution.py:32
  22.1 10.1 %collective-permute-start.12 = (bf16[8,16,128]{2,1,0:T(8,128)(2,1)S(1)}, bf16[8,16,128]{2,1,0:T(8,128)(2,1)S(1)}, u32[]{:S(2)}, u32[]{:S(2)}) collective-permute-start(bf16[8,16,128]{2,1,0:T(8,128)(2,1)S(1)} %slice_add_fusion.refs_6_), channel_id=1, source_target_pairs={{0,8},{4,12},{8,0},{12,4},{1,9},{5,13},{9,1},{13,5},{2,10},{6,14},... | collective-permute-start | bytes 98312 | tf_op jit(solution)/shard_map/ppermute | solution.py:32
  25.4 10.0 %collective-permute-start.8 = (bf16[4,4096]{1,0:T(4,128)(2,1)S(1)}, bf16[4,4096]{1,0:T(4,128)(2,1)S(1)}, u32[]{:S(2)}, u32[]{:S(2)}) collective-permute-start(bf16[4,4096]{1,0:T(4,128)(2,1)S(1)} %get-tuple-element.25), channel_id=1, source_target_pairs={{0,16},{4,20},{8,24},{12,28},{16,0},{20,4},{24,8},{28,12},{1,17},{... | collective-permute-start | bytes 98312 | tf_op jit(solution)/shard_map/ppermute | solution.py:42
  26.9 6.4 %collective-permute-start.11 = (bf16[4,2048]{1,0:T(4,128)(2,1)S(1)}, bf16[4,2048]{1,0:T(4,128)(2,1)S(1)}, u32[]{:S(2)}, u32[]{:S(2)}) collective-permute-start(bf16[4,2048]{1,0:T(4,128)(2,1)S(1)} %get-tuple-element.26), channel_id=1, source_target_pairs={{12,16},{8,20},{4,24},{0,28},{28,0},{24,4},{20,8},{16,12},{13,17},... | collective-permute-start | bytes 49160 | tf_op jit(solution)/shard_map/ppermute | solution.py:42
  28.9 5.5 %collective-permute-start.10 = (bf16[4,2048]{1,0:T(4,128)(2,1)S(1)}, bf16[4,2048]{1,0:T(4,128)(2,1)S(1)}, u32[]{:S(2)}, u32[]{:S(2)}) collective-permute-start(bf16[4,2048]{1,0:T(4,128)(2,1)S(1)} %get-tuple-element.26), channel_id=1, source_target_pairs={{8,16},{12,20},{0,24},{4,28},{24,0},{28,4},{16,8},{20,12},{9,17},{... | collective-permute-start | bytes 49160 | tf_op jit(solution)/shard_map/ppermute | solution.py:42
  30.8 4.6 %collective-permute-start.9 = (bf16[4,2048]{1,0:T(4,128)(2,1)S(1)}, bf16[4,2048]{1,0:T(4,128)(2,1)S(1)}, u32[]{:S(2)}, u32[]{:S(2)}) collective-permute-start(bf16[4,2048]{1,0:T(4,128)(2,1)S(1)} %get-tuple-element.26), channel_id=1, source_target_pairs={{4,16},{0,20},{12,24},{8,28},{20,0},{16,4},{28,8},{24,12},{5,17},{... | collective-permute-start | bytes 49160 | tf_op jit(solution)/shard_map/ppermute | solution.py:42
  36.7 4.0 %collective-permute-start.15 = (bf16[4,6272]{1,0:T(4,128)(2,1)S(1)}, bf16[4,6272]{1,0:T(4,128)(2,1)S(1)}, u32[]{:S(2)}, u32[]{:S(2)}) collective-permute-start(bf16[4,6272]{1,0:T(4,128)(2,1)S(1)} %get-tuple-element.28.refs_0_), channel_id=1, source_target_pairs={{0,3},{1,2},{2,1},{3,0},{4,7},{5,6},{6,5},{7,4},{8,11},{9,10},{10,... | collective-permute-start | bytes 150536 | tf_op jit(solution)/shard_map/ppermute | solution.py:32
  36.7 4.7 %collective-permute-start.14 = (bf16[4,6272]{1,0:T(4,128)(2,1)S(1)}, bf16[4,6272]{1,0:T(4,128)(2,1)S(1)}, u32[]{:S(2)}, u32[]{:S(2)}) collective-permute-start(bf16[4,6272]{1,0:T(4,128)(2,1)S(1)} %get-tuple-element.28.refs_0_), channel_id=1, source_target_pairs={{0,2},{1,3},{2,0},{3,1},{4,6},{5,7},{6,4},{7,5},{8,10},{9,11},{10,... | collective-permute-start | bytes 150536 | tf_op jit(solution)/shard_map/ppermute | solution.py:32
  38.0 3.4 %collective-permute-start.13 = (bf16[4,6272]{1,0:T(4,128)(2,1)S(1)}, bf16[4,6272]{1,0:T(4,128)(2,1)S(1)}, u32[]{:S(2)}, u32[]{:S(2)}) collective-permute-start(bf16[4,6272]{1,0:T(4,128)(2,1)S(1)} %get-tuple-element.28.refs_0_), channel_id=1, source_target_pairs={{0,1},{1,0},{2,3},{3,2},{4,5},{5,4},{6,7},{7,6},{8,9},{9,8},{10,11... | collective-permute-start | bytes 150536 | tf_op jit(solution)/shard_map/ppermute | solution.py:32
  43.3 9.0 %collective-permute-start.16 = (bf16[4,4096]{1,0:T(4,128)(2,1)S(1)}, bf16[4,4096]{1,0:T(4,128)(2,1)S(1)}, u32[]{:S(2)}, u32[]{:S(2)}) collective-permute-start(bf16[4,4096]{1,0:T(4,128)(2,1)S(1)} %get-tuple-element.30), channel_id=1, source_target_pairs={{0,16},{4,20},{8,24},{12,28},{16,0},{20,4},{24,8},{28,12},{1,17},{... | collective-permute-start | bytes 98312 | tf_op jit(solution)/shard_map/ppermute | solution.py:42
  44.0 6.5 %collective-permute-start.19 = (bf16[4,2048]{1,0:T(4,128)(2,1)S(1)}, bf16[4,2048]{1,0:T(4,128)(2,1)S(1)}, u32[]{:S(2)}, u32[]{:S(2)}) collective-permute-start(bf16[4,2048]{1,0:T(4,128)(2,1)S(1)} %get-tuple-element.31), channel_id=1, source_target_pairs={{12,16},{8,20},{4,24},{0,28},{28,0},{24,4},{20,8},{16,12},{13,17},... | collective-permute-start | bytes 49160 | tf_op jit(solution)/shard_map/ppermute | solution.py:42
  46.2 5.5 %collective-permute-start.18 = (bf16[4,2048]{1,0:T(4,128)(2,1)S(1)}, bf16[4,2048]{1,0:T(4,128)(2,1)S(1)}, u32[]{:S(2)}, u32[]{:S(2)}) collective-permute-start(bf16[4,2048]{1,0:T(4,128)(2,1)S(1)} %get-tuple-element.31), channel_id=1, source_target_pairs={{8,16},{12,20},{0,24},{4,28},{24,0},{28,4},{16,8},{20,12},{9,17},{... | collective-permute-start | bytes 49160 | tf_op jit(solution)/shard_map/ppermute | solution.py:42
  47.6 4.6 %collective-permute-start.17 = (bf16[4,2048]{1,0:T(4,128)(2,1)S(1)}, bf16[4,2048]{1,0:T(4,128)(2,1)S(1)}, u32[]{:S(2)}, u32[]{:S(2)}) collective-permute-start(bf16[4,2048]{1,0:T(4,128)(2,1)S(1)} %get-tuple-element.31), channel_id=1, source_target_pairs={{4,16},{0,20},{12,24},{8,28},{20,0},{16,4},{28,8},{24,12},{5,17},{... | collective-permute-start | bytes 49160 | tf_op jit(solution)/shard_map/ppermute | solution.py:42

commit v13 on v12

--- a/solution.py
+++ b/solution.py
@@ -56,7 +56,7 @@
 def pack_kernel(dims, *refs):
     sections, tensors, rows, heads_dev, group, kv_dev = dims
     sources, refs = refs[:8], refs[8:]
-    packs, (h_ref, next_ref, lengths_ref) = refs[:tensors], refs[tensors : tensors + 3]
+    packs, (h_ref, next_ref, facts_ref) = refs[:tensors], refs[tensors : tensors + 3]
     ids, lengths, gains, biases, keys, values, sems = refs[tensors + 3 :]
     held = 2 * sections * kv_dev
     targets = (ids, lengths, keys, values, gains, biases, h_ref, next_ref)
@@ -70,17 +70,16 @@
     tenants = gains.shape[0]
     count = sections * rows
     spot = lax.broadcasted_iota(jnp.int32, (count, tenants), 0)
-    line = lax.broadcasted_iota(jnp.int32, lengths_ref.shape, 0)
+    lane = lax.broadcasted_iota(jnp.int32, facts_ref.shape, 1)
     wanted = jnp.zeros((count, tenants), jnp.int32)
-    kept = jnp.zeros(lengths_ref.shape, jnp.int32)
+    facts = jnp.zeros(facts_ref.shape, jnp.int32)
     copies[0].wait()
     copies[1].wait()
     for tick in range(sections):
         batch = batch_at(tick, sections)
-        kept = jnp.where(line == tick, lengths[batch], kept)
+        facts = jnp.where(lane == tick + 2, lengths[batch], facts)
         for i in range(rows):
             wanted = jnp.where(spot == tick * rows + i, ids[batch, i], wanted)
-    lengths_ref[...] = kept.astype(F32)
     wanted = wanted - at * tenants
     onehot = jnp.where(wanted == lax.broadcasted_iota(jnp.int32, (count, tenants), 1), 1.0, 0.0)
     onehot = onehot.astype(BF)
@@ -111,6 +110,9 @@
             for d in range(tensors if tick == 0 else min(tensors, NEAR)):
                 packs[d][held + tick * blocks + j] = block
     copies[6].wait()
+    h = h_ref[...].astype(F32)
+    facts = jnp.where(lane == 0, jnp.sum(h, axis=-1, keepdims=True), facts.astype(F32))
+    facts_ref[...] = jnp.where(lane == 1, jnp.sum(h * h, axis=-1, keepdims=True), facts)
     copies[7].wait()
 
 
@@ -122,7 +124,7 @@
     out_shape = [
         shape((held + blocks + (later if d < NEAR else 0), pos, HD)) for d in range(tensors)
     ]
-    out_shape += [shape(h.shape), shape(following.shape), shape((sections, HD), F32)]
+    out_shape += [shape(h.shape), shape(following.shape), shape((rows, HD), F32)]
     operands = (tenant, lengths, keys, values, gain, bias, h, following)
     return pl.pallas_call(
         lambda *refs: pack_kernel(dims, *refs),
@@ -148,7 +150,7 @@
     dims = pieces[0].shape
     return pl.pallas_call(
         lambda *refs: join_kernel(count, size, refs),
-        out_shape=shape((count, size) + dims[1:]),
+        out_shape=shape((count, size) + dims[1:], pieces[0].dtype),
         in_specs=[VMEM] * count + [pl.BlockSpec(memory_space=pl.ANY)] * len(after),
         out_specs=VMEM,
         compiler_params=PARAMS,
@@ -199,15 +201,24 @@
     return [high, middle, x - high - middle]
 
 
-def query_sums(first_blocks, length, h, pieces, w_ref, out_ref):
-    rows, width = h.shape
+def affine_rows(first, rows, width, pieces):
     pos, lanes = pieces[0].shape[1:]
     per = pos // (2 * rows)
     cols = []
     for j in range(width // lanes // per):
-        block = tree_sum([piece[first + j] for first, piece in zip(first_blocks, pieces)])
+        block = tree_sum([piece[first + j] for piece in pieces])
         cols += [block[k * 2 * rows : (k + 1) * 2 * rows] for k in range(per)]
-    affine = jnp.concatenate(cols, 1)
+    return jnp.concatenate(cols, 1)
+
+
+def scales(total, squares, width):
+    mean = total * (1.0 / width)
+    return mean, lax.rsqrt(squares * (1.0 / width) - mean * mean + 1e-05)
+
+
+def query_sums(first, h, pieces, w_ref, out_ref):
+    rows, width = h.shape
+    affine = affine_rows(first, rows, width, pieces)
     total = jnp.sum(h, axis=-1, keepdims=True)
     squares = jnp.sum(h * h, axis=-1, keepdims=True)
     centred = (h - total * (1.0 / width)) * affine[:rows]
@@ -219,27 +230,36 @@
             to = slice(k * count + at.start, k * count + at.stop)
             out_ref[:, to] = got[k * rows : (k + 1) * rows].astype(BF)
     lane = lax.broadcasted_iota(jnp.int32, (rows, HD), 1)
-    tail = jnp.broadcast_to(length, (rows, HD))
+    tail = jnp.zeros((rows, HD), F32)
     for i, term in enumerate(thirds(total) + thirds(squares)):
         tail = jnp.where(lane == i, term, tail)
     out_ref[:, 3 * count :] = tail.astype(BF)
 
 
-def first_kernel(tensors, held, lengths_ref, h_ref, *refs):
-    pieces, (w_ref, out_ref) = refs[:tensors], refs[tensors:]
-    query_sums([held] * tensors, lengths_ref[0:1], h_ref[...].astype(F32), pieces, w_ref, out_ref)
-
-
-def first_sums(held, lengths, h, pieces, w):
+def first_kernel(tensors, held, h_ref, *refs):
+    pieces, facts, (w_ref, out_ref) = refs[:tensors], refs[tensors:-2], refs[-2:]
+    rows, width = h_ref.shape
+    facts = [ref[i] for ref in facts for i in range(ref.shape[0])]
+    facts = tree_sum(facts)
+    replicas = lax.axis_size("replica")
+    mean, rstd = scales(facts[:, 0:1], facts[:, 1:2], width * replicas)
+    affine = affine_rows(held, rows, width, pieces)
+    x = (h_ref[...].astype(F32) - mean) * rstd * affine[:rows] + affine[rows:]
+    x = x.astype(BF)
+    for at in tiles(w_ref):
+        out_ref[:, at] = jnp.dot(x, w_ref[:, at], preferred_element_type=F32).astype(BF)
+
+
+def first_sums(held, h, pieces, facts, w):
     tensors = len(pieces)
     return pl.pallas_call(
         lambda *refs: first_kernel(tensors, held, *refs),
-        out_shape=shape((h.shape[0], 3 * w.shape[1] + HD)),
-        in_specs=[VMEM] * (tensors + 3),
+        out_shape=shape((h.shape[0], w.shape[1])),
+        in_specs=[VMEM] * (tensors + len(facts) + 2),
         out_specs=VMEM,
         compiler_params=PARAMS,
         cost_estimate=cost(24 * w.size, 2 * w.size),
-    )(lengths, h, *pieces, w)
+    )(h, *pieces, *facts, w)
 
 
 def arrive(arrivals, following, tick):
@@ -258,7 +278,7 @@
     return h, jnp.where(section == 0, came, carried)
 
 
-def later_kernel(count, tick, lengths_ref, *refs):
+def later_kernel(count, tick, *refs):
     arrivals, next_ref = refs[:count], refs[count]
     pieces, (w_ref, out_ref, carry_ref) = refs[count + 1 : -3], refs[-3:]
     h, emitted = arrive(arrivals, next_ref, tick - 1)
@@ -270,20 +290,20 @@
         carry_ref[:, :width] = h.astype(BF)
         carry_ref[:, width:] = emitted.astype(BF)
     blocks = 2 * h.shape[0] * width // (pieces[0].shape[1] * HD)
-    query_sums([(tick - 1) * blocks] * len(pieces), lengths_ref[tick : tick + 1], h, pieces, w_ref, out_ref)
-
-
-def later_sums(tick, lengths, arrivals, following, pieces, w):
+    query_sums((tick - 1) * blocks, h, pieces, w_ref, out_ref)
+
+
+def later_sums(tick, arrivals, following, pieces, w):
     rows, width = following.shape[1:]
     parts = 1 if following.shape[0] == 2 else 2
     return pl.pallas_call(
         lambda *refs: later_kernel(len(arrivals), tick, *refs),
         out_shape=[shape((rows, 3 * w.shape[1] + HD)), shape((rows, width * parts))],
-        in_specs=[VMEM] * (len(arrivals) + len(pieces) + 3),
+        in_specs=[VMEM] * (len(arrivals) + len(pieces) + 2),
         out_specs=[VMEM] * 2,
         compiler_params=PARAMS,
         cost_estimate=cost(24 * w.size, 2 * w.size),
-    )(lengths, *arrivals, following, *pieces, w)
+    )(*arrivals, following, *pieces, w)
 
 
 def last_kernel(count, *refs):
@@ -307,27 +327,30 @@
     sections, tensors, rows, kv_dev = dims
     count = len(turns)
     pieces, (carry_ref, *w_refs), refs = refs[:count], refs[count : count + 3], refs[count + 3 :]
-    caches, (out_ref, full_ref) = refs[:-2], refs[-2:]
+    (out_ref, full_ref), refs = refs[-2:], refs[:-2]
+    caches, facts = refs[: len(refs) // 2], refs[len(refs) // 2 :]
     each = caches[0].shape[0] // tensors
+    facts = [ref[i] for ref in facts for i in range(ref.shape[0])]
     span = w_refs[0].shape[0]
     half = w_refs[0].shape[1]
     width = 2 * half
     batch = batch_at(tick, sections)
 
-    tails = [piece[:, 3 * span :].astype(F32) for piece in pieces]
-    totals = [tail[:, 0:1] + tail[:, 1:2] + tail[:, 2:3] for tail in tails]
-    squares = [tail[:, 3:4] + tail[:, 4:5] + tail[:, 5:6] for tail in tails]
-    scale = 1.0 / (width * count)
-    mean = tree_sum(totals) * scale
-    rstd = lax.rsqrt(tree_sum(squares) * scale - mean * mean + 1e-05)
-    query = tree_sum(
-        [
-            piece[:, :span].astype(F32)
-            + (total * (1.0 / width) - mean) * piece[:, span : 2 * span].astype(F32)
-            for piece, total in zip(pieces, totals)
-        ]
-    )
-    query = rstd * query + tree_sum([piece[:, 2 * span : 3 * span] for piece in pieces])
+    if tick == 0:
+        query = tree_sum([piece[...] for piece in pieces])
+    else:
+        tails = [piece[:, 3 * span :].astype(F32) for piece in pieces]
+        totals = [tail[:, 0:1] + tail[:, 1:2] + tail[:, 2:3] for tail in tails]
+        squares = [tail[:, 3:4] + tail[:, 4:5] + tail[:, 5:6] for tail in tails]
+        mean, rstd = scales(tree_sum(totals), tree_sum(squares), width * count)
+        query = tree_sum(
+            [
+                piece[:, :span].astype(F32)
+                + (total * (1.0 / width) - mean) * piece[:, span : 2 * span].astype(F32)
+                for piece, total in zip(pieces, totals)
+            ]
+        )
+        query = rstd * query + tree_sum([piece[:, 2 * span : 3 * span] for piece in pieces])
     query = query.astype(BF).astype(F32)
 
     pos = caches[0].shape[2]
@@ -337,8 +360,9 @@
     spots = jnp.bitwise_xor(cols // pos, tensor_at) * pos + cols % pos
     spots = spots.astype(F32)
     keep = []
-    for turn in turns:
-        valid = jnp.logical_and(row == jnp.bitwise_xor(replica_at, turn), spots < tails[turn][:, 6:7])
+    for turn, fact in zip(turns, facts):
+        length = fact[:, tick + 2 : tick + 3]
+        valid = jnp.logical_and(row == jnp.bitwise_xor(replica_at, turn), spots < length)
         keep.append(jnp.where(valid, 0.0, -1e30))
     per_kv = span // HD // kv_dev
     keep = jnp.concatenate([jnp.concatenate(keep, 1)] * per_kv, 0)
@@ -375,16 +399,16 @@
     full_ref[:, width:] = carry_ref[...]
 
 
-def attend(dims, turns, tick, pieces, caches, carry, left, right):
+def attend(dims, turns, tick, pieces, caches, facts, carry, left, right):
     rows, width = carry.shape[0], left.shape[1] + right.shape[1]
     return pl.pallas_call(
         lambda *refs: attend_kernel(dims, turns, tick, *refs),
         out_shape=[shape((rows, width)), shape((rows, width + carry.shape[1]))],
-        in_specs=[VMEM] * (len(pieces) + len(caches) + 3),
+        in_specs=[VMEM] * (len(pieces) + len(caches) + len(facts) + 3),
         out_specs=[VMEM] * 2,
         compiler_params=PARAMS,
         cost_estimate=cost(16 * left.size, 4 * left.size),
-    )(*pieces, carry, left, right, *caches)
+    )(*pieces, carry, left, right, *caches, *facts)
 
 
 def on_device(state, next_embed, tenant, lengths, gain, bias, wq, wo, keys, values):
@@ -397,7 +421,7 @@
     kv_dev = max(1, heads_dev // group)
     dims = (sections, tensors, rows, heads_dev, group, kv_dev)
 
-    *packs, carry, following, lengths = pack(
+    *packs, carry, following, facts = pack(
         dims,
         tenant,
         lengths.reshape(-1),
@@ -410,10 +434,20 @@
     )
     got = [packs[0]] + [swapped(packs[d], "tensor", d) for d in range(1, tensors)]
     half = width // 2
-    wq_held, wo_left = hold([wq[0], wo[0]], [(0, wq.shape[2]), (0, half)], packs[0])
+    (wq_held,) = hold([wq[0]], [(0, wq.shape[2])], packs[0])
+
+    facts = [facts[None]]
+    bit = replicas // 2
+    while bit:
+        if len(facts) > 1:
+            both = join(facts, facts[0].shape[0], [wq_held])
+            facts = [both.reshape((-1,) + both.shape[2:])]
+        facts = [facts[0], swapped(facts[0], "replica", bit)]
+        bit //= 2
+    (wo_left,) = hold([wo[0]], [(0, half)], facts[0])
 
     held = 2 * sections * kv_dev
-    kv = join(got, held, [wq_held, wo_left])
+    kv = join(got, held, [wo_left, facts[-1]])
 
     later = [piece[held + 2 * rows * width // (keys.shape[4] * HD) :] for piece in got[:NEAR]]
     bit = NEAR
@@ -428,9 +462,9 @@
     arrivals = None
     for tick in range(sections):
         if tick == 0:
-            sums = first_sums(held, lengths, carry, got, wq_held)
+            sums = first_sums(held, carry, got, facts, wq_held)
         else:
-            sums, carry = later_sums(tick, lengths, arrivals, following, later, wq_held)
+            sums, carry = later_sums(tick, arrivals, following, later, wq_held)
         pieces = [sums] + [swapped(sums, "replica", d) for d in range(1, replicas)]
         if tick == 0:
             (wo_right,) = hold([wo[0]], [(half, half)], sums)
@@ -442,7 +476,7 @@
                     kv = both.reshape((-1,) + both.shape[2:])
                     waiting = swapped(kv, "replica", bit)
         out, full = attend(
-            (sections, tensors, rows, kv_dev), turns, tick, pieces, caches, carry, wo_left, wo_right
+            (sections, tensors, rows, kv_dev), turns, tick, pieces, caches, facts, carry, wo_left, wo_right
         )
         arrivals = [from_behind(full, 0)] + [from_behind(out, d) for d in range(1, tensors)]
     return tuple(last(arrivals, following))

time: 53.1 us -> 54.5 us (1.026)
  starting transfers between devices: 25.3 us -> 27.4 us
  waiting for transfers between devices: 11.6 us -> 9.92 us
  Pallas kernels: 15.4 us -> 16.3 us
    ppermute x12 -> x14, waiting for transfers between devices: 6.12 us -> 3.98 us  [swapped(): return lax.ppermute(block, axis, route)]
    ppermute x12 -> x14, starting transfers between devices: 11.8 us -> 13.8 us  [swapped(): return lax.ppermute(block, axis, route)]
    pallas_call x2 -> x3, Pallas kernels: 6.91 us -> 7.91 us  [hold(): pl.pallas_call(lambda *refs: hold_kernel(parts, columns, *refs), out_shap...]
  transfers between devices with their start and end apart: 20 -> 22, of which waited for: 12 -> 10; matrix products, arithmetic and copies ran while one was open for 0% -> 0% of each run, Pallas kernels for 19% -> 20%
where the time goes in v13:
time: 54.5 us; the launch traced here: 54.4 us
  starting transfers between devices  27.4 us (50%)
  Pallas kernels  16.3 us (30%)
  waiting for transfers between devices  9.92 us (18%)
  between operations  0.76 us (1%)
    ppermute x14, starting transfers between devices, swapped(): return lax.ppermute(block, axis, route)  13.8 us
    ppermute x8, starting transfers between devices, from_behind(): return lax.ppermute(block, ('section', 'tensor'), route)  13.5 us
    pallas_call x3, Pallas kernels, hold(): pl.pallas_call(lambda *refs: hold_kernel(parts, columns, *refs), out_shap...  7.91 us
    ppermute x8, waiting for transfers between devices, from_behind(): return lax.ppermute(block, ('section', 'tensor'), route)  5.93 us
    ppermute x14, waiting for transfers between devices, swapped(): return lax.ppermute(block, axis, route)  3.98 us
    pallas_call x2, Pallas kernels, attend(): pl.pallas_call(lambda *refs: attend_kernel(dims, turns, tick, *refs), out...  3.53 us
    pallas_call x1, Pallas kernels, pack(): pl.pallas_call(lambda *refs: pack_kernel(dims, *refs), out_shape=out_shap...  1.62 us
    pallas_call x1, Pallas kernels, first_sums(): pl.pallas_call(lambda *refs: first_kernel(tensors, held, *refs), out_shap...  1.31 us
  transfers between devices with their start and end apart: 22, of which 10 were waited for; matrix products, arithmetic and copies ran while one was open for 0% of the time, Pallas kernels for 20%

profile of v13, /device:TPU:0, one launch (start us, length us, event | category | flops | bytes accessed | tf_op | source)
XLA Modules:
  0.0 54.4 jit_solution(120042408466416581)
XLA Ops:
  0.6 1.6 %shard_map.113 = (bf16[24,16,128]{2,1,0:T(8,128)(2,1)S(1)}, bf16[24,16,128]{2,1,0:T(8,128)(2,1)S(1)}, bf16[16,16,128]{2,1,0:T(8,128)(2,1)S(1)}, bf16[16,16,128]{...) custom-call(s32[2,4]{1,0:T(2,128)} %refs_0_.1, ...), custom_call_target="tpu_custom_call" | custom-call | bytes 819200 | tf_op jit(solution)/shard_map/pallas_call | solution.py:129
  2.3 3.1 %collective-permute-start = (bf16[24,16,128]{2,1,0:T(8,128)(2,1)S(1)}, bf16[24,16,128]{2,1,0:T(8,128)(2,1)S(1)}, u32[]{:S(2)}, u32[]{:S(2)}) collective-permute-start(bf16[24,16,128]{2,1,0:T(8,128)(2,1)S(1)} %get-tuple-element.17), channel_id=1, source_target_pairs={{0,4},{4,0},{8,12},{12,8},{1,5},{5,1},{9,13},{13,9},{2,6},{6,2},{1... | collective-permute-start | bytes 294920 | tf_op jit(solution)/shard_map/ppermute | solution.py:32
  5.3 2.6 %collective-permute-start.1 = (bf16[16,16,128]{2,1,0:T(8,128)(2,1)S(1)}, bf16[16,16,128]{2,1,0:T(8,128)(2,1)S(1)}, u32[]{:S(2)}, u32[]{:S(2)}) collective-permute-start(bf16[16,16,128]{2,1,0:T(8,128)(2,1)S(1)} %get-tuple-element.18), channel_id=1, source_target_pairs={{0,8},{4,12},{8,0},{12,4},{1,9},{5,13},{9,1},{13,5},{2,10},{6,14},... | collective-permute-start | bytes 196616 | tf_op jit(solution)/shard_map/ppermute | solution.py:32
  7.9 0.0 collective-permute-start.2
  7.9 1.7 %collective-permute-start.3 = (f32[1,4,128]{2,1,0:T(4,128)S(1)}, f32[1,4,128]{2,1,0:T(4,128)S(1)}, u32[]{:S(2)}, u32[]{:S(2)}) collective-permute-start(f32[1,4,128]{2,1,0:T(4,128)S(1)} %bitcast.19), channel_id=1, source_target_pairs={{0,2},{1,3},{2,0},{3,1},{4,6},{5,7},{6,4},{7,5},{8,10},{9,11},{10,... | collective-permute-start | bytes 6152 | tf_op jit(solution)/shard_map/ppermute | solution.py:32
  9.7 3.5 %shard_map.114.refs_2_.refs_7_ = bf16[2048,2048]{1,0:T(8,128)(2,1)S(1)} custom-call(bf16[24,16,128]{2,1,0:T(8,128)(2,1)S(1)} %get-tuple-element.16.refs_0_.refs_1_, bf16[2048,2048]{1,0:T(8,128)(2,1)} %bitcast.23), custom_call_target="tpu_custom_call" | custom-call | bytes 8388608 | tf_op jit(solution)/shard_map/pallas_call | solution.py:182
  13.2 0.1 collective-permute-start.4
  13.3 2.2 %shard_map.117.refs_4_.refs_5_ = bf16[2048,1024]{1,0:T(8,128)(2,1)S(1)} custom-call(f32[2,4,128]{2,1,0:T(4,128)S(1)} %bitcast.15, bf16[2048,2048]{1,0:T(8,128)(2,1)} %bitcast.21), custom_call_target="tpu_custom_call" | custom-call | bytes 4194304 | tf_op jit(solution)/shard_map/pallas_call | solution.py:182
  15.5 0.0 collective-permute-done.4.refs_6_.refs_5_.refs_10_
  15.5 0.0 collective-permute-done.refs_2_.refs_1_
  15.6 0.4 collective-permute-start.8
  15.9 1.3 %shard_map.116.refs_0_ = bf16[4,2048]{1,0:T(4,128)(2,1)S(1)} custom-call(bf16[4,2048]{1,0:T(4,128)(2,1)S(1)} %get-tuple-element.15.refs_0_.refs_4_, bf16[24,16,128]{2,1,0:T(8,128)(2,1)S(1)} %get-tuple-element.16.refs_0_.refs_1_, bf16[24,16,128]{2,1,0:T(8,128)(2,1)S(1)} %collective-permute-done.refs_2_.refs_1_, ...), custom_call_target="tpu_custom_call" | custom-call | flops 100663296 | bytes 8388608 | tf_op jit(solution)/shard_map/pallas_call | solution.py:255
  17.2 1.6 %collective-permute-start.7 = (bf16[4,2048]{1,0:T(4,128)(2,1)S(1)}, bf16[4,2048]{1,0:T(4,128)(2,1)S(1)}, u32[]{:S(2)}, u32[]{:S(2)}) collective-permute-start(bf16[4,2048]{1,0:T(4,128)(2,1)S(1)} %shard_map.116.refs_0_), channel_id=1, source_target_pairs={{0,3},{1,2},{2,1},{3,0},{4,7},{5,6},{6,5},{7,4},{8,11},{9,10},{10,... | collective-permute-start | bytes 49160 | tf_op jit(solution)/shard_map/ppermute | solution.py:32
  18.8 0.3 collective-permute-start.6
  19.1 2.2 %shard_map.118.refs_4_.refs_6_ = bf16[2048,1024]{1,0:T(8,128)(2,1)S(1)} custom-call(bf16[4,2048]{1,0:T(4,128)(2,1)S(1)} %shard_map.116.refs_0_, bf16[2048,2048]{1,0:T(8,128)(2,1)} %bitcast.22), custom_call_target="tpu_custom_call" | custom-call | bytes 4194304 | tf_op jit(solution)/shard_map/pallas_call | solution.py:182
  21.3 0.2 collective-permute-done.7.refs_3_
  21.5 1.1 %collective-permute-done.6.refs_2_ = bf16[4,2048]{1,0:T(4,128)(2,1)S(1)} collective-permute-done((bf16[4,2048]{1,0:T(4,128)(2,1)S(1)}, bf16[4,2048]{1,0:T(4,128)(2,1)S(1)}, u32[]{:S(2)}, u32[]{:S(2)}) %collective-permute-start.6) | collective-permute-done | bytes 16416 | tf_op jit(solution)/shard_map/ppermute | solution.py:32
  22.5 0.0 collective-permute-done.8.refs_1_
  22.5 0.1 collective-permute-start.9
  22.6 0.5 collective-permute-start.5
  23.1 1.7 %collective-permute-start.14 = (bf16[8,16,128]{2,1,0:T(8,128)(2,1)S(1)}, bf16[8,16,128]{2,1,0:T(8,128)(2,1)S(1)}, u32[]{:S(2)}, u32[]{:S(2)}) collective-permute-start(bf16[8,16,128]{2,1,0:T(8,128)(2,1)S(1)} %slice_add_fusion.refs_5_), channel_id=1, source_target_pairs={{0,8},{4,12},{8,0},{12,4},{1,9},{5,13},{9,1},{13,5},{2,10},{6,14},... | collective-permute-start | bytes 98312 | tf_op jit(solution)/shard_map/ppermute | solution.py:32
  24.8 0.0 collective-permute-done.9.refs_8_
  24.8 1.7 %shard_map.121 = (bf16[4,2048]{1,0:T(4,128)(2,1)S(1)}, bf16[4,4096]{1,0:T(4,128)(2,1)S(1)}) custom-call(bf16[4,2048]{1,0:T(4,128)(2,1)S(1)} %shard_map.116.refs_0_, bf16[4,2048]{1,0:T(4,128)(2,1)S(1)} %collective-permute-done.5.refs_1_, bf16[4,2048]{1,0:T(4,128)(2,1)S(1)} %collective-permute-done.6.refs_2_, ...), custom_call_target="tpu_custom_call" | custom-call | flops 33554432 | bytes 8388608 | tf_op jit(solution)/shard_map/pallas_call | solution.py:404
  26.5 1.5 %collective-permute-start.10 = (bf16[4,4096]{1,0:T(4,128)(2,1)S(1)}, bf16[4,4096]{1,0:T(4,128)(2,1)S(1)}, u32[]{:S(2)}, u32[]{:S(2)}) collective-permute-start(bf16[4,4096]{1,0:T(4,128)(2,1)S(1)} %get-tuple-element.21), channel_id=1, source_target_pairs={{0,16},{4,20},{8,24},{12,28},{16,0},{20,4},{24,8},{28,12},{1,17},{... | collective-permute-start | bytes 98312 | tf_op jit(solution)/shard_map/ppermute | solution.py:42
  28.0 2.9 %collective-permute-start.13 = (bf16[4,2048]{1,0:T(4,128)(2,1)S(1)}, bf16[4,2048]{1,0:T(4,128)(2,1)S(1)}, u32[]{:S(2)}, u32[]{:S(2)}) collective-permute-start(bf16[4,2048]{1,0:T(4,128)(2,1)S(1)} %get-tuple-element.22), channel_id=1, source_target_pairs={{12,16},{8,20},{4,24},{0,28},{28,0},{24,4},{20,8},{16,12},{13,17},... | collective-permute-start | bytes 49160 | tf_op jit(solution)/shard_map/ppermute | solution.py:42
  30.9 1.9 %collective-permute-start.12 = (bf16[4,2048]{1,0:T(4,128)(2,1)S(1)}, bf16[4,2048]{1,0:T(4,128)(2,1)S(1)}, u32[]{:S(2)}, u32[]{:S(2)}) collective-permute-start(bf16[4,2048]{1,0:T(4,128)(2,1)S(1)} %get-tuple-element.22), channel_id=1, source_target_pairs={{8,16},{12,20},{0,24},{4,28},{24,0},{28,4},{16,8},{20,12},{9,17},{... | collective-permute-start | bytes 49160 | tf_op jit(solution)/shard_map/ppermute | solution.py:42
  32.8 0.4 collective-permute-start.11
  33.3 0.0 collective-permute-done.14.refs_6_
  33.3 1.2 %collective-permute-done.13.refs_3_ = bf16[4,2048]{1,0:T(4,128)(2,1)S(1)} collective-permute-done((bf16[4,2048]{1,0:T(4,128)(2,1)S(1)}, bf16[4,2048]{1,0:T(4,128)(2,1)S(1)}, u32[]{:S(2)}, u32[]{:S(2)}) %collective-permute-start.13) | collective-permute-done | bytes 16416 | tf_op jit(solution)/shard_map/ppermute | solution.py:42
  34.4 2.0 %collective-permute-done.12.refs_2_ = bf16[4,2048]{1,0:T(4,128)(2,1)S(1)} collective-permute-done((bf16[4,2048]{1,0:T(4,128)(2,1)S(1)}, bf16[4,2048]{1,0:T(4,128)(2,1)S(1)}, u32[]{:S(2)}, u32[]{:S(2)}) %collective-permute-start.12) | collective-permute-done | bytes 16416 | tf_op jit(solution)/shard_map/ppermute | solution.py:42
  36.5 1.0 %collective-permute-done.11.refs_1_ = bf16[4,2048]{1,0:T(4,128)(2,1)S(1)} collective-permute-done((bf16[4,2048]{1,0:T(4,128)(2,1)S(1)}, bf16[4,2048]{1,0:T(4,128)(2,1)S(1)}, u32[]{:S(2)}, u32[]{:S(2)}) %collective-permute-start.11) | collective-permute-done | bytes 16416 | tf_op jit(solution)/shard_map/ppermute | solution.py:42
  37.5 1.3 %shard_map.122 = (bf16[4,6272]{1,0:T(4,128)(2,1)S(1)}, bf16[4,2048]{1,0:T(4,128)(2,1)S(1)}) custom-call(bf16[4,4096]{1,0:T(4,128)(2,1)S(1)} %collective-permute-done.10.refs_0_, bf16[4,2048]{1,0:T(4,128)(2,1)S(1)} %collective-permute-done.11.refs_1_, bf16[4,2048]{1,0:T(4,128)(2,1)S(1)} %collective-permute-done.12.refs_2_, ...), custom_call_target="tpu_custom_call" | custom-call | flops 100663296 | bytes 8388608 | tf_op jit(solution)/shard_map/pallas_call | solution.py:299
  38.8 0.0 collective-permute-start.17
  38.8 0.6 %collective-permute-start.16 = (bf16[4,6272]{1,0:T(4,128)(2,1)S(1)}, bf16[4,6272]{1,0:T(4,128)(2,1)S(1)}, u32[]{:S(2)}, u32[]{:S(2)}) collective-permute-start(bf16[4,6272]{1,0:T(4,128)(2,1)S(1)} %get-tuple-element.24.refs_0_), channel_id=1, source_target_pairs={{0,2},{1,3},{2,0},{3,1},{4,6},{5,7},{6,4},{7,5},{8,10},{9,11},{10,... | collective-permute-start | bytes 150536 | tf_op jit(solution)/shard_map/ppermute | solution.py:32
  39.4 1.3 %collective-permute-start.15 = (bf16[4,6272]{1,0:T(4,128)(2,1)S(1)}, bf16[4,6272]{1,0:T(4,128)(2,1)S(1)}, u32[]{:S(2)}, u32[]{:S(2)}) collective-permute-start(bf16[4,6272]{1,0:T(4,128)(2,1)S(1)} %get-tuple-element.24.refs_0_), channel_id=1, source_target_pairs={{0,1},{1,0},{2,3},{3,2},{4,5},{5,4},{6,7},{7,6},{8,9},{9,8},{10,11... | collective-permute-start | bytes 150536 | tf_op jit(solution)/shard_map/ppermute | solution.py:32
  40.6 1.7 %collective-permute-done.17.refs_3_ = bf16[4,6272]{1,0:T(4,128)(2,1)S(1)} collective-permute-done((bf16[4,6272]{1,0:T(4,128)(2,1)S(1)}, bf16[4,6272]{1,0:T(4,128)(2,1)S(1)}, u32[]{:S(2)}, u32[]{:S(2)}) %collective-permute-start.17) | collective-permute-done | bytes 50208 | tf_op jit(solution)/shard_map/ppermute | solution.py:32
  42.3 1.1 %collective-permute-done.16.refs_2_ = bf16[4,6272]{1,0:T(4,128)(2,1)S(1)} collective-permute-done((bf16[4,6272]{1,0:T(4,128)(2,1)S(1)}, bf16[4,6272]{1,0:T(4,128)(2,1)S(1)}, u32[]{:S(2)}, u32[]{:S(2)}) %collective-permute-start.16) | collective-permute-done | bytes 50208 | tf_op jit(solution)/shard_map/ppermute | solution.py:32
  43.4 0.0 collective-permute-done.15.refs_1_
  43.4 1.9 %shard_map.123 = (bf16[4,2048]{1,0:T(4,128)(2,1)S(1)}, bf16[4,4096]{1,0:T(4,128)(2,1)S(1)}) custom-call(bf16[4,6272]{1,0:T(4,128)(2,1)S(1)} %get-tuple-element.24.refs_0_, bf16[4,6272]{1,0:T(4,128)(2,1)S(1)} %collective-permute-done.15.refs_1_, bf16[4,6272]{1,0:T(4,128)(2,1)S(1)} %collective-permute-done.16.refs_2_, ...), custom_call_target="tpu_custom_call" | custom-call | flops 33554432 | bytes 8388608 | tf_op jit(solution)/shard_map/pallas_call | solution.py:404
  45.2 0.7 %collective-permute-start.18 = (bf16[4,4096]{1,0:T(4,128)(2,1)S(1)}, bf16[4,4096]{1,0:T(4,128)(2,1)S(1)}, u32[]{:S(2)}, u32[]{:S(2)}) collective-permute-start(bf16[4,4096]{1,0:T(4,128)(2,1)S(1)} %get-tuple-element.26), channel_id=1, source_target_pairs={{0,16},{4,20},{8,24},{12,28},{16,0},{20,4},{24,8},{28,12},{1,17},{... | collective-permute-start | bytes 98312 | tf_op jit(solution)/shard_map/ppermute | solution.py:42
  45.9 1.3 %collective-permute-start.21 = (bf16[4,2048]{1,0:T(4,128)(2,1)S(1)}, bf16[4,2048]{1,0:T(4,128)(2,1)S(1)}, u32[]{:S(2)}, u32[]{:S(2)}) collective-permute-start(bf16[4,2048]{1,0:T(4,128)(2,1)S(1)} %get-tuple-element.27), channel_id=1, source_target_pairs={{12,16},{8,20},{4,24},{0,28},{28,0},{24,4},{20,8},{16,12},{13,17},... | collective-permute-start | bytes 49160 | tf_op jit(solution)/shard_map/ppermute | solution.py:42
  47.2 1.5 %collective-permute-start.20 = (bf16[4,2048]{1,0:T(4,128)(2,1)S(1)}, bf16[4,2048]{1,0:T(4,128)(2,1)S(1)}, u32[]{:S(2)}, u32[]{:S(2)}) collective-permute-start(bf16[4,2048]{1,0:T(4,128)(2,1)S(1)} %get-tuple-element.27), channel_id=1, source_target_pairs={{8,16},{12,20},{0,24},{4,28},{24,0},{28,4},{16,8},{20,12},{9,17},{... | collective-permute-start | bytes 49160 | tf_op jit(solution)/shard_map/ppermute | solution.py:42
  48.7 3.3 %collective-permute-start.19 = (bf16[4,2048]{1,0:T(4,128)(2,1)S(1)}, bf16[4,2048]{1,0:T(4,128)(2,1)S(1)}, u32[]{:S(2)}, u32[]{:S(2)}) collective-permute-start(bf16[4,2048]{1,0:T(4,128)(2,1)S(1)} %get-tuple-element.27), channel_id=1, source_target_pairs={{4,16},{0,20},{12,24},{8,28},{20,0},{16,4},{28,8},{24,12},{5,17},{... | collective-permute-start | bytes 49160 | tf_op jit(solution)/shard_map/ppermute | solution.py:42
  52.0 0.4 collective-permute-done.21.refs_3_
  52.4 0.4 collective-permute-done.20.refs_2_
  52.9 0.8 %collective-permute-done.19.refs_1_ = bf16[4,2048]{1,0:T(4,128)(2,1)S(1)} collective-permute-done((bf16[4,2048]{1,0:T(4,128)(2,1)S(1)}, bf16[4,2048]{1,0:T(4,128)(2,1)S(1)}, u32[]{:S(2)}, u32[]{:S(2)}) %collective-permute-start.19) | collective-permute-done | bytes 16416 | tf_op jit(solution)/shard_map/ppermute | solution.py:42
  53.7 0.0 collective-permute-done.18.refs_0_
  53.7 0.6 %shard_map.124 = (bf16[1,4,2048]{2,1,0:T(4,128)(2,1)}, bf16[1,4,2048]{2,1,0:T(4,128)(2,1)}) custom-call(bf16[4,4096]{1,0:T(4,128)(2,1)S(1)} %collective-permute-done.18.refs_0_, bf16[4,2048]{1,0:T(4,128)(2,1)S(1)} %collective-permute-done.19.refs_1_, bf16[4,2048]{1,0:T(4,128)(2,1)S(1)} %collective-permute-done.20.refs_2_, ...), custom_call_target="tpu_custom_call" | custom-call | tf_op jit(solution)/shard_map/pallas_call | solution.py:317
  (9 shorter events, 0.1 us)
Async XLA Ops:
  2.3 13.3 %collective-permute-start = (bf16[24,16,128]{2,1,0:T(8,128)(2,1)S(1)}, bf16[24,16,128]{2,1,0:T(8,128)(2,1)S(1)}, u32[]{:S(2)}, u32[]{:S(2)}) collective-permute-start(bf16[24,16,128]{2,1,0:T(8,128)(2,1)S(1)} %get-tuple-element.17), channel_id=1, source_target_pairs={{0,4},{4,0},{8,12},{12,8},{1,5},{5,1},{9,13},{13,9},{2,6},{6,2},{1... | collective-permute-start | bytes 294920 | tf_op jit(solution)/shard_map/ppermute | solution.py:32
  5.3 10.2 %collective-permute-start.1 = (bf16[16,16,128]{2,1,0:T(8,128)(2,1)S(1)}, bf16[16,16,128]{2,1,0:T(8,128)(2,1)S(1)}, u32[]{:S(2)}, u32[]{:S(2)}) collective-permute-start(bf16[16,16,128]{2,1,0:T(8,128)(2,1)S(1)} %get-tuple-element.18), channel_id=1, source_target_pairs={{0,8},{4,12},{8,0},{12,4},{1,9},{5,13},{9,1},{13,5},{2,10},{6,14},... | collective-permute-start | bytes 196616 | tf_op jit(solution)/shard_map/ppermute | solution.py:32
  7.9 7.6 %collective-permute-start.2 = (bf16[16,16,128]{2,1,0:T(8,128)(2,1)S(1)}, bf16[16,16,128]{2,1,0:T(8,128)(2,1)S(1)}, u32[]{:S(2)}, u32[]{:S(2)}) collective-permute-start(bf16[16,16,128]{2,1,0:T(8,128)(2,1)S(1)} %get-tuple-element.19), channel_id=1, source_target_pairs={{0,12},{4,8},{8,4},{12,0},{1,13},{5,9},{9,5},{13,1},{2,14},{6,10},... | collective-permute-start | bytes 196616 | tf_op jit(solution)/shard_map/ppermute | solution.py:32
  7.9 5.2 %collective-permute-start.3 = (f32[1,4,128]{2,1,0:T(4,128)S(1)}, f32[1,4,128]{2,1,0:T(4,128)S(1)}, u32[]{:S(2)}, u32[]{:S(2)}) collective-permute-start(f32[1,4,128]{2,1,0:T(4,128)S(1)} %bitcast.19), channel_id=1, source_target_pairs={{0,2},{1,3},{2,0},{3,1},{4,6},{5,7},{6,4},{7,5},{8,10},{9,11},{10,... | collective-permute-start | bytes 6152 | tf_op jit(solution)/shard_map/ppermute | solution.py:32
  13.2 2.3 %collective-permute-start.4 = (f32[2,4,128]{2,1,0:T(4,128)S(1)}, f32[2,4,128]{2,1,0:T(4,128)S(1)}, u32[]{:S(2)}, u32[]{:S(2)}) collective-permute-start(f32[2,4,128]{2,1,0:T(4,128)S(1)} %bitcast.14), channel_id=1, source_target_pairs={{0,1},{1,0},{2,3},{3,2},{4,5},{5,4},{6,7},{7,6},{8,9},{9,8},{10,11... | collective-permute-start | bytes 12296 | tf_op jit(solution)/shard_map/ppermute | solution.py:32
  15.6 7.0 %collective-permute-start.8 = (bf16[4,8,16,128]{3,2,1,0:T(8,128)(2,1)S(1)}, bf16[4,8,16,128]{3,2,1,0:T(8,128)(2,1)S(1)}, u32[]{:S(2)}, u32[]{:S(2)}) collective-permute-start(bf16[4,8,16,128]{3,2,1,0:T(8,128)(2,1)S(1)} %shard_map.119.refs_0_), channel_id=1, source_target_pairs={{0,2},{1,3},{2,0},{3,1},{4,6},{5,7},{6,4},{7,5},{8,10},{9,11},{10,... | collective-permute-start | bytes 393224 | tf_op jit(solution)/shard_map/ppermute | solution.py:32
  17.2 4.2 %collective-permute-start.7 = (bf16[4,2048]{1,0:T(4,128)(2,1)S(1)}, bf16[4,2048]{1,0:T(4,128)(2,1)S(1)}, u32[]{:S(2)}, u32[]{:S(2)}) collective-permute-start(bf16[4,2048]{1,0:T(4,128)(2,1)S(1)} %shard_map.116.refs_0_), channel_id=1, source_target_pairs={{0,3},{1,2},{2,1},{3,0},{4,7},{5,6},{6,5},{7,4},{8,11},{9,10},{10,... | collective-permute-start | bytes 49160 | tf_op jit(solution)/shard_map/ppermute | solution.py:32
  18.8 3.7 %collective-permute-start.6 = (bf16[4,2048]{1,0:T(4,128)(2,1)S(1)}, bf16[4,2048]{1,0:T(4,128)(2,1)S(1)}, u32[]{:S(2)}, u32[]{:S(2)}) collective-permute-start(bf16[4,2048]{1,0:T(4,128)(2,1)S(1)} %shard_map.116.refs_0_), channel_id=1, source_target_pairs={{0,2},{1,3},{2,0},{3,1},{4,6},{5,7},{6,4},{7,5},{8,10},{9,11},{10,... | collective-permute-start | bytes 49160 | tf_op jit(solution)/shard_map/ppermute | solution.py:32
  22.5 2.3 %collective-permute-start.9 = (bf16[8,8,16,128]{3,2,1,0:T(8,128)(2,1)S(1)}, bf16[8,8,16,128]{3,2,1,0:T(8,128)(2,1)S(1)}, u32[]{:S(2)}, u32[]{:S(2)}) collective-permute-start(bf16[8,8,16,128]{3,2,1,0:T(8,128)(2,1)S(1)} %bitcast.11), channel_id=1, source_target_pairs={{0,1},{1,0},{2,3},{3,2},{4,5},{5,4},{6,7},{7,6},{8,9},{9,8},{10,11... | collective-permute-start | bytes 786440 | tf_op jit(solution)/shard_map/ppermute | solution.py:32
  22.6 2.2 %collective-permute-start.5 = (bf16[4,2048]{1,0:T(4,128)(2,1)S(1)}, bf16[4,2048]{1,0:T(4,128)(2,1)S(1)}, u32[]{:S(2)}, u32[]{:S(2)}) collective-permute-start(bf16[4,2048]{1,0:T(4,128)(2,1)S(1)} %shard_map.116.refs_0_), channel_id=1, source_target_pairs={{0,1},{1,0},{2,3},{3,2},{4,5},{5,4},{6,7},{7,6},{8,9},{9,8},{10,11... | collective-permute-start | bytes 49160 | tf_op jit(solution)/shard_map/ppermute | solution.py:32
  23.1 10.1 %collective-permute-start.14 = (bf16[8,16,128]{2,1,0:T(8,128)(2,1)S(1)}, bf16[8,16,128]{2,1,0:T(8,128)(2,1)S(1)}, u32[]{:S(2)}, u32[]{:S(2)}) collective-permute-start(bf16[8,16,128]{2,1,0:T(8,128)(2,1)S(1)} %slice_add_fusion.refs_5_), channel_id=1, source_target_pairs={{0,8},{4,12},{8,0},{12,4},{1,9},{5,13},{9,1},{13,5},{2,10},{6,14},... | collective-permute-start | bytes 98312 | tf_op jit(solution)/shard_map/ppermute | solution.py:32
  26.5 11.0 %collective-permute-start.10 = (bf16[4,4096]{1,0:T(4,128)(2,1)S(1)}, bf16[4,4096]{1,0:T(4,128)(2,1)S(1)}, u32[]{:S(2)}, u32[]{:S(2)}) collective-permute-start(bf16[4,4096]{1,0:T(4,128)(2,1)S(1)} %get-tuple-element.21), channel_id=1, source_target_pairs={{0,16},{4,20},{8,24},{12,28},{16,0},{20,4},{24,8},{28,12},{1,17},{... | collective-permute-start | bytes 98312 | tf_op jit(solution)/shard_map/ppermute | solution.py:42
  28.0 6.4 %collective-permute-start.13 = (bf16[4,2048]{1,0:T(4,128)(2,1)S(1)}, bf16[4,2048]{1,0:T(4,128)(2,1)S(1)}, u32[]{:S(2)}, u32[]{:S(2)}) collective-permute-start(bf16[4,2048]{1,0:T(4,128)(2,1)S(1)} %get-tuple-element.22), channel_id=1, source_target_pairs={{12,16},{8,20},{4,24},{0,28},{28,0},{24,4},{20,8},{16,12},{13,17},... | collective-permute-start | bytes 49160 | tf_op jit(solution)/shard_map/ppermute | solution.py:42
  30.9 5.5 %collective-permute-start.12 = (bf16[4,2048]{1,0:T(4,128)(2,1)S(1)}, bf16[4,2048]{1,0:T(4,128)(2,1)S(1)}, u32[]{:S(2)}, u32[]{:S(2)}) collective-permute-start(bf16[4,2048]{1,0:T(4,128)(2,1)S(1)} %get-tuple-element.22), channel_id=1, source_target_pairs={{8,16},{12,20},{0,24},{4,28},{24,0},{28,4},{16,8},{20,12},{9,17},{... | collective-permute-start | bytes 49160 | tf_op jit(solution)/shard_map/ppermute | solution.py:42
  32.8 4.6 %collective-permute-start.11 = (bf16[4,2048]{1,0:T(4,128)(2,1)S(1)}, bf16[4,2048]{1,0:T(4,128)(2,1)S(1)}, u32[]{:S(2)}, u32[]{:S(2)}) collective-permute-start(bf16[4,2048]{1,0:T(4,128)(2,1)S(1)} %get-tuple-element.22), channel_id=1, source_target_pairs={{4,16},{0,20},{12,24},{8,28},{20,0},{16,4},{28,8},{24,12},{5,17},{... | collective-permute-start | bytes 49160 | tf_op jit(solution)/shard_map/ppermute | solution.py:42
  38.8 3.5 %collective-permute-start.17 = (bf16[4,6272]{1,0:T(4,128)(2,1)S(1)}, bf16[4,6272]{1,0:T(4,128)(2,1)S(1)}, u32[]{:S(2)}, u32[]{:S(2)}) collective-permute-start(bf16[4,6272]{1,0:T(4,128)(2,1)S(1)} %get-tuple-element.24.refs_0_), channel_id=1, source_target_pairs={{0,3},{1,2},{2,1},{3,0},{4,7},{5,6},{6,5},{7,4},{8,11},{9,10},{10,... | collective-permute-start | bytes 150536 | tf_op jit(solution)/shard_map/ppermute | solution.py:32
  38.8 4.6 %collective-permute-start.16 = (bf16[4,6272]{1,0:T(4,128)(2,1)S(1)}, bf16[4,6272]{1,0:T(4,128)(2,1)S(1)}, u32[]{:S(2)}, u32[]{:S(2)}) collective-permute-start(bf16[4,6272]{1,0:T(4,128)(2,1)S(1)} %get-tuple-element.24.refs_0_), channel_id=1, source_target_pairs={{0,2},{1,3},{2,0},{3,1},{4,6},{5,7},{6,4},{7,5},{8,10},{9,11},{10,... | collective-permute-start | bytes 150536 | tf_op jit(solution)/shard_map/ppermute | solution.py:32
  39.4 4.0 %collective-permute-start.15 = (bf16[4,6272]{1,0:T(4,128)(2,1)S(1)}, bf16[4,6272]{1,0:T(4,128)(2,1)S(1)}, u32[]{:S(2)}, u32[]{:S(2)}) collective-permute-start(bf16[4,6272]{1,0:T(4,128)(2,1)S(1)} %get-tuple-element.24.refs_0_), channel_id=1, source_target_pairs={{0,1},{1,0},{2,3},{3,2},{4,5},{5,4},{6,7},{7,6},{8,9},{9,8},{10,11... | collective-permute-start | bytes 150536 | tf_op jit(solution)/shard_map/ppermute | solution.py:32
  45.2 8.5 %collective-permute-start.18 = (bf16[4,4096]{1,0:T(4,128)(2,1)S(1)}, bf16[4,4096]{1,0:T(4,128)(2,1)S(1)}, u32[]{:S(2)}, u32[]{:S(2)}) collective-permute-start(bf16[4,4096]{1,0:T(4,128)(2,1)S(1)} %get-tuple-element.26), channel_id=1, source_target_pairs={{0,16},{4,20},{8,24},{12,28},{16,0},{20,4},{24,8},{28,12},{1,17},{... | collective-permute-start | bytes 98312 | tf_op jit(solution)/shard_map/ppermute | solution.py:42
  45.9 6.5 %collective-permute-start.21 = (bf16[4,2048]{1,0:T(4,128)(2,1)S(1)}, bf16[4,2048]{1,0:T(4,128)(2,1)S(1)}, u32[]{:S(2)}, u32[]{:S(2)}) collective-permute-start(bf16[4,2048]{1,0:T(4,128)(2,1)S(1)} %get-tuple-element.27), channel_id=1, source_target_pairs={{12,16},{8,20},{4,24},{0,28},{28,0},{24,4},{20,8},{16,12},{13,17},... | collective-permute-start | bytes 49160 | tf_op jit(solution)/shard_map/ppermute | solution.py:42
  47.2 5.7 %collective-permute-start.20 = (bf16[4,2048]{1,0:T(4,128)(2,1)S(1)}, bf16[4,2048]{1,0:T(4,128)(2,1)S(1)}, u32[]{:S(2)}, u32[]{:S(2)}) collective-permute-start(bf16[4,2048]{1,0:T(4,128)(2,1)S(1)} %get-tuple-element.27), channel_id=1, source_target_pairs={{8,16},{12,20},{0,24},{4,28},{24,0},{28,4},{16,8},{20,12},{9,17},{... | collective-permute-start | bytes 49160 | tf_op jit(solution)/shard_map/ppermute | solution.py:42
  48.7 5.1 %collective-permute-start.19 = (bf16[4,2048]{1,0:T(4,128)(2,1)S(1)}, bf16[4,2048]{1,0:T(4,128)(2,1)S(1)}, u32[]{:S(2)}, u32[]{:S(2)}) collective-permute-start(bf16[4,2048]{1,0:T(4,128)(2,1)S(1)} %get-tuple-element.27), channel_id=1, source_target_pairs={{4,16},{0,20},{12,24},{8,28},{20,0},{16,4},{28,8},{24,12},{5,17},{... | collective-permute-start | bytes 49160 | tf_op jit(solution)/shard_map/ppermute | solution.py:42

commit v14 on v12

--- a/solution.py
+++ b/solution.py
@@ -244,7 +244,10 @@
 
 def arrive(arrivals, following, tick):
     sections, rows, width = following.shape
-    rest = arrivals[0][:, width:].astype(F32)
+    if arrivals[0].shape[1] == width:
+        arrivals, rest = arrivals[:-1], arrivals[-1][...].astype(F32)
+    else:
+        rest = arrivals[0][:, width:].astype(F32)
     section = jnp.full((rows, width), lax.axis_index("section"))
     left, carried = rest[:, :width], jnp.zeros((rows, width), F32)
     if sections == 2 and tick > 0:
@@ -433,18 +436,22 @@
             sums, carry = later_sums(tick, lengths, arrivals, following, later, wq_held)
         pieces = [sums] + [swapped(sums, "replica", d) for d in range(1, replicas)]
         if tick == 0:
+            behind = from_behind(carry, 0)
             (wo_right,) = hold([wo[0]], [(half, half)], sums)
             while bit:
                 turns = turns + [turn ^ bit for turn in turns]
                 caches, bit = [kv, waiting], bit // 2
                 if bit:
-                    both = join(caches, kv.shape[0], pieces[2:] + [wo_right])
+                    both = join(caches, kv.shape[0], pieces[2:] + [wo_right, behind])
                     kv = both.reshape((-1,) + both.shape[2:])
                     waiting = swapped(kv, "replica", bit)
         out, full = attend(
             (sections, tensors, rows, kv_dev), turns, tick, pieces, caches, carry, wo_left, wo_right
         )
-        arrivals = [from_behind(full, 0)] + [from_behind(out, d) for d in range(1, tensors)]
+        arrivals = [from_behind(out if tick == 0 else full, 0)]
+        arrivals += [from_behind(out, d) for d in range(1, tensors)]
+        if tick == 0:
+            arrivals += [behind]
     return tuple(last(arrivals, following))
 
 

time: 53.1 us -> 53.7 us (1.011)
  waiting for transfers between devices: 11.6 us -> 9.78 us
  starting transfers between devices: 25.3 us -> 27.1 us
  Pallas kernels: 15.4 us -> 16 us
    ppermute x12, waiting for transfers between devices: 6.12 us -> 4.61 us  [swapped(): return lax.ppermute(block, axis, route)]
    ppermute x8 -> x9, starting transfers between devices: 13.5 us -> 15 us  [from_behind(): return lax.ppermute(block, ('section', 'tensor'), route)]
    pallas_call x2, Pallas kernels: 3.71 us -> 4.33 us  [attend(): pl.pallas_call(lambda *refs: attend_kernel(dims, turns, tick, *refs), out...]
    ppermute x8 -> x9, waiting for transfers between devices: 5.45 us -> 5.17 us  [from_behind(): return lax.ppermute(block, ('section', 'tensor'), route)]
  transfers between devices with their start and end apart: 20 -> 21, of which waited for: 12 -> 10; matrix products, arithmetic and copies ran while one was open for 0% -> 0% of each run, Pallas kernels for 19% -> 20%
where the time goes in v14:
time: 53.7 us; the launch traced here: 53.5 us
  starting transfers between devices  27.1 us (50%)
  Pallas kernels  16 us (30%)
  waiting for transfers between devices  9.78 us (18%)
  between operations  0.69 us (1%)
    ppermute x9, starting transfers between devices, from_behind(): return lax.ppermute(block, ('section', 'tensor'), route)  15 us
    ppermute x12, starting transfers between devices, swapped(): return lax.ppermute(block, axis, route)  12.1 us
    pallas_call x2, Pallas kernels, hold(): pl.pallas_call(lambda *refs: hold_kernel(parts, columns, *refs), out_shap...  6.91 us
    ppermute x9, waiting for transfers between devices, from_behind(): return lax.ppermute(block, ('section', 'tensor'), route)  5.17 us
    ppermute x12, waiting for transfers between devices, swapped(): return lax.ppermute(block, axis, route)  4.61 us
    pallas_call x2, Pallas kernels, attend(): pl.pallas_call(lambda *refs: attend_kernel(dims, turns, tick, *refs), out...  4.33 us
    pallas_call x1, Pallas kernels, pack(): pl.pallas_call(lambda *refs: pack_kernel(dims, *refs), out_shape=out_shap...  1.52 us
    pallas_call x1, Pallas kernels, later_sums(): pl.pallas_call(lambda *refs: later_kernel(len(arrivals), tick, *refs), ou...  1.28 us
  transfers between devices with their start and end apart: 21, of which 10 were waited for; matrix products, arithmetic and copies ran while one was open for 0% of the time, Pallas kernels for 20%

profile of v14, /device:TPU:0, one launch (start us, length us, event | category | flops | bytes accessed | tf_op | source)
XLA Modules:
  0.0 53.5 jit_solution(16404165440979375001)
XLA Ops:
  0.6 1.5 %shard_map.113 = (bf16[24,16,128]{2,1,0:T(8,128)(2,1)S(1)}, bf16[24,16,128]{2,1,0:T(8,128)(2,1)S(1)}, bf16[16,16,128]{2,1,0:T(8,128)(2,1)S(1)}, bf16[16,16,128]{...) custom-call(s32[2,4]{1,0:T(2,128)} %refs_0_.1, ...), custom_call_target="tpu_custom_call" | custom-call | bytes 819200 | tf_op jit(solution)/shard_map/pallas_call | solution.py:127
  2.2 3.1 %collective-permute-start = (bf16[24,16,128]{2,1,0:T(8,128)(2,1)S(1)}, bf16[24,16,128]{2,1,0:T(8,128)(2,1)S(1)}, u32[]{:S(2)}, u32[]{:S(2)}) collective-permute-start(bf16[24,16,128]{2,1,0:T(8,128)(2,1)S(1)} %get-tuple-element.19), channel_id=1, source_target_pairs={{0,4},{4,0},{8,12},{12,8},{1,5},{5,1},{9,13},{13,9},{2,6},{6,2},{1... | collective-permute-start | bytes 294920 | tf_op jit(solution)/shard_map/ppermute | solution.py:32
  5.3 2.6 %collective-permute-start.1 = (bf16[16,16,128]{2,1,0:T(8,128)(2,1)S(1)}, bf16[16,16,128]{2,1,0:T(8,128)(2,1)S(1)}, u32[]{:S(2)}, u32[]{:S(2)}) collective-permute-start(bf16[16,16,128]{2,1,0:T(8,128)(2,1)S(1)} %get-tuple-element.20), channel_id=1, source_target_pairs={{0,8},{4,12},{8,0},{12,4},{1,9},{5,13},{9,1},{13,5},{2,10},{6,14},... | collective-permute-start | bytes 196616 | tf_op jit(solution)/shard_map/ppermute | solution.py:32
  7.8 0.0 collective-permute-start.2
  7.8 4.7 %shard_map.114 = (bf16[2048,2048]{1,0:T(8,128)(2,1)S(1)}, bf16[2048,1024]{1,0:T(8,128)(2,1)S(1)}) custom-call(bf16[24,16,128]{2,1,0:T(8,128)(2,1)S(1)} %get-tuple-element.18.refs_0_.refs_2_, bf16[2048,2048]{1,0:T(8,128)(2,1)} %bitcast.14, bf16[2048,2048]{1,0:T(8,128)(2,1)} %bitcast.12), custom_call_target="tpu_custom_call" | custom-call | bytes 12582912 | tf_op jit(solution)/shard_map/pallas_call | solution.py:180
  12.5 0.3 collective-permute-done.1.refs_4_.refs_2_
  12.9 1.2 %collective-permute-done.2.refs_5_.refs_3_ = bf16[16,16,128]{2,1,0:T(8,128)(2,1)S(1)} collective-permute-done((bf16[16,16,128]{2,1,0:T(8,128)(2,1)S(1)}, bf16[16,16,128]{2,1,0:T(8,128)(2,1)S(1)}, u32[]{:S(2)}, u32[]{:S(2)}) %collective-permute-start.2) | collective-permute-done | bytes 65568 | tf_op jit(solution)/shard_map/ppermute | solution.py:32
  14.0 0.0 collective-permute-done.refs_3_.refs_1_
  14.0 1.6 %collective-permute-start.6 = (bf16[4,8,16,128]{3,2,1,0:T(8,128)(2,1)S(1)}, bf16[4,8,16,128]{3,2,1,0:T(8,128)(2,1)S(1)}, u32[]{:S(2)}, u32[]{:S(2)}) collective-permute-start(bf16[4,8,16,128]{3,2,1,0:T(8,128)(2,1)S(1)} %shard_map.117.refs_0_), channel_id=1, source_target_pairs={{0,2},{1,3},{2,0},{3,1},{4,6},{5,7},{6,4},{7,5},{8,10},{9,11},{10,... | collective-permute-start | bytes 393224 | tf_op jit(solution)/shard_map/ppermute | solution.py:32
  15.6 1.3 %shard_map.115.refs_0_ = bf16[4,6272]{1,0:T(4,128)(2,1)S(1)} custom-call(f32[2,128]{1,0:T(2,128)S(1)} %get-tuple-element.16.refs_0_, bf16[4,2048]{1,0:T(4,128)(2,1)S(1)} %get-tuple-element.17.refs_1_.refs_4_, bf16[24,16,128]{2,1,0:T(8,128)(2,1)S(1)} %get-tuple-element.18.refs_0_.refs_2_, bf16[24,16,128]{2,1,0:T(8,128)(2,1)S(1)} %collective-permute-done.refs_3_.refs_1_, ...), custom_call_target="tpu_custom_call" | custom-call | flops 100663296 | bytes 8388608 | tf_op jit(solution)/shard_map/pallas_call | solution.py:235
  16.9 0.0 collective-permute-start.5
  16.9 0.6 %collective-permute-start.4 = (bf16[4,6272]{1,0:T(4,128)(2,1)S(1)}, bf16[4,6272]{1,0:T(4,128)(2,1)S(1)}, u32[]{:S(2)}, u32[]{:S(2)}) collective-permute-start(bf16[4,6272]{1,0:T(4,128)(2,1)S(1)} %shard_map.115.refs_0_), channel_id=1, source_target_pairs={{0,2},{1,3},{2,0},{3,1},{4,6},{5,7},{6,4},{7,5},{8,10},{9,11},{10,... | collective-permute-start | bytes 150536 | tf_op jit(solution)/shard_map/ppermute | solution.py:32
  17.4 1.5 %collective-permute-start.7 = (bf16[4,2048]{1,0:T(4,128)(2,1)S(1)}, bf16[4,2048]{1,0:T(4,128)(2,1)S(1)}, u32[]{:S(2)}, u32[]{:S(2)}) collective-permute-start(bf16[4,2048]{1,0:T(4,128)(2,1)S(1)} %get-tuple-element.17.refs_1_.refs_4_), channel_id=1, source_target_pairs={{0,16},{4,20},{8,24},{12,28},{16,0},{20,4},{24,8},{28,12},{1,17},{... | collective-permute-start | bytes 49160 | tf_op jit(solution)/shard_map/ppermute | solution.py:42
  18.9 2.2 %shard_map.116.refs_4_.refs_6_ = bf16[2048,1024]{1,0:T(8,128)(2,1)S(1)} custom-call(bf16[4,6272]{1,0:T(4,128)(2,1)S(1)} %shard_map.115.refs_0_, bf16[2048,2048]{1,0:T(8,128)(2,1)} %bitcast.13), custom_call_target="tpu_custom_call" | custom-call | bytes 4194304 | tf_op jit(solution)/shard_map/pallas_call | solution.py:180
  21.2 0.0 collective-permute-done.7.refs_5_
  21.2 0.0 collective-permute-done.5.refs_3_
  21.2 0.3 collective-permute-done.4.refs_2_
  21.5 0.0 collective-permute-done.6.refs_1_
  21.5 0.8 %collective-permute-start.8 = (bf16[8,8,16,128]{3,2,1,0:T(8,128)(2,1)S(1)}, bf16[8,8,16,128]{3,2,1,0:T(8,128)(2,1)S(1)}, u32[]{:S(2)}, u32[]{:S(2)}) collective-permute-start(bf16[8,8,16,128]{3,2,1,0:T(8,128)(2,1)S(1)} %bitcast.9), channel_id=1, source_target_pairs={{0,1},{1,0},{2,3},{3,2},{4,5},{5,4},{6,7},{7,6},{8,9},{9,8},{10,11... | collective-permute-start | bytes 786440 | tf_op jit(solution)/shard_map/ppermute | solution.py:32
  22.3 0.1 collective-permute-start.3
  22.4 1.5 %collective-permute-start.13 = (bf16[8,16,128]{2,1,0:T(8,128)(2,1)S(1)}, bf16[8,16,128]{2,1,0:T(8,128)(2,1)S(1)}, u32[]{:S(2)}, u32[]{:S(2)}) collective-permute-start(bf16[8,16,128]{2,1,0:T(8,128)(2,1)S(1)} %slice_add_fusion.refs_7_), channel_id=1, source_target_pairs={{0,8},{4,12},{8,0},{12,4},{1,9},{5,13},{9,1},{13,5},{2,10},{6,14},... | collective-permute-start | bytes 98312 | tf_op jit(solution)/shard_map/ppermute | solution.py:32
  23.9 0.0 collective-permute-done.3.refs_1_
  23.9 0.0 collective-permute-done.8.refs_8_
  23.9 2.5 %shard_map.119 = (bf16[4,2048]{1,0:T(4,128)(2,1)S(1)}, bf16[4,4096]{1,0:T(4,128)(2,1)}) custom-call(bf16[4,6272]{1,0:T(4,128)(2,1)S(1)} %shard_map.115.refs_0_, bf16[4,6272]{1,0:T(4,128)(2,1)S(1)} %collective-permute-done.3.refs_1_, bf16[4,6272]{1,0:T(4,128)(2,1)S(1)} %collective-permute-done.4.refs_2_, bf16[4,6272]{1,0:T(4,128)(2,1)S(1)} %collective-permute-done.5.refs_3_, ...), custom_call_target="tpu_custom_call" | custom-call | flops 33554432 | bytes 8388608 | tf_op jit(solution)/shard_map/pallas_call | solution.py:383
  26.4 2.6 %collective-permute-start.12 = (bf16[4,2048]{1,0:T(4,128)(2,1)S(1)}, bf16[4,2048]{1,0:T(4,128)(2,1)S(1)}, u32[]{:S(2)}, u32[]{:S(2)}) collective-permute-start(bf16[4,2048]{1,0:T(4,128)(2,1)S(1)} %get-tuple-element.24), channel_id=1, source_target_pairs={{12,16},{8,20},{4,24},{0,28},{28,0},{24,4},{20,8},{16,12},{13,17},... | collective-permute-start | bytes 49160 | tf_op jit(solution)/shard_map/ppermute | solution.py:42
  29.0 1.2 %collective-permute-start.11 = (bf16[4,2048]{1,0:T(4,128)(2,1)S(1)}, bf16[4,2048]{1,0:T(4,128)(2,1)S(1)}, u32[]{:S(2)}, u32[]{:S(2)}) collective-permute-start(bf16[4,2048]{1,0:T(4,128)(2,1)S(1)} %get-tuple-element.24), channel_id=1, source_target_pairs={{8,16},{12,20},{0,24},{4,28},{24,0},{28,4},{16,8},{20,12},{9,17},{... | collective-permute-start | bytes 49160 | tf_op jit(solution)/shard_map/ppermute | solution.py:42
  30.2 2.1 %collective-permute-start.10 = (bf16[4,2048]{1,0:T(4,128)(2,1)S(1)}, bf16[4,2048]{1,0:T(4,128)(2,1)S(1)}, u32[]{:S(2)}, u32[]{:S(2)}) collective-permute-start(bf16[4,2048]{1,0:T(4,128)(2,1)S(1)} %get-tuple-element.24), channel_id=1, source_target_pairs={{4,16},{0,20},{12,24},{8,28},{20,0},{16,4},{28,8},{24,12},{5,17},{... | collective-permute-start | bytes 49160 | tf_op jit(solution)/shard_map/ppermute | solution.py:42
  32.3 0.8 %collective-permute-start.9 = (bf16[4,2048]{1,0:T(4,128)(2,1)S(1)}, bf16[4,2048]{1,0:T(4,128)(2,1)S(1)}, u32[]{:S(2)}, u32[]{:S(2)}) collective-permute-start(bf16[4,2048]{1,0:T(4,128)(2,1)S(1)} %get-tuple-element.24), channel_id=1, source_target_pairs={{0,16},{4,20},{8,24},{12,28},{16,0},{20,4},{24,8},{28,12},{1,17},{... | collective-permute-start | bytes 49160 | tf_op jit(solution)/shard_map/ppermute | solution.py:42
  33.1 0.0 collective-permute-done.13.refs_8_
  33.1 1.4 %collective-permute-done.11.refs_3_ = bf16[4,2048]{1,0:T(4,128)(2,1)S(1)} collective-permute-done((bf16[4,2048]{1,0:T(4,128)(2,1)S(1)}, bf16[4,2048]{1,0:T(4,128)(2,1)S(1)}, u32[]{:S(2)}, u32[]{:S(2)}) %collective-permute-start.11) | collective-permute-done | bytes 16416 | tf_op jit(solution)/shard_map/ppermute | solution.py:42
  34.5 0.3 collective-permute-done.10.refs_2_
  34.8 1.2 %collective-permute-done.9.refs_1_ = bf16[4,2048]{1,0:T(4,128)(2,1)S(1)} collective-permute-done((bf16[4,2048]{1,0:T(4,128)(2,1)S(1)}, bf16[4,2048]{1,0:T(4,128)(2,1)S(1)}, u32[]{:S(2)}, u32[]{:S(2)}) %collective-permute-start.9) | collective-permute-done | bytes 16416 | tf_op jit(solution)/shard_map/ppermute | solution.py:42
  36.0 1.3 %shard_map.120 = (bf16[4,6272]{1,0:T(4,128)(2,1)S(1)}, bf16[4,2048]{1,0:T(4,128)(2,1)S(1)}) custom-call(f32[2,128]{1,0:T(2,128)S(1)} %get-tuple-element.16.refs_0_, bf16[4,2048]{1,0:T(4,128)(2,1)S(1)} %collective-permute-done.9.refs_1_, bf16[4,2048]{1,0:T(4,128)(2,1)S(1)} %collective-permute-done.10.refs_2_, ...), custom_call_target="tpu_custom_call" | custom-call | flops 100663296 | bytes 8388608 | tf_op jit(solution)/shard_map/pallas_call | solution.py:282
  37.3 0.0 collective-permute-start.16
  37.3 1.3 %collective-permute-start.15 = (bf16[4,6272]{1,0:T(4,128)(2,1)S(1)}, bf16[4,6272]{1,0:T(4,128)(2,1)S(1)}, u32[]{:S(2)}, u32[]{:S(2)}) collective-permute-start(bf16[4,6272]{1,0:T(4,128)(2,1)S(1)} %get-tuple-element.26.refs_0_), channel_id=1, source_target_pairs={{0,2},{1,3},{2,0},{3,1},{4,6},{5,7},{6,4},{7,5},{8,10},{9,11},{10,... | collective-permute-start | bytes 150536 | tf_op jit(solution)/shard_map/ppermute | solution.py:32
  38.6 0.6 %collective-permute-start.14 = (bf16[4,6272]{1,0:T(4,128)(2,1)S(1)}, bf16[4,6272]{1,0:T(4,128)(2,1)S(1)}, u32[]{:S(2)}, u32[]{:S(2)}) collective-permute-start(bf16[4,6272]{1,0:T(4,128)(2,1)S(1)} %get-tuple-element.26.refs_0_), channel_id=1, source_target_pairs={{0,1},{1,0},{2,3},{3,2},{4,5},{5,4},{6,7},{7,6},{8,9},{9,8},{10,11... | collective-permute-start | bytes 150536 | tf_op jit(solution)/shard_map/ppermute | solution.py:32
  39.2 2.2 %collective-permute-done.16.refs_3_ = bf16[4,6272]{1,0:T(4,128)(2,1)S(1)} collective-permute-done((bf16[4,6272]{1,0:T(4,128)(2,1)S(1)}, bf16[4,6272]{1,0:T(4,128)(2,1)S(1)}, u32[]{:S(2)}, u32[]{:S(2)}) %collective-permute-start.16) | collective-permute-done | bytes 50208 | tf_op jit(solution)/shard_map/ppermute | solution.py:32
  41.4 0.6 %collective-permute-done.15.refs_2_ = bf16[4,6272]{1,0:T(4,128)(2,1)S(1)} collective-permute-done((bf16[4,6272]{1,0:T(4,128)(2,1)S(1)}, bf16[4,6272]{1,0:T(4,128)(2,1)S(1)}, u32[]{:S(2)}, u32[]{:S(2)}) %collective-permute-start.15) | collective-permute-done | bytes 50208 | tf_op jit(solution)/shard_map/ppermute | solution.py:32
  42.0 1.9 %shard_map.121 = (bf16[4,2048]{1,0:T(4,128)(2,1)S(1)}, bf16[4,4096]{1,0:T(4,128)(2,1)S(1)}) custom-call(bf16[4,6272]{1,0:T(4,128)(2,1)S(1)} %get-tuple-element.26.refs_0_, bf16[4,6272]{1,0:T(4,128)(2,1)S(1)} %collective-permute-done.14.refs_1_, bf16[4,6272]{1,0:T(4,128)(2,1)S(1)} %collective-permute-done.15.refs_2_, ...), custom_call_target="tpu_custom_call" | custom-call | flops 33554432 | bytes 8388608 | tf_op jit(solution)/shard_map/pallas_call | solution.py:383
  43.8 0.8 %collective-permute-start.17 = (bf16[4,4096]{1,0:T(4,128)(2,1)S(1)}, bf16[4,4096]{1,0:T(4,128)(2,1)S(1)}, u32[]{:S(2)}, u32[]{:S(2)}) collective-permute-start(bf16[4,4096]{1,0:T(4,128)(2,1)S(1)} %get-tuple-element.28), channel_id=1, source_target_pairs={{0,16},{4,20},{8,24},{12,28},{16,0},{20,4},{24,8},{28,12},{1,17},{... | collective-permute-start | bytes 98312 | tf_op jit(solution)/shard_map/ppermute | solution.py:42
  44.7 2.6 %collective-permute-start.20 = (bf16[4,2048]{1,0:T(4,128)(2,1)S(1)}, bf16[4,2048]{1,0:T(4,128)(2,1)S(1)}, u32[]{:S(2)}, u32[]{:S(2)}) collective-permute-start(bf16[4,2048]{1,0:T(4,128)(2,1)S(1)} %get-tuple-element.29), channel_id=1, source_target_pairs={{12,16},{8,20},{4,24},{0,28},{28,0},{24,4},{20,8},{16,12},{13,17},... | collective-permute-start | bytes 49160 | tf_op jit(solution)/shard_map/ppermute | solution.py:42
  47.3 0.4 collective-permute-start.19
  47.8 2.9 %collective-permute-start.18 = (bf16[4,2048]{1,0:T(4,128)(2,1)S(1)}, bf16[4,2048]{1,0:T(4,128)(2,1)S(1)}, u32[]{:S(2)}, u32[]{:S(2)}) collective-permute-start(bf16[4,2048]{1,0:T(4,128)(2,1)S(1)} %get-tuple-element.29), channel_id=1, source_target_pairs={{4,16},{0,20},{12,24},{8,28},{20,0},{16,4},{28,8},{24,12},{5,17},{... | collective-permute-start | bytes 49160 | tf_op jit(solution)/shard_map/ppermute | solution.py:42
  50.6 0.5 collective-permute-done.20.refs_3_
  51.1 1.7 %collective-permute-done.19.refs_2_ = bf16[4,2048]{1,0:T(4,128)(2,1)S(1)} collective-permute-done((bf16[4,2048]{1,0:T(4,128)(2,1)S(1)}, bf16[4,2048]{1,0:T(4,128)(2,1)S(1)}, u32[]{:S(2)}, u32[]{:S(2)}) %collective-permute-start.19) | collective-permute-done | bytes 16416 | tf_op jit(solution)/shard_map/ppermute | solution.py:42
  52.9 0.0 collective-permute-done.18.refs_1_
  52.9 0.0 collective-permute-done.17.refs_0_
  52.9 0.6 %shard_map.122 = (bf16[1,4,2048]{2,1,0:T(4,128)(2,1)}, bf16[1,4,2048]{2,1,0:T(4,128)(2,1)}) custom-call(bf16[4,4096]{1,0:T(4,128)(2,1)S(1)} %collective-permute-done.17.refs_0_, bf16[4,2048]{1,0:T(4,128)(2,1)S(1)} %collective-permute-done.18.refs_1_, bf16[4,2048]{1,0:T(4,128)(2,1)S(1)} %collective-permute-done.19.refs_2_, ...), custom_call_target="tpu_custom_call" | custom-call | tf_op jit(solution)/shard_map/pallas_call | solution.py:300
  (5 shorter events, 0.0 us)
Async XLA Ops:
  2.2 11.9 %collective-permute-start = (bf16[24,16,128]{2,1,0:T(8,128)(2,1)S(1)}, bf16[24,16,128]{2,1,0:T(8,128)(2,1)S(1)}, u32[]{:S(2)}, u32[]{:S(2)}) collective-permute-start(bf16[24,16,128]{2,1,0:T(8,128)(2,1)S(1)} %get-tuple-element.19), channel_id=1, source_target_pairs={{0,4},{4,0},{8,12},{12,8},{1,5},{5,1},{9,13},{13,9},{2,6},{6,2},{1... | collective-permute-start | bytes 294920 | tf_op jit(solution)/shard_map/ppermute | solution.py:32
  5.3 7.6 %collective-permute-start.1 = (bf16[16,16,128]{2,1,0:T(8,128)(2,1)S(1)}, bf16[16,16,128]{2,1,0:T(8,128)(2,1)S(1)}, u32[]{:S(2)}, u32[]{:S(2)}) collective-permute-start(bf16[16,16,128]{2,1,0:T(8,128)(2,1)S(1)} %get-tuple-element.20), channel_id=1, source_target_pairs={{0,8},{4,12},{8,0},{12,4},{1,9},{5,13},{9,1},{13,5},{2,10},{6,14},... | collective-permute-start | bytes 196616 | tf_op jit(solution)/shard_map/ppermute | solution.py:32
  7.8 6.2 %collective-permute-start.2 = (bf16[16,16,128]{2,1,0:T(8,128)(2,1)S(1)}, bf16[16,16,128]{2,1,0:T(8,128)(2,1)S(1)}, u32[]{:S(2)}, u32[]{:S(2)}) collective-permute-start(bf16[16,16,128]{2,1,0:T(8,128)(2,1)S(1)} %get-tuple-element.21), channel_id=1, source_target_pairs={{0,12},{4,8},{8,4},{12,0},{1,13},{5,9},{9,5},{13,1},{2,14},{6,10},... | collective-permute-start | bytes 196616 | tf_op jit(solution)/shard_map/ppermute | solution.py:32
  14.0 7.5 %collective-permute-start.6 = (bf16[4,8,16,128]{3,2,1,0:T(8,128)(2,1)S(1)}, bf16[4,8,16,128]{3,2,1,0:T(8,128)(2,1)S(1)}, u32[]{:S(2)}, u32[]{:S(2)}) collective-permute-start(bf16[4,8,16,128]{3,2,1,0:T(8,128)(2,1)S(1)} %shard_map.117.refs_0_), channel_id=1, source_target_pairs={{0,2},{1,3},{2,0},{3,1},{4,6},{5,7},{6,4},{7,5},{8,10},{9,11},{10,... | collective-permute-start | bytes 393224 | tf_op jit(solution)/shard_map/ppermute | solution.py:32
  16.9 4.3 %collective-permute-start.5 = (bf16[4,6272]{1,0:T(4,128)(2,1)S(1)}, bf16[4,6272]{1,0:T(4,128)(2,1)S(1)}, u32[]{:S(2)}, u32[]{:S(2)}) collective-permute-start(bf16[4,6272]{1,0:T(4,128)(2,1)S(1)} %shard_map.115.refs_0_), channel_id=1, source_target_pairs={{0,3},{1,2},{2,1},{3,0},{4,7},{5,6},{6,5},{7,4},{8,11},{9,10},{10,... | collective-permute-start | bytes 150536 | tf_op jit(solution)/shard_map/ppermute | solution.py:32
  16.9 4.6 %collective-permute-start.4 = (bf16[4,6272]{1,0:T(4,128)(2,1)S(1)}, bf16[4,6272]{1,0:T(4,128)(2,1)S(1)}, u32[]{:S(2)}, u32[]{:S(2)}) collective-permute-start(bf16[4,6272]{1,0:T(4,128)(2,1)S(1)} %shard_map.115.refs_0_), channel_id=1, source_target_pairs={{0,2},{1,3},{2,0},{3,1},{4,6},{5,7},{6,4},{7,5},{8,10},{9,11},{10,... | collective-permute-start | bytes 150536 | tf_op jit(solution)/shard_map/ppermute | solution.py:32
  17.4 3.7 %collective-permute-start.7 = (bf16[4,2048]{1,0:T(4,128)(2,1)S(1)}, bf16[4,2048]{1,0:T(4,128)(2,1)S(1)}, u32[]{:S(2)}, u32[]{:S(2)}) collective-permute-start(bf16[4,2048]{1,0:T(4,128)(2,1)S(1)} %get-tuple-element.17.refs_1_.refs_4_), channel_id=1, source_target_pairs={{0,16},{4,20},{8,24},{12,28},{16,0},{20,4},{24,8},{28,12},{1,17},{... | collective-permute-start | bytes 49160 | tf_op jit(solution)/shard_map/ppermute | solution.py:42
  21.5 2.4 %collective-permute-start.8 = (bf16[8,8,16,128]{3,2,1,0:T(8,128)(2,1)S(1)}, bf16[8,8,16,128]{3,2,1,0:T(8,128)(2,1)S(1)}, u32[]{:S(2)}, u32[]{:S(2)}) collective-permute-start(bf16[8,8,16,128]{3,2,1,0:T(8,128)(2,1)S(1)} %bitcast.9), channel_id=1, source_target_pairs={{0,1},{1,0},{2,3},{3,2},{4,5},{5,4},{6,7},{7,6},{8,9},{9,8},{10,11... | collective-permute-start | bytes 786440 | tf_op jit(solution)/shard_map/ppermute | solution.py:32
  22.3 1.6 %collective-permute-start.3 = (bf16[4,6272]{1,0:T(4,128)(2,1)S(1)}, bf16[4,6272]{1,0:T(4,128)(2,1)S(1)}, u32[]{:S(2)}, u32[]{:S(2)}) collective-permute-start(bf16[4,6272]{1,0:T(4,128)(2,1)S(1)} %shard_map.115.refs_0_), channel_id=1, source_target_pairs={{0,1},{1,0},{2,3},{3,2},{4,5},{5,4},{6,7},{7,6},{8,9},{9,8},{10,11... | collective-permute-start | bytes 150536 | tf_op jit(solution)/shard_map/ppermute | solution.py:32
  22.4 10.7 %collective-permute-start.13 = (bf16[8,16,128]{2,1,0:T(8,128)(2,1)S(1)}, bf16[8,16,128]{2,1,0:T(8,128)(2,1)S(1)}, u32[]{:S(2)}, u32[]{:S(2)}) collective-permute-start(bf16[8,16,128]{2,1,0:T(8,128)(2,1)S(1)} %slice_add_fusion.refs_7_), channel_id=1, source_target_pairs={{0,8},{4,12},{8,0},{12,4},{1,9},{5,13},{9,1},{13,5},{2,10},{6,14},... | collective-permute-start | bytes 98312 | tf_op jit(solution)/shard_map/ppermute | solution.py:32
  26.4 6.8 %collective-permute-start.12 = (bf16[4,2048]{1,0:T(4,128)(2,1)S(1)}, bf16[4,2048]{1,0:T(4,128)(2,1)S(1)}, u32[]{:S(2)}, u32[]{:S(2)}) collective-permute-start(bf16[4,2048]{1,0:T(4,128)(2,1)S(1)} %get-tuple-element.24), channel_id=1, source_target_pairs={{12,16},{8,20},{4,24},{0,28},{28,0},{24,4},{20,8},{16,12},{13,17},... | collective-permute-start | bytes 49160 | tf_op jit(solution)/shard_map/ppermute | solution.py:42
  29.0 5.5 %collective-permute-start.11 = (bf16[4,2048]{1,0:T(4,128)(2,1)S(1)}, bf16[4,2048]{1,0:T(4,128)(2,1)S(1)}, u32[]{:S(2)}, u32[]{:S(2)}) collective-permute-start(bf16[4,2048]{1,0:T(4,128)(2,1)S(1)} %get-tuple-element.24), channel_id=1, source_target_pairs={{8,16},{12,20},{0,24},{4,28},{24,0},{28,4},{16,8},{20,12},{9,17},{... | collective-permute-start | bytes 49160 | tf_op jit(solution)/shard_map/ppermute | solution.py:42
  30.2 4.6 %collective-permute-start.10 = (bf16[4,2048]{1,0:T(4,128)(2,1)S(1)}, bf16[4,2048]{1,0:T(4,128)(2,1)S(1)}, u32[]{:S(2)}, u32[]{:S(2)}) collective-permute-start(bf16[4,2048]{1,0:T(4,128)(2,1)S(1)} %get-tuple-element.24), channel_id=1, source_target_pairs={{4,16},{0,20},{12,24},{8,28},{20,0},{16,4},{28,8},{24,12},{5,17},{... | collective-permute-start | bytes 49160 | tf_op jit(solution)/shard_map/ppermute | solution.py:42
  32.3 3.7 %collective-permute-start.9 = (bf16[4,2048]{1,0:T(4,128)(2,1)S(1)}, bf16[4,2048]{1,0:T(4,128)(2,1)S(1)}, u32[]{:S(2)}, u32[]{:S(2)}) collective-permute-start(bf16[4,2048]{1,0:T(4,128)(2,1)S(1)} %get-tuple-element.24), channel_id=1, source_target_pairs={{0,16},{4,20},{8,24},{12,28},{16,0},{20,4},{24,8},{28,12},{1,17},{... | collective-permute-start | bytes 49160 | tf_op jit(solution)/shard_map/ppermute | solution.py:42
  37.3 4.1 %collective-permute-start.16 = (bf16[4,6272]{1,0:T(4,128)(2,1)S(1)}, bf16[4,6272]{1,0:T(4,128)(2,1)S(1)}, u32[]{:S(2)}, u32[]{:S(2)}) collective-permute-start(bf16[4,6272]{1,0:T(4,128)(2,1)S(1)} %get-tuple-element.26.refs_0_), channel_id=1, source_target_pairs={{0,3},{1,2},{2,1},{3,0},{4,7},{5,6},{6,5},{7,4},{8,11},{9,10},{10,... | collective-permute-start | bytes 150536 | tf_op jit(solution)/shard_map/ppermute | solution.py:32
  37.3 4.7 %collective-permute-start.15 = (bf16[4,6272]{1,0:T(4,128)(2,1)S(1)}, bf16[4,6272]{1,0:T(4,128)(2,1)S(1)}, u32[]{:S(2)}, u32[]{:S(2)}) collective-permute-start(bf16[4,6272]{1,0:T(4,128)(2,1)S(1)} %get-tuple-element.26.refs_0_), channel_id=1, source_target_pairs={{0,2},{1,3},{2,0},{3,1},{4,6},{5,7},{6,4},{7,5},{8,10},{9,11},{10,... | collective-permute-start | bytes 150536 | tf_op jit(solution)/shard_map/ppermute | solution.py:32
  38.6 3.4 %collective-permute-start.14 = (bf16[4,6272]{1,0:T(4,128)(2,1)S(1)}, bf16[4,6272]{1,0:T(4,128)(2,1)S(1)}, u32[]{:S(2)}, u32[]{:S(2)}) collective-permute-start(bf16[4,6272]{1,0:T(4,128)(2,1)S(1)} %get-tuple-element.26.refs_0_), channel_id=1, source_target_pairs={{0,1},{1,0},{2,3},{3,2},{4,5},{5,4},{6,7},{7,6},{8,9},{9,8},{10,11... | collective-permute-start | bytes 150536 | tf_op jit(solution)/shard_map/ppermute | solution.py:32
  43.8 9.0 %collective-permute-start.17 = (bf16[4,4096]{1,0:T(4,128)(2,1)S(1)}, bf16[4,4096]{1,0:T(4,128)(2,1)S(1)}, u32[]{:S(2)}, u32[]{:S(2)}) collective-permute-start(bf16[4,4096]{1,0:T(4,128)(2,1)S(1)} %get-tuple-element.28), channel_id=1, source_target_pairs={{0,16},{4,20},{8,24},{12,28},{16,0},{20,4},{24,8},{28,12},{1,17},{... | collective-permute-start | bytes 98312 | tf_op jit(solution)/shard_map/ppermute | solution.py:42
  44.7 6.4 %collective-permute-start.20 = (bf16[4,2048]{1,0:T(4,128)(2,1)S(1)}, bf16[4,2048]{1,0:T(4,128)(2,1)S(1)}, u32[]{:S(2)}, u32[]{:S(2)}) collective-permute-start(bf16[4,2048]{1,0:T(4,128)(2,1)S(1)} %get-tuple-element.29), channel_id=1, source_target_pairs={{12,16},{8,20},{4,24},{0,28},{28,0},{24,4},{20,8},{16,12},{13,17},... | collective-permute-start | bytes 49160 | tf_op jit(solution)/shard_map/ppermute | solution.py:42
  47.3 5.5 %collective-permute-start.19 = (bf16[4,2048]{1,0:T(4,128)(2,1)S(1)}, bf16[4,2048]{1,0:T(4,128)(2,1)S(1)}, u32[]{:S(2)}, u32[]{:S(2)}) collective-permute-start(bf16[4,2048]{1,0:T(4,128)(2,1)S(1)} %get-tuple-element.29), channel_id=1, source_target_pairs={{8,16},{12,20},{0,24},{4,28},{24,0},{28,4},{16,8},{20,12},{9,17},{... | collective-permute-start | bytes 49160 | tf_op jit(solution)/shard_map/ppermute | solution.py:42
  47.8 5.1 %collective-permute-start.18 = (bf16[4,2048]{1,0:T(4,128)(2,1)S(1)}, bf16[4,2048]{1,0:T(4,128)(2,1)S(1)}, u32[]{:S(2)}, u32[]{:S(2)}) collective-permute-start(bf16[4,2048]{1,0:T(4,128)(2,1)S(1)} %get-tuple-element.29), channel_id=1, source_target_pairs={{4,16},{0,20},{12,24},{8,28},{20,0},{16,4},{28,8},{24,12},{5,17},{... | collective-permute-start | bytes 49160 | tf_op jit(solution)/shard_map/ppermute | solution.py:42

commit v15 on v12

--- a/solution.py
+++ b/solution.py
@@ -64,7 +64,19 @@
         pltpu.make_async_copy(source, target, sems.at[i])
         for i, (source, target) in enumerate(zip(sources, targets))
     ]
-    for copy in copies:
+    quarter = gains.shape[1] // 4
+    tables = [
+        [
+            pltpu.make_async_copy(
+                sources[which].at[:, pl.ds(i * quarter, quarter)],
+                targets[which].at[:, pl.ds(i * quarter, quarter)],
+                sems.at[4 * (which - 2) + i],
+            )
+            for i in range(4)
+        ]
+        for which in (4, 5)
+    ]
+    for copy in copies[:2] + tables[0] + tables[1] + copies[2:4] + copies[6:]:
         copy.start()
     at = lax.axis_index("tensor")
     tenants = gains.shape[0]
@@ -97,9 +109,11 @@
                 for g in range(kv_dev):
                     to = (which * sections + b) * kv_dev + g
                     packs[d][to] = cache[b, start + g]
-    copies[4].wait()
+    for copy in tables[0]:
+        copy.wait()
     gain_rows = jnp.dot(onehot, gains[...], preferred_element_type=F32)
-    copies[5].wait()
+    for copy in tables[1]:
+        copy.wait()
     bias_rows = jnp.dot(onehot, biases[...], preferred_element_type=F32)
     for tick in range(sections):
         mine = slice(tick * rows, (tick + 1) * rows)
@@ -131,7 +145,7 @@
         out_specs=[VMEM] * len(out_shape),
         scratch_shapes=[pltpu.SMEM(x.shape, jnp.int32) for x in (tenant, lengths)]
         + [pltpu.VMEM(x.shape, BF) for x in (gain, bias, keys, values)]
-        + [pltpu.SemaphoreType.DMA((len(operands),))],
+        + [pltpu.SemaphoreType.DMA((16,))],
         compiler_params=PARAMS,
         cost_estimate=cost(0, 4 * gain.size),
     )(*[in_hbm(x) for x in operands])

time: 53.1 us -> 53.3 us (level)
  no operation moved by 1% of the time
where the time goes in v15:
time: 53.3 us; the launch traced here: 53.1 us
  starting transfers between devices  25.3 us (47%)
  Pallas kernels  15.6 us (29%)
  waiting for transfers between devices  11.6 us (22%)
  between operations  0.69 us (1%)
    ppermute x8, starting transfers between devices, from_behind(): return lax.ppermute(block, ('section', 'tensor'), route)  13.5 us
    ppermute x12, starting transfers between devices, swapped(): return lax.ppermute(block, axis, route)  11.8 us
    pallas_call x2, Pallas kernels, hold(): pl.pallas_call(lambda *refs: hold_kernel(parts, columns, *refs), out_shap...  6.91 us
    ppermute x12, waiting for transfers between devices, swapped(): return lax.ppermute(block, axis, route)  6.12 us
    ppermute x8, waiting for transfers between devices, from_behind(): return lax.ppermute(block, ('section', 'tensor'), route)  5.45 us
    pallas_call x2, Pallas kernels, attend(): pl.pallas_call(lambda *refs: attend_kernel(dims, turns, tick, *refs), out...  3.71 us
    pallas_call x1, Pallas kernels, pack(): pl.pallas_call(lambda *refs: pack_kernel(dims, *refs), out_shape=out_shap...  1.75 us
    pallas_call x1, Pallas kernels, later_sums(): pl.pallas_call(lambda *refs: later_kernel(len(arrivals), tick, *refs), ou...  1.28 us
  transfers between devices with their start and end apart: 20, of which 12 were waited for; matrix products, arithmetic and copies ran while one was open for 0% of the time, Pallas kernels for 19%

profile of v15, /device:TPU:0, one launch (start us, length us, event | category | flops | bytes accessed | tf_op | source)
XLA Modules:
  0.0 53.1 jit_solution(14179252339197933168)
XLA Ops:
  0.6 1.7 %shard_map.113 = (bf16[24,16,128]{2,1,0:T(8,128)(2,1)S(1)}, bf16[24,16,128]{2,1,0:T(8,128)(2,1)S(1)}, bf16[16,16,128]{2,1,0:T(8,128)(2,1)S(1)}, bf16[16,16,128]{...) custom-call(s32[2,4]{1,0:T(2,128)} %refs_0_.1, ...), custom_call_target="tpu_custom_call" | custom-call | bytes 819200 | tf_op jit(solution)/shard_map/pallas_call | solution.py:141
  2.4 3.1 %collective-permute-start = (bf16[24,16,128]{2,1,0:T(8,128)(2,1)S(1)}, bf16[24,16,128]{2,1,0:T(8,128)(2,1)S(1)}, u32[]{:S(2)}, u32[]{:S(2)}) collective-permute-start(bf16[24,16,128]{2,1,0:T(8,128)(2,1)S(1)} %get-tuple-element.20), channel_id=1, source_target_pairs={{0,4},{4,0},{8,12},{12,8},{1,5},{5,1},{9,13},{13,9},{2,6},{6,2},{1... | collective-permute-start | bytes 294920 | tf_op jit(solution)/shard_map/ppermute | solution.py:32
  5.5 2.6 %collective-permute-start.1 = (bf16[16,16,128]{2,1,0:T(8,128)(2,1)S(1)}, bf16[16,16,128]{2,1,0:T(8,128)(2,1)S(1)}, u32[]{:S(2)}, u32[]{:S(2)}) collective-permute-start(bf16[16,16,128]{2,1,0:T(8,128)(2,1)S(1)} %get-tuple-element.21), channel_id=1, source_target_pairs={{0,8},{4,12},{8,0},{12,4},{1,9},{5,13},{9,1},{13,5},{2,10},{6,14},... | collective-permute-start | bytes 196616 | tf_op jit(solution)/shard_map/ppermute | solution.py:32
  8.1 0.0 collective-permute-start.2
  8.1 4.7 %shard_map.114 = (bf16[2048,2048]{1,0:T(8,128)(2,1)S(1)}, bf16[2048,1024]{1,0:T(8,128)(2,1)S(1)}) custom-call(bf16[24,16,128]{2,1,0:T(8,128)(2,1)S(1)} %get-tuple-element.19.refs_0_.refs_2_, bf16[2048,2048]{1,0:T(8,128)(2,1)} %bitcast.14, bf16[2048,2048]{1,0:T(8,128)(2,1)} %bitcast.12), custom_call_target="tpu_custom_call" | custom-call | bytes 12582912 | tf_op jit(solution)/shard_map/pallas_call | solution.py:194
  12.8 0.3 collective-permute-done.1.refs_4_.refs_2_
  13.1 1.2 %collective-permute-done.2.refs_5_.refs_3_ = bf16[16,16,128]{2,1,0:T(8,128)(2,1)S(1)} collective-permute-done((bf16[16,16,128]{2,1,0:T(8,128)(2,1)S(1)}, bf16[16,16,128]{2,1,0:T(8,128)(2,1)S(1)}, u32[]{:S(2)}, u32[]{:S(2)}) %collective-permute-start.2) | collective-permute-done | bytes 65568 | tf_op jit(solution)/shard_map/ppermute | solution.py:32
  14.2 0.0 collective-permute-done.refs_3_.refs_1_
  14.3 1.6 %collective-permute-start.6 = (bf16[4,8,16,128]{3,2,1,0:T(8,128)(2,1)S(1)}, bf16[4,8,16,128]{3,2,1,0:T(8,128)(2,1)S(1)}, u32[]{:S(2)}, u32[]{:S(2)}) collective-permute-start(bf16[4,8,16,128]{3,2,1,0:T(8,128)(2,1)S(1)} %shard_map.117.refs_0_), channel_id=1, source_target_pairs={{0,2},{1,3},{2,0},{3,1},{4,6},{5,7},{6,4},{7,5},{8,10},{9,11},{10,... | collective-permute-start | bytes 393224 | tf_op jit(solution)/shard_map/ppermute | solution.py:32
  15.8 1.3 %shard_map.115.refs_0_ = bf16[4,6272]{1,0:T(4,128)(2,1)S(1)} custom-call(f32[2,128]{1,0:T(2,128)S(1)} %get-tuple-element.17.refs_0_, bf16[4,2048]{1,0:T(4,128)(2,1)S(1)} %get-tuple-element.18.refs_1_.refs_4_, bf16[24,16,128]{2,1,0:T(8,128)(2,1)S(1)} %get-tuple-element.19.refs_0_.refs_2_, bf16[24,16,128]{2,1,0:T(8,128)(2,1)S(1)} %collective-permute-done.refs_3_.refs_1_, ...), custom_call_target="tpu_custom_call" | custom-call | flops 100663296 | bytes 8388608 | tf_op jit(solution)/shard_map/pallas_call | solution.py:249
  17.1 0.0 collective-permute-start.5
  17.1 0.6 %collective-permute-start.4 = (bf16[4,6272]{1,0:T(4,128)(2,1)S(1)}, bf16[4,6272]{1,0:T(4,128)(2,1)S(1)}, u32[]{:S(2)}, u32[]{:S(2)}) collective-permute-start(bf16[4,6272]{1,0:T(4,128)(2,1)S(1)} %shard_map.115.refs_0_), channel_id=1, source_target_pairs={{0,2},{1,3},{2,0},{3,1},{4,6},{5,7},{6,4},{7,5},{8,10},{9,11},{10,... | collective-permute-start | bytes 150536 | tf_op jit(solution)/shard_map/ppermute | solution.py:32
  17.7 2.2 %shard_map.116.refs_4_.refs_6_ = bf16[2048,1024]{1,0:T(8,128)(2,1)S(1)} custom-call(bf16[4,6272]{1,0:T(4,128)(2,1)S(1)} %shard_map.115.refs_0_, bf16[2048,2048]{1,0:T(8,128)(2,1)} %bitcast.13), custom_call_target="tpu_custom_call" | custom-call | bytes 4194304 | tf_op jit(solution)/shard_map/pallas_call | solution.py:194
  19.9 0.8 %collective-permute-done.5.refs_3_ = bf16[4,6272]{1,0:T(4,128)(2,1)S(1)} collective-permute-done((bf16[4,6272]{1,0:T(4,128)(2,1)S(1)}, bf16[4,6272]{1,0:T(4,128)(2,1)S(1)}, u32[]{:S(2)}, u32[]{:S(2)}) %collective-permute-start.5) | collective-permute-done | bytes 50208 | tf_op jit(solution)/shard_map/ppermute | solution.py:32
  20.6 1.1 %collective-permute-done.4.refs_2_ = bf16[4,6272]{1,0:T(4,128)(2,1)S(1)} collective-permute-done((bf16[4,6272]{1,0:T(4,128)(2,1)S(1)}, bf16[4,6272]{1,0:T(4,128)(2,1)S(1)}, u32[]{:S(2)}, u32[]{:S(2)}) %collective-permute-start.4) | collective-permute-done | bytes 50208 | tf_op jit(solution)/shard_map/ppermute | solution.py:32
  21.7 0.0 collective-permute-done.6.refs_1_
  21.7 0.1 collective-permute-start.7
  21.9 0.4 collective-permute-start.3
  22.3 1.5 %collective-permute-start.12 = (bf16[8,16,128]{2,1,0:T(8,128)(2,1)S(1)}, bf16[8,16,128]{2,1,0:T(8,128)(2,1)S(1)}, u32[]{:S(2)}, u32[]{:S(2)}) collective-permute-start(bf16[8,16,128]{2,1,0:T(8,128)(2,1)S(1)} %slice_add_fusion.refs_6_), channel_id=1, source_target_pairs={{0,8},{4,12},{8,0},{12,4},{1,9},{5,13},{9,1},{13,5},{2,10},{6,14},... | collective-permute-start | bytes 98312 | tf_op jit(solution)/shard_map/ppermute | solution.py:32
  23.8 0.0 collective-permute-done.3.refs_1_
  23.8 0.0 collective-permute-done.7.refs_8_
  23.8 1.9 %shard_map.119 = (bf16[4,2048]{1,0:T(4,128)(2,1)S(1)}, bf16[4,4096]{1,0:T(4,128)(2,1)S(1)}) custom-call(bf16[4,6272]{1,0:T(4,128)(2,1)S(1)} %shard_map.115.refs_0_, bf16[4,6272]{1,0:T(4,128)(2,1)S(1)} %collective-permute-done.3.refs_1_, bf16[4,6272]{1,0:T(4,128)(2,1)S(1)} %collective-permute-done.4.refs_2_, ...), custom_call_target="tpu_custom_call" | custom-call | flops 33554432 | bytes 8388608 | tf_op jit(solution)/shard_map/pallas_call | solution.py:394
  25.7 1.5 %collective-permute-start.8 = (bf16[4,4096]{1,0:T(4,128)(2,1)S(1)}, bf16[4,4096]{1,0:T(4,128)(2,1)S(1)}, u32[]{:S(2)}, u32[]{:S(2)}) collective-permute-start(bf16[4,4096]{1,0:T(4,128)(2,1)S(1)} %get-tuple-element.25), channel_id=1, source_target_pairs={{0,16},{4,20},{8,24},{12,28},{16,0},{20,4},{24,8},{28,12},{1,17},{... | collective-permute-start | bytes 98312 | tf_op jit(solution)/shard_map/ppermute | solution.py:42
  27.2 2.0 %collective-permute-start.11 = (bf16[4,2048]{1,0:T(4,128)(2,1)S(1)}, bf16[4,2048]{1,0:T(4,128)(2,1)S(1)}, u32[]{:S(2)}, u32[]{:S(2)}) collective-permute-start(bf16[4,2048]{1,0:T(4,128)(2,1)S(1)} %get-tuple-element.26), channel_id=1, source_target_pairs={{12,16},{8,20},{4,24},{0,28},{28,0},{24,4},{20,8},{16,12},{13,17},... | collective-permute-start | bytes 49160 | tf_op jit(solution)/shard_map/ppermute | solution.py:42
  29.1 1.9 %collective-permute-start.10 = (bf16[4,2048]{1,0:T(4,128)(2,1)S(1)}, bf16[4,2048]{1,0:T(4,128)(2,1)S(1)}, u32[]{:S(2)}, u32[]{:S(2)}) collective-permute-start(bf16[4,2048]{1,0:T(4,128)(2,1)S(1)} %get-tuple-element.26), channel_id=1, source_target_pairs={{8,16},{12,20},{0,24},{4,28},{24,0},{28,4},{16,8},{20,12},{9,17},{... | collective-permute-start | bytes 49160 | tf_op jit(solution)/shard_map/ppermute | solution.py:42
  31.0 1.4 %collective-permute-start.9 = (bf16[4,2048]{1,0:T(4,128)(2,1)S(1)}, bf16[4,2048]{1,0:T(4,128)(2,1)S(1)}, u32[]{:S(2)}, u32[]{:S(2)}) collective-permute-start(bf16[4,2048]{1,0:T(4,128)(2,1)S(1)} %get-tuple-element.26), channel_id=1, source_target_pairs={{4,16},{0,20},{12,24},{8,28},{20,0},{16,4},{28,8},{24,12},{5,17},{... | collective-permute-start | bytes 49160 | tf_op jit(solution)/shard_map/ppermute | solution.py:42
  32.4 0.0 collective-permute-done.12.refs_7_
  32.4 1.2 %collective-permute-done.11.refs_4_ = bf16[4,2048]{1,0:T(4,128)(2,1)S(1)} collective-permute-done((bf16[4,2048]{1,0:T(4,128)(2,1)S(1)}, bf16[4,2048]{1,0:T(4,128)(2,1)S(1)}, u32[]{:S(2)}, u32[]{:S(2)}) %collective-permute-start.11) | collective-permute-done | bytes 16416 | tf_op jit(solution)/shard_map/ppermute | solution.py:42
  33.6 1.1 %collective-permute-done.10.refs_3_ = bf16[4,2048]{1,0:T(4,128)(2,1)S(1)} collective-permute-done((bf16[4,2048]{1,0:T(4,128)(2,1)S(1)}, bf16[4,2048]{1,0:T(4,128)(2,1)S(1)}, u32[]{:S(2)}, u32[]{:S(2)}) %collective-permute-start.10) | collective-permute-done | bytes 16416 | tf_op jit(solution)/shard_map/ppermute | solution.py:42
  34.7 1.0 %collective-permute-done.9.refs_2_ = bf16[4,2048]{1,0:T(4,128)(2,1)S(1)} collective-permute-done((bf16[4,2048]{1,0:T(4,128)(2,1)S(1)}, bf16[4,2048]{1,0:T(4,128)(2,1)S(1)}, u32[]{:S(2)}, u32[]{:S(2)}) %collective-permute-start.9) | collective-permute-done | bytes 16416 | tf_op jit(solution)/shard_map/ppermute | solution.py:42
  35.6 0.0 collective-permute-done.8.refs_1_
  35.6 1.3 %shard_map.120 = (bf16[4,6272]{1,0:T(4,128)(2,1)S(1)}, bf16[4,2048]{1,0:T(4,128)(2,1)S(1)}) custom-call(f32[2,128]{1,0:T(2,128)S(1)} %get-tuple-element.17.refs_0_, bf16[4,4096]{1,0:T(4,128)(2,1)S(1)} %collective-permute-done.8.refs_1_, bf16[4,2048]{1,0:T(4,128)(2,1)S(1)} %collective-permute-done.9.refs_2_, ...), custom_call_target="tpu_custom_call" | custom-call | flops 100663296 | bytes 8388608 | tf_op jit(solution)/shard_map/pallas_call | solution.py:293
  36.9 0.0 collective-permute-start.15
  36.9 1.3 %collective-permute-start.14 = (bf16[4,6272]{1,0:T(4,128)(2,1)S(1)}, bf16[4,6272]{1,0:T(4,128)(2,1)S(1)}, u32[]{:S(2)}, u32[]{:S(2)}) collective-permute-start(bf16[4,6272]{1,0:T(4,128)(2,1)S(1)} %get-tuple-element.28.refs_0_), channel_id=1, source_target_pairs={{0,2},{1,3},{2,0},{3,1},{4,6},{5,7},{6,4},{7,5},{8,10},{9,11},{10,... | collective-permute-start | bytes 150536 | tf_op jit(solution)/shard_map/ppermute | solution.py:32
  38.2 0.6 %collective-permute-start.13 = (bf16[4,6272]{1,0:T(4,128)(2,1)S(1)}, bf16[4,6272]{1,0:T(4,128)(2,1)S(1)}, u32[]{:S(2)}, u32[]{:S(2)}) collective-permute-start(bf16[4,6272]{1,0:T(4,128)(2,1)S(1)} %get-tuple-element.28.refs_0_), channel_id=1, source_target_pairs={{0,1},{1,0},{2,3},{3,2},{4,5},{5,4},{6,7},{7,6},{8,9},{9,8},{10,11... | collective-permute-start | bytes 150536 | tf_op jit(solution)/shard_map/ppermute | solution.py:32
  38.8 2.2 %collective-permute-done.15.refs_3_ = bf16[4,6272]{1,0:T(4,128)(2,1)S(1)} collective-permute-done((bf16[4,6272]{1,0:T(4,128)(2,1)S(1)}, bf16[4,6272]{1,0:T(4,128)(2,1)S(1)}, u32[]{:S(2)}, u32[]{:S(2)}) %collective-permute-start.15) | collective-permute-done | bytes 50208 | tf_op jit(solution)/shard_map/ppermute | solution.py:32
  41.0 0.6 %collective-permute-done.14.refs_2_ = bf16[4,6272]{1,0:T(4,128)(2,1)S(1)} collective-permute-done((bf16[4,6272]{1,0:T(4,128)(2,1)S(1)}, bf16[4,6272]{1,0:T(4,128)(2,1)S(1)}, u32[]{:S(2)}, u32[]{:S(2)}) %collective-permute-start.14) | collective-permute-done | bytes 50208 | tf_op jit(solution)/shard_map/ppermute | solution.py:32
  41.6 0.0 collective-permute-done.13.refs_1_
  41.6 1.9 %shard_map.121 = (bf16[4,2048]{1,0:T(4,128)(2,1)S(1)}, bf16[4,4096]{1,0:T(4,128)(2,1)S(1)}) custom-call(bf16[4,6272]{1,0:T(4,128)(2,1)S(1)} %get-tuple-element.28.refs_0_, bf16[4,6272]{1,0:T(4,128)(2,1)S(1)} %collective-permute-done.13.refs_1_, bf16[4,6272]{1,0:T(4,128)(2,1)S(1)} %collective-permute-done.14.refs_2_, ...), custom_call_target="tpu_custom_call" | custom-call | flops 33554432 | bytes 8388608 | tf_op jit(solution)/shard_map/pallas_call | solution.py:394
  43.5 0.7 %collective-permute-start.16 = (bf16[4,4096]{1,0:T(4,128)(2,1)S(1)}, bf16[4,4096]{1,0:T(4,128)(2,1)S(1)}, u32[]{:S(2)}, u32[]{:S(2)}) collective-permute-start(bf16[4,4096]{1,0:T(4,128)(2,1)S(1)} %get-tuple-element.30), channel_id=1, source_target_pairs={{0,16},{4,20},{8,24},{12,28},{16,0},{20,4},{24,8},{28,12},{1,17},{... | collective-permute-start | bytes 98312 | tf_op jit(solution)/shard_map/ppermute | solution.py:42
  44.2 2.2 %collective-permute-start.19 = (bf16[4,2048]{1,0:T(4,128)(2,1)S(1)}, bf16[4,2048]{1,0:T(4,128)(2,1)S(1)}, u32[]{:S(2)}, u32[]{:S(2)}) collective-permute-start(bf16[4,2048]{1,0:T(4,128)(2,1)S(1)} %get-tuple-element.31), channel_id=1, source_target_pairs={{12,16},{8,20},{4,24},{0,28},{28,0},{24,4},{20,8},{16,12},{13,17},... | collective-permute-start | bytes 49160 | tf_op jit(solution)/shard_map/ppermute | solution.py:42
  46.4 1.5 %collective-permute-start.18 = (bf16[4,2048]{1,0:T(4,128)(2,1)S(1)}, bf16[4,2048]{1,0:T(4,128)(2,1)S(1)}, u32[]{:S(2)}, u32[]{:S(2)}) collective-permute-start(bf16[4,2048]{1,0:T(4,128)(2,1)S(1)} %get-tuple-element.31), channel_id=1, source_target_pairs={{8,16},{12,20},{0,24},{4,28},{24,0},{28,4},{16,8},{20,12},{9,17},{... | collective-permute-start | bytes 49160 | tf_op jit(solution)/shard_map/ppermute | solution.py:42
  47.8 2.4 %collective-permute-start.17 = (bf16[4,2048]{1,0:T(4,128)(2,1)S(1)}, bf16[4,2048]{1,0:T(4,128)(2,1)S(1)}, u32[]{:S(2)}, u32[]{:S(2)}) collective-permute-start(bf16[4,2048]{1,0:T(4,128)(2,1)S(1)} %get-tuple-element.31), channel_id=1, source_target_pairs={{4,16},{0,20},{12,24},{8,28},{20,0},{16,4},{28,8},{24,12},{5,17},{... | collective-permute-start | bytes 49160 | tf_op jit(solution)/shard_map/ppermute | solution.py:42
  50.2 0.4 collective-permute-done.19.refs_3_
  50.7 1.2 %collective-permute-done.18.refs_2_ = bf16[4,2048]{1,0:T(4,128)(2,1)S(1)} collective-permute-done((bf16[4,2048]{1,0:T(4,128)(2,1)S(1)}, bf16[4,2048]{1,0:T(4,128)(2,1)S(1)}, u32[]{:S(2)}, u32[]{:S(2)}) %collective-permute-start.18) | collective-permute-done | bytes 16416 | tf_op jit(solution)/shard_map/ppermute | solution.py:42
  51.9 0.6 %collective-permute-done.17.refs_1_ = bf16[4,2048]{1,0:T(4,128)(2,1)S(1)} collective-permute-done((bf16[4,2048]{1,0:T(4,128)(2,1)S(1)}, bf16[4,2048]{1,0:T(4,128)(2,1)S(1)}, u32[]{:S(2)}, u32[]{:S(2)}) %collective-permute-start.17) | collective-permute-done | bytes 16416 | tf_op jit(solution)/shard_map/ppermute | solution.py:42
  52.5 0.0 collective-permute-done.16.refs_0_
  52.5 0.6 %shard_map.122 = (bf16[1,4,2048]{2,1,0:T(4,128)(2,1)}, bf16[1,4,2048]{2,1,0:T(4,128)(2,1)}) custom-call(bf16[4,4096]{1,0:T(4,128)(2,1)S(1)} %collective-permute-done.16.refs_0_, bf16[4,2048]{1,0:T(4,128)(2,1)S(1)} %collective-permute-done.17.refs_1_, bf16[4,2048]{1,0:T(4,128)(2,1)S(1)} %collective-permute-done.18.refs_2_, ...), custom_call_target="tpu_custom_call" | custom-call | tf_op jit(solution)/shard_map/pallas_call | solution.py:311
  (3 shorter events, 0.0 us)
Async XLA Ops:
  2.4 11.9 %collective-permute-start = (bf16[24,16,128]{2,1,0:T(8,128)(2,1)S(1)}, bf16[24,16,128]{2,1,0:T(8,128)(2,1)S(1)}, u32[]{:S(2)}, u32[]{:S(2)}) collective-permute-start(bf16[24,16,128]{2,1,0:T(8,128)(2,1)S(1)} %get-tuple-element.20), channel_id=1, source_target_pairs={{0,4},{4,0},{8,12},{12,8},{1,5},{5,1},{9,13},{13,9},{2,6},{6,2},{1... | collective-permute-start | bytes 294920 | tf_op jit(solution)/shard_map/ppermute | solution.py:32
  5.5 7.6 %collective-permute-start.1 = (bf16[16,16,128]{2,1,0:T(8,128)(2,1)S(1)}, bf16[16,16,128]{2,1,0:T(8,128)(2,1)S(1)}, u32[]{:S(2)}, u32[]{:S(2)}) collective-permute-start(bf16[16,16,128]{2,1,0:T(8,128)(2,1)S(1)} %get-tuple-element.21), channel_id=1, source_target_pairs={{0,8},{4,12},{8,0},{12,4},{1,9},{5,13},{9,1},{13,5},{2,10},{6,14},... | collective-permute-start | bytes 196616 | tf_op jit(solution)/shard_map/ppermute | solution.py:32
  8.1 6.2 %collective-permute-start.2 = (bf16[16,16,128]{2,1,0:T(8,128)(2,1)S(1)}, bf16[16,16,128]{2,1,0:T(8,128)(2,1)S(1)}, u32[]{:S(2)}, u32[]{:S(2)}) collective-permute-start(bf16[16,16,128]{2,1,0:T(8,128)(2,1)S(1)} %get-tuple-element.22), channel_id=1, source_target_pairs={{0,12},{4,8},{8,4},{12,0},{1,13},{5,9},{9,5},{13,1},{2,14},{6,10},... | collective-permute-start | bytes 196616 | tf_op jit(solution)/shard_map/ppermute | solution.py:32
  14.3 7.5 %collective-permute-start.6 = (bf16[4,8,16,128]{3,2,1,0:T(8,128)(2,1)S(1)}, bf16[4,8,16,128]{3,2,1,0:T(8,128)(2,1)S(1)}, u32[]{:S(2)}, u32[]{:S(2)}) collective-permute-start(bf16[4,8,16,128]{3,2,1,0:T(8,128)(2,1)S(1)} %shard_map.117.refs_0_), channel_id=1, source_target_pairs={{0,2},{1,3},{2,0},{3,1},{4,6},{5,7},{6,4},{7,5},{8,10},{9,11},{10,... | collective-permute-start | bytes 393224 | tf_op jit(solution)/shard_map/ppermute | solution.py:32
  17.1 3.5 %collective-permute-start.5 = (bf16[4,6272]{1,0:T(4,128)(2,1)S(1)}, bf16[4,6272]{1,0:T(4,128)(2,1)S(1)}, u32[]{:S(2)}, u32[]{:S(2)}) collective-permute-start(bf16[4,6272]{1,0:T(4,128)(2,1)S(1)} %shard_map.115.refs_0_), channel_id=1, source_target_pairs={{0,3},{1,2},{2,1},{3,0},{4,7},{5,6},{6,5},{7,4},{8,11},{9,10},{10,... | collective-permute-start | bytes 150536 | tf_op jit(solution)/shard_map/ppermute | solution.py:32
  17.1 4.6 %collective-permute-start.4 = (bf16[4,6272]{1,0:T(4,128)(2,1)S(1)}, bf16[4,6272]{1,0:T(4,128)(2,1)S(1)}, u32[]{:S(2)}, u32[]{:S(2)}) collective-permute-start(bf16[4,6272]{1,0:T(4,128)(2,1)S(1)} %shard_map.115.refs_0_), channel_id=1, source_target_pairs={{0,2},{1,3},{2,0},{3,1},{4,6},{5,7},{6,4},{7,5},{8,10},{9,11},{10,... | collective-permute-start | bytes 150536 | tf_op jit(solution)/shard_map/ppermute | solution.py:32
  21.7 2.1 %collective-permute-start.7 = (bf16[8,8,16,128]{3,2,1,0:T(8,128)(2,1)S(1)}, bf16[8,8,16,128]{3,2,1,0:T(8,128)(2,1)S(1)}, u32[]{:S(2)}, u32[]{:S(2)}) collective-permute-start(bf16[8,8,16,128]{3,2,1,0:T(8,128)(2,1)S(1)} %bitcast.9), channel_id=1, source_target_pairs={{0,1},{1,0},{2,3},{3,2},{4,5},{5,4},{6,7},{7,6},{8,9},{9,8},{10,11... | collective-permute-start | bytes 786440 | tf_op jit(solution)/shard_map/ppermute | solution.py:32
  21.9 1.9 %collective-permute-start.3 = (bf16[4,6272]{1,0:T(4,128)(2,1)S(1)}, bf16[4,6272]{1,0:T(4,128)(2,1)S(1)}, u32[]{:S(2)}, u32[]{:S(2)}) collective-permute-start(bf16[4,6272]{1,0:T(4,128)(2,1)S(1)} %shard_map.115.refs_0_), channel_id=1, source_target_pairs={{0,1},{1,0},{2,3},{3,2},{4,5},{5,4},{6,7},{7,6},{8,9},{9,8},{10,11... | collective-permute-start | bytes 150536 | tf_op jit(solution)/shard_map/ppermute | solution.py:32
  22.3 10.1 %collective-permute-start.12 = (bf16[8,16,128]{2,1,0:T(8,128)(2,1)S(1)}, bf16[8,16,128]{2,1,0:T(8,128)(2,1)S(1)}, u32[]{:S(2)}, u32[]{:S(2)}) collective-permute-start(bf16[8,16,128]{2,1,0:T(8,128)(2,1)S(1)} %slice_add_fusion.refs_6_), channel_id=1, source_target_pairs={{0,8},{4,12},{8,0},{12,4},{1,9},{5,13},{9,1},{13,5},{2,10},{6,14},... | collective-permute-start | bytes 98312 | tf_op jit(solution)/shard_map/ppermute | solution.py:32
  25.7 10.0 %collective-permute-start.8 = (bf16[4,4096]{1,0:T(4,128)(2,1)S(1)}, bf16[4,4096]{1,0:T(4,128)(2,1)S(1)}, u32[]{:S(2)}, u32[]{:S(2)}) collective-permute-start(bf16[4,4096]{1,0:T(4,128)(2,1)S(1)} %get-tuple-element.25), channel_id=1, source_target_pairs={{0,16},{4,20},{8,24},{12,28},{16,0},{20,4},{24,8},{28,12},{1,17},{... | collective-permute-start | bytes 98312 | tf_op jit(solution)/shard_map/ppermute | solution.py:42
  27.2 6.4 %collective-permute-start.11 = (bf16[4,2048]{1,0:T(4,128)(2,1)S(1)}, bf16[4,2048]{1,0:T(4,128)(2,1)S(1)}, u32[]{:S(2)}, u32[]{:S(2)}) collective-permute-start(bf16[4,2048]{1,0:T(4,128)(2,1)S(1)} %get-tuple-element.26), channel_id=1, source_target_pairs={{12,16},{8,20},{4,24},{0,28},{28,0},{24,4},{20,8},{16,12},{13,17},... | collective-permute-start | bytes 49160 | tf_op jit(solution)/shard_map/ppermute | solution.py:42
  29.1 5.5 %collective-permute-start.10 = (bf16[4,2048]{1,0:T(4,128)(2,1)S(1)}, bf16[4,2048]{1,0:T(4,128)(2,1)S(1)}, u32[]{:S(2)}, u32[]{:S(2)}) collective-permute-start(bf16[4,2048]{1,0:T(4,128)(2,1)S(1)} %get-tuple-element.26), channel_id=1, source_target_pairs={{8,16},{12,20},{0,24},{4,28},{24,0},{28,4},{16,8},{20,12},{9,17},{... | collective-permute-start | bytes 49160 | tf_op jit(solution)/shard_map/ppermute | solution.py:42
  31.0 4.6 %collective-permute-start.9 = (bf16[4,2048]{1,0:T(4,128)(2,1)S(1)}, bf16[4,2048]{1,0:T(4,128)(2,1)S(1)}, u32[]{:S(2)}, u32[]{:S(2)}) collective-permute-start(bf16[4,2048]{1,0:T(4,128)(2,1)S(1)} %get-tuple-element.26), channel_id=1, source_target_pairs={{4,16},{0,20},{12,24},{8,28},{20,0},{16,4},{28,8},{24,12},{5,17},{... | collective-permute-start | bytes 49160 | tf_op jit(solution)/shard_map/ppermute | solution.py:42
  36.9 4.0 %collective-permute-start.15 = (bf16[4,6272]{1,0:T(4,128)(2,1)S(1)}, bf16[4,6272]{1,0:T(4,128)(2,1)S(1)}, u32[]{:S(2)}, u32[]{:S(2)}) collective-permute-start(bf16[4,6272]{1,0:T(4,128)(2,1)S(1)} %get-tuple-element.28.refs_0_), channel_id=1, source_target_pairs={{0,3},{1,2},{2,1},{3,0},{4,7},{5,6},{6,5},{7,4},{8,11},{9,10},{10,... | collective-permute-start | bytes 150536 | tf_op jit(solution)/shard_map/ppermute | solution.py:32
  36.9 4.7 %collective-permute-start.14 = (bf16[4,6272]{1,0:T(4,128)(2,1)S(1)}, bf16[4,6272]{1,0:T(4,128)(2,1)S(1)}, u32[]{:S(2)}, u32[]{:S(2)}) collective-permute-start(bf16[4,6272]{1,0:T(4,128)(2,1)S(1)} %get-tuple-element.28.refs_0_), channel_id=1, source_target_pairs={{0,2},{1,3},{2,0},{3,1},{4,6},{5,7},{6,4},{7,5},{8,10},{9,11},{10,... | collective-permute-start | bytes 150536 | tf_op jit(solution)/shard_map/ppermute | solution.py:32
  38.2 3.4 %collective-permute-start.13 = (bf16[4,6272]{1,0:T(4,128)(2,1)S(1)}, bf16[4,6272]{1,0:T(4,128)(2,1)S(1)}, u32[]{:S(2)}, u32[]{:S(2)}) collective-permute-start(bf16[4,6272]{1,0:T(4,128)(2,1)S(1)} %get-tuple-element.28.refs_0_), channel_id=1, source_target_pairs={{0,1},{1,0},{2,3},{3,2},{4,5},{5,4},{6,7},{7,6},{8,9},{9,8},{10,11... | collective-permute-start | bytes 150536 | tf_op jit(solution)/shard_map/ppermute | solution.py:32
  43.5 9.0 %collective-permute-start.16 = (bf16[4,4096]{1,0:T(4,128)(2,1)S(1)}, bf16[4,4096]{1,0:T(4,128)(2,1)S(1)}, u32[]{:S(2)}, u32[]{:S(2)}) collective-permute-start(bf16[4,4096]{1,0:T(4,128)(2,1)S(1)} %get-tuple-element.30), channel_id=1, source_target_pairs={{0,16},{4,20},{8,24},{12,28},{16,0},{20,4},{24,8},{28,12},{1,17},{... | collective-permute-start | bytes 98312 | tf_op jit(solution)/shard_map/ppermute | solution.py:42
  44.2 6.5 %collective-permute-start.19 = (bf16[4,2048]{1,0:T(4,128)(2,1)S(1)}, bf16[4,2048]{1,0:T(4,128)(2,1)S(1)}, u32[]{:S(2)}, u32[]{:S(2)}) collective-permute-start(bf16[4,2048]{1,0:T(4,128)(2,1)S(1)} %get-tuple-element.31), channel_id=1, source_target_pairs={{12,16},{8,20},{4,24},{0,28},{28,0},{24,4},{20,8},{16,12},{13,17},... | collective-permute-start | bytes 49160 | tf_op jit(solution)/shard_map/ppermute | solution.py:42
  46.4 5.5 %collective-permute-start.18 = (bf16[4,2048]{1,0:T(4,128)(2,1)S(1)}, bf16[4,2048]{1,0:T(4,128)(2,1)S(1)}, u32[]{:S(2)}, u32[]{:S(2)}) collective-permute-start(bf16[4,2048]{1,0:T(4,128)(2,1)S(1)} %get-tuple-element.31), channel_id=1, source_target_pairs={{8,16},{12,20},{0,24},{4,28},{24,0},{28,4},{16,8},{20,12},{9,17},{... | collective-permute-start | bytes 49160 | tf_op jit(solution)/shard_map/ppermute | solution.py:42
  47.8 4.6 %collective-permute-start.17 = (bf16[4,2048]{1,0:T(4,128)(2,1)S(1)}, bf16[4,2048]{1,0:T(4,128)(2,1)S(1)}, u32[]{:S(2)}, u32[]{:S(2)}) collective-permute-start(bf16[4,2048]{1,0:T(4,128)(2,1)S(1)} %get-tuple-element.31), channel_id=1, source_target_pairs={{4,16},{0,20},{12,24},{8,28},{20,0},{16,4},{28,8},{24,12},{5,17},{... | collective-permute-start | bytes 49160 | tf_op jit(solution)/shard_map/ppermute | solution.py:42

commit v16 on v12

--- a/solution.py
+++ b/solution.py
@@ -438,7 +438,7 @@
                 turns = turns + [turn ^ bit for turn in turns]
                 caches, bit = [kv, waiting], bit // 2
                 if bit:
-                    both = join(caches, kv.shape[0], pieces[2:] + [wo_right])
+                    both = join(caches, kv.shape[0], pieces[1:] + [wo_right])
                     kv = both.reshape((-1,) + both.shape[2:])
                     waiting = swapped(kv, "replica", bit)
         out, full = attend(

time: 53.1 us -> 52.8 us (level)
  waiting for transfers between devices: 11.6 us -> 10.4 us
  starting transfers between devices: 25.3 us -> 26.2 us
    ppermute x12, waiting for transfers between devices: 6.12 us -> 4.91 us  [swapped(): return lax.ppermute(block, axis, route)]
    ppermute x12, starting transfers between devices: 11.8 us -> 12.6 us  [swapped(): return lax.ppermute(block, axis, route)]
  transfers between devices with their start and end apart: 20 -> 20, of which waited for: 12 -> 11; matrix products, arithmetic and copies ran while one was open for 0% -> 0% of each run, Pallas kernels for 19% -> 19%
where the time goes in v16:
time: 52.8 us; the launch traced here: 52.6 us
  starting transfers between devices  26.2 us (50%)
  Pallas kernels  15.4 us (29%)
  waiting for transfers between devices  10.4 us (20%)
  between operations  0.7 us (1%)
    ppermute x8, starting transfers between devices, from_behind(): return lax.ppermute(block, ('section', 'tensor'), route)  13.5 us
    ppermute x12, starting transfers between devices, swapped(): return lax.ppermute(block, axis, route)  12.6 us
    pallas_call x2, Pallas kernels, hold(): pl.pallas_call(lambda *refs: hold_kernel(parts, columns, *refs), out_shap...  6.91 us
    ppermute x8, waiting for transfers between devices, from_behind(): return lax.ppermute(block, ('section', 'tensor'), route)  5.45 us
    ppermute x12, waiting for transfers between devices, swapped(): return lax.ppermute(block, axis, route)  4.91 us
    pallas_call x2, Pallas kernels, attend(): pl.pallas_call(lambda *refs: attend_kernel(dims, turns, tick, *refs), out...  3.71 us
    pallas_call x1, Pallas kernels, pack(): pl.pallas_call(lambda *refs: pack_kernel(dims, *refs), out_shape=out_shap...  1.52 us
    pallas_call x1, Pallas kernels, later_sums(): pl.pallas_call(lambda *refs: later_kernel(len(arrivals), tick, *refs), ou...  1.28 us
  transfers between devices with their start and end apart: 20, of which 11 were waited for; matrix products, arithmetic and copies ran while one was open for 0% of the time, Pallas kernels for 19%

profile of v16, /device:TPU:0, one launch (start us, length us, event | category | flops | bytes accessed | tf_op | source)
XLA Modules:
  0.0 52.6 jit_solution(10585724870350325637)
XLA Ops:
  0.6 1.5 %shard_map.113 = (bf16[24,16,128]{2,1,0:T(8,128)(2,1)S(1)}, bf16[24,16,128]{2,1,0:T(8,128)(2,1)S(1)}, bf16[16,16,128]{2,1,0:T(8,128)(2,1)S(1)}, bf16[16,16,128]{...) custom-call(s32[2,4]{1,0:T(2,128)} %refs_0_.1, ...), custom_call_target="tpu_custom_call" | custom-call | bytes 819200 | tf_op jit(solution)/shard_map/pallas_call | solution.py:127
  2.2 3.1 %collective-permute-start = (bf16[24,16,128]{2,1,0:T(8,128)(2,1)S(1)}, bf16[24,16,128]{2,1,0:T(8,128)(2,1)S(1)}, u32[]{:S(2)}, u32[]{:S(2)}) collective-permute-start(bf16[24,16,128]{2,1,0:T(8,128)(2,1)S(1)} %get-tuple-element.20), channel_id=1, source_target_pairs={{0,4},{4,0},{8,12},{12,8},{1,5},{5,1},{9,13},{13,9},{2,6},{6,2},{1... | collective-permute-start | bytes 294920 | tf_op jit(solution)/shard_map/ppermute | solution.py:32
  5.3 2.6 %collective-permute-start.1 = (bf16[16,16,128]{2,1,0:T(8,128)(2,1)S(1)}, bf16[16,16,128]{2,1,0:T(8,128)(2,1)S(1)}, u32[]{:S(2)}, u32[]{:S(2)}) collective-permute-start(bf16[16,16,128]{2,1,0:T(8,128)(2,1)S(1)} %get-tuple-element.21), channel_id=1, source_target_pairs={{0,8},{4,12},{8,0},{12,4},{1,9},{5,13},{9,1},{13,5},{2,10},{6,14},... | collective-permute-start | bytes 196616 | tf_op jit(solution)/shard_map/ppermute | solution.py:32
  7.8 0.0 collective-permute-start.2
  7.8 4.7 %shard_map.114 = (bf16[2048,2048]{1,0:T(8,128)(2,1)S(1)}, bf16[2048,1024]{1,0:T(8,128)(2,1)S(1)}) custom-call(bf16[24,16,128]{2,1,0:T(8,128)(2,1)S(1)} %get-tuple-element.19.refs_0_.refs_2_, bf16[2048,2048]{1,0:T(8,128)(2,1)} %bitcast.14, bf16[2048,2048]{1,0:T(8,128)(2,1)} %bitcast.12), custom_call_target="tpu_custom_call" | custom-call | bytes 12582912 | tf_op jit(solution)/shard_map/pallas_call | solution.py:180
  12.5 0.3 collective-permute-done.1.refs_4_.refs_2_
  12.9 1.2 %collective-permute-done.2.refs_5_.refs_3_ = bf16[16,16,128]{2,1,0:T(8,128)(2,1)S(1)} collective-permute-done((bf16[16,16,128]{2,1,0:T(8,128)(2,1)S(1)}, bf16[16,16,128]{2,1,0:T(8,128)(2,1)S(1)}, u32[]{:S(2)}, u32[]{:S(2)}) %collective-permute-start.2) | collective-permute-done | bytes 65568 | tf_op jit(solution)/shard_map/ppermute | solution.py:32
  14.0 0.0 collective-permute-done.refs_3_.refs_1_
  14.0 1.6 %collective-permute-start.6 = (bf16[4,8,16,128]{3,2,1,0:T(8,128)(2,1)S(1)}, bf16[4,8,16,128]{3,2,1,0:T(8,128)(2,1)S(1)}, u32[]{:S(2)}, u32[]{:S(2)}) collective-permute-start(bf16[4,8,16,128]{3,2,1,0:T(8,128)(2,1)S(1)} %shard_map.117.refs_0_), channel_id=1, source_target_pairs={{0,2},{1,3},{2,0},{3,1},{4,6},{5,7},{6,4},{7,5},{8,10},{9,11},{10,... | collective-permute-start | bytes 393224 | tf_op jit(solution)/shard_map/ppermute | solution.py:32
  15.6 1.3 %shard_map.115.refs_0_ = bf16[4,6272]{1,0:T(4,128)(2,1)S(1)} custom-call(f32[2,128]{1,0:T(2,128)S(1)} %get-tuple-element.17.refs_0_, bf16[4,2048]{1,0:T(4,128)(2,1)S(1)} %get-tuple-element.18.refs_1_.refs_4_, bf16[24,16,128]{2,1,0:T(8,128)(2,1)S(1)} %get-tuple-element.19.refs_0_.refs_2_, bf16[24,16,128]{2,1,0:T(8,128)(2,1)S(1)} %collective-permute-done.refs_3_.refs_1_, ...), custom_call_target="tpu_custom_call" | custom-call | flops 100663296 | bytes 8388608 | tf_op jit(solution)/shard_map/pallas_call | solution.py:235
  16.9 0.0 collective-permute-start.5
  16.9 0.6 %collective-permute-start.4 = (bf16[4,6272]{1,0:T(4,128)(2,1)S(1)}, bf16[4,6272]{1,0:T(4,128)(2,1)S(1)}, u32[]{:S(2)}, u32[]{:S(2)}) collective-permute-start(bf16[4,6272]{1,0:T(4,128)(2,1)S(1)} %shard_map.115.refs_0_), channel_id=1, source_target_pairs={{0,2},{1,3},{2,0},{3,1},{4,6},{5,7},{6,4},{7,5},{8,10},{9,11},{10,... | collective-permute-start | bytes 150536 | tf_op jit(solution)/shard_map/ppermute | solution.py:32
  17.4 1.3 %collective-permute-start.3 = (bf16[4,6272]{1,0:T(4,128)(2,1)S(1)}, bf16[4,6272]{1,0:T(4,128)(2,1)S(1)}, u32[]{:S(2)}, u32[]{:S(2)}) collective-permute-start(bf16[4,6272]{1,0:T(4,128)(2,1)S(1)} %shard_map.115.refs_0_), channel_id=1, source_target_pairs={{0,1},{1,0},{2,3},{3,2},{4,5},{5,4},{6,7},{7,6},{8,9},{9,8},{10,11... | collective-permute-start | bytes 150536 | tf_op jit(solution)/shard_map/ppermute | solution.py:32
  18.7 2.2 %shard_map.116.refs_5_.refs_6_ = bf16[2048,1024]{1,0:T(8,128)(2,1)S(1)} custom-call(bf16[4,6272]{1,0:T(4,128)(2,1)S(1)} %shard_map.115.refs_0_, bf16[2048,2048]{1,0:T(8,128)(2,1)} %bitcast.13), custom_call_target="tpu_custom_call" | custom-call | bytes 4194304 | tf_op jit(solution)/shard_map/pallas_call | solution.py:180
  21.0 0.0 collective-permute-done.5.refs_4_.refs_3_
  21.0 0.5 collective-permute-done.4.refs_3_.refs_2_
  21.5 0.0 collective-permute-done.3.refs_2_.refs_1_
  21.5 0.0 collective-permute-done.6.refs_1_
  21.5 0.1 collective-permute-start.7
  21.7 1.5 %collective-permute-start.12 = (bf16[8,16,128]{2,1,0:T(8,128)(2,1)S(1)}, bf16[8,16,128]{2,1,0:T(8,128)(2,1)S(1)}, u32[]{:S(2)}, u32[]{:S(2)}) collective-permute-start(bf16[8,16,128]{2,1,0:T(8,128)(2,1)S(1)} %slice_add_fusion.refs_6_), channel_id=1, source_target_pairs={{0,8},{4,12},{8,0},{12,4},{1,9},{5,13},{9,1},{13,5},{2,10},{6,14},... | collective-permute-start | bytes 98312 | tf_op jit(solution)/shard_map/ppermute | solution.py:32
  23.2 0.0 collective-permute-done.7.refs_8_
  23.2 1.9 %shard_map.119 = (bf16[4,2048]{1,0:T(4,128)(2,1)S(1)}, bf16[4,4096]{1,0:T(4,128)(2,1)S(1)}) custom-call(bf16[4,6272]{1,0:T(4,128)(2,1)S(1)} %shard_map.115.refs_0_, bf16[4,6272]{1,0:T(4,128)(2,1)S(1)} %collective-permute-done.3.refs_2_.refs_1_, bf16[4,6272]{1,0:T(4,128)(2,1)S(1)} %collective-permute-done.4.refs_3_.refs_2_, ...), custom_call_target="tpu_custom_call" | custom-call | flops 33554432 | bytes 8388608 | tf_op jit(solution)/shard_map/pallas_call | solution.py:380
  25.0 1.5 %collective-permute-start.8 = (bf16[4,4096]{1,0:T(4,128)(2,1)S(1)}, bf16[4,4096]{1,0:T(4,128)(2,1)S(1)}, u32[]{:S(2)}, u32[]{:S(2)}) collective-permute-start(bf16[4,4096]{1,0:T(4,128)(2,1)S(1)} %get-tuple-element.25), channel_id=1, source_target_pairs={{0,16},{4,20},{8,24},{12,28},{16,0},{20,4},{24,8},{28,12},{1,17},{... | collective-permute-start | bytes 98312 | tf_op jit(solution)/shard_map/ppermute | solution.py:42
  26.5 2.3 %collective-permute-start.11 = (bf16[4,2048]{1,0:T(4,128)(2,1)S(1)}, bf16[4,2048]{1,0:T(4,128)(2,1)S(1)}, u32[]{:S(2)}, u32[]{:S(2)}) collective-permute-start(bf16[4,2048]{1,0:T(4,128)(2,1)S(1)} %get-tuple-element.26), channel_id=1, source_target_pairs={{12,16},{8,20},{4,24},{0,28},{28,0},{24,4},{20,8},{16,12},{13,17},... | collective-permute-start | bytes 49160 | tf_op jit(solution)/shard_map/ppermute | solution.py:42
  28.8 1.5 %collective-permute-start.10 = (bf16[4,2048]{1,0:T(4,128)(2,1)S(1)}, bf16[4,2048]{1,0:T(4,128)(2,1)S(1)}, u32[]{:S(2)}, u32[]{:S(2)}) collective-permute-start(bf16[4,2048]{1,0:T(4,128)(2,1)S(1)} %get-tuple-element.26), channel_id=1, source_target_pairs={{8,16},{12,20},{0,24},{4,28},{24,0},{28,4},{16,8},{20,12},{9,17},{... | collective-permute-start | bytes 49160 | tf_op jit(solution)/shard_map/ppermute | solution.py:42
  30.4 1.4 %collective-permute-start.9 = (bf16[4,2048]{1,0:T(4,128)(2,1)S(1)}, bf16[4,2048]{1,0:T(4,128)(2,1)S(1)}, u32[]{:S(2)}, u32[]{:S(2)}) collective-permute-start(bf16[4,2048]{1,0:T(4,128)(2,1)S(1)} %get-tuple-element.26), channel_id=1, source_target_pairs={{4,16},{0,20},{12,24},{8,28},{20,0},{16,4},{28,8},{24,12},{5,17},{... | collective-permute-start | bytes 49160 | tf_op jit(solution)/shard_map/ppermute | solution.py:42
  31.8 0.0 collective-permute-done.12.refs_7_
  31.8 1.2 %collective-permute-done.11.refs_4_ = bf16[4,2048]{1,0:T(4,128)(2,1)S(1)} collective-permute-done((bf16[4,2048]{1,0:T(4,128)(2,1)S(1)}, bf16[4,2048]{1,0:T(4,128)(2,1)S(1)}, u32[]{:S(2)}, u32[]{:S(2)}) %collective-permute-start.11) | collective-permute-done | bytes 16416 | tf_op jit(solution)/shard_map/ppermute | solution.py:42
  33.0 1.4 %collective-permute-done.10.refs_3_ = bf16[4,2048]{1,0:T(4,128)(2,1)S(1)} collective-permute-done((bf16[4,2048]{1,0:T(4,128)(2,1)S(1)}, bf16[4,2048]{1,0:T(4,128)(2,1)S(1)}, u32[]{:S(2)}, u32[]{:S(2)}) %collective-permute-start.10) | collective-permute-done | bytes 16416 | tf_op jit(solution)/shard_map/ppermute | solution.py:42
  34.4 0.6 %collective-permute-done.9.refs_2_ = bf16[4,2048]{1,0:T(4,128)(2,1)S(1)} collective-permute-done((bf16[4,2048]{1,0:T(4,128)(2,1)S(1)}, bf16[4,2048]{1,0:T(4,128)(2,1)S(1)}, u32[]{:S(2)}, u32[]{:S(2)}) %collective-permute-start.9) | collective-permute-done | bytes 16416 | tf_op jit(solution)/shard_map/ppermute | solution.py:42
  35.0 0.0 collective-permute-done.8.refs_1_
  35.0 1.3 %shard_map.120 = (bf16[4,6272]{1,0:T(4,128)(2,1)S(1)}, bf16[4,2048]{1,0:T(4,128)(2,1)S(1)}) custom-call(f32[2,128]{1,0:T(2,128)S(1)} %get-tuple-element.17.refs_0_, bf16[4,4096]{1,0:T(4,128)(2,1)S(1)} %collective-permute-done.8.refs_1_, bf16[4,2048]{1,0:T(4,128)(2,1)S(1)} %collective-permute-done.9.refs_2_, ...), custom_call_target="tpu_custom_call" | custom-call | flops 100663296 | bytes 8388608 | tf_op jit(solution)/shard_map/pallas_call | solution.py:279
  36.3 0.0 collective-permute-start.15
  36.3 1.3 %collective-permute-start.14 = (bf16[4,6272]{1,0:T(4,128)(2,1)S(1)}, bf16[4,6272]{1,0:T(4,128)(2,1)S(1)}, u32[]{:S(2)}, u32[]{:S(2)}) collective-permute-start(bf16[4,6272]{1,0:T(4,128)(2,1)S(1)} %get-tuple-element.28.refs_0_), channel_id=1, source_target_pairs={{0,2},{1,3},{2,0},{3,1},{4,6},{5,7},{6,4},{7,5},{8,10},{9,11},{10,... | collective-permute-start | bytes 150536 | tf_op jit(solution)/shard_map/ppermute | solution.py:32
  37.6 0.5 %collective-permute-start.13 = (bf16[4,6272]{1,0:T(4,128)(2,1)S(1)}, bf16[4,6272]{1,0:T(4,128)(2,1)S(1)}, u32[]{:S(2)}, u32[]{:S(2)}) collective-permute-start(bf16[4,6272]{1,0:T(4,128)(2,1)S(1)} %get-tuple-element.28.refs_0_), channel_id=1, source_target_pairs={{0,1},{1,0},{2,3},{3,2},{4,5},{5,4},{6,7},{7,6},{8,9},{9,8},{10,11... | collective-permute-start | bytes 150536 | tf_op jit(solution)/shard_map/ppermute | solution.py:32
  38.2 2.2 %collective-permute-done.15.refs_3_ = bf16[4,6272]{1,0:T(4,128)(2,1)S(1)} collective-permute-done((bf16[4,6272]{1,0:T(4,128)(2,1)S(1)}, bf16[4,6272]{1,0:T(4,128)(2,1)S(1)}, u32[]{:S(2)}, u32[]{:S(2)}) %collective-permute-start.15) | collective-permute-done | bytes 50208 | tf_op jit(solution)/shard_map/ppermute | solution.py:32
  40.4 0.7 %collective-permute-done.14.refs_2_ = bf16[4,6272]{1,0:T(4,128)(2,1)S(1)} collective-permute-done((bf16[4,6272]{1,0:T(4,128)(2,1)S(1)}, bf16[4,6272]{1,0:T(4,128)(2,1)S(1)}, u32[]{:S(2)}, u32[]{:S(2)}) %collective-permute-start.14) | collective-permute-done | bytes 50208 | tf_op jit(solution)/shard_map/ppermute | solution.py:32
  41.1 0.0 collective-permute-done.13.refs_1_
  41.1 1.9 %shard_map.121 = (bf16[4,2048]{1,0:T(4,128)(2,1)S(1)}, bf16[4,4096]{1,0:T(4,128)(2,1)S(1)}) custom-call(bf16[4,6272]{1,0:T(4,128)(2,1)S(1)} %get-tuple-element.28.refs_0_, bf16[4,6272]{1,0:T(4,128)(2,1)S(1)} %collective-permute-done.13.refs_1_, bf16[4,6272]{1,0:T(4,128)(2,1)S(1)} %collective-permute-done.14.refs_2_, ...), custom_call_target="tpu_custom_call" | custom-call | flops 33554432 | bytes 8388608 | tf_op jit(solution)/shard_map/pallas_call | solution.py:380
  42.9 0.8 %collective-permute-start.16 = (bf16[4,4096]{1,0:T(4,128)(2,1)S(1)}, bf16[4,4096]{1,0:T(4,128)(2,1)S(1)}, u32[]{:S(2)}, u32[]{:S(2)}) collective-permute-start(bf16[4,4096]{1,0:T(4,128)(2,1)S(1)} %get-tuple-element.30), channel_id=1, source_target_pairs={{0,16},{4,20},{8,24},{12,28},{16,0},{20,4},{24,8},{28,12},{1,17},{... | collective-permute-start | bytes 98312 | tf_op jit(solution)/shard_map/ppermute | solution.py:42
  43.7 2.1 %collective-permute-start.19 = (bf16[4,2048]{1,0:T(4,128)(2,1)S(1)}, bf16[4,2048]{1,0:T(4,128)(2,1)S(1)}, u32[]{:S(2)}, u32[]{:S(2)}) collective-permute-start(bf16[4,2048]{1,0:T(4,128)(2,1)S(1)} %get-tuple-element.31), channel_id=1, source_target_pairs={{12,16},{8,20},{4,24},{0,28},{28,0},{24,4},{20,8},{16,12},{13,17},... | collective-permute-start | bytes 49160 | tf_op jit(solution)/shard_map/ppermute | solution.py:42
  45.8 1.5 %collective-permute-start.18 = (bf16[4,2048]{1,0:T(4,128)(2,1)S(1)}, bf16[4,2048]{1,0:T(4,128)(2,1)S(1)}, u32[]{:S(2)}, u32[]{:S(2)}) collective-permute-start(bf16[4,2048]{1,0:T(4,128)(2,1)S(1)} %get-tuple-element.31), channel_id=1, source_target_pairs={{8,16},{12,20},{0,24},{4,28},{24,0},{28,4},{16,8},{20,12},{9,17},{... | collective-permute-start | bytes 49160 | tf_op jit(solution)/shard_map/ppermute | solution.py:42
  47.3 2.4 %collective-permute-start.17 = (bf16[4,2048]{1,0:T(4,128)(2,1)S(1)}, bf16[4,2048]{1,0:T(4,128)(2,1)S(1)}, u32[]{:S(2)}, u32[]{:S(2)}) collective-permute-start(bf16[4,2048]{1,0:T(4,128)(2,1)S(1)} %get-tuple-element.31), channel_id=1, source_target_pairs={{4,16},{0,20},{12,24},{8,28},{20,0},{16,4},{28,8},{24,12},{5,17},{... | collective-permute-start | bytes 49160 | tf_op jit(solution)/shard_map/ppermute | solution.py:42
  49.7 0.5 collective-permute-done.19.refs_3_
  50.2 1.2 %collective-permute-done.18.refs_2_ = bf16[4,2048]{1,0:T(4,128)(2,1)S(1)} collective-permute-done((bf16[4,2048]{1,0:T(4,128)(2,1)S(1)}, bf16[4,2048]{1,0:T(4,128)(2,1)S(1)}, u32[]{:S(2)}, u32[]{:S(2)}) %collective-permute-start.18) | collective-permute-done | bytes 16416 | tf_op jit(solution)/shard_map/ppermute | solution.py:42
  51.4 0.6 %collective-permute-done.17.refs_1_ = bf16[4,2048]{1,0:T(4,128)(2,1)S(1)} collective-permute-done((bf16[4,2048]{1,0:T(4,128)(2,1)S(1)}, bf16[4,2048]{1,0:T(4,128)(2,1)S(1)}, u32[]{:S(2)}, u32[]{:S(2)}) %collective-permute-start.17) | collective-permute-done | bytes 16416 | tf_op jit(solution)/shard_map/ppermute | solution.py:42
  51.9 0.0 collective-permute-done.16.refs_0_
  51.9 0.6 %shard_map.122 = (bf16[1,4,2048]{2,1,0:T(4,128)(2,1)}, bf16[1,4,2048]{2,1,0:T(4,128)(2,1)}) custom-call(bf16[4,4096]{1,0:T(4,128)(2,1)S(1)} %collective-permute-done.16.refs_0_, bf16[4,2048]{1,0:T(4,128)(2,1)S(1)} %collective-permute-done.17.refs_1_, bf16[4,2048]{1,0:T(4,128)(2,1)S(1)} %collective-permute-done.18.refs_2_, ...), custom_call_target="tpu_custom_call" | custom-call | tf_op jit(solution)/shard_map/pallas_call | solution.py:297
  (3 shorter events, 0.0 us)
Async XLA Ops:
  2.2 11.9 %collective-permute-start = (bf16[24,16,128]{2,1,0:T(8,128)(2,1)S(1)}, bf16[24,16,128]{2,1,0:T(8,128)(2,1)S(1)}, u32[]{:S(2)}, u32[]{:S(2)}) collective-permute-start(bf16[24,16,128]{2,1,0:T(8,128)(2,1)S(1)} %get-tuple-element.20), channel_id=1, source_target_pairs={{0,4},{4,0},{8,12},{12,8},{1,5},{5,1},{9,13},{13,9},{2,6},{6,2},{1... | collective-permute-start | bytes 294920 | tf_op jit(solution)/shard_map/ppermute | solution.py:32
  5.3 7.6 %collective-permute-start.1 = (bf16[16,16,128]{2,1,0:T(8,128)(2,1)S(1)}, bf16[16,16,128]{2,1,0:T(8,128)(2,1)S(1)}, u32[]{:S(2)}, u32[]{:S(2)}) collective-permute-start(bf16[16,16,128]{2,1,0:T(8,128)(2,1)S(1)} %get-tuple-element.21), channel_id=1, source_target_pairs={{0,8},{4,12},{8,0},{12,4},{1,9},{5,13},{9,1},{13,5},{2,10},{6,14},... | collective-permute-start | bytes 196616 | tf_op jit(solution)/shard_map/ppermute | solution.py:32
  7.8 6.2 %collective-permute-start.2 = (bf16[16,16,128]{2,1,0:T(8,128)(2,1)S(1)}, bf16[16,16,128]{2,1,0:T(8,128)(2,1)S(1)}, u32[]{:S(2)}, u32[]{:S(2)}) collective-permute-start(bf16[16,16,128]{2,1,0:T(8,128)(2,1)S(1)} %get-tuple-element.22), channel_id=1, source_target_pairs={{0,12},{4,8},{8,4},{12,0},{1,13},{5,9},{9,5},{13,1},{2,14},{6,10},... | collective-permute-start | bytes 196616 | tf_op jit(solution)/shard_map/ppermute | solution.py:32
  14.0 7.5 %collective-permute-start.6 = (bf16[4,8,16,128]{3,2,1,0:T(8,128)(2,1)S(1)}, bf16[4,8,16,128]{3,2,1,0:T(8,128)(2,1)S(1)}, u32[]{:S(2)}, u32[]{:S(2)}) collective-permute-start(bf16[4,8,16,128]{3,2,1,0:T(8,128)(2,1)S(1)} %shard_map.117.refs_0_), channel_id=1, source_target_pairs={{0,2},{1,3},{2,0},{3,1},{4,6},{5,7},{6,4},{7,5},{8,10},{9,11},{10,... | collective-permute-start | bytes 393224 | tf_op jit(solution)/shard_map/ppermute | solution.py:32
  16.9 4.1 %collective-permute-start.5 = (bf16[4,6272]{1,0:T(4,128)(2,1)S(1)}, bf16[4,6272]{1,0:T(4,128)(2,1)S(1)}, u32[]{:S(2)}, u32[]{:S(2)}) collective-permute-start(bf16[4,6272]{1,0:T(4,128)(2,1)S(1)} %shard_map.115.refs_0_), channel_id=1, source_target_pairs={{0,3},{1,2},{2,1},{3,0},{4,7},{5,6},{6,5},{7,4},{8,11},{9,10},{10,... | collective-permute-start | bytes 150536 | tf_op jit(solution)/shard_map/ppermute | solution.py:32
  16.9 4.6 %collective-permute-start.4 = (bf16[4,6272]{1,0:T(4,128)(2,1)S(1)}, bf16[4,6272]{1,0:T(4,128)(2,1)S(1)}, u32[]{:S(2)}, u32[]{:S(2)}) collective-permute-start(bf16[4,6272]{1,0:T(4,128)(2,1)S(1)} %shard_map.115.refs_0_), channel_id=1, source_target_pairs={{0,2},{1,3},{2,0},{3,1},{4,6},{5,7},{6,4},{7,5},{8,10},{9,11},{10,... | collective-permute-start | bytes 150536 | tf_op jit(solution)/shard_map/ppermute | solution.py:32
  17.4 4.1 %collective-permute-start.3 = (bf16[4,6272]{1,0:T(4,128)(2,1)S(1)}, bf16[4,6272]{1,0:T(4,128)(2,1)S(1)}, u32[]{:S(2)}, u32[]{:S(2)}) collective-permute-start(bf16[4,6272]{1,0:T(4,128)(2,1)S(1)} %shard_map.115.refs_0_), channel_id=1, source_target_pairs={{0,1},{1,0},{2,3},{3,2},{4,5},{5,4},{6,7},{7,6},{8,9},{9,8},{10,11... | collective-permute-start | bytes 150536 | tf_op jit(solution)/shard_map/ppermute | solution.py:32
  21.5 1.6 %collective-permute-start.7 = (bf16[8,8,16,128]{3,2,1,0:T(8,128)(2,1)S(1)}, bf16[8,8,16,128]{3,2,1,0:T(8,128)(2,1)S(1)}, u32[]{:S(2)}, u32[]{:S(2)}) collective-permute-start(bf16[8,8,16,128]{3,2,1,0:T(8,128)(2,1)S(1)} %bitcast.9), channel_id=1, source_target_pairs={{0,1},{1,0},{2,3},{3,2},{4,5},{5,4},{6,7},{7,6},{8,9},{9,8},{10,11... | collective-permute-start | bytes 786440 | tf_op jit(solution)/shard_map/ppermute | solution.py:32
  21.7 10.1 %collective-permute-start.12 = (bf16[8,16,128]{2,1,0:T(8,128)(2,1)S(1)}, bf16[8,16,128]{2,1,0:T(8,128)(2,1)S(1)}, u32[]{:S(2)}, u32[]{:S(2)}) collective-permute-start(bf16[8,16,128]{2,1,0:T(8,128)(2,1)S(1)} %slice_add_fusion.refs_6_), channel_id=1, source_target_pairs={{0,8},{4,12},{8,0},{12,4},{1,9},{5,13},{9,1},{13,5},{2,10},{6,14},... | collective-permute-start | bytes 98312 | tf_op jit(solution)/shard_map/ppermute | solution.py:32
  25.0 10.0 %collective-permute-start.8 = (bf16[4,4096]{1,0:T(4,128)(2,1)S(1)}, bf16[4,4096]{1,0:T(4,128)(2,1)S(1)}, u32[]{:S(2)}, u32[]{:S(2)}) collective-permute-start(bf16[4,4096]{1,0:T(4,128)(2,1)S(1)} %get-tuple-element.25), channel_id=1, source_target_pairs={{0,16},{4,20},{8,24},{12,28},{16,0},{20,4},{24,8},{28,12},{1,17},{... | collective-permute-start | bytes 98312 | tf_op jit(solution)/shard_map/ppermute | solution.py:42
  26.5 6.4 %collective-permute-start.11 = (bf16[4,2048]{1,0:T(4,128)(2,1)S(1)}, bf16[4,2048]{1,0:T(4,128)(2,1)S(1)}, u32[]{:S(2)}, u32[]{:S(2)}) collective-permute-start(bf16[4,2048]{1,0:T(4,128)(2,1)S(1)} %get-tuple-element.26), channel_id=1, source_target_pairs={{12,16},{8,20},{4,24},{0,28},{28,0},{24,4},{20,8},{16,12},{13,17},... | collective-permute-start | bytes 49160 | tf_op jit(solution)/shard_map/ppermute | solution.py:42
  28.8 5.5 %collective-permute-start.10 = (bf16[4,2048]{1,0:T(4,128)(2,1)S(1)}, bf16[4,2048]{1,0:T(4,128)(2,1)S(1)}, u32[]{:S(2)}, u32[]{:S(2)}) collective-permute-start(bf16[4,2048]{1,0:T(4,128)(2,1)S(1)} %get-tuple-element.26), channel_id=1, source_target_pairs={{8,16},{12,20},{0,24},{4,28},{24,0},{28,4},{16,8},{20,12},{9,17},{... | collective-permute-start | bytes 49160 | tf_op jit(solution)/shard_map/ppermute | solution.py:42
  30.4 4.6 %collective-permute-start.9 = (bf16[4,2048]{1,0:T(4,128)(2,1)S(1)}, bf16[4,2048]{1,0:T(4,128)(2,1)S(1)}, u32[]{:S(2)}, u32[]{:S(2)}) collective-permute-start(bf16[4,2048]{1,0:T(4,128)(2,1)S(1)} %get-tuple-element.26), channel_id=1, source_target_pairs={{4,16},{0,20},{12,24},{8,28},{20,0},{16,4},{28,8},{24,12},{5,17},{... | collective-permute-start | bytes 49160 | tf_op jit(solution)/shard_map/ppermute | solution.py:42
  36.3 4.1 %collective-permute-start.15 = (bf16[4,6272]{1,0:T(4,128)(2,1)S(1)}, bf16[4,6272]{1,0:T(4,128)(2,1)S(1)}, u32[]{:S(2)}, u32[]{:S(2)}) collective-permute-start(bf16[4,6272]{1,0:T(4,128)(2,1)S(1)} %get-tuple-element.28.refs_0_), channel_id=1, source_target_pairs={{0,3},{1,2},{2,1},{3,0},{4,7},{5,6},{6,5},{7,4},{8,11},{9,10},{10,... | collective-permute-start | bytes 150536 | tf_op jit(solution)/shard_map/ppermute | solution.py:32
  36.3 4.8 %collective-permute-start.14 = (bf16[4,6272]{1,0:T(4,128)(2,1)S(1)}, bf16[4,6272]{1,0:T(4,128)(2,1)S(1)}, u32[]{:S(2)}, u32[]{:S(2)}) collective-permute-start(bf16[4,6272]{1,0:T(4,128)(2,1)S(1)} %get-tuple-element.28.refs_0_), channel_id=1, source_target_pairs={{0,2},{1,3},{2,0},{3,1},{4,6},{5,7},{6,4},{7,5},{8,10},{9,11},{10,... | collective-permute-start | bytes 150536 | tf_op jit(solution)/shard_map/ppermute | solution.py:32
  37.6 3.5 %collective-permute-start.13 = (bf16[4,6272]{1,0:T(4,128)(2,1)S(1)}, bf16[4,6272]{1,0:T(4,128)(2,1)S(1)}, u32[]{:S(2)}, u32[]{:S(2)}) collective-permute-start(bf16[4,6272]{1,0:T(4,128)(2,1)S(1)} %get-tuple-element.28.refs_0_), channel_id=1, source_target_pairs={{0,1},{1,0},{2,3},{3,2},{4,5},{5,4},{6,7},{7,6},{8,9},{9,8},{10,11... | collective-permute-start | bytes 150536 | tf_op jit(solution)/shard_map/ppermute | solution.py:32
  42.9 9.0 %collective-permute-start.16 = (bf16[4,4096]{1,0:T(4,128)(2,1)S(1)}, bf16[4,4096]{1,0:T(4,128)(2,1)S(1)}, u32[]{:S(2)}, u32[]{:S(2)}) collective-permute-start(bf16[4,4096]{1,0:T(4,128)(2,1)S(1)} %get-tuple-element.30), channel_id=1, source_target_pairs={{0,16},{4,20},{8,24},{12,28},{16,0},{20,4},{24,8},{28,12},{1,17},{... | collective-permute-start | bytes 98312 | tf_op jit(solution)/shard_map/ppermute | solution.py:42
  43.7 6.4 %collective-permute-start.19 = (bf16[4,2048]{1,0:T(4,128)(2,1)S(1)}, bf16[4,2048]{1,0:T(4,128)(2,1)S(1)}, u32[]{:S(2)}, u32[]{:S(2)}) collective-permute-start(bf16[4,2048]{1,0:T(4,128)(2,1)S(1)} %get-tuple-element.31), channel_id=1, source_target_pairs={{12,16},{8,20},{4,24},{0,28},{28,0},{24,4},{20,8},{16,12},{13,17},... | collective-permute-start | bytes 49160 | tf_op jit(solution)/shard_map/ppermute | solution.py:42
  45.8 5.5 %collective-permute-start.18 = (bf16[4,2048]{1,0:T(4,128)(2,1)S(1)}, bf16[4,2048]{1,0:T(4,128)(2,1)S(1)}, u32[]{:S(2)}, u32[]{:S(2)}) collective-permute-start(bf16[4,2048]{1,0:T(4,128)(2,1)S(1)} %get-tuple-element.31), channel_id=1, source_target_pairs={{8,16},{12,20},{0,24},{4,28},{24,0},{28,4},{16,8},{20,12},{9,17},{... | collective-permute-start | bytes 49160 | tf_op jit(solution)/shard_map/ppermute | solution.py:42
  47.3 4.6 %collective-permute-start.17 = (bf16[4,2048]{1,0:T(4,128)(2,1)S(1)}, bf16[4,2048]{1,0:T(4,128)(2,1)S(1)}, u32[]{:S(2)}, u32[]{:S(2)}) collective-permute-start(bf16[4,2048]{1,0:T(4,128)(2,1)S(1)} %get-tuple-element.31), channel_id=1, source_target_pairs={{4,16},{0,20},{12,24},{8,28},{20,0},{16,4},{28,8},{24,12},{5,17},{... | collective-permute-start | bytes 49160 | tf_op jit(solution)/shard_map/ppermute | solution.py:42
